TPU v7x, 32 devices: a whole 2x2x4 slice. The times are simulated.
32 devices in a mesh: job: 2 (over x), gddi: 4 (over y, core), intra: 4 (over z).
Axes of the slice: x: 2, y: 2, z: 4, core: 2. Of those that a mesh axis runs over, the one named last changes fastest.
Arguments:
- density: bfloat16 [64, 256, 256], P(('job', 'gddi', 'intra')), parts along dimension 0, as said below
- h_core: bfloat16 [64, 256, 256], P(('job', 'gddi', 'intra')), parts along dimension 0, may hold values from -6 to 6
- esp_block: bfloat16 [64, 8, 256, 256], P(('job', 'gddi'), 'intra'), parts along dimension 0, may hold values from -0.1875 to 0.1875
- nbr: int32 [64, 8], P('job'), parts along dimension 0, may hold values from 0 to 31, as said below
Outputs:
- fock: float32 [64, 256, 256], P(('job', 'gddi', 'intra')), parts along dimension 0
There are 2 independent parts, one for each index of `job`. A program takes and returns all parts, laid end to end along the dimension named above; each array names one. Nothing has to cross between parts.
Inputs may be any that keep to these rules, and one draw needn't show every extreme that they name: nbr[I, c] is never I. Group g holds fragments g * 8 to (g + 1) * 8 - 1. For a group h and d of 0 to 3, take the 16 pairs of fragments of group h with slots d * 2 to (d + 1) * 2 - 1: at most 8 of them name fragments of any one group, and they name at most 4 distinct fragments of any one group; both bounds are reached for every such set of pairs. `density`: symmetric.
All inputs are finite; a program needn't handle non-finite values.
Results may differ from a plain program's by a relative error of at most 0.0003.
Values may be sent and summed in bfloat16 or wider, within the bound.
No kernel may reach another device: no remote copies, remote signals or barrier semaphores. Data moves between devices by JAX's collectives and lax.ppermute only.
A program may use at most 128 MiB of HBM per device.

v0:
```python
import jax
import jax.numpy as jnp
from jax import lax
from jax.sharding import PartitionSpec as P


def local(density, h_core, esp_block, nbr):
    group_count = lax.axis_size("gddi")
    lane_count = lax.axis_size("intra")
    my_group = lax.axis_index("gddi")
    my_lane = lax.axis_index("intra")
    mono_dev = density.shape[0]
    basis = density.shape[1]
    mono_grp = mono_dev * lane_count
    slot_dev = esp_block.shape[1]
    pairs = mono_grp * slot_dev
    distinct_cap = pairs // group_count
    group_dens = lax.all_gather(density, "intra", axis=0, tiled=True).reshape(
        mono_grp, basis * basis
    )
    neighbour_table = nbr.reshape(group_count, mono_grp, lane_count * slot_dev)
    slot_ids = lax.dynamic_slice_in_dim(neighbour_table, my_lane * slot_dev, slot_dev, 2).reshape(
        group_count, pairs
    )
    source = slot_ids // mono_grp
    member = slot_ids % mono_grp
    from_here = source == my_group
    member_hot = member[:, :, None] == jnp.arange(mono_grp, dtype=jnp.int32)[None, None, :]
    own_ids = lax.dynamic_index_in_dim(slot_ids, my_group, 0, keepdims=False)
    own_src = own_ids // mono_grp
    src_hot = own_src[:, None] == jnp.arange(group_count, dtype=jnp.int32)[None, :]
    capacity = 2 * distinct_cap
    pair_rank = jnp.cumsum(from_here.astype(jnp.int32), axis=1) - 1
    rank_hot = from_here[:, :, None] & (
        pair_rank[:, :, None] == jnp.arange(capacity, dtype=jnp.int32)[None, None, :]
    )
    select = jnp.einsum(
        "hpr,hpm->hrm", rank_hot.astype(jnp.float32), member_hot.astype(jnp.float32)
    )
    outgoing = jnp.einsum(
        "hrm,mx->hrx", select.astype(jnp.bfloat16), group_dens, preferred_element_type=jnp.float32
    ).astype(jnp.bfloat16)
    arrived = lax.all_to_all(outgoing, "gddi", split_axis=0, concat_axis=0, tiled=True)
    running = jnp.cumsum(src_hot.astype(jnp.int32), axis=0) - 1
    own_rank = jnp.sum(jnp.where(src_hot, running, 0), axis=1)
    position = own_src * capacity + own_rank
    nearby = arrived.reshape(group_count * capacity, basis, basis)[position]
    blocks = esp_block.reshape(pairs, basis, basis)
    half_term = jnp.einsum("pab,pbc->pac", blocks, nearby, preferred_element_type=jnp.float32)
    field_term = jnp.einsum(
        "pac,pdc->pad", half_term, blocks.astype(jnp.float32), precision=lax.Precision.HIGHEST
    )
    partial_fock = jnp.sum(field_term.reshape(mono_grp, slot_dev, basis, basis), axis=1)
    summed = lax.psum_scatter(partial_fock, "intra", scatter_dimension=0, tiled=True)
    return h_core.astype(jnp.float32) + summed


def solution(mesh):
    return jax.shard_map(
        local,
        mesh=mesh,
        in_specs=(
            P(("job", "gddi", "intra"), None, None),
            P(("job", "gddi", "intra"), None, None),
            P(("job", "gddi"), "intra", None, None),
            P("job", None),
        ),
        out_specs=P(("job", "gddi", "intra"), None, None),
        check_vma=False,
    )
```

profile of v0, /device:TPU:0, one launch (start us, length us, event | category | flops | bytes accessed | tf_op | source)
XLA Modules:
  0.0 164.3 jit_solution(4200376172819639745)
XLA Ops:
  6.5 0.0 copy-start
  6.5 0.0 all-gather.2.cloned.1.call-start
  6.5 0.7 all-gather.2.cloned.1.call-update
  7.3 0.8 reshape.202
  8.0 0.1 copy.30
  8.1 0.1 copy.22
  8.2 0.2 reduce_window_sum.22
  8.4 31.2 %all-gather.2.cloned.1.call-done = bf16[8,256,256]{2,1,0:T(8,128)(2,1)} async-done(((bf16[2,256,256]{2,1,0:T(8,128)(2,1)}), bf16[8,256,256]{2,1,0:T(8,128)(2,1)}) %all-gather.2.cloned.1.call-update) | async-done | bytes 1048592 | tf_op jit(solution)/shard_map/all_gather | solution.py:18
  39.6 1.7 %reshape.216 = bf16[8,65536,1]{1,0,2:T(8,128)(2,1)S(1)} reshape(bf16[8,256,256]{2,1,0:T(8,128)(2,1)} %all-gather.2.cloned.1.call-done) | data formatting | bytes 2097152 | tf_op jit(solution)/shard_map/reshape | solution.py:18
  41.3 3.3 %convolution_convert_fusion = bf16[4,8,65536]{2,1,0:T(8,128)(2,1)} fusion(bf16[8,65536,1]{1,0,2:T(8,128)(2,1)S(1)} %reshape.216, s32[4,16]{1,0:T(4,128)S(1)} %get-tuple-element.7, s32[4,16]{1,0:T(4,128)S(1)} %get-tuple-element.8, pred[4,16]{1,0:T(4,128)(4,1)S(1)} %get-tuple-element.6), kind=kOutput, calls=%fused_computation.1 | convolution fusion | flops 35661568 | bytes 5243456 | tf_op jit(solution)/shard_map/hrm,mx->hrx/dot_general | solution.py:40
  44.6 4.9 %all-to-all-start = ((bf16[4,8,65536]{2,1,0:T(8,128)(2,1)}), bf16[4,8,65536]{2,1,0:T(8,128)(2,1)}, u32[]{:S(2)}, u32[]{:S(2)}) async-start(bf16[4,8,65536]{2,1,0:T(8,128)(2,1)} %convolution_convert_fusion), calls=%async_computation | async-start | bytes 8388608 | tf_op jit(solution)/shard_map/all_to_all | solution.py:43
  49.5 0.0 reduce-scatter.2.cloned.1.call-start
  49.5 0.2 dynamic-slice_reduce_fusion
  49.7 0.1 fusion.3
  49.8 0.2 select_reduce_fusion
  50.0 47.6 %all-to-all-done = bf16[4,8,65536]{2,1,0:T(8,128)(2,1)} async-done(((bf16[4,8,65536]{2,1,0:T(8,128)(2,1)}), bf16[4,8,65536]{2,1,0:T(8,128)(2,1)}, u32[]{:S(2)}, u32[]{:S(2)}) %all-to-all-start) | async-done | bytes 4194336 | tf_op jit(solution)/shard_map/all_to_all | solution.py:43
  97.7 5.2 %copy.31 = bf16[4,8,256,256]{3,2,1,0:T(8,128)(2,1)} copy(bf16[4,8,256,256]{3,1,2,0:T(8,128)(2,1)} %bitcast.8) | data formatting | bytes 8388608
  102.9 4.2 %gather_fusion = bf16[16,256,256]{2,1,0:T(8,128)(2,1)} fusion(bf16[32,256,256]{2,1,0:T(8,128)(2,1)} %bitcast.32, s32[1024]{0:T(1024)S(1)} %pad_clamp_fusion), kind=kCustom, calls=%fused_computation | custom fusion | bytes 4194368 | tf_op jit(solution)/shard_map/gather | solution.py:47
  107.1 0.0 copy-done
  107.1 2.3 %fusion.15 = f32[16,256,256]{1,2,0:T(8,128)S(1)} fusion(bf16[16,256,256]{2,1,0:T(8,128)(2,1)S(1)} %bitcast.30, bf16[16,256,256]{2,1,0:T(8,128)(2,1)} %gather_fusion), kind=kOutput, calls=%fused_computation.40 | convolution fusion | flops 536870912 | bytes 8388608 | tf_op jit(solution)/shard_map/pab,pbc->pac/dot_general | solution.py:49
  109.4 3.6 %bitcast_reduce_fusion = f32[8,256,256]{2,1,0:T(8,128)} fusion(f32[16,256,256]{1,2,0:T(8,128)S(1)} %fusion.15, bf16[16,256,256]{2,1,0:T(8,128)(2,1)S(1)} %bitcast.31), kind=kOutput, calls=%fused_computation.2 | convolution fusion | flops 3221749760 | bytes 8388608 | tf_op jit(solution)/shard_map/pac,pdc->pad/dot_general | solution.py:50
  113.0 0.0 reduce-scatter.2.cloned.1.call-update
  113.0 42.6 %reduce-scatter.2.cloned.1.call-done = f32[2,256,256]{2,1,0:T(8,128)} async-done(((f32[8,256,256]{2,1,0:T(8,128)}), f32[2,256,256]{2,1,0:T(8,128)}) %reduce-scatter.2.cloned.1.call-update) | async-done | bytes 524304 | tf_op jit(solution)/shard_map/reduce_scatter | solution.py:54
  155.6 1.9 %convert_add_fusion = f32[2,256,256]{2,1,0:T(8,128)} fusion(f32[2,256,256]{2,1,0:T(8,128)} %reduce-scatter.2.cloned.1.call-done, bf16[2,256,256]{2,1,0:T(8,128)(2,1)S(1)} %copy-done.1), kind=kLoop, calls=%fused_computation.4 | loop fusion | flops 262144 | bytes 1310720 | tf_op jit(solution)/shard_map/add | solution.py:55
  (9 shorter events, 0.1 us)
Async XLA Ops:
  6.5 100.5 %copy-start = (bf16[8,2,256,256]{3,2,1,0:T(8,128)(2,1)S(1)}, bf16[8,2,256,256]{3,2,1,0:T(8,128)(2,1)}, u32[]{:S(2)}) copy-start(bf16[8,2,256,256]{3,2,1,0:T(8,128)(2,1)} %param.6) | copy-start | bytes 6291460
  6.5 33.1 %all-gather.2.cloned.1.call-start = ((), (), s32[]{:S(2)}) async-start(), calls=%async_computation.2 | async-start | bytes 1310720 | tf_op jit(solution)/shard_map/all_gather | solution.py:18
  44.6 53.1 %all-to-all-start = ((bf16[4,8,65536]{2,1,0:T(8,128)(2,1)}), bf16[4,8,65536]{2,1,0:T(8,128)(2,1)}, u32[]{:S(2)}, u32[]{:S(2)}) async-start(bf16[4,8,65536]{2,1,0:T(8,128)(2,1)} %convolution_convert_fusion), calls=%async_computation | async-start | bytes 8388608 | tf_op jit(solution)/shard_map/all_to_all | solution.py:43
  49.5 106.1 %reduce-scatter.2.cloned.1.call-start = ((), (), s32[]{:S(2)}) async-start(), calls=%async_computation.3 | async-start | bytes 2621440 | tf_op jit(solution)/shard_map/reduce_scatter | solution.py:54
  113.0 42.6 %copy-start.1 = (bf16[2,256,256]{2,1,0:T(8,128)(2,1)S(1)}, bf16[2,256,256]{2,1,0:T(8,128)(2,1)}, u32[]{:S(2)}) copy-start(bf16[2,256,256]{2,1,0:T(8,128)(2,1)} %param.5) | copy-start | bytes 786436
Sparse Core Ops, SparseCore 0:
  8.9 30.6 all-gather.1
  113.1 42.4 reduce-scatter.1
where the time goes:
time: 165 us; the launch traced here: 164 us
  waiting for transfers between devices  122 us (74%)
  between operations  13.4 us (8%)
  local copies, waits for them, and re-layouts  12.2 us (7%)
  matrix products  9.17 us (6%)
  starting transfers between devices  4.9 us (3%)
  other arithmetic  2.43 us (1%)
    all_to_all x1, waiting for transfers between devices, local(): lax.all_to_all(outgoing, 'gddi', split_axis=0, concat_axis=0, tiled=True)  47.6 us
    reduce_scatter x1, waiting for transfers between devices, local(): lax.psum_scatter(partial_fock, 'intra', scatter_dimension=0, tiled=True)  42.6 us
    all_gather x1, waiting for transfers between devices, local(): lax.all_gather(density, 'intra', axis=0, tiled=True)  31.2 us
    unnamed x6, local copies, waits for them, and re-layouts  5.27 us
    all_to_all x1, starting transfers between devices, local(): lax.all_to_all(outgoing, 'gddi', split_axis=0, concat_axis=0, tiled=True)  4.86 us
    gather x1, local copies, waits for them, and re-layouts, local(): nearby = arrived.reshape(group_count * capacity, basis, basis)[position]  4.22 us
    dot_general x1, matrix products, local(): jnp.einsum('pac,pdc->pad', half_term, blocks.astype(jnp.float32), precisi...  3.57 us
    dot_general x1, matrix products, local(): jnp.einsum('hrm,mx->hrx', select.astype(jnp.bfloat16), group_dens, prefer...  3.3 us
  transfers between devices with their start and end apart: 3, of which 3 were waited for; matrix products, arithmetic and copies ran while one was open for 1% of the time, Pallas kernels for 0%

commit v1 on v0

v1 whole, which is shorter than its diff:
```python
import functools

import jax
import jax.numpy as jnp
from jax import lax
from jax.experimental import pallas as pl
from jax.experimental.pallas import tpu as pltpu
from jax.sharding import PartitionSpec as P


def xor_pairs(size, k):
    return [(i, i ^ k) for i in range(size)]


def transposed_dot(a, b):
    return lax.dot_general(a, b, (((1,), (1,)), ((), ())), preferred_element_type=jnp.float32)


def fold(f):
    half = f.shape[0] // 2
    first, off, second = f[:half, :half], f[:half, half:], f[half:, half:]
    row = lax.broadcasted_iota(jnp.int32, (half, half), 0)
    col = lax.broadcasted_iota(jnp.int32, (half, half), 1)
    mixed = jnp.where(row <= col, first, second)
    diag = jnp.sum(jnp.where(row == col, second, 0.0), axis=0, keepdims=True)
    return off, mixed, jnp.broadcast_to(diag, (8, half))


def unfold(off, mixed, diag):
    half = off.shape[0]
    row = lax.broadcasted_iota(jnp.int32, (half, half), 0)
    col = lax.broadcasted_iota(jnp.int32, (half, half), 1)
    turned = mixed.T
    first = jnp.where(row <= col, mixed, turned)
    second = jnp.where(row > col, mixed, jnp.where(row < col, turned, diag))
    return first, off, off.T, second


def couple_kernel(groups, lanes, mono_dev, slot_dev, nbr_ref, esp_ref, *refs):
    n_pieces = groups * lanes
    pieces = refs[:n_pieces]
    outs = refs[n_pieces : n_pieces + lanes]
    esp, dens, esp_sem, dens_sem = refs[n_pieces + lanes :]
    my_group = lax.axis_index("gddi")
    my_lane = lax.axis_index("intra")
    mono_grp = mono_dev * lanes
    half = outs[0].shape[2]
    esp_copy = pltpu.make_async_copy(esp_ref, esp, esp_sem)
    esp_copy.start()
    copies = []
    for i, piece in enumerate(pieces):
        copy = pltpu.make_async_copy(piece, dens.at[pl.ds(i * mono_dev, mono_dev)], dens_sem.at[i])
        copy.start()
        copies.append(copy)
    esp_copy.wait()
    for copy in copies:
        copy.wait()

    def slot_of(fragment):
        apart = (fragment // mono_grp) ^ my_group
        lane = ((fragment % mono_grp) // mono_dev) ^ my_lane
        place = (apart & 1) * (groups // 2) + (apart >> 1)
        return (place * lanes + lane) * mono_dev + fragment % mono_dev

    for k in range(lanes):
        for m in range(mono_dev):
            mine = (my_lane ^ k) * mono_dev + m
            total = None
            for s in range(slot_dev):
                name = nbr_ref[my_group * mono_grp + mine, my_lane * slot_dev + s]
                block = esp[mine, s]
                half_term = jnp.dot(block, dens[slot_of(name)], preferred_element_type=jnp.float32)
                high = half_term.astype(jnp.bfloat16)
                low = (half_term - high.astype(jnp.float32)).astype(jnp.bfloat16)
                term = transposed_dot(high, block) + transposed_dot(low, block)
                total = term if total is None else total + term
            off, mixed, diag = fold(total)
            outs[k][m, :half] = off
            outs[k][m, half : 2 * half] = mixed
            outs[k][m, 2 * half :] = diag


def finish_kernel(core_ref, *refs):
    parts, out_ref = refs[:-1], refs[-1]
    half = out_ref.shape[1] // 2
    for m in range(out_ref.shape[0]):
        total = parts[0][m]
        for part in parts[1:]:
            total = total + part[m]
        first, off, off_t, second = unfold(total[:half], total[half : 2 * half], total[2 * half : 2 * half + 1])
        core = core_ref[m].astype(jnp.float32)
        out_ref[m, :half, :half] = core[:half, :half] + first
        out_ref[m, :half, half:] = core[:half, half:] + off
        out_ref[m, half:, :half] = core[half:, :half] + off_t
        out_ref[m, half:, half:] = core[half:, half:] + second


def local(density, h_core, esp_block, nbr):
    groups = lax.axis_size("gddi")
    lanes = lax.axis_size("intra")
    mono_dev, basis = density.shape[0], density.shape[1]
    mono_grp, slot_dev = esp_block.shape[0], esp_block.shape[1]
    half = basis // 2

    row = [density if k == 0 else lax.ppermute(density, "intra", xor_pairs(lanes, k)) for k in range(lanes)]
    near = []
    for k in range(groups // 2):
        for piece in row:
            near.append(piece if k == 0 else lax.ppermute(piece, "gddi", xor_pairs(groups, 2 * k)))
    pieces = near + [lax.ppermute(piece, "gddi", xor_pairs(groups, 1)) for piece in near]

    folded = jax.ShapeDtypeStruct((mono_dev, basis + 8, half), jnp.float32)
    any_space = pl.BlockSpec(memory_space=pl.ANY)
    in_vmem = pl.BlockSpec(memory_space=pltpu.VMEM)
    partials = pl.pallas_call(
        functools.partial(couple_kernel, groups, lanes, mono_dev, slot_dev),
        out_shape=[folded] * lanes,
        in_specs=[pl.BlockSpec(memory_space=pltpu.SMEM)] + [any_space] * (1 + len(pieces)),
        out_specs=[in_vmem] * lanes,
        scratch_shapes=[
            pltpu.VMEM(esp_block.shape, esp_block.dtype),
            pltpu.VMEM((mono_dev * len(pieces), basis, basis), density.dtype),
            pltpu.SemaphoreType.DMA,
            pltpu.SemaphoreType.DMA((len(pieces),)),
        ],
        compiler_params=pltpu.CompilerParams(vmem_limit_bytes=56 * 2**20),
        name="couple",
    )(nbr, esp_block, *pieces)

    terms = [partials[0]] + [lax.ppermute(partials[k], "intra", xor_pairs(lanes, k)) for k in range(1, lanes)]
    return pl.pallas_call(
        finish_kernel,
        out_shape=jax.ShapeDtypeStruct((mono_dev, basis, basis), jnp.float32),
        in_specs=[in_vmem] * (1 + lanes),
        out_specs=in_vmem,
        name="finish",
    )(h_core, *terms)


def solution(mesh):
    return jax.shard_map(
        local,
        mesh=mesh,
        in_specs=(
            P(("job", "gddi", "intra"), None, None),
            P(("job", "gddi", "intra"), None, None),
            P(("job", "gddi"), "intra", None, None),
            P("job", None),
        ),
        out_specs=P(("job", "gddi", "intra"), None, None),
        check_vma=False,
    )
```

time: 165 us -> 85 us (0.52)
  the two profiles are of different devices: /device:TPU:0 before, /device:TPU:10 now
where the time goes in v1:
time: 85 us; the launch traced here: 84.7 us
  waiting for transfers between devices  59.7 us (70%)
  starting transfers between devices  12.9 us (15%)
  Pallas kernels  9.31 us (11%)
  local copies, waits for them, and re-layouts  2.65 us (3%)
    ppermute x3, waiting for transfers between devices, local(): lax.ppermute(partials[k], 'intra', xor_pairs(lanes, k))  24.5 us
    ppermute x4, waiting for transfers between devices, local(): lax.ppermute(piece, 'gddi', xor_pairs(groups, 2 * k))  17.7 us
    ppermute x3, waiting for transfers between devices, local(): lax.ppermute(density, 'intra', xor_pairs(lanes, k))  17.3 us
    pallas_call x1, Pallas kernels, local(): pl.pallas_call(functools.partial(couple_kernel, groups, lanes, mono_dev,...  7.1 us
    ppermute x3, starting transfers between devices, local(): lax.ppermute(partials[k], 'intra', xor_pairs(lanes, k))  4.3 us
    ppermute x3, starting transfers between devices, local(): lax.ppermute(density, 'intra', xor_pairs(lanes, k))  4.05 us
    ppermute x4, starting transfers between devices, local(): lax.ppermute(piece, 'gddi', xor_pairs(groups, 2 * k))  4.05 us
    unnamed x33, local copies, waits for them, and re-layouts  2.65 us
  transfers between devices with their start and end apart: 18, of which 10 were waited for; matrix products, arithmetic and copies ran while one was open for 2% of the time, Pallas kernels for 0%

profile of v1, /device:TPU:10, one launch (start us, length us, event | category | flops | bytes accessed | tf_op | source)
XLA Modules:
  0.0 84.7 jit_solution(13939258944284309841)
XLA Ops:
  0.0 1.5 %collective-permute-start.3 = (bf16[2,256,256]{2,1,0:T(8,128)(2,1)}, bf16[2,256,256]{2,1,0:T(8,128)(2,1)S(1)}, u32[]{:S(2)}, u32[]{:S(2)}) collective-permute-start(bf16[2,256,256]{2,1,0:T(8,128)(2,1)} %refs_0_.1), channel_id=1, source_target_pairs={{0,8},{4,12},{8,0},{12,4},{1,9},{5,13},{9,1},{13,5},{2,10},{6,14},... | collective-permute-start | bytes 786440 | tf_op jit(solution)/shard_map/ppermute | solution.py:109
  1.5 1.6 %collective-permute-start.2 = (bf16[2,256,256]{2,1,0:T(8,128)(2,1)}, bf16[2,256,256]{2,1,0:T(8,128)(2,1)S(1)}, u32[]{:S(2)}, u32[]{:S(2)}) collective-permute-start(bf16[2,256,256]{2,1,0:T(8,128)(2,1)} %refs_0_.1), channel_id=1, source_target_pairs={{0,3},{1,2},{2,1},{3,0},{4,7},{5,6},{6,5},{7,4},{8,11},{9,10},{10,... | collective-permute-start | bytes 786440 | tf_op jit(solution)/shard_map/ppermute | solution.py:105
  3.1 1.2 %collective-permute-start.1 = (bf16[2,256,256]{2,1,0:T(8,128)(2,1)}, bf16[2,256,256]{2,1,0:T(8,128)(2,1)S(1)}, u32[]{:S(2)}, u32[]{:S(2)}) collective-permute-start(bf16[2,256,256]{2,1,0:T(8,128)(2,1)} %refs_0_.1), channel_id=1, source_target_pairs={{0,2},{1,3},{2,0},{3,1},{4,6},{5,7},{6,4},{7,5},{8,10},{9,11},{10,... | collective-permute-start | bytes 786440 | tf_op jit(solution)/shard_map/ppermute | solution.py:105
  4.3 1.2 %collective-permute-start = (bf16[2,256,256]{2,1,0:T(8,128)(2,1)}, bf16[2,256,256]{2,1,0:T(8,128)(2,1)S(1)}, u32[]{:S(2)}, u32[]{:S(2)}) collective-permute-start(bf16[2,256,256]{2,1,0:T(8,128)(2,1)} %refs_0_.1), channel_id=1, source_target_pairs={{0,1},{1,0},{2,3},{3,2},{4,5},{5,4},{6,7},{7,6},{8,9},{9,8},{10,11... | collective-permute-start | bytes 786440 | tf_op jit(solution)/shard_map/ppermute | solution.py:105
  5.6 2.7 %collective-permute-done.3.refs_4_ = bf16[2,256,256]{2,1,0:T(8,128)(2,1)S(1)} collective-permute-done((bf16[2,256,256]{2,1,0:T(8,128)(2,1)}, bf16[2,256,256]{2,1,0:T(8,128)(2,1)S(1)}, u32[]{:S(2)}, u32[]{:S(2)}) %collective-permute-start.3) | collective-permute-done | bytes 262176 | tf_op jit(solution)/shard_map/ppermute | solution.py:109
  8.3 13.5 %collective-permute-done.2.refs_3_ = bf16[2,256,256]{2,1,0:T(8,128)(2,1)S(1)} collective-permute-done((bf16[2,256,256]{2,1,0:T(8,128)(2,1)}, bf16[2,256,256]{2,1,0:T(8,128)(2,1)S(1)}, u32[]{:S(2)}, u32[]{:S(2)}) %collective-permute-start.2) | collective-permute-done | bytes 262176 | tf_op jit(solution)/shard_map/ppermute | solution.py:105
  21.8 3.8 %collective-permute-done.1.refs_2_ = bf16[2,256,256]{2,1,0:T(8,128)(2,1)S(1)} collective-permute-done((bf16[2,256,256]{2,1,0:T(8,128)(2,1)}, bf16[2,256,256]{2,1,0:T(8,128)(2,1)S(1)}, u32[]{:S(2)}, u32[]{:S(2)}) %collective-permute-start.1) | collective-permute-done | bytes 262176 | tf_op jit(solution)/shard_map/ppermute | solution.py:105
  25.6 0.5 collective-permute-start.6
  26.1 1.5 %collective-permute-start.5 = (bf16[2,256,256]{2,1,0:T(8,128)(2,1)S(1)}, bf16[2,256,256]{2,1,0:T(8,128)(2,1)S(1)}, u32[]{:S(2)}, u32[]{:S(2)}) collective-permute-start(bf16[2,256,256]{2,1,0:T(8,128)(2,1)S(1)} %collective-permute-done.1.refs_2_), channel_id=1, source_target_pairs={{0,8},{4,12},{8,0},{12,4},{1,9},{5,13},{9,1},{13,5},{2,10},{6,14},... | collective-permute-start | bytes 786440 | tf_op jit(solution)/shard_map/ppermute | solution.py:109
  27.6 0.5 collective-permute-start.4
  28.1 0.5 collective-permute-start.8
  28.6 6.2 %collective-permute-done.6.refs_7_ = bf16[2,256,256]{2,1,0:T(8,128)(2,1)S(1)} collective-permute-done((bf16[2,256,256]{2,1,0:T(8,128)(2,1)S(1)}, bf16[2,256,256]{2,1,0:T(8,128)(2,1)S(1)}, u32[]{:S(2)}, u32[]{:S(2)}) %collective-permute-start.6) | collective-permute-done | bytes 262176 | tf_op jit(solution)/shard_map/ppermute | solution.py:109
  34.8 5.6 %collective-permute-done.5.refs_6_ = bf16[2,256,256]{2,1,0:T(8,128)(2,1)S(1)} collective-permute-done((bf16[2,256,256]{2,1,0:T(8,128)(2,1)S(1)}, bf16[2,256,256]{2,1,0:T(8,128)(2,1)S(1)}, u32[]{:S(2)}, u32[]{:S(2)}) %collective-permute-start.5) | collective-permute-done | bytes 262176 | tf_op jit(solution)/shard_map/ppermute | solution.py:109
  40.4 3.2 %collective-permute-done.4.refs_5_ = bf16[2,256,256]{2,1,0:T(8,128)(2,1)S(1)} collective-permute-done((bf16[2,256,256]{2,1,0:T(8,128)(2,1)S(1)}, bf16[2,256,256]{2,1,0:T(8,128)(2,1)S(1)}, u32[]{:S(2)}, u32[]{:S(2)}) %collective-permute-start.4) | collective-permute-done | bytes 262176 | tf_op jit(solution)/shard_map/ppermute | solution.py:109
  43.7 1.4 %copy.5.nbr_ref = s32[32,8]{1,0:T(8,128)} copy(s32[32,8]{0,1:T(8,128)} %param.7) | data formatting | bytes 2048 | tf_op args[3]
  45.9 7.1 %couple.1 = (f32[2,264,128]{2,1,0:T(8,128)}, f32[2,264,128]{2,1,0:T(8,128)}, f32[2,264,128]{2,1,0:T(8,128)}, f32[2,264,128]{2,1,0:T(8,128)}) custom-call(s32[32,8]{1,0:T(8,128)} %copy.5.nbr_ref, bf16[8,2,256,256]{3,2,1,0:T(8,128)(2,1)} %esp_ref.1, bf16[2,256,256]{2,1,0:T(8,128)(2,1)} %refs_0_.1, bf16[2,256,256]{2,1,0:T(8,128)(2,1)} %copy-done.6, ...), custom_call_target="tpu_custom_call" | custom-call | tf_op jit(solution)/shard_map/couple/pallas_call | solution.py:115
  53.0 2.8 %collective-permute-start.15 = (f32[2,264,128]{2,1,0:T(8,128)}, f32[2,264,128]{2,1,0:T(8,128)S(1)}, u32[]{:S(2)}, u32[]{:S(2)}) collective-permute-start(f32[2,264,128]{2,1,0:T(8,128)} %get-tuple-element.10), channel_id=1, source_target_pairs={{0,1},{1,0},{2,3},{3,2},{4,5},{5,4},{6,7},{7,6},{8,9},{9,8},{10,11... | collective-permute-start | bytes 811016 | tf_op jit(solution)/shard_map/ppermute | solution.py:130
  55.8 0.7 collective-permute-start.16
  56.4 0.9 %collective-permute-start.17 = (f32[2,264,128]{2,1,0:T(8,128)}, f32[2,264,128]{2,1,0:T(8,128)S(1)}, u32[]{:S(2)}, u32[]{:S(2)}) collective-permute-start(f32[2,264,128]{2,1,0:T(8,128)} %get-tuple-element.12), channel_id=1, source_target_pairs={{0,3},{1,2},{2,1},{3,0},{4,7},{5,6},{6,5},{7,4},{8,11},{9,10},{10,... | collective-permute-start | bytes 811016 | tf_op jit(solution)/shard_map/ppermute | solution.py:130
  57.3 10.3 %collective-permute-done.15.refs_1_ = f32[2,264,128]{2,1,0:T(8,128)S(1)} collective-permute-done((f32[2,264,128]{2,1,0:T(8,128)}, f32[2,264,128]{2,1,0:T(8,128)S(1)}, u32[]{:S(2)}, u32[]{:S(2)}) %collective-permute-start.15) | collective-permute-done | bytes 270368 | tf_op jit(solution)/shard_map/ppermute | solution.py:130
  67.7 7.5 %collective-permute-done.16.refs_2_ = f32[2,264,128]{2,1,0:T(8,128)S(1)} collective-permute-done((f32[2,264,128]{2,1,0:T(8,128)}, f32[2,264,128]{2,1,0:T(8,128)S(1)}, u32[]{:S(2)}, u32[]{:S(2)}) %collective-permute-start.16) | collective-permute-done | bytes 270368 | tf_op jit(solution)/shard_map/ppermute | solution.py:130
  75.2 6.6 %collective-permute-done.17.refs_3_ = f32[2,264,128]{2,1,0:T(8,128)S(1)} collective-permute-done((f32[2,264,128]{2,1,0:T(8,128)}, f32[2,264,128]{2,1,0:T(8,128)S(1)}, u32[]{:S(2)}, u32[]{:S(2)}) %collective-permute-start.17) | collective-permute-done | bytes 270368 | tf_op jit(solution)/shard_map/ppermute | solution.py:130
  81.8 0.7 copy-done.2
  82.5 2.2 %finish.1 = f32[2,256,256]{2,1,0:T(8,128)} custom-call(bf16[2,256,256]{2,1,0:T(8,128)(2,1)} %core_ref.1, f32[2,264,128]{2,1,0:T(8,128)} %get-tuple-element.9.refs_0_, f32[2,264,128]{2,1,0:T(8,128)} %copy-done, f32[2,264,128]{2,1,0:T(8,128)} %copy-done.1, f32[2,264,128]{2,1,0:T(8,128)} %copy-done.2), custom_call_target="tpu_custom_call" | custom-call | tf_op jit(solution)/shard_map/finish/pallas_call | solution.py:131
  (47 shorter events, 0.8 us)
Async XLA Ops:
  0.0 8.3 %collective-permute-start.3 = (bf16[2,256,256]{2,1,0:T(8,128)(2,1)}, bf16[2,256,256]{2,1,0:T(8,128)(2,1)S(1)}, u32[]{:S(2)}, u32[]{:S(2)}) collective-permute-start(bf16[2,256,256]{2,1,0:T(8,128)(2,1)} %refs_0_.1), channel_id=1, source_target_pairs={{0,8},{4,12},{8,0},{12,4},{1,9},{5,13},{9,1},{13,5},{2,10},{6,14},... | collective-permute-start | bytes 786440 | tf_op jit(solution)/shard_map/ppermute | solution.py:109
  1.5 20.2 %collective-permute-start.2 = (bf16[2,256,256]{2,1,0:T(8,128)(2,1)}, bf16[2,256,256]{2,1,0:T(8,128)(2,1)S(1)}, u32[]{:S(2)}, u32[]{:S(2)}) collective-permute-start(bf16[2,256,256]{2,1,0:T(8,128)(2,1)} %refs_0_.1), channel_id=1, source_target_pairs={{0,3},{1,2},{2,1},{3,0},{4,7},{5,6},{6,5},{7,4},{8,11},{9,10},{10,... | collective-permute-start | bytes 786440 | tf_op jit(solution)/shard_map/ppermute | solution.py:105
  3.1 22.5 %collective-permute-start.1 = (bf16[2,256,256]{2,1,0:T(8,128)(2,1)}, bf16[2,256,256]{2,1,0:T(8,128)(2,1)S(1)}, u32[]{:S(2)}, u32[]{:S(2)}) collective-permute-start(bf16[2,256,256]{2,1,0:T(8,128)(2,1)} %refs_0_.1), channel_id=1, source_target_pairs={{0,2},{1,3},{2,0},{3,1},{4,6},{5,7},{6,4},{7,5},{8,10},{9,11},{10,... | collective-permute-start | bytes 786440 | tf_op jit(solution)/shard_map/ppermute | solution.py:105
  4.3 21.7 %collective-permute-start = (bf16[2,256,256]{2,1,0:T(8,128)(2,1)}, bf16[2,256,256]{2,1,0:T(8,128)(2,1)S(1)}, u32[]{:S(2)}, u32[]{:S(2)}) collective-permute-start(bf16[2,256,256]{2,1,0:T(8,128)(2,1)} %refs_0_.1), channel_id=1, source_target_pairs={{0,1},{1,0},{2,3},{3,2},{4,5},{5,4},{6,7},{7,6},{8,9},{9,8},{10,11... | collective-permute-start | bytes 786440 | tf_op jit(solution)/shard_map/ppermute | solution.py:105
  5.6 22.0 %collective-permute-start.7 = (bf16[2,256,256]{2,1,0:T(8,128)(2,1)}, bf16[2,256,256]{2,1,0:T(8,128)(2,1)S(1)}, u32[]{:S(2)}, u32[]{:S(2)}) collective-permute-start(bf16[2,256,256]{2,1,0:T(8,128)(2,1)} %refs_0_.1), channel_id=1, source_target_pairs={{0,4},{4,0},{8,12},{12,8},{1,5},{5,1},{9,13},{13,9},{2,6},{6,2},{1... | collective-permute-start | bytes 786440 | tf_op jit(solution)/shard_map/ppermute | solution.py:110
  8.3 37.1 %copy-start.3 = (bf16[2,256,256]{2,1,0:T(8,128)(2,1)}, bf16[2,256,256]{2,1,0:T(8,128)(2,1)S(1)}, u32[]{:S(2)}) copy-start(bf16[2,256,256]{2,1,0:T(8,128)(2,1)S(1)} %collective-permute-done.3.refs_4_) | copy-start | bytes 786436
  8.3 19.8 %collective-permute-start.11 = (bf16[2,256,256]{2,1,0:T(8,128)(2,1)S(1)}, bf16[2,256,256]{2,1,0:T(8,128)(2,1)S(1)}, u32[]{:S(2)}, u32[]{:S(2)}) collective-permute-start(bf16[2,256,256]{2,1,0:T(8,128)(2,1)S(1)} %collective-permute-done.3.refs_4_), channel_id=1, source_target_pairs={{0,4},{4,0},{8,12},{12,8},{1,5},{5,1},{9,13},{13,9},{2,6},{6,2},{1... | collective-permute-start | bytes 786440 | tf_op jit(solution)/shard_map/ppermute | solution.py:110
  21.8 23.6 %copy-start.4 = (bf16[2,256,256]{2,1,0:T(8,128)(2,1)}, bf16[2,256,256]{2,1,0:T(8,128)(2,1)S(1)}, u32[]{:S(2)}) copy-start(bf16[2,256,256]{2,1,0:T(8,128)(2,1)S(1)} %collective-permute-done.2.refs_3_) | copy-start | bytes 786436
  21.8 6.3 %collective-permute-start.10 = (bf16[2,256,256]{2,1,0:T(8,128)(2,1)S(1)}, bf16[2,256,256]{2,1,0:T(8,128)(2,1)S(1)}, u32[]{:S(2)}, u32[]{:S(2)}) collective-permute-start(bf16[2,256,256]{2,1,0:T(8,128)(2,1)S(1)} %collective-permute-done.2.refs_3_), channel_id=1, source_target_pairs={{0,4},{4,0},{8,12},{12,8},{1,5},{5,1},{9,13},{13,9},{2,6},{6,2},{1... | collective-permute-start | bytes 786440 | tf_op jit(solution)/shard_map/ppermute | solution.py:110
  25.6 19.8 %copy-start.5 = (bf16[2,256,256]{2,1,0:T(8,128)(2,1)}, bf16[2,256,256]{2,1,0:T(8,128)(2,1)S(1)}, u32[]{:S(2)}) copy-start(bf16[2,256,256]{2,1,0:T(8,128)(2,1)S(1)} %collective-permute-done.1.refs_2_) | copy-start | bytes 786436
  25.6 9.2 %collective-permute-start.6 = (bf16[2,256,256]{2,1,0:T(8,128)(2,1)S(1)}, bf16[2,256,256]{2,1,0:T(8,128)(2,1)S(1)}, u32[]{:S(2)}, u32[]{:S(2)}) collective-permute-start(bf16[2,256,256]{2,1,0:T(8,128)(2,1)S(1)} %collective-permute-done.2.refs_3_), channel_id=1, source_target_pairs={{0,8},{4,12},{8,0},{12,4},{1,9},{5,13},{9,1},{13,5},{2,10},{6,14},... | collective-permute-start | bytes 786440 | tf_op jit(solution)/shard_map/ppermute | solution.py:109
  26.1 19.3 %copy-start.6 = (bf16[2,256,256]{2,1,0:T(8,128)(2,1)}, bf16[2,256,256]{2,1,0:T(8,128)(2,1)S(1)}, u32[]{:S(2)}) copy-start(bf16[2,256,256]{2,1,0:T(8,128)(2,1)S(1)} %collective-permute-done.refs_1_) | copy-start | bytes 786436
  26.1 14.3 %collective-permute-start.5 = (bf16[2,256,256]{2,1,0:T(8,128)(2,1)S(1)}, bf16[2,256,256]{2,1,0:T(8,128)(2,1)S(1)}, u32[]{:S(2)}, u32[]{:S(2)}) collective-permute-start(bf16[2,256,256]{2,1,0:T(8,128)(2,1)S(1)} %collective-permute-done.1.refs_2_), channel_id=1, source_target_pairs={{0,8},{4,12},{8,0},{12,4},{1,9},{5,13},{9,1},{13,5},{2,10},{6,14},... | collective-permute-start | bytes 786440 | tf_op jit(solution)/shard_map/ppermute | solution.py:109
  27.6 17.7 %copy-start.7 = (bf16[2,256,256]{2,1,0:T(8,128)(2,1)}, bf16[2,256,256]{2,1,0:T(8,128)(2,1)S(1)}, u32[]{:S(2)}) copy-start(bf16[2,256,256]{2,1,0:T(8,128)(2,1)S(1)} %collective-permute-done.7.refs_8_) | copy-start | bytes 786436
  27.6 16.1 %collective-permute-start.4 = (bf16[2,256,256]{2,1,0:T(8,128)(2,1)S(1)}, bf16[2,256,256]{2,1,0:T(8,128)(2,1)S(1)}, u32[]{:S(2)}, u32[]{:S(2)}) collective-permute-start(bf16[2,256,256]{2,1,0:T(8,128)(2,1)S(1)} %collective-permute-done.refs_1_), channel_id=1, source_target_pairs={{0,8},{4,12},{8,0},{12,4},{1,9},{5,13},{9,1},{13,5},{2,10},{6,14},... | collective-permute-start | bytes 786440 | tf_op jit(solution)/shard_map/ppermute | solution.py:109
  28.1 17.2 %copy-start.8 = (bf16[2,256,256]{2,1,0:T(8,128)(2,1)}, bf16[2,256,256]{2,1,0:T(8,128)(2,1)S(1)}, u32[]{:S(2)}) copy-start(bf16[2,256,256]{2,1,0:T(8,128)(2,1)S(1)} %collective-permute-done.11.refs_12_) | copy-start | bytes 786436
  28.1 16.9 %collective-permute-start.9 = (bf16[2,256,256]{2,1,0:T(8,128)(2,1)S(1)}, bf16[2,256,256]{2,1,0:T(8,128)(2,1)S(1)}, u32[]{:S(2)}, u32[]{:S(2)}) collective-permute-start(bf16[2,256,256]{2,1,0:T(8,128)(2,1)S(1)} %collective-permute-done.1.refs_2_), channel_id=1, source_target_pairs={{0,4},{4,0},{8,12},{12,8},{1,5},{5,1},{9,13},{13,9},{2,6},{6,2},{1... | collective-permute-start | bytes 786440 | tf_op jit(solution)/shard_map/ppermute | solution.py:110
  28.1 16.9 %collective-permute-start.8 = (bf16[2,256,256]{2,1,0:T(8,128)(2,1)S(1)}, bf16[2,256,256]{2,1,0:T(8,128)(2,1)S(1)}, u32[]{:S(2)}, u32[]{:S(2)}) collective-permute-start(bf16[2,256,256]{2,1,0:T(8,128)(2,1)S(1)} %collective-permute-done.refs_1_), channel_id=1, source_target_pairs={{0,4},{4,0},{8,12},{12,8},{1,5},{5,1},{9,13},{13,9},{2,6},{6,2},{1... | collective-permute-start | bytes 786440 | tf_op jit(solution)/shard_map/ppermute | solution.py:110
  34.8 10.3 %collective-permute-start.14 = (bf16[2,256,256]{2,1,0:T(8,128)(2,1)S(1)}, bf16[2,256,256]{2,1,0:T(8,128)(2,1)S(1)}, u32[]{:S(2)}, u32[]{:S(2)}) collective-permute-start(bf16[2,256,256]{2,1,0:T(8,128)(2,1)S(1)} %collective-permute-done.6.refs_7_), channel_id=1, source_target_pairs={{0,4},{4,0},{8,12},{12,8},{1,5},{5,1},{9,13},{13,9},{2,6},{6,2},{1... | collective-permute-start | bytes 786440 | tf_op jit(solution)/shard_map/ppermute | solution.py:110
  40.4 4.7 %collective-permute-start.13 = (bf16[2,256,256]{2,1,0:T(8,128)(2,1)S(1)}, bf16[2,256,256]{2,1,0:T(8,128)(2,1)}, u32[]{:S(2)}, u32[]{:S(2)}) collective-permute-start(bf16[2,256,256]{2,1,0:T(8,128)(2,1)S(1)} %collective-permute-done.5.refs_6_), channel_id=1, source_target_pairs={{0,4},{4,0},{8,12},{12,8},{1,5},{5,1},{9,13},{13,9},{2,6},{6,2},{1... | collective-permute-start | bytes 786440 | tf_op jit(solution)/shard_map/ppermute | solution.py:110
  43.6 1.7 %collective-permute-start.12 = (bf16[2,256,256]{2,1,0:T(8,128)(2,1)S(1)}, bf16[2,256,256]{2,1,0:T(8,128)(2,1)}, u32[]{:S(2)}, u32[]{:S(2)}) collective-permute-start(bf16[2,256,256]{2,1,0:T(8,128)(2,1)S(1)} %collective-permute-done.4.refs_5_), channel_id=1, source_target_pairs={{0,4},{4,0},{8,12},{12,8},{1,5},{5,1},{9,13},{13,9},{2,6},{6,2},{1... | collective-permute-start | bytes 786440 | tf_op jit(solution)/shard_map/ppermute | solution.py:110
  53.0 14.6 %collective-permute-start.15 = (f32[2,264,128]{2,1,0:T(8,128)}, f32[2,264,128]{2,1,0:T(8,128)S(1)}, u32[]{:S(2)}, u32[]{:S(2)}) collective-permute-start(f32[2,264,128]{2,1,0:T(8,128)} %get-tuple-element.10), channel_id=1, source_target_pairs={{0,1},{1,0},{2,3},{3,2},{4,5},{5,4},{6,7},{7,6},{8,9},{9,8},{10,11... | collective-permute-start | bytes 811016 | tf_op jit(solution)/shard_map/ppermute | solution.py:130
  55.8 19.4 %collective-permute-start.16 = (f32[2,264,128]{2,1,0:T(8,128)}, f32[2,264,128]{2,1,0:T(8,128)S(1)}, u32[]{:S(2)}, u32[]{:S(2)}) collective-permute-start(f32[2,264,128]{2,1,0:T(8,128)} %get-tuple-element.11), channel_id=1, source_target_pairs={{0,2},{1,3},{2,0},{3,1},{4,6},{5,7},{6,4},{7,5},{8,10},{9,11},{10,... | collective-permute-start | bytes 811016 | tf_op jit(solution)/shard_map/ppermute | solution.py:130
  56.4 25.4 %collective-permute-start.17 = (f32[2,264,128]{2,1,0:T(8,128)}, f32[2,264,128]{2,1,0:T(8,128)S(1)}, u32[]{:S(2)}, u32[]{:S(2)}) collective-permute-start(f32[2,264,128]{2,1,0:T(8,128)} %get-tuple-element.12), channel_id=1, source_target_pairs={{0,3},{1,2},{2,1},{3,0},{4,7},{5,6},{6,5},{7,4},{8,11},{9,10},{10,... | collective-permute-start | bytes 811016 | tf_op jit(solution)/shard_map/ppermute | solution.py:130
  (10 other events, 58.3 us)

commit v2 on v1

v2 whole, which is shorter than its diff:
```python
import functools

import jax
import jax.numpy as jnp
from jax import lax
from jax.experimental import pallas as pl
from jax.experimental.pallas import tpu as pltpu
from jax.sharding import PartitionSpec as P

STEPS = 32.0
TOP = 32000.0
SHRINK = 1.0 / 16.0
IN_VMEM = pl.BlockSpec(memory_space=pltpu.VMEM)
IN_SMEM = pl.BlockSpec(memory_space=pltpu.SMEM)


def xor_pairs(size, k):
    return [(i, i ^ k) for i in range(size)]


def round_up(n, to):
    return -(-n // to) * to


def transposed_dot(a, b):
    return lax.dot_general(a, b, (((1,), (1,)), ((), ())), preferred_element_type=jnp.float32)


def square_iotas(half):
    row = lax.broadcasted_iota(jnp.int32, (half, half), 0)
    col = lax.broadcasted_iota(jnp.int32, (half, half), 1)
    return row, col


def fold(first, second):
    row, col = square_iotas(first.shape[0])
    mixed = jnp.where(row <= col, first, second)
    diag = jnp.sum(jnp.where(row == col, second, 0.0), axis=0, keepdims=True)
    return mixed, diag


def unfold(mixed, diag):
    row, col = square_iotas(mixed.shape[0])
    turned = mixed.T
    first = jnp.where(row <= col, mixed, turned)
    second = jnp.where(row > col, mixed, jnp.where(row < col, turned, diag))
    return first, second


def scale_code(peak):
    wanted = jnp.log(jnp.maximum(peak * SHRINK, 2.0**-120)) * STEPS
    return jnp.floor(wanted + 1.5).astype(jnp.int32)


def encode(x, code):
    units = jnp.exp(code.astype(jnp.float32) * (-1.0 / STEPS)) * TOP
    return jnp.floor(x * SHRINK * units + 0.5).astype(jnp.int32)


def decode(q, code):
    units = jnp.exp(code.astype(jnp.float32) * (1.0 / STEPS)) * (1.0 / TOP)
    return q.astype(jnp.float32) * units * (1.0 / SHRINK)


def pack(high, low):
    return lax.shift_left(high, 16) | (low & 0xFFFF)


def unpack(word):
    return lax.shift_right_arithmetic(word, 16), lax.shift_right_arithmetic(lax.shift_left(word, 16), 16)


def peak_of(x):
    return jnp.max(jnp.abs(x), axis=0, keepdims=True)


def fold_kernel(dens_ref, out_ref):
    mono_dev, basis, _ = dens_ref.shape
    half = basis // 2
    diags = []
    for m in range(mono_dev):
        out_ref[pl.ds(m * basis, half)] = dens_ref[m, :half, half:]
        mixed, diag = fold(
            dens_ref[m, :half, :half].astype(jnp.float32), dens_ref[m, half:, half:].astype(jnp.float32)
        )
        out_ref[pl.ds(m * basis + half, half)] = mixed.astype(out_ref.dtype)
        diags.append(diag)
    rows = out_ref.shape[0] - mono_dev * basis
    row = lax.broadcasted_iota(jnp.int32, (rows, half), 0)
    tail = jnp.zeros((rows, half), jnp.float32)
    for m in range(mono_dev):
        tail = jnp.where(row == m, diags[m], tail)
    out_ref[pl.ds(mono_dev * basis, rows)] = tail.astype(out_ref.dtype)


def couple_kernel(groups, lanes, mono_dev, nbr_ref, esp_ref, *refs):
    n_pieces = groups * lanes
    pieces = refs[:n_pieces]
    own_ref = refs[n_pieces]
    outs = refs[n_pieces + 1 : n_pieces + lanes]
    store = refs[n_pieces + lanes]
    my_group = lax.axis_index("gddi")
    my_lane = lax.axis_index("intra")
    mono_grp, slot_dev, basis, _ = esp_ref.shape
    half = basis // 2
    tail_rows = store.shape[1] - mono_dev * basis
    for i, piece in enumerate(pieces):
        store[i] = piece[...]

    def near_density(fragment):
        apart = (fragment // mono_grp) ^ my_group
        lane = ((fragment % mono_grp) // mono_dev) ^ my_lane
        place = ((apart & 1) * (groups // 2) + (apart >> 1)) * lanes + lane
        member = fragment % mono_dev
        start = pl.multiple_of(member * basis, basis)
        off = store[place, pl.ds(start, half)]
        mixed = store[place, pl.ds(start + half, half)].astype(jnp.float32)
        tail = store[place, pl.ds(mono_dev * basis, tail_rows)].astype(jnp.float32)
        row = lax.broadcasted_iota(jnp.int32, (tail_rows, half), 0)
        diag = jnp.sum(jnp.where(row == member, tail, 0.0), axis=0, keepdims=True)
        first, second = unfold(mixed, diag)
        top = jnp.concatenate([first.astype(off.dtype), off], axis=1)
        bottom = jnp.concatenate([off.T, second.astype(off.dtype)], axis=1)
        return jnp.concatenate([top, bottom], axis=0)

    def partial_of(mine):
        total = None
        for s in range(slot_dev):
            name = nbr_ref[my_group * mono_grp + mine, my_lane * slot_dev + s]
            block = esp_ref[mine, s]
            half_term = jnp.dot(block, near_density(name), preferred_element_type=jnp.float32)
            high = half_term.astype(jnp.bfloat16)
            low = (half_term - high.astype(jnp.float32)).astype(jnp.bfloat16)
            term = transposed_dot(high, block) + transposed_dot(low, block)
            total = term if total is None else total + term
        mixed, diag = fold(total[:half, :half], total[half:, half:])
        return total[:half, half:], mixed, diag

    for k in range(1, lanes):
        out = outs[k - 1]
        tail = []
        for m in range(mono_dev):
            off, mixed, diag = partial_of((my_lane ^ k) * mono_dev + m)
            off_code = scale_code(peak_of(off))
            mixed_code = scale_code(jnp.maximum(peak_of(mixed), jnp.abs(diag)))
            out[pl.ds(m * half, half)] = pack(encode(off, off_code), encode(mixed, mixed_code))
            tail += [pack(off_code, mixed_code), encode(diag, mixed_code)]
        row = lax.broadcasted_iota(jnp.int32, (out.shape[0] - mono_dev * half, half), 0)
        last = jnp.zeros(row.shape, jnp.int32)
        for i, values in enumerate(tail):
            last = jnp.where(row == i, values, last)
        out[pl.ds(mono_dev * half, row.shape[0])] = last
    for m in range(mono_dev):
        off, mixed, diag = partial_of(my_lane * mono_dev + m)
        own_ref[m, :half] = off
        own_ref[m, half : 2 * half] = mixed
        own_ref[m, 2 * half :] = jnp.broadcast_to(diag, (8, half))


def finish_kernel(core_ref, own_ref, *refs):
    parts, out_ref = refs[:-1], refs[-1]
    mono_dev, basis, _ = out_ref.shape
    half = basis // 2
    for m in range(mono_dev):
        off = own_ref[m, :half]
        mixed = own_ref[m, half : 2 * half]
        diag = own_ref[m, 2 * half : 2 * half + 1]
        for part in parts:
            tail = mono_dev * half + 2 * m
            off_code, mixed_code = unpack(part[tail : tail + 1])
            off_q, mixed_q = unpack(part[m * half : (m + 1) * half])
            off = off + decode(off_q, off_code)
            mixed = mixed + decode(mixed_q, mixed_code)
            diag = diag + decode(part[tail + 1 : tail + 2], mixed_code)
        first, second = unfold(mixed, diag)
        core = core_ref[m].astype(jnp.float32)
        out_ref[m, :half, :half] = core[:half, :half] + first
        out_ref[m, :half, half:] = core[:half, half:] + off
        out_ref[m, half:, :half] = core[half:, :half] + off.T
        out_ref[m, half:, half:] = core[half:, half:] + second


def local(density, h_core, esp_block, nbr):
    groups = lax.axis_size("gddi")
    lanes = lax.axis_size("intra")
    mono_dev, basis = density.shape[0], density.shape[1]
    half = basis // 2

    rows = mono_dev * basis + round_up(mono_dev, 16)
    shard = pl.pallas_call(
        fold_kernel,
        out_shape=jax.ShapeDtypeStruct((rows, half), density.dtype),
        in_specs=[IN_VMEM],
        out_specs=IN_VMEM,
        name="fold",
    )(density)
    row = [shard if k == 0 else lax.ppermute(shard, "intra", xor_pairs(lanes, k)) for k in range(lanes)]
    near = []
    for k in range(groups // 2):
        for piece in row:
            near.append(piece if k == 0 else lax.ppermute(piece, "gddi", xor_pairs(groups, 2 * k)))
    pieces = near + [lax.ppermute(piece, "gddi", xor_pairs(groups, 1)) for piece in near]

    own = jax.ShapeDtypeStruct((mono_dev, basis + 8, half), jnp.float32)
    coded = jax.ShapeDtypeStruct((mono_dev * half + round_up(2 * mono_dev, 8), half), jnp.int32)
    piece_bytes = len(pieces) * rows * half * 2
    partials = pl.pallas_call(
        functools.partial(couple_kernel, groups, lanes, mono_dev),
        out_shape=[own] + [coded] * (lanes - 1),
        in_specs=[IN_SMEM] + [IN_VMEM] * (1 + len(pieces)),
        out_specs=[IN_VMEM] * lanes,
        scratch_shapes=[pltpu.VMEM((len(pieces), rows, half), density.dtype)],
        compiler_params=pltpu.CompilerParams(
            vmem_limit_bytes=2 * (piece_bytes + esp_block.size * 2) + 8 * 2**20
        ),
        name="couple",
    )(nbr, esp_block, *pieces)

    terms = [lax.ppermute(partials[k], "intra", xor_pairs(lanes, k)) for k in range(1, lanes)]
    return pl.pallas_call(
        finish_kernel,
        out_shape=jax.ShapeDtypeStruct((mono_dev, basis, basis), jnp.float32),
        in_specs=[IN_VMEM] * (1 + lanes),
        out_specs=IN_VMEM,
        name="finish",
    )(h_core, partials[0], *terms)


def solution(mesh):
    return jax.shard_map(
        local,
        mesh=mesh,
        in_specs=(
            P(("job", "gddi", "intra"), None, None),
            P(("job", "gddi", "intra"), None, None),
            P(("job", "gddi"), "intra", None, None),
            P("job", None),
        ),
        out_specs=P(("job", "gddi", "intra"), None, None),
        check_vma=False,
    )
```

time: 85 us -> 54.6 us (0.64)
  the two profiles are of different devices: /device:TPU:10 before, /device:TPU:0 now
where the time goes in v2:
time: 54.6 us; the launch traced here: 54.3 us
  waiting for transfers between devices  26.3 us (48%)
  starting transfers between devices  15.9 us (29%)
  Pallas kernels  7.46 us (14%)
  local copies, waits for them, and re-layouts  4.66 us (9%)
    ppermute x3, waiting for transfers between devices, local(): lax.ppermute(partials[k], 'intra', xor_pairs(lanes, k))  10.8 us
    ppermute x3, waiting for transfers between devices, local(): lax.ppermute(shard, 'intra', xor_pairs(lanes, k))  10 us
    ppermute x4, starting transfers between devices, local(): lax.ppermute(piece, 'gddi', xor_pairs(groups, 2 * k))  5.5 us
    ppermute x3, starting transfers between devices, local(): lax.ppermute(partials[k], 'intra', xor_pairs(lanes, k))  5.38 us
    ppermute x4, waiting for transfers between devices, local(): lax.ppermute(piece, 'gddi', xor_pairs(groups, 2 * k))  4.84 us
    unnamed x13, local copies, waits for them, and re-layouts  4.66 us
    ppermute x3, starting transfers between devices, local(): lax.ppermute(shard, 'intra', xor_pairs(lanes, k))  4.39 us
    pallas_call x1, Pallas kernels, local(): pl.pallas_call(functools.partial(couple_kernel, groups, lanes, mono_dev),...  3.61 us
  transfers between devices with their start and end apart: 18, of which 7 were waited for; matrix products, arithmetic and copies ran while one was open for 1% of the time, Pallas kernels for 0%

profile of v2, /device:TPU:0, one launch (start us, length us, event | category | flops | bytes accessed | tf_op | source)
XLA Modules:
  0.0 54.3 jit_solution(1175321480266928743)
XLA Ops:
  0.0 1.7 %fold.1.refs_0_ = bf16[528,128]{1,0:T(8,128)(2,1)} custom-call(bf16[2,256,256]{2,1,0:T(8,128)(2,1)} %dens_ref.1), custom_call_target="tpu_custom_call" | custom-call | tf_op jit(solution)/shard_map/fold/pallas_call | solution.py:190
  1.7 3.0 %collective-permute-start.3 = (bf16[528,128]{1,0:T(8,128)(2,1)}, bf16[528,128]{1,0:T(8,128)(2,1)S(1)}, u32[]{:S(2)}, u32[]{:S(2)}) collective-permute-start(bf16[528,128]{1,0:T(8,128)(2,1)} %fold.1.refs_0_), channel_id=1, source_target_pairs={{0,8},{4,12},{8,0},{12,4},{1,9},{5,13},{9,1},{13,5},{2,10},{6,14},... | collective-permute-start | bytes 405512 | tf_op jit(solution)/shard_map/ppermute | solution.py:201
  4.6 3.6 %collective-permute-start.2 = (bf16[528,128]{1,0:T(8,128)(2,1)}, bf16[528,128]{1,0:T(8,128)(2,1)S(1)}, u32[]{:S(2)}, u32[]{:S(2)}) collective-permute-start(bf16[528,128]{1,0:T(8,128)(2,1)} %fold.1.refs_0_), channel_id=1, source_target_pairs={{0,3},{1,2},{2,1},{3,0},{4,7},{5,6},{6,5},{7,4},{8,11},{9,10},{10,... | collective-permute-start | bytes 405512 | tf_op jit(solution)/shard_map/ppermute | solution.py:197
  8.2 0.8 %collective-permute-start = (bf16[528,128]{1,0:T(8,128)(2,1)}, bf16[528,128]{1,0:T(8,128)(2,1)S(1)}, u32[]{:S(2)}, u32[]{:S(2)}) collective-permute-start(bf16[528,128]{1,0:T(8,128)(2,1)} %fold.1.refs_0_), channel_id=1, source_target_pairs={{0,1},{1,0},{2,3},{3,2},{4,5},{5,4},{6,7},{7,6},{8,9},{9,8},{10,11... | collective-permute-start | bytes 405512 | tf_op jit(solution)/shard_map/ppermute | solution.py:197
  9.0 3.5 %collective-permute-done.2.refs_3_ = bf16[528,128]{1,0:T(8,128)(2,1)S(1)} collective-permute-done((bf16[528,128]{1,0:T(8,128)(2,1)}, bf16[528,128]{1,0:T(8,128)(2,1)S(1)}, u32[]{:S(2)}, u32[]{:S(2)}) %collective-permute-start.2) | collective-permute-done | bytes 135200 | tf_op jit(solution)/shard_map/ppermute | solution.py:197
  12.6 0.5 collective-permute-start.6
  13.1 6.5 %collective-permute-done.1.refs_2_ = bf16[528,128]{1,0:T(8,128)(2,1)S(1)} collective-permute-done((bf16[528,128]{1,0:T(8,128)(2,1)}, bf16[528,128]{1,0:T(8,128)(2,1)S(1)}, u32[]{:S(2)}, u32[]{:S(2)}) %collective-permute-start.1) | collective-permute-done | bytes 135200 | tf_op jit(solution)/shard_map/ppermute | solution.py:197
  19.6 0.5 collective-permute-start.5
  20.1 1.5 %collective-permute-start.4 = (bf16[528,128]{1,0:T(8,128)(2,1)S(1)}, bf16[528,128]{1,0:T(8,128)(2,1)S(1)}, u32[]{:S(2)}, u32[]{:S(2)}) collective-permute-start(bf16[528,128]{1,0:T(8,128)(2,1)S(1)} %collective-permute-done.refs_1_), channel_id=1, source_target_pairs={{0,8},{4,12},{8,0},{12,4},{1,9},{5,13},{9,1},{13,5},{2,10},{6,14},... | collective-permute-start | bytes 405512 | tf_op jit(solution)/shard_map/ppermute | solution.py:201
  22.2 3.4 %collective-permute-done.5.refs_6_ = bf16[528,128]{1,0:T(8,128)(2,1)S(1)} collective-permute-done((bf16[528,128]{1,0:T(8,128)(2,1)S(1)}, bf16[528,128]{1,0:T(8,128)(2,1)S(1)}, u32[]{:S(2)}, u32[]{:S(2)}) %collective-permute-start.5) | collective-permute-done | bytes 135200 | tf_op jit(solution)/shard_map/ppermute | solution.py:201
  25.6 1.4 %collective-permute-done.4.refs_5_ = bf16[528,128]{1,0:T(8,128)(2,1)S(1)} collective-permute-done((bf16[528,128]{1,0:T(8,128)(2,1)S(1)}, bf16[528,128]{1,0:T(8,128)(2,1)S(1)}, u32[]{:S(2)}, u32[]{:S(2)}) %collective-permute-start.4) | collective-permute-done | bytes 135200 | tf_op jit(solution)/shard_map/ppermute | solution.py:201
  27.1 0.8 %copy.5.nbr_ref = s32[32,8]{1,0:T(8,128)S(1)} copy(s32[32,8]{0,1:T(8,128)} %param.7) | data formatting | bytes 2048 | tf_op args[3]
  27.8 0.6 %collective-permute-done.12.refs_13_ = bf16[528,128]{1,0:T(8,128)(2,1)S(1)} collective-permute-done((bf16[528,128]{1,0:T(8,128)(2,1)S(1)}, bf16[528,128]{1,0:T(8,128)(2,1)S(1)}, u32[]{:S(2)}, u32[]{:S(2)}) %collective-permute-start.12) | collective-permute-done | bytes 135200 | tf_op jit(solution)/shard_map/ppermute | solution.py:202
  28.4 1.6 %copy-done = bf16[8,2,256,256]{3,2,1,0:T(8,128)(2,1)S(1)} copy-done((bf16[8,2,256,256]{3,2,1,0:T(8,128)(2,1)S(1)}, bf16[8,2,256,256]{3,2,1,0:T(8,128)(2,1)}, u32[]{:S(2)}) %copy-start) | copy-done | bytes 2097176
  30.0 0.9 %copy-done.1 = bf16[528,128]{1,0:T(8,128)(2,1)S(1)} copy-done((bf16[528,128]{1,0:T(8,128)(2,1)S(1)}, bf16[528,128]{1,0:T(8,128)(2,1)}, u32[]{:S(2)}) %copy-start.1) | copy-done | bytes 135192
  30.9 3.6 %couple.1 = (f32[2,264,128]{2,1,0:T(8,128)S(1)}, s32[264,128]{1,0:T(8,128)S(1)}, s32[264,128]{1,0:T(8,128)S(1)}, s32[264,128]{1,0:T(8,128)S(1)}) custom-call(s32[32,8]{1,0:T(8,128)S(1)} %copy.5.nbr_ref, bf16[8,2,256,256]{3,2,1,0:T(8,128)(2,1)S(1)} %copy-done, bf16[528,128]{1,0:T(8,128)(2,1)S(1)} %copy-done.1, ...), custom_call_target="tpu_custom_call" | custom-call | tf_op jit(solution)/shard_map/couple/pallas_call | solution.py:207
  34.5 0.7 %copy-done.2 = f32[2,264,128]{2,1,0:T(8,128)} copy-done((f32[2,264,128]{2,1,0:T(8,128)}, f32[2,264,128]{2,1,0:T(8,128)S(1)}, u32[]{:S(2)}) %copy-start.2) | copy-done | bytes 270360
  35.2 3.0 %collective-permute-start.15 = (s32[264,128]{1,0:T(8,128)S(1)}, s32[264,128]{1,0:T(8,128)S(1)}, u32[]{:S(2)}, u32[]{:S(2)}) collective-permute-start(s32[264,128]{1,0:T(8,128)S(1)} %get-tuple-element.10), channel_id=1, source_target_pairs={{0,1},{1,0},{2,3},{3,2},{4,5},{5,4},{6,7},{7,6},{8,9},{9,8},{10,11... | collective-permute-start | bytes 405512 | tf_op jit(solution)/shard_map/ppermute | solution.py:219
  38.2 0.9 %collective-permute-start.16 = (s32[264,128]{1,0:T(8,128)S(1)}, s32[264,128]{1,0:T(8,128)S(1)}, u32[]{:S(2)}, u32[]{:S(2)}) collective-permute-start(s32[264,128]{1,0:T(8,128)S(1)} %get-tuple-element.11), channel_id=1, source_target_pairs={{0,2},{1,3},{2,0},{3,1},{4,6},{5,7},{6,4},{7,5},{8,10},{9,11},{10,... | collective-permute-start | bytes 405512 | tf_op jit(solution)/shard_map/ppermute | solution.py:219
  39.2 1.5 %collective-permute-start.17 = (s32[264,128]{1,0:T(8,128)S(1)}, s32[264,128]{1,0:T(8,128)S(1)}, u32[]{:S(2)}, u32[]{:S(2)}) collective-permute-start(s32[264,128]{1,0:T(8,128)S(1)} %get-tuple-element.12), channel_id=1, source_target_pairs={{0,3},{1,2},{2,1},{3,0},{4,7},{5,6},{6,5},{7,4},{8,11},{9,10},{10,... | collective-permute-start | bytes 405512 | tf_op jit(solution)/shard_map/ppermute | solution.py:219
  40.6 3.5 %collective-permute-done.15.refs_0_ = s32[264,128]{1,0:T(8,128)S(1)} collective-permute-done((s32[264,128]{1,0:T(8,128)S(1)}, s32[264,128]{1,0:T(8,128)S(1)}, u32[]{:S(2)}, u32[]{:S(2)}) %collective-permute-start.15) | collective-permute-done | bytes 135200 | tf_op jit(solution)/shard_map/ppermute | solution.py:219
  44.1 7.3 %collective-permute-done.16.refs_1_ = s32[264,128]{1,0:T(8,128)S(1)} collective-permute-done((s32[264,128]{1,0:T(8,128)S(1)}, s32[264,128]{1,0:T(8,128)S(1)}, u32[]{:S(2)}, u32[]{:S(2)}) %collective-permute-start.16) | collective-permute-done | bytes 135200 | tf_op jit(solution)/shard_map/ppermute | solution.py:219
  51.4 0.7 %copy-done.4 = s32[264,128]{1,0:T(8,128)} copy-done((s32[264,128]{1,0:T(8,128)}, s32[264,128]{1,0:T(8,128)S(1)}, u32[]{:S(2)}) %copy-start.4) | copy-done | bytes 135192
  52.1 2.2 %finish.1 = f32[2,256,256]{2,1,0:T(8,128)} custom-call(bf16[2,256,256]{2,1,0:T(8,128)(2,1)} %core_ref.1, f32[2,264,128]{2,1,0:T(8,128)} %copy-done.2, s32[264,128]{1,0:T(8,128)} %copy-done.3, s32[264,128]{1,0:T(8,128)} %copy-done.4, s32[264,128]{1,0:T(8,128)} %copy-done.5), custom_call_target="tpu_custom_call" | custom-call | tf_op jit(solution)/shard_map/finish/pallas_call | solution.py:220
  (28 shorter events, 0.7 us)
Async XLA Ops:
  1.7 7.4 %collective-permute-start.3 = (bf16[528,128]{1,0:T(8,128)(2,1)}, bf16[528,128]{1,0:T(8,128)(2,1)S(1)}, u32[]{:S(2)}, u32[]{:S(2)}) collective-permute-start(bf16[528,128]{1,0:T(8,128)(2,1)} %fold.1.refs_0_), channel_id=1, source_target_pairs={{0,8},{4,12},{8,0},{12,4},{1,9},{5,13},{9,1},{13,5},{2,10},{6,14},... | collective-permute-start | bytes 405512 | tf_op jit(solution)/shard_map/ppermute | solution.py:201
  4.6 7.9 %collective-permute-start.2 = (bf16[528,128]{1,0:T(8,128)(2,1)}, bf16[528,128]{1,0:T(8,128)(2,1)S(1)}, u32[]{:S(2)}, u32[]{:S(2)}) collective-permute-start(bf16[528,128]{1,0:T(8,128)(2,1)} %fold.1.refs_0_), channel_id=1, source_target_pairs={{0,3},{1,2},{2,1},{3,0},{4,7},{5,6},{6,5},{7,4},{8,11},{9,10},{10,... | collective-permute-start | bytes 405512 | tf_op jit(solution)/shard_map/ppermute | solution.py:197
  8.2 4.4 %collective-permute-start.7 = (bf16[528,128]{1,0:T(8,128)(2,1)}, bf16[528,128]{1,0:T(8,128)(2,1)S(1)}, u32[]{:S(2)}, u32[]{:S(2)}) collective-permute-start(bf16[528,128]{1,0:T(8,128)(2,1)} %fold.1.refs_0_), channel_id=1, source_target_pairs={{0,4},{4,0},{8,12},{12,8},{1,5},{5,1},{9,13},{13,9},{2,6},{6,2},{1... | collective-permute-start | bytes 405512 | tf_op jit(solution)/shard_map/ppermute | solution.py:202
  8.2 11.4 %collective-permute-start.1 = (bf16[528,128]{1,0:T(8,128)(2,1)}, bf16[528,128]{1,0:T(8,128)(2,1)S(1)}, u32[]{:S(2)}, u32[]{:S(2)}) collective-permute-start(bf16[528,128]{1,0:T(8,128)(2,1)} %fold.1.refs_0_), channel_id=1, source_target_pairs={{0,2},{1,3},{2,0},{3,1},{4,6},{5,7},{6,4},{7,5},{8,10},{9,11},{10,... | collective-permute-start | bytes 405512 | tf_op jit(solution)/shard_map/ppermute | solution.py:197
  8.2 11.9 %collective-permute-start = (bf16[528,128]{1,0:T(8,128)(2,1)}, bf16[528,128]{1,0:T(8,128)(2,1)S(1)}, u32[]{:S(2)}, u32[]{:S(2)}) collective-permute-start(bf16[528,128]{1,0:T(8,128)(2,1)} %fold.1.refs_0_), channel_id=1, source_target_pairs={{0,1},{1,0},{2,3},{3,2},{4,5},{5,4},{6,7},{7,6},{8,9},{9,8},{10,11... | collective-permute-start | bytes 405512 | tf_op jit(solution)/shard_map/ppermute | solution.py:197
  9.0 12.6 %collective-permute-start.11 = (bf16[528,128]{1,0:T(8,128)(2,1)S(1)}, bf16[528,128]{1,0:T(8,128)(2,1)S(1)}, u32[]{:S(2)}, u32[]{:S(2)}) collective-permute-start(bf16[528,128]{1,0:T(8,128)(2,1)S(1)} %collective-permute-done.3.refs_4_), channel_id=1, source_target_pairs={{0,4},{4,0},{8,12},{12,8},{1,5},{5,1},{9,13},{13,9},{2,6},{6,2},{1... | collective-permute-start | bytes 405512 | tf_op jit(solution)/shard_map/ppermute | solution.py:202
  12.6 9.0 %collective-permute-start.10 = (bf16[528,128]{1,0:T(8,128)(2,1)S(1)}, bf16[528,128]{1,0:T(8,128)(2,1)S(1)}, u32[]{:S(2)}, u32[]{:S(2)}) collective-permute-start(bf16[528,128]{1,0:T(8,128)(2,1)S(1)} %collective-permute-done.2.refs_3_), channel_id=1, source_target_pairs={{0,4},{4,0},{8,12},{12,8},{1,5},{5,1},{9,13},{13,9},{2,6},{6,2},{1... | collective-permute-start | bytes 405512 | tf_op jit(solution)/shard_map/ppermute | solution.py:202
  12.6 9.6 %collective-permute-start.6 = (bf16[528,128]{1,0:T(8,128)(2,1)S(1)}, bf16[528,128]{1,0:T(8,128)(2,1)S(1)}, u32[]{:S(2)}, u32[]{:S(2)}) collective-permute-start(bf16[528,128]{1,0:T(8,128)(2,1)S(1)} %collective-permute-done.2.refs_3_), channel_id=1, source_target_pairs={{0,8},{4,12},{8,0},{12,4},{1,9},{5,13},{9,1},{13,5},{2,10},{6,14},... | collective-permute-start | bytes 405512 | tf_op jit(solution)/shard_map/ppermute | solution.py:201
  19.6 6.0 %collective-permute-start.5 = (bf16[528,128]{1,0:T(8,128)(2,1)S(1)}, bf16[528,128]{1,0:T(8,128)(2,1)S(1)}, u32[]{:S(2)}, u32[]{:S(2)}) collective-permute-start(bf16[528,128]{1,0:T(8,128)(2,1)S(1)} %collective-permute-done.1.refs_2_), channel_id=1, source_target_pairs={{0,8},{4,12},{8,0},{12,4},{1,9},{5,13},{9,1},{13,5},{2,10},{6,14},... | collective-permute-start | bytes 405512 | tf_op jit(solution)/shard_map/ppermute | solution.py:201
  20.1 7.0 %collective-permute-start.4 = (bf16[528,128]{1,0:T(8,128)(2,1)S(1)}, bf16[528,128]{1,0:T(8,128)(2,1)S(1)}, u32[]{:S(2)}, u32[]{:S(2)}) collective-permute-start(bf16[528,128]{1,0:T(8,128)(2,1)S(1)} %collective-permute-done.refs_1_), channel_id=1, source_target_pairs={{0,8},{4,12},{8,0},{12,4},{1,9},{5,13},{9,1},{13,5},{2,10},{6,14},... | collective-permute-start | bytes 405512 | tf_op jit(solution)/shard_map/ppermute | solution.py:201
  21.6 6.2 %collective-permute-start.9 = (bf16[528,128]{1,0:T(8,128)(2,1)S(1)}, bf16[528,128]{1,0:T(8,128)(2,1)S(1)}, u32[]{:S(2)}, u32[]{:S(2)}) collective-permute-start(bf16[528,128]{1,0:T(8,128)(2,1)S(1)} %collective-permute-done.1.refs_2_), channel_id=1, source_target_pairs={{0,4},{4,0},{8,12},{12,8},{1,5},{5,1},{9,13},{13,9},{2,6},{6,2},{1... | collective-permute-start | bytes 405512 | tf_op jit(solution)/shard_map/ppermute | solution.py:202
  21.6 6.2 %collective-permute-start.8 = (bf16[528,128]{1,0:T(8,128)(2,1)S(1)}, bf16[528,128]{1,0:T(8,128)(2,1)S(1)}, u32[]{:S(2)}, u32[]{:S(2)}) collective-permute-start(bf16[528,128]{1,0:T(8,128)(2,1)S(1)} %collective-permute-done.refs_1_), channel_id=1, source_target_pairs={{0,4},{4,0},{8,12},{12,8},{1,5},{5,1},{9,13},{13,9},{2,6},{6,2},{1... | collective-permute-start | bytes 405512 | tf_op jit(solution)/shard_map/ppermute | solution.py:202
  22.1 5.7 %collective-permute-start.14 = (bf16[528,128]{1,0:T(8,128)(2,1)S(1)}, bf16[528,128]{1,0:T(8,128)(2,1)S(1)}, u32[]{:S(2)}, u32[]{:S(2)}) collective-permute-start(bf16[528,128]{1,0:T(8,128)(2,1)S(1)} %collective-permute-done.6.refs_7_), channel_id=1, source_target_pairs={{0,4},{4,0},{8,12},{12,8},{1,5},{5,1},{9,13},{13,9},{2,6},{6,2},{1... | collective-permute-start | bytes 405512 | tf_op jit(solution)/shard_map/ppermute | solution.py:202
  25.6 2.2 %collective-permute-start.13 = (bf16[528,128]{1,0:T(8,128)(2,1)S(1)}, bf16[528,128]{1,0:T(8,128)(2,1)S(1)}, u32[]{:S(2)}, u32[]{:S(2)}) collective-permute-start(bf16[528,128]{1,0:T(8,128)(2,1)S(1)} %collective-permute-done.5.refs_6_), channel_id=1, source_target_pairs={{0,4},{4,0},{8,12},{12,8},{1,5},{5,1},{9,13},{13,9},{2,6},{6,2},{1... | collective-permute-start | bytes 405512 | tf_op jit(solution)/shard_map/ppermute | solution.py:202
  27.1 1.4 %collective-permute-start.12 = (bf16[528,128]{1,0:T(8,128)(2,1)S(1)}, bf16[528,128]{1,0:T(8,128)(2,1)S(1)}, u32[]{:S(2)}, u32[]{:S(2)}) collective-permute-start(bf16[528,128]{1,0:T(8,128)(2,1)S(1)} %collective-permute-done.4.refs_5_), channel_id=1, source_target_pairs={{0,4},{4,0},{8,12},{12,8},{1,5},{5,1},{9,13},{13,9},{2,6},{6,2},{1... | collective-permute-start | bytes 405512 | tf_op jit(solution)/shard_map/ppermute | solution.py:202
  28.4 1.6 %copy-start = (bf16[8,2,256,256]{3,2,1,0:T(8,128)(2,1)S(1)}, bf16[8,2,256,256]{3,2,1,0:T(8,128)(2,1)}, u32[]{:S(2)}) copy-start(bf16[8,2,256,256]{3,2,1,0:T(8,128)(2,1)} %esp_ref.1) | copy-start | bytes 6291460
  30.0 0.9 %copy-start.1 = (bf16[528,128]{1,0:T(8,128)(2,1)S(1)}, bf16[528,128]{1,0:T(8,128)(2,1)}, u32[]{:S(2)}) copy-start(bf16[528,128]{1,0:T(8,128)(2,1)} %fold.1.refs_0_) | copy-start | bytes 405508
  34.5 0.7 %copy-start.2 = (f32[2,264,128]{2,1,0:T(8,128)}, f32[2,264,128]{2,1,0:T(8,128)S(1)}, u32[]{:S(2)}) copy-start(f32[2,264,128]{2,1,0:T(8,128)S(1)} %get-tuple-element.9.own_ref) | copy-start | bytes 811012
  35.2 8.9 %collective-permute-start.15 = (s32[264,128]{1,0:T(8,128)S(1)}, s32[264,128]{1,0:T(8,128)S(1)}, u32[]{:S(2)}, u32[]{:S(2)}) collective-permute-start(s32[264,128]{1,0:T(8,128)S(1)} %get-tuple-element.10), channel_id=1, source_target_pairs={{0,1},{1,0},{2,3},{3,2},{4,5},{5,4},{6,7},{7,6},{8,9},{9,8},{10,11... | collective-permute-start | bytes 405512 | tf_op jit(solution)/shard_map/ppermute | solution.py:219
  38.2 13.2 %collective-permute-start.16 = (s32[264,128]{1,0:T(8,128)S(1)}, s32[264,128]{1,0:T(8,128)S(1)}, u32[]{:S(2)}, u32[]{:S(2)}) collective-permute-start(s32[264,128]{1,0:T(8,128)S(1)} %get-tuple-element.11), channel_id=1, source_target_pairs={{0,2},{1,3},{2,0},{3,1},{4,6},{5,7},{6,4},{7,5},{8,10},{9,11},{10,... | collective-permute-start | bytes 405512 | tf_op jit(solution)/shard_map/ppermute | solution.py:219
  39.2 12.3 %collective-permute-start.17 = (s32[264,128]{1,0:T(8,128)S(1)}, s32[264,128]{1,0:T(8,128)S(1)}, u32[]{:S(2)}, u32[]{:S(2)}) collective-permute-start(s32[264,128]{1,0:T(8,128)S(1)} %get-tuple-element.12), channel_id=1, source_target_pairs={{0,3},{1,2},{2,1},{3,0},{4,7},{5,6},{6,5},{7,4},{8,11},{9,10},{10,... | collective-permute-start | bytes 405512 | tf_op jit(solution)/shard_map/ppermute | solution.py:219
  44.1 7.3 %copy-start.3 = (s32[264,128]{1,0:T(8,128)}, s32[264,128]{1,0:T(8,128)S(1)}, u32[]{:S(2)}) copy-start(s32[264,128]{1,0:T(8,128)S(1)} %collective-permute-done.15.refs_0_) | copy-start | bytes 405508
  51.4 0.7 %copy-start.4 = (s32[264,128]{1,0:T(8,128)}, s32[264,128]{1,0:T(8,128)S(1)}, u32[]{:S(2)}) copy-start(s32[264,128]{1,0:T(8,128)S(1)} %collective-permute-done.16.refs_1_) | copy-start | bytes 405508
  51.4 0.7 %copy-start.5 = (s32[264,128]{1,0:T(8,128)}, s32[264,128]{1,0:T(8,128)S(1)}, u32[]{:S(2)}) copy-start(s32[264,128]{1,0:T(8,128)S(1)} %collective-permute-done.17.refs_2_) | copy-start | bytes 405508

commit v3 on v2

--- a/solution.py
+++ b/solution.py
@@ -93,17 +93,20 @@
     out_ref[pl.ds(mono_dev * basis, rows)] = tail.astype(out_ref.dtype)
 
 
-def couple_kernel(groups, lanes, mono_dev, nbr_ref, esp_ref, *refs):
-    n_pieces = groups * lanes
-    pieces = refs[:n_pieces]
-    own_ref = refs[n_pieces]
-    outs = refs[n_pieces + 1 : n_pieces + lanes]
-    store = refs[n_pieces + lanes]
+def couple_kernel(groups, lanes, mono_dev, units, nbr_ref, esp_ref, *refs):
+    outs = refs[-3 - len(units) : -3]
+    pieces = refs[: -3 - len(units)]
+    store, blocks, sems = refs[-3:]
     my_group = lax.axis_index("gddi")
     my_lane = lax.axis_index("intra")
-    mono_grp, slot_dev, basis, _ = esp_ref.shape
+    _, slot_dev, basis, _ = esp_ref.shape
+    mono_grp = mono_dev * lanes
     half = basis // 2
     tail_rows = store.shape[1] - mono_dev * basis
+    fragments = [(my_lane ^ k) * mono_dev + m for k in units for m in range(mono_dev)]
+    copies = [pltpu.make_async_copy(esp_ref.at[f], blocks.at[i], sems.at[i]) for i, f in enumerate(fragments)]
+    for copy in copies:
+        copy.start()
     for i, piece in enumerate(pieces):
         store[i] = piece[...]
 
@@ -123,11 +126,12 @@
         bottom = jnp.concatenate([off.T, second.astype(off.dtype)], axis=1)
         return jnp.concatenate([top, bottom], axis=0)
 
-    def partial_of(mine):
+    def partial_of(i):
+        copies[i].wait()
         total = None
         for s in range(slot_dev):
-            name = nbr_ref[my_group * mono_grp + mine, my_lane * slot_dev + s]
-            block = esp_ref[mine, s]
+            name = nbr_ref[my_lane * slot_dev + s, my_group * mono_grp + fragments[i]]
+            block = blocks[i, s]
             half_term = jnp.dot(block, near_density(name), preferred_element_type=jnp.float32)
             high = half_term.astype(jnp.bfloat16)
             low = (half_term - high.astype(jnp.float32)).astype(jnp.bfloat16)
@@ -136,11 +140,17 @@
         mixed, diag = fold(total[:half, :half], total[half:, half:])
         return total[:half, half:], mixed, diag
 
-    for k in range(1, lanes):
-        out = outs[k - 1]
+    for i, (k, out) in enumerate(zip(units, outs)):
+        if k == 0:
+            for m in range(mono_dev):
+                off, mixed, diag = partial_of(i * mono_dev + m)
+                out[m, :half] = off
+                out[m, half : 2 * half] = mixed
+                out[m, 2 * half :] = jnp.broadcast_to(diag, (8, half))
+            continue
         tail = []
         for m in range(mono_dev):
-            off, mixed, diag = partial_of((my_lane ^ k) * mono_dev + m)
+            off, mixed, diag = partial_of(i * mono_dev + m)
             off_code = scale_code(peak_of(off))
             mixed_code = scale_code(jnp.maximum(peak_of(mixed), jnp.abs(diag)))
             out[pl.ds(m * half, half)] = pack(encode(off, off_code), encode(mixed, mixed_code))
@@ -150,11 +160,6 @@
         for i, values in enumerate(tail):
             last = jnp.where(row == i, values, last)
         out[pl.ds(mono_dev * half, row.shape[0])] = last
-    for m in range(mono_dev):
-        off, mixed, diag = partial_of(my_lane * mono_dev + m)
-        own_ref[m, :half] = off
-        own_ref[m, half : 2 * half] = mixed
-        own_ref[m, 2 * half :] = jnp.broadcast_to(diag, (8, half))
 
 
 def finish_kernel(core_ref, own_ref, *refs):
@@ -185,6 +190,7 @@
     lanes = lax.axis_size("intra")
     mono_dev, basis = density.shape[0], density.shape[1]
     half = basis // 2
+    small = pltpu.CompilerParams(vmem_limit_bytes=8 * 2**20)
 
     rows = mono_dev * basis + round_up(mono_dev, 16)
     shard = pl.pallas_call(
@@ -192,38 +198,60 @@
         out_shape=jax.ShapeDtypeStruct((rows, half), density.dtype),
         in_specs=[IN_VMEM],
         out_specs=IN_VMEM,
+        compiler_params=small,
         name="fold",
     )(density)
-    row = [shard if k == 0 else lax.ppermute(shard, "intra", xor_pairs(lanes, k)) for k in range(lanes)]
+    row = {0: shard}
+    bit = lanes // 2
+    while bit:
+        for k in list(row):
+            row[k ^ bit] = lax.ppermute(row[k], "intra", xor_pairs(lanes, bit))
+        bit //= 2
     near = []
-    for k in range(groups // 2):
-        for piece in row:
-            near.append(piece if k == 0 else lax.ppermute(piece, "gddi", xor_pairs(groups, 2 * k)))
+    for y in range(groups // 2):
+        for k in range(lanes):
+            near.append(row[k] if y == 0 else lax.ppermute(row[k], "gddi", xor_pairs(groups, 2 * y)))
     pieces = near + [lax.ppermute(piece, "gddi", xor_pairs(groups, 1)) for piece in near]
 
     own = jax.ShapeDtypeStruct((mono_dev, basis + 8, half), jnp.float32)
     coded = jax.ShapeDtypeStruct((mono_dev * half + round_up(2 * mono_dev, 8), half), jnp.int32)
     piece_bytes = len(pieces) * rows * half * 2
-    partials = pl.pallas_call(
-        functools.partial(couple_kernel, groups, lanes, mono_dev),
-        out_shape=[own] + [coded] * (lanes - 1),
-        in_specs=[IN_SMEM] + [IN_VMEM] * (1 + len(pieces)),
-        out_specs=[IN_VMEM] * lanes,
-        scratch_shapes=[pltpu.VMEM((len(pieces), rows, half), density.dtype)],
-        compiler_params=pltpu.CompilerParams(
-            vmem_limit_bytes=2 * (piece_bytes + esp_block.size * 2) + 8 * 2**20
-        ),
-        name="couple",
-    )(nbr, esp_block, *pieces)
-
-    terms = [lax.ppermute(partials[k], "intra", xor_pairs(lanes, k)) for k in range(1, lanes)]
+
+    blocks = pltpu.with_memory_space_constraint(esp_block, pltpu.HBM)
+
+    names = pltpu.with_memory_space_constraint(nbr.T, pltpu.HBM)
+
+    def couple(units, name):
+        return pl.pallas_call(
+            functools.partial(couple_kernel, groups, lanes, mono_dev, units),
+            out_shape=[own if k == 0 else coded for k in units],
+            in_specs=[IN_SMEM, pl.BlockSpec(memory_space=pl.ANY)] + [IN_VMEM] * len(pieces),
+            out_specs=[IN_VMEM] * len(units),
+            scratch_shapes=[
+                pltpu.VMEM((len(pieces), rows, half), density.dtype),
+                pltpu.VMEM((len(units) * mono_dev,) + esp_block.shape[1:], esp_block.dtype),
+                pltpu.SemaphoreType.DMA((len(units) * mono_dev,)),
+            ],
+            compiler_params=pltpu.CompilerParams(
+                vmem_limit_bytes=2 * (piece_bytes + esp_block.size * 2) + 8 * 2**20
+            ),
+            name=name,
+        )(names, blocks, *pieces)
+
+    far_units = range(lanes // 2, lanes)
+    near_units = range(lanes // 2)
+    far = couple(far_units, "couple_far")
+    far_terms = [lax.ppermute(far[k - lanes // 2], "intra", xor_pairs(lanes, k)) for k in far_units]
+    close = couple(near_units, "couple_near")
+    close_terms = [lax.ppermute(close[k], "intra", xor_pairs(lanes, k)) for k in near_units[1:]]
     return pl.pallas_call(
         finish_kernel,
         out_shape=jax.ShapeDtypeStruct((mono_dev, basis, basis), jnp.float32),
         in_specs=[IN_VMEM] * (1 + lanes),
         out_specs=IN_VMEM,
+        compiler_params=small,
         name="finish",
-    )(h_core, partials[0], *terms)
+    )(h_core, close[0], *close_terms, *far_terms)
 
 
 def solution(mesh):

time: 54.6 us -> 46.2 us (0.85)
  waiting for transfers between devices: 26.3 us -> 18.3 us
  local copies, waits for them, and re-layouts: 4.66 us -> 0.95 us
  Pallas kernels: 7.46 us -> 10.2 us
  starting transfers between devices: 15.9 us -> 16.5 us
    ppermute x10, waiting for transfers between devices: 25.7 us -> 17 us  [the longest x3 5.33 us: local(): row[k ^ bit] = lax.ppermute(row[k], 'intra', xor_pairs(lanes, bit))]
    pallas_call x1 -> x2, Pallas kernels: 3.61 us -> 9.07 us  [couple(): pl.pallas_call(functools.partial(couple_kernel, groups, lanes, mono_dev,...]
    unnamed x13 -> x4, local copies, waits for them, and re-layouts: 4.66 us -> 0.95 us
    pallas_call x1, Pallas kernels: 1.66 us -> 0.06 us  [local(): pl.pallas_call(fold_kernel, out_shape=jax.ShapeDtypeStruct((rows, half),...]
    pallas_call x1, Pallas kernels: 2.2 us -> 1.04 us  [local(): pl.pallas_call(finish_kernel, out_shape=jax.ShapeDtypeStruct((mono_dev, b...]
    ppermute x8, waiting for transfers between devices: 0.58 us -> 1.35 us  [local(): lax.ppermute(piece, 'gddi', xor_pairs(groups, 1))]
  transfers between devices with their start and end apart: 18 -> 18, of which waited for: 7 -> 9; matrix products, arithmetic and copies ran while one was open for 1% -> 0% of each run, Pallas kernels for 0% -> 10%
where the time goes in v3:
time: 46.2 us; the launch traced here: 46 us
  waiting for transfers between devices  18.3 us (40%)
  starting transfers between devices  16.5 us (36%)
  Pallas kernels  10.2 us (22%)
  local copies, waits for them, and re-layouts  0.95 us (2%)
    pallas_call x2, Pallas kernels, couple(): pl.pallas_call(functools.partial(couple_kernel, groups, lanes, mono_dev,...  9.07 us
    ppermute x3, starting transfers between devices, local(): row[k ^ bit] = lax.ppermute(row[k], 'intra', xor_pairs(lanes, bit))  6.29 us
    ppermute x3, waiting for transfers between devices, local(): row[k ^ bit] = lax.ppermute(row[k], 'intra', xor_pairs(lanes, bit))  5.33 us
    ppermute x4, starting transfers between devices, local(): lax.ppermute(row[k], 'gddi', xor_pairs(groups, 2 * y))  5.11 us
    ppermute x4, waiting for transfers between devices, local(): lax.ppermute(row[k], 'gddi', xor_pairs(groups, 2 * y))  4.47 us
    ppermute x2, waiting for transfers between devices, local(): lax.ppermute(far[k - lanes // 2], 'intra', xor_pairs(lanes, k))  4.37 us
    ppermute x2, starting transfers between devices, local(): lax.ppermute(far[k - lanes // 2], 'intra', xor_pairs(lanes, k))  3.45 us
    ppermute x1, waiting for transfers between devices, local(): lax.ppermute(close[k], 'intra', xor_pairs(lanes, k))  2.79 us
  transfers between devices with their start and end apart: 18, of which 9 were waited for; matrix products, arithmetic and copies ran while one was open for 0% of the time, Pallas kernels for 10%

profile of v3, /device:TPU:0, one launch (start us, length us, event | category | flops | bytes accessed | tf_op | source)
XLA Modules:
  0.0 46.0 jit_solution(6356992476142832893)
XLA Ops:
  0.0 0.9 %copy-done = bf16[2,256,256]{2,1,0:T(8,128)(2,1)S(1)} copy-done((bf16[2,256,256]{2,1,0:T(8,128)(2,1)S(1)}, bf16[2,256,256]{2,1,0:T(8,128)(2,1)}, u32[]{:S(2)}) %copy-start) | copy-done | bytes 262168
  1.0 4.1 %collective-permute-start.1 = (bf16[528,128]{1,0:T(8,128)(2,1)S(1)}, bf16[528,128]{1,0:T(8,128)(2,1)S(1)}, u32[]{:S(2)}, u32[]{:S(2)}) collective-permute-start(bf16[528,128]{1,0:T(8,128)(2,1)S(1)} %fold.1.refs_0_), channel_id=1, source_target_pairs={{0,2},{1,3},{2,0},{3,1},{4,6},{5,7},{6,4},{7,5},{8,10},{9,11},{10,... | collective-permute-start | bytes 405512 | tf_op jit(solution)/shard_map/ppermute | solution.py:208
  5.1 1.6 %collective-permute-start = (bf16[528,128]{1,0:T(8,128)(2,1)S(1)}, bf16[528,128]{1,0:T(8,128)(2,1)S(1)}, u32[]{:S(2)}, u32[]{:S(2)}) collective-permute-start(bf16[528,128]{1,0:T(8,128)(2,1)S(1)} %fold.1.refs_0_), channel_id=1, source_target_pairs={{0,1},{1,0},{2,3},{3,2},{4,5},{5,4},{6,7},{7,6},{8,9},{9,8},{10,11... | collective-permute-start | bytes 405512 | tf_op jit(solution)/shard_map/ppermute | solution.py:208
  6.7 1.5 %collective-permute-start.3 = (bf16[528,128]{1,0:T(8,128)(2,1)S(1)}, bf16[528,128]{1,0:T(8,128)(2,1)S(1)}, u32[]{:S(2)}, u32[]{:S(2)}) collective-permute-start(bf16[528,128]{1,0:T(8,128)(2,1)S(1)} %fold.1.refs_0_), channel_id=1, source_target_pairs={{0,8},{4,12},{8,0},{12,4},{1,9},{5,13},{9,1},{13,5},{2,10},{6,14},... | collective-permute-start | bytes 405512 | tf_op jit(solution)/shard_map/ppermute | solution.py:213
  8.2 3.5 %collective-permute-done.1.refs_2_ = bf16[528,128]{1,0:T(8,128)(2,1)S(1)} collective-permute-done((bf16[528,128]{1,0:T(8,128)(2,1)S(1)}, bf16[528,128]{1,0:T(8,128)(2,1)S(1)}, u32[]{:S(2)}, u32[]{:S(2)}) %collective-permute-start.1) | collective-permute-done | bytes 135200 | tf_op jit(solution)/shard_map/ppermute | solution.py:208
  11.7 0.6 %collective-permute-start.2 = (bf16[528,128]{1,0:T(8,128)(2,1)S(1)}, bf16[528,128]{1,0:T(8,128)(2,1)S(1)}, u32[]{:S(2)}, u32[]{:S(2)}) collective-permute-start(bf16[528,128]{1,0:T(8,128)(2,1)S(1)} %collective-permute-done.1.refs_2_), channel_id=1, source_target_pairs={{0,1},{1,0},{2,3},{3,2},{4,5},{5,4},{6,7},{7,6},{8,9},{9,8},{10,11... | collective-permute-start | bytes 405512 | tf_op jit(solution)/shard_map/ppermute | solution.py:208
  12.3 1.5 %collective-permute-start.5 = (bf16[528,128]{1,0:T(8,128)(2,1)S(1)}, bf16[528,128]{1,0:T(8,128)(2,1)S(1)}, u32[]{:S(2)}, u32[]{:S(2)}) collective-permute-start(bf16[528,128]{1,0:T(8,128)(2,1)S(1)} %collective-permute-done.1.refs_2_), channel_id=1, source_target_pairs={{0,8},{4,12},{8,0},{12,4},{1,9},{5,13},{9,1},{13,5},{2,10},{6,14},... | collective-permute-start | bytes 405512 | tf_op jit(solution)/shard_map/ppermute | solution.py:213
  13.8 0.5 %collective-permute-start.4 = (bf16[528,128]{1,0:T(8,128)(2,1)S(1)}, bf16[528,128]{1,0:T(8,128)(2,1)S(1)}, u32[]{:S(2)}, u32[]{:S(2)}) collective-permute-start(bf16[528,128]{1,0:T(8,128)(2,1)S(1)} %collective-permute-done.refs_1_), channel_id=1, source_target_pairs={{0,8},{4,12},{8,0},{12,4},{1,9},{5,13},{9,1},{13,5},{2,10},{6,14},... | collective-permute-start | bytes 405512 | tf_op jit(solution)/shard_map/ppermute | solution.py:213
  14.4 0.5 %collective-permute-start.8 = (bf16[528,128]{1,0:T(8,128)(2,1)S(1)}, bf16[528,128]{1,0:T(8,128)(2,1)S(1)}, u32[]{:S(2)}, u32[]{:S(2)}) collective-permute-start(bf16[528,128]{1,0:T(8,128)(2,1)S(1)} %collective-permute-done.refs_1_), channel_id=1, source_target_pairs={{0,4},{4,0},{8,12},{12,8},{1,5},{5,1},{9,13},{13,9},{2,6},{6,2},{1... | collective-permute-start | bytes 405512 | tf_op jit(solution)/shard_map/ppermute | solution.py:214
  14.9 1.8 %collective-permute-done.2.refs_3_ = bf16[528,128]{1,0:T(8,128)(2,1)S(1)} collective-permute-done((bf16[528,128]{1,0:T(8,128)(2,1)S(1)}, bf16[528,128]{1,0:T(8,128)(2,1)S(1)}, u32[]{:S(2)}, u32[]{:S(2)}) %collective-permute-start.2) | collective-permute-done | bytes 135200 | tf_op jit(solution)/shard_map/ppermute | solution.py:208
  16.7 1.6 %collective-permute-start.6 = (bf16[528,128]{1,0:T(8,128)(2,1)S(1)}, bf16[528,128]{1,0:T(8,128)(2,1)S(1)}, u32[]{:S(2)}, u32[]{:S(2)}) collective-permute-start(bf16[528,128]{1,0:T(8,128)(2,1)S(1)} %collective-permute-done.2.refs_3_), channel_id=1, source_target_pairs={{0,8},{4,12},{8,0},{12,4},{1,9},{5,13},{9,1},{13,5},{2,10},{6,14},... | collective-permute-start | bytes 405512 | tf_op jit(solution)/shard_map/ppermute | solution.py:213
  18.3 0.5 %collective-permute-done.5.refs_6_ = bf16[528,128]{1,0:T(8,128)(2,1)S(1)} collective-permute-done((bf16[528,128]{1,0:T(8,128)(2,1)S(1)}, bf16[528,128]{1,0:T(8,128)(2,1)S(1)}, u32[]{:S(2)}, u32[]{:S(2)}) %collective-permute-start.5) | collective-permute-done | bytes 135200 | tf_op jit(solution)/shard_map/ppermute | solution.py:213
  18.8 2.9 %collective-permute-done.4.refs_5_ = bf16[528,128]{1,0:T(8,128)(2,1)S(1)} collective-permute-done((bf16[528,128]{1,0:T(8,128)(2,1)S(1)}, bf16[528,128]{1,0:T(8,128)(2,1)S(1)}, u32[]{:S(2)}, u32[]{:S(2)}) %collective-permute-start.4) | collective-permute-done | bytes 135200 | tf_op jit(solution)/shard_map/ppermute | solution.py:213
  21.7 0.5 %collective-permute-start.13 = (bf16[528,128]{1,0:T(8,128)(2,1)S(1)}, bf16[528,128]{1,0:T(8,128)(2,1)S(1)}, u32[]{:S(2)}, u32[]{:S(2)}) collective-permute-start(bf16[528,128]{1,0:T(8,128)(2,1)S(1)} %collective-permute-done.5.refs_6_), channel_id=1, source_target_pairs={{0,4},{4,0},{8,12},{12,8},{1,5},{5,1},{9,13},{13,9},{2,6},{6,2},{1... | collective-permute-start | bytes 405512 | tf_op jit(solution)/shard_map/ppermute | solution.py:214
  22.3 1.0 %collective-permute-done.6.refs_7_ = bf16[528,128]{1,0:T(8,128)(2,1)S(1)} collective-permute-done((bf16[528,128]{1,0:T(8,128)(2,1)S(1)}, bf16[528,128]{1,0:T(8,128)(2,1)S(1)}, u32[]{:S(2)}, u32[]{:S(2)}) %collective-permute-start.6) | collective-permute-done | bytes 135200 | tf_op jit(solution)/shard_map/ppermute | solution.py:213
  23.4 0.2 collective-permute-done.12.refs_13_
  23.6 1.1 %collective-permute-done.14.refs_15_ = bf16[528,128]{1,0:T(8,128)(2,1)S(1)} collective-permute-done((bf16[528,128]{1,0:T(8,128)(2,1)S(1)}, bf16[528,128]{1,0:T(8,128)(2,1)S(1)}, u32[]{:S(2)}, u32[]{:S(2)}) %collective-permute-start.14) | collective-permute-done | bytes 135200 | tf_op jit(solution)/shard_map/ppermute | solution.py:214
  24.7 4.5 %couple_far.1 = (s32[264,128]{1,0:T(8,128)S(1)}, s32[264,128]{1,0:T(8,128)S(1)}) custom-call(s32[8,32]{1,0:T(8,128)} %bitcast.1, bf16[8,2,256,256]{3,2,1,0:T(8,128)(2,1)} %esp_ref.3, bf16[528,128]{1,0:T(8,128)(2,1)S(1)} %fold.1.refs_0_, bf16[528,128]{1,0:T(8,128)(2,1)S(1)} %collective-permute-done.refs_1_, ...), custom_call_target="tpu_custom_call" | custom-call | tf_op jit(solution)/shard_map/couple_far/pallas_call | solution.py:225
  29.2 3.4 %collective-permute-start.16 = (s32[264,128]{1,0:T(8,128)S(1)}, s32[264,128]{1,0:T(8,128)S(1)}, u32[]{:S(2)}, u32[]{:S(2)}) collective-permute-start(s32[264,128]{1,0:T(8,128)S(1)} %get-tuple-element.11), channel_id=1, source_target_pairs={{0,2},{1,3},{2,0},{3,1},{4,6},{5,7},{6,4},{7,5},{8,10},{9,11},{10,... | collective-permute-start | bytes 405512 | tf_op jit(solution)/shard_map/ppermute | solution.py:244
  32.7 4.6 %couple_near.1 = (f32[2,264,128]{2,1,0:T(8,128)S(1)}, s32[264,128]{1,0:T(8,128)S(1)}) custom-call(s32[8,32]{1,0:T(8,128)} %bitcast.2, bf16[8,2,256,256]{3,2,1,0:T(8,128)(2,1)} %esp_ref.3, bf16[528,128]{1,0:T(8,128)(2,1)S(1)} %fold.1.refs_0_, bf16[528,128]{1,0:T(8,128)(2,1)S(1)} %collective-permute-done.refs_1_, ...), custom_call_target="tpu_custom_call" | custom-call | tf_op jit(solution)/shard_map/couple_near/pallas_call | solution.py:225
  37.2 0.6 %collective-permute-start.15 = (s32[264,128]{1,0:T(8,128)S(1)}, s32[264,128]{1,0:T(8,128)S(1)}, u32[]{:S(2)}, u32[]{:S(2)}) collective-permute-start(s32[264,128]{1,0:T(8,128)S(1)} %get-tuple-element.10), channel_id=1, source_target_pairs={{0,1},{1,0},{2,3},{3,2},{4,5},{5,4},{6,7},{7,6},{8,9},{9,8},{10,11... | collective-permute-start | bytes 405512 | tf_op jit(solution)/shard_map/ppermute | solution.py:246
  37.8 4.4 %collective-permute-done.16.refs_1_ = s32[264,128]{1,0:T(8,128)S(1)} collective-permute-done((s32[264,128]{1,0:T(8,128)S(1)}, s32[264,128]{1,0:T(8,128)S(1)}, u32[]{:S(2)}, u32[]{:S(2)}) %collective-permute-start.16) | collective-permute-done | bytes 135200 | tf_op jit(solution)/shard_map/ppermute | solution.py:244
  42.2 2.8 %collective-permute-done.15.refs_0_ = s32[264,128]{1,0:T(8,128)S(1)} collective-permute-done((s32[264,128]{1,0:T(8,128)S(1)}, s32[264,128]{1,0:T(8,128)S(1)}, u32[]{:S(2)}, u32[]{:S(2)}) %collective-permute-start.15) | collective-permute-done | bytes 135200 | tf_op jit(solution)/shard_map/ppermute | solution.py:246
  45.0 1.0 %finish.1 = f32[2,256,256]{2,1,0:T(8,128)} custom-call(bf16[2,256,256]{2,1,0:T(8,128)(2,1)S(1)} %copy-done.1, f32[2,264,128]{2,1,0:T(8,128)S(1)} %get-tuple-element.9.own_ref, s32[264,128]{1,0:T(8,128)S(1)} %collective-permute-done.15.refs_0_, s32[264,128]{1,0:T(8,128)S(1)} %collective-permute-done.16.refs_1_, s32[264,128]{1,0:T(8,128)S(1)} %collective-permute-done.17.refs_2_), custom_call_target="tpu_custom_call" | custom-call | tf_op jit(solution)/shard_map/finish/pallas_call | solution.py:247
  (20 shorter events, 0.2 us)
Async XLA Ops:
  0.0 0.9 %copy-start = (bf16[2,256,256]{2,1,0:T(8,128)(2,1)S(1)}, bf16[2,256,256]{2,1,0:T(8,128)(2,1)}, u32[]{:S(2)}) copy-start(bf16[2,256,256]{2,1,0:T(8,128)(2,1)} %dens_ref.1) | copy-start | bytes 786436
  1.0 10.7 %collective-permute-start.1 = (bf16[528,128]{1,0:T(8,128)(2,1)S(1)}, bf16[528,128]{1,0:T(8,128)(2,1)S(1)}, u32[]{:S(2)}, u32[]{:S(2)}) collective-permute-start(bf16[528,128]{1,0:T(8,128)(2,1)S(1)} %fold.1.refs_0_), channel_id=1, source_target_pairs={{0,2},{1,3},{2,0},{3,1},{4,6},{5,7},{6,4},{7,5},{8,10},{9,11},{10,... | collective-permute-start | bytes 405512 | tf_op jit(solution)/shard_map/ppermute | solution.py:208
  5.1 8.7 %collective-permute-start = (bf16[528,128]{1,0:T(8,128)(2,1)S(1)}, bf16[528,128]{1,0:T(8,128)(2,1)S(1)}, u32[]{:S(2)}, u32[]{:S(2)}) collective-permute-start(bf16[528,128]{1,0:T(8,128)(2,1)S(1)} %fold.1.refs_0_), channel_id=1, source_target_pairs={{0,1},{1,0},{2,3},{3,2},{4,5},{5,4},{6,7},{7,6},{8,9},{9,8},{10,11... | collective-permute-start | bytes 405512 | tf_op jit(solution)/shard_map/ppermute | solution.py:208
  6.7 7.7 %collective-permute-start.3 = (bf16[528,128]{1,0:T(8,128)(2,1)S(1)}, bf16[528,128]{1,0:T(8,128)(2,1)S(1)}, u32[]{:S(2)}, u32[]{:S(2)}) collective-permute-start(bf16[528,128]{1,0:T(8,128)(2,1)S(1)} %fold.1.refs_0_), channel_id=1, source_target_pairs={{0,8},{4,12},{8,0},{12,4},{1,9},{5,13},{9,1},{13,5},{2,10},{6,14},... | collective-permute-start | bytes 405512 | tf_op jit(solution)/shard_map/ppermute | solution.py:213
  8.2 6.1 %collective-permute-start.7 = (bf16[528,128]{1,0:T(8,128)(2,1)S(1)}, bf16[528,128]{1,0:T(8,128)(2,1)S(1)}, u32[]{:S(2)}, u32[]{:S(2)}) collective-permute-start(bf16[528,128]{1,0:T(8,128)(2,1)S(1)} %fold.1.refs_0_), channel_id=1, source_target_pairs={{0,4},{4,0},{8,12},{12,8},{1,5},{5,1},{9,13},{13,9},{2,6},{6,2},{1... | collective-permute-start | bytes 405512 | tf_op jit(solution)/shard_map/ppermute | solution.py:214
  11.7 5.0 %collective-permute-start.2 = (bf16[528,128]{1,0:T(8,128)(2,1)S(1)}, bf16[528,128]{1,0:T(8,128)(2,1)S(1)}, u32[]{:S(2)}, u32[]{:S(2)}) collective-permute-start(bf16[528,128]{1,0:T(8,128)(2,1)S(1)} %collective-permute-done.1.refs_2_), channel_id=1, source_target_pairs={{0,1},{1,0},{2,3},{3,2},{4,5},{5,4},{6,7},{7,6},{8,9},{9,8},{10,11... | collective-permute-start | bytes 405512 | tf_op jit(solution)/shard_map/ppermute | solution.py:208
  12.3 6.5 %collective-permute-start.5 = (bf16[528,128]{1,0:T(8,128)(2,1)S(1)}, bf16[528,128]{1,0:T(8,128)(2,1)S(1)}, u32[]{:S(2)}, u32[]{:S(2)}) collective-permute-start(bf16[528,128]{1,0:T(8,128)(2,1)S(1)} %collective-permute-done.1.refs_2_), channel_id=1, source_target_pairs={{0,8},{4,12},{8,0},{12,4},{1,9},{5,13},{9,1},{13,5},{2,10},{6,14},... | collective-permute-start | bytes 405512 | tf_op jit(solution)/shard_map/ppermute | solution.py:213
  13.8 7.9 %collective-permute-start.4 = (bf16[528,128]{1,0:T(8,128)(2,1)S(1)}, bf16[528,128]{1,0:T(8,128)(2,1)S(1)}, u32[]{:S(2)}, u32[]{:S(2)}) collective-permute-start(bf16[528,128]{1,0:T(8,128)(2,1)S(1)} %collective-permute-done.refs_1_), channel_id=1, source_target_pairs={{0,8},{4,12},{8,0},{12,4},{1,9},{5,13},{9,1},{13,5},{2,10},{6,14},... | collective-permute-start | bytes 405512 | tf_op jit(solution)/shard_map/ppermute | solution.py:213
  14.3 7.4 %collective-permute-start.9 = (bf16[528,128]{1,0:T(8,128)(2,1)S(1)}, bf16[528,128]{1,0:T(8,128)(2,1)S(1)}, u32[]{:S(2)}, u32[]{:S(2)}) collective-permute-start(bf16[528,128]{1,0:T(8,128)(2,1)S(1)} %collective-permute-done.1.refs_2_), channel_id=1, source_target_pairs={{0,4},{4,0},{8,12},{12,8},{1,5},{5,1},{9,13},{13,9},{2,6},{6,2},{1... | collective-permute-start | bytes 405512 | tf_op jit(solution)/shard_map/ppermute | solution.py:214
  14.4 7.9 %collective-permute-start.8 = (bf16[528,128]{1,0:T(8,128)(2,1)S(1)}, bf16[528,128]{1,0:T(8,128)(2,1)S(1)}, u32[]{:S(2)}, u32[]{:S(2)}) collective-permute-start(bf16[528,128]{1,0:T(8,128)(2,1)S(1)} %collective-permute-done.refs_1_), channel_id=1, source_target_pairs={{0,4},{4,0},{8,12},{12,8},{1,5},{5,1},{9,13},{13,9},{2,6},{6,2},{1... | collective-permute-start | bytes 405512 | tf_op jit(solution)/shard_map/ppermute | solution.py:214
  16.7 6.6 %collective-permute-start.6 = (bf16[528,128]{1,0:T(8,128)(2,1)S(1)}, bf16[528,128]{1,0:T(8,128)(2,1)S(1)}, u32[]{:S(2)}, u32[]{:S(2)}) collective-permute-start(bf16[528,128]{1,0:T(8,128)(2,1)S(1)} %collective-permute-done.2.refs_3_), channel_id=1, source_target_pairs={{0,8},{4,12},{8,0},{12,4},{1,9},{5,13},{9,1},{13,5},{2,10},{6,14},... | collective-permute-start | bytes 405512 | tf_op jit(solution)/shard_map/ppermute | solution.py:213
  18.8 4.5 %collective-permute-start.11 = (bf16[528,128]{1,0:T(8,128)(2,1)S(1)}, bf16[528,128]{1,0:T(8,128)(2,1)S(1)}, u32[]{:S(2)}, u32[]{:S(2)}) collective-permute-start(bf16[528,128]{1,0:T(8,128)(2,1)S(1)} %collective-permute-done.3.refs_4_), channel_id=1, source_target_pairs={{0,4},{4,0},{8,12},{12,8},{1,5},{5,1},{9,13},{13,9},{2,6},{6,2},{1... | collective-permute-start | bytes 405512 | tf_op jit(solution)/shard_map/ppermute | solution.py:214
  21.7 1.6 %collective-permute-start.10 = (bf16[528,128]{1,0:T(8,128)(2,1)S(1)}, bf16[528,128]{1,0:T(8,128)(2,1)S(1)}, u32[]{:S(2)}, u32[]{:S(2)}) collective-permute-start(bf16[528,128]{1,0:T(8,128)(2,1)S(1)} %collective-permute-done.2.refs_3_), channel_id=1, source_target_pairs={{0,4},{4,0},{8,12},{12,8},{1,5},{5,1},{9,13},{13,9},{2,6},{6,2},{1... | collective-permute-start | bytes 405512 | tf_op jit(solution)/shard_map/ppermute | solution.py:214
  21.7 1.6 %collective-permute-start.13 = (bf16[528,128]{1,0:T(8,128)(2,1)S(1)}, bf16[528,128]{1,0:T(8,128)(2,1)S(1)}, u32[]{:S(2)}, u32[]{:S(2)}) collective-permute-start(bf16[528,128]{1,0:T(8,128)(2,1)S(1)} %collective-permute-done.5.refs_6_), channel_id=1, source_target_pairs={{0,4},{4,0},{8,12},{12,8},{1,5},{5,1},{9,13},{13,9},{2,6},{6,2},{1... | collective-permute-start | bytes 405512 | tf_op jit(solution)/shard_map/ppermute | solution.py:214
  22.2 1.4 %collective-permute-start.12 = (bf16[528,128]{1,0:T(8,128)(2,1)S(1)}, bf16[528,128]{1,0:T(8,128)(2,1)S(1)}, u32[]{:S(2)}, u32[]{:S(2)}) collective-permute-start(bf16[528,128]{1,0:T(8,128)(2,1)S(1)} %collective-permute-done.4.refs_5_), channel_id=1, source_target_pairs={{0,4},{4,0},{8,12},{12,8},{1,5},{5,1},{9,13},{13,9},{2,6},{6,2},{1... | collective-permute-start | bytes 405512 | tf_op jit(solution)/shard_map/ppermute | solution.py:214
  23.3 1.4 %collective-permute-start.14 = (bf16[528,128]{1,0:T(8,128)(2,1)S(1)}, bf16[528,128]{1,0:T(8,128)(2,1)S(1)}, u32[]{:S(2)}, u32[]{:S(2)}) collective-permute-start(bf16[528,128]{1,0:T(8,128)(2,1)S(1)} %collective-permute-done.6.refs_7_), channel_id=1, source_target_pairs={{0,4},{4,0},{8,12},{12,8},{1,5},{5,1},{9,13},{13,9},{2,6},{6,2},{1... | collective-permute-start | bytes 405512 | tf_op jit(solution)/shard_map/ppermute | solution.py:214
  29.2 13.0 %collective-permute-start.16 = (s32[264,128]{1,0:T(8,128)S(1)}, s32[264,128]{1,0:T(8,128)S(1)}, u32[]{:S(2)}, u32[]{:S(2)}) collective-permute-start(s32[264,128]{1,0:T(8,128)S(1)} %get-tuple-element.11), channel_id=1, source_target_pairs={{0,2},{1,3},{2,0},{3,1},{4,6},{5,7},{6,4},{7,5},{8,10},{9,11},{10,... | collective-permute-start | bytes 405512 | tf_op jit(solution)/shard_map/ppermute | solution.py:244
  32.7 12.3 %copy-start.1 = (bf16[2,256,256]{2,1,0:T(8,128)(2,1)S(1)}, bf16[2,256,256]{2,1,0:T(8,128)(2,1)}, u32[]{:S(2)}) copy-start(bf16[2,256,256]{2,1,0:T(8,128)(2,1)} %core_ref.1) | copy-start | bytes 786436
  32.7 9.5 %collective-permute-start.17 = (s32[264,128]{1,0:T(8,128)S(1)}, s32[264,128]{1,0:T(8,128)S(1)}, u32[]{:S(2)}, u32[]{:S(2)}) collective-permute-start(s32[264,128]{1,0:T(8,128)S(1)} %get-tuple-element.12), channel_id=1, source_target_pairs={{0,3},{1,2},{2,1},{3,0},{4,7},{5,6},{6,5},{7,4},{8,11},{9,10},{10,... | collective-permute-start | bytes 405512 | tf_op jit(solution)/shard_map/ppermute | solution.py:244
  37.2 7.7 %collective-permute-start.15 = (s32[264,128]{1,0:T(8,128)S(1)}, s32[264,128]{1,0:T(8,128)S(1)}, u32[]{:S(2)}, u32[]{:S(2)}) collective-permute-start(s32[264,128]{1,0:T(8,128)S(1)} %get-tuple-element.10), channel_id=1, source_target_pairs={{0,1},{1,0},{2,3},{3,2},{4,5},{5,4},{6,7},{7,6},{8,9},{9,8},{10,11... | collective-permute-start | bytes 405512 | tf_op jit(solution)/shard_map/ppermute | solution.py:246

commit v4 on v3

--- a/solution.py
+++ b/solution.py
@@ -93,22 +93,40 @@
     out_ref[pl.ds(mono_dev * basis, rows)] = tail.astype(out_ref.dtype)
 
 
-def couple_kernel(groups, lanes, mono_dev, units, nbr_ref, esp_ref, *refs):
-    outs = refs[-3 - len(units) : -3]
-    pieces = refs[: -3 - len(units)]
-    store, blocks, sems = refs[-3:]
+def gate_kernel(piece_ref, *refs):
+    refs[-1][...] = piece_ref[...]
+
+
+def gather_kernel(*refs):
+    for i, piece in enumerate(refs[:-1]):
+        refs[-1][i] = piece[...]
+
+
+def stage_kernel(nbr_ref, esp_ref, *refs):
+    nbr_out, esp_out, row_out, sems = refs[-4:]
+    copies = [
+        pltpu.make_async_copy(esp_ref, esp_out, sems.at[0]),
+        pltpu.make_async_copy(nbr_ref, nbr_out, sems.at[1]),
+    ]
+    for copy in copies:
+        copy.start()
+    for i, piece in enumerate(refs[:-4]):
+        row_out[i] = piece[...]
+    for copy in copies:
+        copy.wait()
+
+
+def couple_kernel(groups, lanes, mono_dev, units, places, nbr_ref, esp_ref, *refs):
+    pieces, outs, store = refs[: len(places)], refs[len(places) : -1], refs[-1]
     my_group = lax.axis_index("gddi")
     my_lane = lax.axis_index("intra")
     _, slot_dev, basis, _ = esp_ref.shape
     mono_grp = mono_dev * lanes
     half = basis // 2
     tail_rows = store.shape[1] - mono_dev * basis
-    fragments = [(my_lane ^ k) * mono_dev + m for k in units for m in range(mono_dev)]
-    copies = [pltpu.make_async_copy(esp_ref.at[f], blocks.at[i], sems.at[i]) for i, f in enumerate(fragments)]
-    for copy in copies:
-        copy.start()
-    for i, piece in enumerate(pieces):
-        store[i] = piece[...]
+    for piece, where in zip(pieces, places):
+        for i, place in enumerate(where):
+            store[place] = piece[i]
 
     def near_density(fragment):
         apart = (fragment // mono_grp) ^ my_group
@@ -126,12 +144,11 @@
         bottom = jnp.concatenate([off.T, second.astype(off.dtype)], axis=1)
         return jnp.concatenate([top, bottom], axis=0)
 
-    def partial_of(i):
-        copies[i].wait()
+    def partial_of(fragment):
         total = None
         for s in range(slot_dev):
-            name = nbr_ref[my_lane * slot_dev + s, my_group * mono_grp + fragments[i]]
-            block = blocks[i, s]
+            name = nbr_ref[my_lane * slot_dev + s, my_group * mono_grp + fragment]
+            block = esp_ref[fragment, s]
             half_term = jnp.dot(block, near_density(name), preferred_element_type=jnp.float32)
             high = half_term.astype(jnp.bfloat16)
             low = (half_term - high.astype(jnp.float32)).astype(jnp.bfloat16)
@@ -140,17 +157,17 @@
         mixed, diag = fold(total[:half, :half], total[half:, half:])
         return total[:half, half:], mixed, diag
 
-    for i, (k, out) in enumerate(zip(units, outs)):
+    for k, out in zip(units, outs):
         if k == 0:
             for m in range(mono_dev):
-                off, mixed, diag = partial_of(i * mono_dev + m)
+                off, mixed, diag = partial_of((my_lane ^ k) * mono_dev + m)
                 out[m, :half] = off
                 out[m, half : 2 * half] = mixed
                 out[m, 2 * half :] = jnp.broadcast_to(diag, (8, half))
             continue
         tail = []
         for m in range(mono_dev):
-            off, mixed, diag = partial_of(i * mono_dev + m)
+            off, mixed, diag = partial_of((my_lane ^ k) * mono_dev + m)
             off_code = scale_code(peak_of(off))
             mixed_code = scale_code(jnp.maximum(peak_of(mixed), jnp.abs(diag)))
             out[pl.ds(m * half, half)] = pack(encode(off, off_code), encode(mixed, mixed_code))
@@ -190,6 +207,7 @@
     lanes = lax.axis_size("intra")
     mono_dev, basis = density.shape[0], density.shape[1]
     half = basis // 2
+    hbm = pl.BlockSpec(memory_space=pl.ANY)
     small = pltpu.CompilerParams(vmem_limit_bytes=8 * 2**20)
 
     rows = mono_dev * basis + round_up(mono_dev, 16)
@@ -201,37 +219,87 @@
         compiler_params=small,
         name="fold",
     )(density)
-    row = {0: shard}
-    bit = lanes // 2
+    def along_z(piece, bit):
+        return lax.ppermute(piece, "intra", xor_pairs(lanes, bit))
+
+    def along_y(piece, y):
+        return lax.ppermute(piece, "gddi", xor_pairs(groups, 2 * y))
+
+    rows_y = groups // 2
+    top = lanes // 2
+    near = {(0, 0): shard, (0, top): along_z(shard, top)}
+    bit = top // 2
     while bit:
-        for k in list(row):
-            row[k ^ bit] = lax.ppermute(row[k], "intra", xor_pairs(lanes, bit))
+        near[0, bit] = along_z(shard, bit)
         bit //= 2
-    near = []
-    for y in range(groups // 2):
-        for k in range(lanes):
-            near.append(row[k] if y == 0 else lax.ppermute(row[k], "gddi", xor_pairs(groups, 2 * y)))
-    pieces = near + [lax.ppermute(piece, "gddi", xor_pairs(groups, 1)) for piece in near]
+    for y in range(1, rows_y):
+        near[y, 0] = along_y(shard, y)
+    others = [piece for key, piece in near.items() if key != (0, top)]
+    for after in ([], others):
+        near[0, top] = pl.pallas_call(
+            gate_kernel,
+            out_shape=pltpu.VMEM(shard.shape, shard.dtype),
+            in_specs=[IN_VMEM] + [hbm] * len(after),
+            out_specs=IN_VMEM,
+            compiler_params=small,
+            name="gate",
+        )(near[0, top], *after)
+    bit = top // 2
+    while bit:
+        for k in [k for y, k in near if y == 0 and k and (0, k ^ bit) not in near]:
+            near[0, k ^ bit] = along_z(near[0, k], bit)
+        bit //= 2
+    for y in range(1, rows_y):
+        for k in range(1, lanes):
+            near[y, k] = along_y(near[0, k], y)
+
+    early = [(y, k) for y, k in near if (y > 0) + bin(k).count("1") <= 1]
+    later = [key for key in near if key not in early]
+
+    def shape(count):
+        return pltpu.VMEM((count, rows, half), density.dtype)
+
+    names, blocks, first = pl.pallas_call(
+        stage_kernel,
+        out_shape=[
+            pltpu.SMEM((nbr.shape[1], nbr.shape[0]), nbr.dtype),
+            pltpu.VMEM(esp_block.shape, esp_block.dtype),
+            shape(len(early)),
+        ],
+        in_specs=[hbm, hbm] + [IN_VMEM] * len(early),
+        out_specs=[IN_SMEM, IN_VMEM, IN_VMEM],
+        scratch_shapes=[pltpu.SemaphoreType.DMA((2,))],
+        compiler_params=small,
+        name="stage",
+    )(
+        pltpu.with_memory_space_constraint(nbr.T, pltpu.HBM),
+        pltpu.with_memory_space_constraint(esp_block, pltpu.HBM),
+        *[near[key] for key in early],
+    )
+    second = pl.pallas_call(
+        gather_kernel,
+        out_shape=shape(len(later)),
+        in_specs=[IN_VMEM] * len(later),
+        out_specs=IN_VMEM,
+        compiler_params=pltpu.CompilerParams(vmem_limit_bytes=2 * len(later) * rows * half * 2 + 4 * 2**20),
+        name="gather",
+    )(*[near[key] for key in later])
+    mine = [first, second]
+    pieces = mine + [lax.ppermute(piece, "gddi", xor_pairs(groups, 1)) for piece in mine]
+    places = [[y * lanes + k for y, k in keys] for keys in (early, later)]
+    places += [[rows_y * lanes + place for place in keys] for keys in places]
 
     own = jax.ShapeDtypeStruct((mono_dev, basis + 8, half), jnp.float32)
     coded = jax.ShapeDtypeStruct((mono_dev * half + round_up(2 * mono_dev, 8), half), jnp.int32)
-    piece_bytes = len(pieces) * rows * half * 2
-
-    blocks = pltpu.with_memory_space_constraint(esp_block, pltpu.HBM)
-
-    names = pltpu.with_memory_space_constraint(nbr.T, pltpu.HBM)
+    piece_bytes = groups * lanes * rows * half * 2
 
     def couple(units, name):
         return pl.pallas_call(
-            functools.partial(couple_kernel, groups, lanes, mono_dev, units),
+            functools.partial(couple_kernel, groups, lanes, mono_dev, units, places),
             out_shape=[own if k == 0 else coded for k in units],
-            in_specs=[IN_SMEM, pl.BlockSpec(memory_space=pl.ANY)] + [IN_VMEM] * len(pieces),
+            in_specs=[IN_SMEM] + [IN_VMEM] * (1 + len(pieces)),
             out_specs=[IN_VMEM] * len(units),
-            scratch_shapes=[
-                pltpu.VMEM((len(pieces), rows, half), density.dtype),
-                pltpu.VMEM((len(units) * mono_dev,) + esp_block.shape[1:], esp_block.dtype),
-                pltpu.SemaphoreType.DMA((len(units) * mono_dev,)),
-            ],
+            scratch_shapes=[pltpu.VMEM((groups * lanes, rows, half), density.dtype)],
             compiler_params=pltpu.CompilerParams(
                 vmem_limit_bytes=2 * (piece_bytes + esp_block.size * 2) + 8 * 2**20
             ),

time: 46.2 us -> 44.2 us (0.957)
  Pallas kernels: 10.2 us -> 6.12 us
  waiting for transfers between devices: 18.3 us -> 20.3 us
    pallas_call x2, Pallas kernels: 9.07 us -> 3.36 us  [couple(): pl.pallas_call(functools.partial(couple_kernel, groups, lanes, mono_dev,...]
    ppermute x2, waiting for transfers between devices: 4.37 us -> 7.18 us  [local(): lax.ppermute(far[k - lanes // 2], 'intra', xor_pairs(lanes, k))]
    pallas_call x0 -> x4, Pallas kernels: none -> 1.67 us  [the longest x1 1.62 us: local(): pl.pallas_call(stage_kernel, out_shape=[pltpu.SMEM((nbr.shape[1], nbr.sha...]
    ppermute x7, waiting for transfers between devices: 9.8 us -> 8.38 us  [the longest x3 5.19 us: along_z(): return lax.ppermute(piece, 'intra', xor_pairs(lanes, bit))]
    ppermute x8 -> x2, starting transfers between devices: 1.1 us -> 0.14 us  [local(): lax.ppermute(piece, 'gddi', xor_pairs(groups, 1))]
    ppermute x7, starting transfers between devices: 11.4 us -> 12.3 us  [the longest x3 7.2 us: along_z(): return lax.ppermute(piece, 'intra', xor_pairs(lanes, bit))]
    ppermute x8 -> x2, waiting for transfers between devices: 1.35 us -> 1.91 us  [local(): lax.ppermute(piece, 'gddi', xor_pairs(groups, 1))]
  transfers between devices with their start and end apart: 18 -> 12, of which waited for: 9 -> 8; matrix products, arithmetic and copies ran while one was open for 0% -> 0% of each run, Pallas kernels for 10% -> 8%
where the time goes in v4:
time: 44.2 us; the launch traced here: 44.1 us
  waiting for transfers between devices  20.3 us (46%)
  starting transfers between devices  16.6 us (38%)
  Pallas kernels  6.12 us (14%)
  local copies, waits for them, and re-layouts  0.95 us (2%)
    ppermute x3, starting transfers between devices, along_z(): return lax.ppermute(piece, 'intra', xor_pairs(lanes, bit))  7.2 us
    ppermute x2, waiting for transfers between devices, local(): lax.ppermute(far[k - lanes // 2], 'intra', xor_pairs(lanes, k))  7.18 us
    ppermute x3, waiting for transfers between devices, along_z(): return lax.ppermute(piece, 'intra', xor_pairs(lanes, bit))  5.19 us
    ppermute x4, starting transfers between devices, along_y(): return lax.ppermute(piece, 'gddi', xor_pairs(groups, 2 * y))  5.11 us
    ppermute x2, starting transfers between devices, local(): lax.ppermute(far[k - lanes // 2], 'intra', xor_pairs(lanes, k))  3.46 us
    pallas_call x2, Pallas kernels, couple(): pl.pallas_call(functools.partial(couple_kernel, groups, lanes, mono_dev,...  3.36 us
    ppermute x4, waiting for transfers between devices, along_y(): return lax.ppermute(piece, 'gddi', xor_pairs(groups, 2 * y))  3.19 us
    ppermute x1, waiting for transfers between devices, local(): lax.ppermute(close[k], 'intra', xor_pairs(lanes, k))  2.79 us
  transfers between devices with their start and end apart: 12, of which 8 were waited for; matrix products, arithmetic and copies ran while one was open for 0% of the time, Pallas kernels for 8%

profile of v4, /device:TPU:0, one launch (start us, length us, event | category | flops | bytes accessed | tf_op | source)
XLA Modules:
  0.0 44.1 jit_solution(434936483225529114)
XLA Ops:
  0.0 0.9 %copy-done = bf16[2,256,256]{2,1,0:T(8,128)(2,1)S(1)} copy-done((bf16[2,256,256]{2,1,0:T(8,128)(2,1)S(1)}, bf16[2,256,256]{2,1,0:T(8,128)(2,1)}, u32[]{:S(2)}) %copy-start) | copy-done | bytes 262168
  1.0 4.1 %collective-permute-start = (bf16[528,128]{1,0:T(8,128)(2,1)S(1)}, bf16[528,128]{1,0:T(8,128)(2,1)S(1)}, u32[]{:S(2)}, u32[]{:S(2)}) collective-permute-start(bf16[528,128]{1,0:T(8,128)(2,1)S(1)} %fold.1.refs_0_), channel_id=1, source_target_pairs={{0,2},{1,3},{2,0},{3,1},{4,6},{5,7},{6,4},{7,5},{8,10},{9,11},{10,... | collective-permute-start | bytes 405512 | tf_op jit(solution)/shard_map/ppermute | solution.py:223
  5.1 1.6 %collective-permute-start.1 = (bf16[528,128]{1,0:T(8,128)(2,1)S(1)}, bf16[528,128]{1,0:T(8,128)(2,1)S(1)}, u32[]{:S(2)}, u32[]{:S(2)}) collective-permute-start(bf16[528,128]{1,0:T(8,128)(2,1)S(1)} %fold.1.refs_0_), channel_id=1, source_target_pairs={{0,1},{1,0},{2,3},{3,2},{4,5},{5,4},{6,7},{7,6},{8,9},{9,8},{10,11... | collective-permute-start | bytes 405512 | tf_op jit(solution)/shard_map/ppermute | solution.py:223
  6.7 1.5 %collective-permute-start.2 = (bf16[528,128]{1,0:T(8,128)(2,1)S(1)}, bf16[528,128]{1,0:T(8,128)(2,1)S(1)}, u32[]{:S(2)}, u32[]{:S(2)}) collective-permute-start(bf16[528,128]{1,0:T(8,128)(2,1)S(1)} %fold.1.refs_0_), channel_id=1, source_target_pairs={{0,8},{4,12},{8,0},{12,4},{1,9},{5,13},{9,1},{13,5},{2,10},{6,14},... | collective-permute-start | bytes 405512 | tf_op jit(solution)/shard_map/ppermute | solution.py:226
  8.2 3.5 %collective-permute-done.piece_ref = bf16[528,128]{1,0:T(8,128)(2,1)S(1)} collective-permute-done((bf16[528,128]{1,0:T(8,128)(2,1)S(1)}, bf16[528,128]{1,0:T(8,128)(2,1)S(1)}, u32[]{:S(2)}, u32[]{:S(2)}) %collective-permute-start) | collective-permute-done | bytes 135200 | tf_op jit(solution)/shard_map/ppermute | solution.py:223
  11.7 0.2 collective-permute-done.1.refs_1_.refs_2_
  11.9 1.5 %collective-permute-start.3 = (bf16[528,128]{1,0:T(8,128)(2,1)S(1)}, bf16[528,128]{1,0:T(8,128)(2,1)S(1)}, u32[]{:S(2)}, u32[]{:S(2)}) collective-permute-start(bf16[528,128]{1,0:T(8,128)(2,1)S(1)} %gate.3.refs_1_), channel_id=1, source_target_pairs={{0,1},{1,0},{2,3},{3,2},{4,5},{5,4},{6,7},{7,6},{8,9},{9,8},{10,11... | collective-permute-start | bytes 405512 | tf_op jit(solution)/shard_map/ppermute | solution.py:223
  13.4 1.5 %collective-permute-start.5 = (bf16[528,128]{1,0:T(8,128)(2,1)S(1)}, bf16[528,128]{1,0:T(8,128)(2,1)S(1)}, u32[]{:S(2)}, u32[]{:S(2)}) collective-permute-start(bf16[528,128]{1,0:T(8,128)(2,1)S(1)} %gate.3.refs_1_), channel_id=1, source_target_pairs={{0,8},{4,12},{8,0},{12,4},{1,9},{5,13},{9,1},{13,5},{2,10},{6,14},... | collective-permute-start | bytes 405512 | tf_op jit(solution)/shard_map/ppermute | solution.py:226
  14.9 0.5 %collective-permute-start.4 = (bf16[528,128]{1,0:T(8,128)(2,1)S(1)}, bf16[528,128]{1,0:T(8,128)(2,1)S(1)}, u32[]{:S(2)}, u32[]{:S(2)}) collective-permute-start(bf16[528,128]{1,0:T(8,128)(2,1)S(1)} %collective-permute-done.1.refs_1_.refs_2_), channel_id=1, source_target_pairs={{0,8},{4,12},{8,0},{12,4},{1,9},{5,13},{9,1},{13,5},{2,10},{6,14},... | collective-permute-start | bytes 405512 | tf_op jit(solution)/shard_map/ppermute | solution.py:226
  15.5 1.5 %collective-permute-done.3.refs_0_ = bf16[528,128]{1,0:T(8,128)(2,1)S(1)} collective-permute-done((bf16[528,128]{1,0:T(8,128)(2,1)S(1)}, bf16[528,128]{1,0:T(8,128)(2,1)S(1)}, u32[]{:S(2)}, u32[]{:S(2)}) %collective-permute-start.3) | collective-permute-done | bytes 135200 | tf_op jit(solution)/shard_map/ppermute | solution.py:223
  17.0 1.6 %collective-permute-start.6 = (bf16[528,128]{1,0:T(8,128)(2,1)S(1)}, bf16[528,128]{1,0:T(8,128)(2,1)S(1)}, u32[]{:S(2)}, u32[]{:S(2)}) collective-permute-start(bf16[528,128]{1,0:T(8,128)(2,1)S(1)} %collective-permute-done.3.refs_0_), channel_id=1, source_target_pairs={{0,8},{4,12},{8,0},{12,4},{1,9},{5,13},{9,1},{13,5},{2,10},{6,14},... | collective-permute-start | bytes 405512 | tf_op jit(solution)/shard_map/ppermute | solution.py:226
  18.6 1.6 %stage.1 = (s32[8,32]{1,0:T(8,128)S(4)}, bf16[8,2,256,256]{3,2,1,0:T(8,128)(2,1)S(1)}, bf16[4,528,128]{2,1,0:T(8,128)(2,1)S(1)}) custom-call(s32[8,32]{1,0:T(8,128)} %bitcast.1, bf16[8,2,256,256]{3,2,1,0:T(8,128)(2,1)} %esp_ref.1, bf16[528,128]{1,0:T(8,128)(2,1)S(1)} %fold.1.refs_0_, bf16[528,128]{1,0:T(8,128)(2,1)S(1)} %gate.3.refs_1_, ...), custom_call_target="tpu_custom_call" | custom-call | tf_op jit(solution)/shard_map/stage/pallas_call | solution.py:262
  20.2 0.1 collective-permute-start.7
  20.3 1.7 %collective-permute-done.4.refs_1_ = bf16[528,128]{1,0:T(8,128)(2,1)S(1)} collective-permute-done((bf16[528,128]{1,0:T(8,128)(2,1)S(1)}, bf16[528,128]{1,0:T(8,128)(2,1)S(1)}, u32[]{:S(2)}, u32[]{:S(2)}) %collective-permute-start.4) | collective-permute-done | bytes 135200 | tf_op jit(solution)/shard_map/ppermute | solution.py:226
  22.0 1.4 %collective-permute-done.6.refs_3_ = bf16[528,128]{1,0:T(8,128)(2,1)S(1)} collective-permute-done((bf16[528,128]{1,0:T(8,128)(2,1)S(1)}, bf16[528,128]{1,0:T(8,128)(2,1)S(1)}, u32[]{:S(2)}, u32[]{:S(2)}) %collective-permute-start.6) | collective-permute-done | bytes 135200 | tf_op jit(solution)/shard_map/ppermute | solution.py:226
  23.5 0.1 collective-permute-start.8
  23.6 1.9 %collective-permute-done.8.refs_3_ = bf16[4,528,128]{2,1,0:T(8,128)(2,1)S(1)} collective-permute-done((bf16[4,528,128]{2,1,0:T(8,128)(2,1)S(1)}, bf16[4,528,128]{2,1,0:T(8,128)(2,1)S(1)}, u32[]{:S(2)}, u32[]{:S(2)}) %collective-permute-start.8) | collective-permute-done | bytes 540704 | tf_op jit(solution)/shard_map/ppermute | solution.py:288
  25.5 1.7 %couple_far.1 = (s32[264,128]{1,0:T(8,128)S(1)}, s32[264,128]{1,0:T(8,128)S(1)}) custom-call(s32[8,32]{1,0:T(8,128)S(4)} %get-tuple-element.12.nbr_ref, bf16[8,2,256,256]{3,2,1,0:T(8,128)(2,1)S(1)} %get-tuple-element.13.esp_ref, bf16[4,528,128]{2,1,0:T(8,128)(2,1)S(1)} %get-tuple-element.14.refs_0_, bf16[4,528,128]{2,1,0:T(8,128)(2,1)S(1)} %gather.1.refs_1_, ...), custom_call_target="tpu_custom_call" | custom-call | tf_op jit(solution)/shard_map/couple_far/pallas_call | solution.py:297
  27.2 3.5 %collective-permute-start.10 = (s32[264,128]{1,0:T(8,128)S(1)}, s32[264,128]{1,0:T(8,128)S(1)}, u32[]{:S(2)}, u32[]{:S(2)}) collective-permute-start(s32[264,128]{1,0:T(8,128)S(1)} %get-tuple-element.17), channel_id=1, source_target_pairs={{0,2},{1,3},{2,0},{3,1},{4,6},{5,7},{6,4},{7,5},{8,10},{9,11},{10,... | collective-permute-start | bytes 405512 | tf_op jit(solution)/shard_map/ppermute | solution.py:312
  30.7 1.7 %couple_near.1 = (f32[2,264,128]{2,1,0:T(8,128)S(1)}, s32[264,128]{1,0:T(8,128)S(1)}) custom-call(s32[8,32]{1,0:T(8,128)S(4)} %get-tuple-element.12.nbr_ref, bf16[8,2,256,256]{3,2,1,0:T(8,128)(2,1)S(1)} %get-tuple-element.13.esp_ref, bf16[4,528,128]{2,1,0:T(8,128)(2,1)S(1)} %get-tuple-element.14.refs_0_, bf16[4,528,128]{2,1,0:T(8,128)(2,1)S(1)} %gather.1.refs_1_, ...), custom_call_target="tpu_custom_call" | custom-call | tf_op jit(solution)/shard_map/couple_near/pallas_call | solution.py:297
  32.3 0.7 %collective-permute-start.9 = (s32[264,128]{1,0:T(8,128)S(1)}, s32[264,128]{1,0:T(8,128)S(1)}, u32[]{:S(2)}, u32[]{:S(2)}) collective-permute-start(s32[264,128]{1,0:T(8,128)S(1)} %get-tuple-element.16), channel_id=1, source_target_pairs={{0,1},{1,0},{2,3},{3,2},{4,5},{5,4},{6,7},{7,6},{8,9},{9,8},{10,11... | collective-permute-start | bytes 405512 | tf_op jit(solution)/shard_map/ppermute | solution.py:314
  33.0 7.2 %collective-permute-done.10.refs_1_ = s32[264,128]{1,0:T(8,128)S(1)} collective-permute-done((s32[264,128]{1,0:T(8,128)S(1)}, s32[264,128]{1,0:T(8,128)S(1)}, u32[]{:S(2)}, u32[]{:S(2)}) %collective-permute-start.10) | collective-permute-done | bytes 135200 | tf_op jit(solution)/shard_map/ppermute | solution.py:312
  40.2 2.8 %collective-permute-done.9.refs_0_ = s32[264,128]{1,0:T(8,128)S(1)} collective-permute-done((s32[264,128]{1,0:T(8,128)S(1)}, s32[264,128]{1,0:T(8,128)S(1)}, u32[]{:S(2)}, u32[]{:S(2)}) %collective-permute-start.9) | collective-permute-done | bytes 135200 | tf_op jit(solution)/shard_map/ppermute | solution.py:314
  43.0 1.0 %finish.1 = f32[2,256,256]{2,1,0:T(8,128)} custom-call(bf16[2,256,256]{2,1,0:T(8,128)(2,1)S(1)} %copy-done.1, f32[2,264,128]{2,1,0:T(8,128)S(1)} %get-tuple-element.15.own_ref, s32[264,128]{1,0:T(8,128)S(1)} %collective-permute-done.9.refs_0_, s32[264,128]{1,0:T(8,128)S(1)} %collective-permute-done.10.refs_1_, s32[264,128]{1,0:T(8,128)S(1)} %collective-permute-done.11.refs_2_), custom_call_target="tpu_custom_call" | custom-call | tf_op jit(solution)/shard_map/finish/pallas_call | solution.py:315
  (12 shorter events, 0.1 us)
Async XLA Ops:
  0.0 0.9 %copy-start = (bf16[2,256,256]{2,1,0:T(8,128)(2,1)S(1)}, bf16[2,256,256]{2,1,0:T(8,128)(2,1)}, u32[]{:S(2)}) copy-start(bf16[2,256,256]{2,1,0:T(8,128)(2,1)} %dens_ref.1) | copy-start | bytes 786436
  1.0 10.7 %collective-permute-start = (bf16[528,128]{1,0:T(8,128)(2,1)S(1)}, bf16[528,128]{1,0:T(8,128)(2,1)S(1)}, u32[]{:S(2)}, u32[]{:S(2)}) collective-permute-start(bf16[528,128]{1,0:T(8,128)(2,1)S(1)} %fold.1.refs_0_), channel_id=1, source_target_pairs={{0,2},{1,3},{2,0},{3,1},{4,6},{5,7},{6,4},{7,5},{8,10},{9,11},{10,... | collective-permute-start | bytes 405512 | tf_op jit(solution)/shard_map/ppermute | solution.py:223
  5.1 6.8 %collective-permute-start.1 = (bf16[528,128]{1,0:T(8,128)(2,1)S(1)}, bf16[528,128]{1,0:T(8,128)(2,1)S(1)}, u32[]{:S(2)}, u32[]{:S(2)}) collective-permute-start(bf16[528,128]{1,0:T(8,128)(2,1)S(1)} %fold.1.refs_0_), channel_id=1, source_target_pairs={{0,1},{1,0},{2,3},{3,2},{4,5},{5,4},{6,7},{7,6},{8,9},{9,8},{10,11... | collective-permute-start | bytes 405512 | tf_op jit(solution)/shard_map/ppermute | solution.py:223
  6.7 5.2 %collective-permute-start.2 = (bf16[528,128]{1,0:T(8,128)(2,1)S(1)}, bf16[528,128]{1,0:T(8,128)(2,1)S(1)}, u32[]{:S(2)}, u32[]{:S(2)}) collective-permute-start(bf16[528,128]{1,0:T(8,128)(2,1)S(1)} %fold.1.refs_0_), channel_id=1, source_target_pairs={{0,8},{4,12},{8,0},{12,4},{1,9},{5,13},{9,1},{13,5},{2,10},{6,14},... | collective-permute-start | bytes 405512 | tf_op jit(solution)/shard_map/ppermute | solution.py:226
  11.9 5.1 %collective-permute-start.3 = (bf16[528,128]{1,0:T(8,128)(2,1)S(1)}, bf16[528,128]{1,0:T(8,128)(2,1)S(1)}, u32[]{:S(2)}, u32[]{:S(2)}) collective-permute-start(bf16[528,128]{1,0:T(8,128)(2,1)S(1)} %gate.3.refs_1_), channel_id=1, source_target_pairs={{0,1},{1,0},{2,3},{3,2},{4,5},{5,4},{6,7},{7,6},{8,9},{9,8},{10,11... | collective-permute-start | bytes 405512 | tf_op jit(solution)/shard_map/ppermute | solution.py:223
  13.4 6.8 %collective-permute-start.5 = (bf16[528,128]{1,0:T(8,128)(2,1)S(1)}, bf16[528,128]{1,0:T(8,128)(2,1)S(1)}, u32[]{:S(2)}, u32[]{:S(2)}) collective-permute-start(bf16[528,128]{1,0:T(8,128)(2,1)S(1)} %gate.3.refs_1_), channel_id=1, source_target_pairs={{0,8},{4,12},{8,0},{12,4},{1,9},{5,13},{9,1},{13,5},{2,10},{6,14},... | collective-permute-start | bytes 405512 | tf_op jit(solution)/shard_map/ppermute | solution.py:226
  14.9 7.1 %collective-permute-start.4 = (bf16[528,128]{1,0:T(8,128)(2,1)S(1)}, bf16[528,128]{1,0:T(8,128)(2,1)S(1)}, u32[]{:S(2)}, u32[]{:S(2)}) collective-permute-start(bf16[528,128]{1,0:T(8,128)(2,1)S(1)} %collective-permute-done.1.refs_1_.refs_2_), channel_id=1, source_target_pairs={{0,8},{4,12},{8,0},{12,4},{1,9},{5,13},{9,1},{13,5},{2,10},{6,14},... | collective-permute-start | bytes 405512 | tf_op jit(solution)/shard_map/ppermute | solution.py:226
  17.0 6.5 %collective-permute-start.6 = (bf16[528,128]{1,0:T(8,128)(2,1)S(1)}, bf16[528,128]{1,0:T(8,128)(2,1)S(1)}, u32[]{:S(2)}, u32[]{:S(2)}) collective-permute-start(bf16[528,128]{1,0:T(8,128)(2,1)S(1)} %collective-permute-done.3.refs_0_), channel_id=1, source_target_pairs={{0,8},{4,12},{8,0},{12,4},{1,9},{5,13},{9,1},{13,5},{2,10},{6,14},... | collective-permute-start | bytes 405512 | tf_op jit(solution)/shard_map/ppermute | solution.py:226
  20.2 3.4 %collective-permute-start.7 = (bf16[4,528,128]{2,1,0:T(8,128)(2,1)S(1)}, bf16[4,528,128]{2,1,0:T(8,128)(2,1)S(1)}, u32[]{:S(2)}, u32[]{:S(2)}) collective-permute-start(bf16[4,528,128]{2,1,0:T(8,128)(2,1)S(1)} %get-tuple-element.14.refs_0_), channel_id=1, source_target_pairs={{0,4},{4,0},{8,12},{12,8},{1,5},{5,1},{9,13},{13,9},{2,6},{6,2},{1... | collective-permute-start | bytes 1622024 | tf_op jit(solution)/shard_map/ppermute | solution.py:288
  23.5 2.0 %collective-permute-start.8 = (bf16[4,528,128]{2,1,0:T(8,128)(2,1)S(1)}, bf16[4,528,128]{2,1,0:T(8,128)(2,1)S(1)}, u32[]{:S(2)}, u32[]{:S(2)}) collective-permute-start(bf16[4,528,128]{2,1,0:T(8,128)(2,1)S(1)} %gather.1.refs_1_), channel_id=1, source_target_pairs={{0,4},{4,0},{8,12},{12,8},{1,5},{5,1},{9,13},{13,9},{2,6},{6,2},{1... | collective-permute-start | bytes 1622024 | tf_op jit(solution)/shard_map/ppermute | solution.py:288
  27.2 13.0 %collective-permute-start.10 = (s32[264,128]{1,0:T(8,128)S(1)}, s32[264,128]{1,0:T(8,128)S(1)}, u32[]{:S(2)}, u32[]{:S(2)}) collective-permute-start(s32[264,128]{1,0:T(8,128)S(1)} %get-tuple-element.17), channel_id=1, source_target_pairs={{0,2},{1,3},{2,0},{3,1},{4,6},{5,7},{6,4},{7,5},{8,10},{9,11},{10,... | collective-permute-start | bytes 405512 | tf_op jit(solution)/shard_map/ppermute | solution.py:312
  30.6 12.4 %copy-start.1 = (bf16[2,256,256]{2,1,0:T(8,128)(2,1)S(1)}, bf16[2,256,256]{2,1,0:T(8,128)(2,1)}, u32[]{:S(2)}) copy-start(bf16[2,256,256]{2,1,0:T(8,128)(2,1)} %core_ref.1) | copy-start | bytes 786436
  30.6 9.6 %collective-permute-start.11 = (s32[264,128]{1,0:T(8,128)S(1)}, s32[264,128]{1,0:T(8,128)S(1)}, u32[]{:S(2)}, u32[]{:S(2)}) collective-permute-start(s32[264,128]{1,0:T(8,128)S(1)} %get-tuple-element.18), channel_id=1, source_target_pairs={{0,3},{1,2},{2,1},{3,0},{4,7},{5,6},{6,5},{7,4},{8,11},{9,10},{10,... | collective-permute-start | bytes 405512 | tf_op jit(solution)/shard_map/ppermute | solution.py:312
  32.3 10.7 %collective-permute-start.9 = (s32[264,128]{1,0:T(8,128)S(1)}, s32[264,128]{1,0:T(8,128)S(1)}, u32[]{:S(2)}, u32[]{:S(2)}) collective-permute-start(s32[264,128]{1,0:T(8,128)S(1)} %get-tuple-element.16), channel_id=1, source_target_pairs={{0,1},{1,0},{2,3},{3,2},{4,5},{5,4},{6,7},{7,6},{8,9},{9,8},{10,11... | collective-permute-start | bytes 405512 | tf_op jit(solution)/shard_map/ppermute | solution.py:314

commit v5 on v4

--- a/solution.py
+++ b/solution.py
@@ -228,30 +228,42 @@
     rows_y = groups // 2
     top = lanes // 2
     near = {(0, 0): shard, (0, top): along_z(shard, top)}
-    bit = top // 2
-    while bit:
-        near[0, bit] = along_z(shard, bit)
-        bit //= 2
+
+    def double(start):
+        bit = top // 2
+        while bit:
+            for k in range(start, start + top):
+                if (0, k) in near and (0, k ^ bit) not in near:
+                    near[0, k ^ bit] = along_z(near[0, k], bit)
+            bit //= 2
+
+    double(0)
     for y in range(1, rows_y):
         near[y, 0] = along_y(shard, y)
-    others = [piece for key, piece in near.items() if key != (0, top)]
-    for after in ([], others):
-        near[0, top] = pl.pallas_call(
+
+    def gate(piece, *after):
+        return pl.pallas_call(
             gate_kernel,
             out_shape=pltpu.VMEM(shard.shape, shard.dtype),
             in_specs=[IN_VMEM] + [hbm] * len(after),
             out_specs=IN_VMEM,
             compiler_params=small,
             name="gate",
-        )(near[0, top], *after)
-    bit = top // 2
-    while bit:
-        for k in [k for y, k in near if y == 0 and k and (0, k ^ bit) not in near]:
-            near[0, k ^ bit] = along_z(near[0, k], bit)
-        bit //= 2
+        )(piece, *after)
+
+    others = [piece for key, piece in near.items() if key != (0, top)]
+    near[0, top] = gate(gate(near[0, top]), *others)
     for y in range(1, rows_y):
-        for k in range(1, lanes):
+        for k in range(1, top):
             near[y, k] = along_y(near[0, k], y)
+    double(top)
+    ahead = [near[y, k] for y in range(1, rows_y) for k in range(1, top)]
+    for _ in range(3):
+        ahead = [gate(ahead[0], *ahead[1:])]
+    for y in range(1, rows_y):
+        near[y, top] = along_y(near[0, top], y)
+        for k in range(top + 1, lanes):
+            near[y, k] = along_y(gate(near[0, k], *ahead), y)
 
     early = [(y, k) for y, k in near if (y > 0) + bin(k).count("1") <= 1]
     later = [key for key in near if key not in early]

time: 44.2 us -> 43 us (0.973)
  waiting for transfers between devices: 20.3 us -> 19.2 us
    ppermute x4, waiting for transfers between devices: 3.19 us -> 1.79 us  [along_y(): return lax.ppermute(piece, 'gddi', xor_pairs(groups, 2 * y))]
    ppermute x4, starting transfers between devices: 5.11 us -> 6.47 us  [along_y(): return lax.ppermute(piece, 'gddi', xor_pairs(groups, 2 * y))]
    ppermute x3, starting transfers between devices: 7.2 us -> 6.19 us  [along_z(): return lax.ppermute(piece, 'intra', xor_pairs(lanes, bit))]
    ppermute x3, waiting for transfers between devices: 5.19 us -> 5.92 us  [along_z(): return lax.ppermute(piece, 'intra', xor_pairs(lanes, bit))]
    ppermute x2, starting transfers between devices: 3.46 us -> 2.86 us  [local(): lax.ppermute(far[k - lanes // 2], 'intra', xor_pairs(lanes, k))]
  transfers between devices with their start and end apart: 12 -> 12, of which waited for: 8 -> 7; matrix products, arithmetic and copies ran while one was open for 0% -> 0% of each run, Pallas kernels for 8% -> 8%
where the time goes in v5:
time: 43 us; the launch traced here: 42.9 us
  waiting for transfers between devices  19.2 us (45%)
  starting transfers between devices  16.4 us (38%)
  Pallas kernels  6.18 us (14%)
  local copies, waits for them, and re-layouts  0.95 us (2%)
    ppermute x2, waiting for transfers between devices, local(): lax.ppermute(far[k - lanes // 2], 'intra', xor_pairs(lanes, k))  7.1 us
    ppermute x4, starting transfers between devices, along_y(): return lax.ppermute(piece, 'gddi', xor_pairs(groups, 2 * y))  6.47 us
    ppermute x3, starting transfers between devices, along_z(): return lax.ppermute(piece, 'intra', xor_pairs(lanes, bit))  6.19 us
    ppermute x3, waiting for transfers between devices, along_z(): return lax.ppermute(piece, 'intra', xor_pairs(lanes, bit))  5.92 us
    pallas_call x2, Pallas kernels, couple(): pl.pallas_call(functools.partial(couple_kernel, groups, lanes, mono_dev,...  3.37 us
    ppermute x2, starting transfers between devices, local(): lax.ppermute(far[k - lanes // 2], 'intra', xor_pairs(lanes, k))  2.86 us
    ppermute x1, waiting for transfers between devices, local(): lax.ppermute(close[k], 'intra', xor_pairs(lanes, k))  2.49 us
    ppermute x2, waiting for transfers between devices, local(): lax.ppermute(piece, 'gddi', xor_pairs(groups, 1))  1.92 us
  transfers between devices with their start and end apart: 12, of which 7 were waited for; matrix products, arithmetic and copies ran while one was open for 0% of the time, Pallas kernels for 8%

profile of v5, /device:TPU:0, one launch (start us, length us, event | category | flops | bytes accessed | tf_op | source)
XLA Modules:
  0.0 42.9 jit_solution(13129308779781804845)
XLA Ops:
  0.0 0.9 %copy-done = bf16[2,256,256]{2,1,0:T(8,128)(2,1)S(1)} copy-done((bf16[2,256,256]{2,1,0:T(8,128)(2,1)S(1)}, bf16[2,256,256]{2,1,0:T(8,128)(2,1)}, u32[]{:S(2)}) %copy-start) | copy-done | bytes 262168
  1.0 3.1 %collective-permute-start.1 = (bf16[528,128]{1,0:T(8,128)(2,1)S(1)}, bf16[528,128]{1,0:T(8,128)(2,1)S(1)}, u32[]{:S(2)}, u32[]{:S(2)}) collective-permute-start(bf16[528,128]{1,0:T(8,128)(2,1)S(1)} %fold.1.refs_0_), channel_id=1, source_target_pairs={{0,1},{1,0},{2,3},{3,2},{4,5},{5,4},{6,7},{7,6},{8,9},{9,8},{10,11... | collective-permute-start | bytes 405512 | tf_op jit(solution)/shard_map/ppermute | solution.py:223
  4.1 2.6 %collective-permute-start = (bf16[528,128]{1,0:T(8,128)(2,1)S(1)}, bf16[528,128]{1,0:T(8,128)(2,1)S(1)}, u32[]{:S(2)}, u32[]{:S(2)}) collective-permute-start(bf16[528,128]{1,0:T(8,128)(2,1)S(1)} %fold.1.refs_0_), channel_id=1, source_target_pairs={{0,2},{1,3},{2,0},{3,1},{4,6},{5,7},{6,4},{7,5},{8,10},{9,11},{10,... | collective-permute-start | bytes 405512 | tf_op jit(solution)/shard_map/ppermute | solution.py:223
  6.7 1.5 %collective-permute-start.2 = (bf16[528,128]{1,0:T(8,128)(2,1)S(1)}, bf16[528,128]{1,0:T(8,128)(2,1)S(1)}, u32[]{:S(2)}, u32[]{:S(2)}) collective-permute-start(bf16[528,128]{1,0:T(8,128)(2,1)S(1)} %fold.1.refs_0_), channel_id=1, source_target_pairs={{0,8},{4,12},{8,0},{12,4},{1,9},{5,13},{9,1},{13,5},{2,10},{6,14},... | collective-permute-start | bytes 405512 | tf_op jit(solution)/shard_map/ppermute | solution.py:226
  8.2 1.5 %collective-permute-done.1.refs_1_.refs_2_ = bf16[528,128]{1,0:T(8,128)(2,1)S(1)} collective-permute-done((bf16[528,128]{1,0:T(8,128)(2,1)S(1)}, bf16[528,128]{1,0:T(8,128)(2,1)S(1)}, u32[]{:S(2)}, u32[]{:S(2)}) %collective-permute-start.1) | collective-permute-done | bytes 135200 | tf_op jit(solution)/shard_map/ppermute | solution.py:223
  9.7 1.8 %collective-permute-start.3 = (bf16[528,128]{1,0:T(8,128)(2,1)S(1)}, bf16[528,128]{1,0:T(8,128)(2,1)S(1)}, u32[]{:S(2)}, u32[]{:S(2)}) collective-permute-start(bf16[528,128]{1,0:T(8,128)(2,1)S(1)} %collective-permute-done.1.refs_1_.refs_2_), channel_id=1, source_target_pairs={{0,8},{4,12},{8,0},{12,4},{1,9},{5,13},{9,1},{13,5},{2,10},{6,14},... | collective-permute-start | bytes 405512 | tf_op jit(solution)/shard_map/ppermute | solution.py:226
  11.5 1.4 %collective-permute-done.piece_ref = bf16[528,128]{1,0:T(8,128)(2,1)S(1)} collective-permute-done((bf16[528,128]{1,0:T(8,128)(2,1)S(1)}, bf16[528,128]{1,0:T(8,128)(2,1)S(1)}, u32[]{:S(2)}, u32[]{:S(2)}) %collective-permute-start) | collective-permute-done | bytes 135200 | tf_op jit(solution)/shard_map/ppermute | solution.py:223
  13.0 0.5 %collective-permute-start.4 = (bf16[528,128]{1,0:T(8,128)(2,1)S(1)}, bf16[528,128]{1,0:T(8,128)(2,1)S(1)}, u32[]{:S(2)}, u32[]{:S(2)}) collective-permute-start(bf16[528,128]{1,0:T(8,128)(2,1)S(1)} %gate.7.refs_1_), channel_id=1, source_target_pairs={{0,1},{1,0},{2,3},{3,2},{4,5},{5,4},{6,7},{7,6},{8,9},{9,8},{10,11... | collective-permute-start | bytes 405512 | tf_op jit(solution)/shard_map/ppermute | solution.py:223
  13.5 1.5 %collective-permute-start.5 = (bf16[528,128]{1,0:T(8,128)(2,1)S(1)}, bf16[528,128]{1,0:T(8,128)(2,1)S(1)}, u32[]{:S(2)}, u32[]{:S(2)}) collective-permute-start(bf16[528,128]{1,0:T(8,128)(2,1)S(1)} %gate.7.refs_1_), channel_id=1, source_target_pairs={{0,8},{4,12},{8,0},{12,4},{1,9},{5,13},{9,1},{13,5},{2,10},{6,14},... | collective-permute-start | bytes 405512 | tf_op jit(solution)/shard_map/ppermute | solution.py:226
  15.1 3.0 %collective-permute-done.4.piece_ref.refs_1_ = bf16[528,128]{1,0:T(8,128)(2,1)S(1)} collective-permute-done((bf16[528,128]{1,0:T(8,128)(2,1)S(1)}, bf16[528,128]{1,0:T(8,128)(2,1)S(1)}, u32[]{:S(2)}, u32[]{:S(2)}) %collective-permute-start.4) | collective-permute-done | bytes 135200 | tf_op jit(solution)/shard_map/ppermute | solution.py:223
  18.1 1.6 %collective-permute-start.6 = (bf16[528,128]{1,0:T(8,128)(2,1)S(1)}, bf16[528,128]{1,0:T(8,128)(2,1)S(1)}, u32[]{:S(2)}, u32[]{:S(2)}) collective-permute-start(bf16[528,128]{1,0:T(8,128)(2,1)S(1)} %gate.11), channel_id=1, source_target_pairs={{0,8},{4,12},{8,0},{12,4},{1,9},{5,13},{9,1},{13,5},{2,10},{6,14},... | collective-permute-start | bytes 405512 | tf_op jit(solution)/shard_map/ppermute | solution.py:226
  19.7 1.6 %stage.1 = (s32[8,32]{1,0:T(8,128)S(4)}, bf16[8,2,256,256]{3,2,1,0:T(8,128)(2,1)S(1)}, bf16[4,528,128]{2,1,0:T(8,128)(2,1)S(1)}) custom-call(s32[8,32]{1,0:T(8,128)} %bitcast.1, bf16[8,2,256,256]{3,2,1,0:T(8,128)(2,1)} %esp_ref.1, bf16[528,128]{1,0:T(8,128)(2,1)S(1)} %fold.1.refs_0_, bf16[528,128]{1,0:T(8,128)(2,1)S(1)} %gate.7.refs_1_, ...), custom_call_target="tpu_custom_call" | custom-call | tf_op jit(solution)/shard_map/stage/pallas_call | solution.py:274
  21.3 0.1 collective-permute-start.7
  21.4 1.8 %collective-permute-done.6.refs_3_ = bf16[528,128]{1,0:T(8,128)(2,1)S(1)} collective-permute-done((bf16[528,128]{1,0:T(8,128)(2,1)S(1)}, bf16[528,128]{1,0:T(8,128)(2,1)S(1)}, u32[]{:S(2)}, u32[]{:S(2)}) %collective-permute-start.6) | collective-permute-done | bytes 135200 | tf_op jit(solution)/shard_map/ppermute | solution.py:226
  23.2 0.1 collective-permute-start.8
  23.3 1.9 %collective-permute-done.8.refs_3_ = bf16[4,528,128]{2,1,0:T(8,128)(2,1)S(1)} collective-permute-done((bf16[4,528,128]{2,1,0:T(8,128)(2,1)S(1)}, bf16[4,528,128]{2,1,0:T(8,128)(2,1)S(1)}, u32[]{:S(2)}, u32[]{:S(2)}) %collective-permute-start.8) | collective-permute-done | bytes 540704 | tf_op jit(solution)/shard_map/ppermute | solution.py:300
  25.2 1.7 %couple_far.1 = (s32[264,128]{1,0:T(8,128)S(1)}, s32[264,128]{1,0:T(8,128)S(1)}) custom-call(s32[8,32]{1,0:T(8,128)S(4)} %get-tuple-element.12.nbr_ref, bf16[8,2,256,256]{3,2,1,0:T(8,128)(2,1)S(1)} %get-tuple-element.13.esp_ref, bf16[4,528,128]{2,1,0:T(8,128)(2,1)S(1)} %get-tuple-element.14.refs_0_, bf16[4,528,128]{2,1,0:T(8,128)(2,1)S(1)} %gather.1.refs_1_, ...), custom_call_target="tpu_custom_call" | custom-call | tf_op jit(solution)/shard_map/couple_far/pallas_call | solution.py:309
  26.9 1.1 %collective-permute-start.10 = (s32[264,128]{1,0:T(8,128)S(1)}, s32[264,128]{1,0:T(8,128)S(1)}, u32[]{:S(2)}, u32[]{:S(2)}) collective-permute-start(s32[264,128]{1,0:T(8,128)S(1)} %get-tuple-element.17), channel_id=1, source_target_pairs={{0,2},{1,3},{2,0},{3,1},{4,6},{5,7},{6,4},{7,5},{8,10},{9,11},{10,... | collective-permute-start | bytes 405512 | tf_op jit(solution)/shard_map/ppermute | solution.py:324
  28.0 1.8 %collective-permute-start.11 = (s32[264,128]{1,0:T(8,128)S(1)}, s32[264,128]{1,0:T(8,128)S(1)}, u32[]{:S(2)}, u32[]{:S(2)}) collective-permute-start(s32[264,128]{1,0:T(8,128)S(1)} %get-tuple-element.18), channel_id=1, source_target_pairs={{0,3},{1,2},{2,1},{3,0},{4,7},{5,6},{6,5},{7,4},{8,11},{9,10},{10,... | collective-permute-start | bytes 405512 | tf_op jit(solution)/shard_map/ppermute | solution.py:324
  29.8 1.7 %couple_near.1 = (f32[2,264,128]{2,1,0:T(8,128)S(1)}, s32[264,128]{1,0:T(8,128)S(1)}) custom-call(s32[8,32]{1,0:T(8,128)S(4)} %get-tuple-element.12.nbr_ref, bf16[8,2,256,256]{3,2,1,0:T(8,128)(2,1)S(1)} %get-tuple-element.13.esp_ref, bf16[4,528,128]{2,1,0:T(8,128)(2,1)S(1)} %get-tuple-element.14.refs_0_, bf16[4,528,128]{2,1,0:T(8,128)(2,1)S(1)} %gather.1.refs_1_, ...), custom_call_target="tpu_custom_call" | custom-call | tf_op jit(solution)/shard_map/couple_near/pallas_call | solution.py:309
  31.5 0.8 %collective-permute-start.9 = (s32[264,128]{1,0:T(8,128)S(1)}, s32[264,128]{1,0:T(8,128)S(1)}, u32[]{:S(2)}, u32[]{:S(2)}) collective-permute-start(s32[264,128]{1,0:T(8,128)S(1)} %get-tuple-element.16), channel_id=1, source_target_pairs={{0,1},{1,0},{2,3},{3,2},{4,5},{5,4},{6,7},{7,6},{8,9},{9,8},{10,11... | collective-permute-start | bytes 405512 | tf_op jit(solution)/shard_map/ppermute | solution.py:326
  32.2 7.1 %collective-permute-done.10.refs_1_ = s32[264,128]{1,0:T(8,128)S(1)} collective-permute-done((s32[264,128]{1,0:T(8,128)S(1)}, s32[264,128]{1,0:T(8,128)S(1)}, u32[]{:S(2)}, u32[]{:S(2)}) %collective-permute-start.10) | collective-permute-done | bytes 135200 | tf_op jit(solution)/shard_map/ppermute | solution.py:324
  39.3 2.5 %collective-permute-done.9.refs_0_ = s32[264,128]{1,0:T(8,128)S(1)} collective-permute-done((s32[264,128]{1,0:T(8,128)S(1)}, s32[264,128]{1,0:T(8,128)S(1)}, u32[]{:S(2)}, u32[]{:S(2)}) %collective-permute-start.9) | collective-permute-done | bytes 135200 | tf_op jit(solution)/shard_map/ppermute | solution.py:326
  41.8 1.0 %finish.1 = f32[2,256,256]{2,1,0:T(8,128)} custom-call(bf16[2,256,256]{2,1,0:T(8,128)(2,1)S(1)} %copy-done.1, f32[2,264,128]{2,1,0:T(8,128)S(1)} %get-tuple-element.15.own_ref, s32[264,128]{1,0:T(8,128)S(1)} %collective-permute-done.9.refs_0_, s32[264,128]{1,0:T(8,128)S(1)} %collective-permute-done.10.refs_1_, s32[264,128]{1,0:T(8,128)S(1)} %collective-permute-done.11.refs_2_), custom_call_target="tpu_custom_call" | custom-call | tf_op jit(solution)/shard_map/finish/pallas_call | solution.py:327
  (16 shorter events, 0.2 us)
Async XLA Ops:
  0.0 0.9 %copy-start = (bf16[2,256,256]{2,1,0:T(8,128)(2,1)S(1)}, bf16[2,256,256]{2,1,0:T(8,128)(2,1)}, u32[]{:S(2)}) copy-start(bf16[2,256,256]{2,1,0:T(8,128)(2,1)} %dens_ref.1) | copy-start | bytes 786436
  1.0 8.7 %collective-permute-start.1 = (bf16[528,128]{1,0:T(8,128)(2,1)S(1)}, bf16[528,128]{1,0:T(8,128)(2,1)S(1)}, u32[]{:S(2)}, u32[]{:S(2)}) collective-permute-start(bf16[528,128]{1,0:T(8,128)(2,1)S(1)} %fold.1.refs_0_), channel_id=1, source_target_pairs={{0,1},{1,0},{2,3},{3,2},{4,5},{5,4},{6,7},{7,6},{8,9},{9,8},{10,11... | collective-permute-start | bytes 405512 | tf_op jit(solution)/shard_map/ppermute | solution.py:223
  4.1 8.9 %collective-permute-start = (bf16[528,128]{1,0:T(8,128)(2,1)S(1)}, bf16[528,128]{1,0:T(8,128)(2,1)S(1)}, u32[]{:S(2)}, u32[]{:S(2)}) collective-permute-start(bf16[528,128]{1,0:T(8,128)(2,1)S(1)} %fold.1.refs_0_), channel_id=1, source_target_pairs={{0,2},{1,3},{2,0},{3,1},{4,6},{5,7},{6,4},{7,5},{8,10},{9,11},{10,... | collective-permute-start | bytes 405512 | tf_op jit(solution)/shard_map/ppermute | solution.py:223
  6.7 6.3 %collective-permute-start.2 = (bf16[528,128]{1,0:T(8,128)(2,1)S(1)}, bf16[528,128]{1,0:T(8,128)(2,1)S(1)}, u32[]{:S(2)}, u32[]{:S(2)}) collective-permute-start(bf16[528,128]{1,0:T(8,128)(2,1)S(1)} %fold.1.refs_0_), channel_id=1, source_target_pairs={{0,8},{4,12},{8,0},{12,4},{1,9},{5,13},{9,1},{13,5},{2,10},{6,14},... | collective-permute-start | bytes 405512 | tf_op jit(solution)/shard_map/ppermute | solution.py:226
  9.7 5.4 %collective-permute-start.3 = (bf16[528,128]{1,0:T(8,128)(2,1)S(1)}, bf16[528,128]{1,0:T(8,128)(2,1)S(1)}, u32[]{:S(2)}, u32[]{:S(2)}) collective-permute-start(bf16[528,128]{1,0:T(8,128)(2,1)S(1)} %collective-permute-done.1.refs_1_.refs_2_), channel_id=1, source_target_pairs={{0,8},{4,12},{8,0},{12,4},{1,9},{5,13},{9,1},{13,5},{2,10},{6,14},... | collective-permute-start | bytes 405512 | tf_op jit(solution)/shard_map/ppermute | solution.py:226
  13.0 5.1 %collective-permute-start.4 = (bf16[528,128]{1,0:T(8,128)(2,1)S(1)}, bf16[528,128]{1,0:T(8,128)(2,1)S(1)}, u32[]{:S(2)}, u32[]{:S(2)}) collective-permute-start(bf16[528,128]{1,0:T(8,128)(2,1)S(1)} %gate.7.refs_1_), channel_id=1, source_target_pairs={{0,1},{1,0},{2,3},{3,2},{4,5},{5,4},{6,7},{7,6},{8,9},{9,8},{10,11... | collective-permute-start | bytes 405512 | tf_op jit(solution)/shard_map/ppermute | solution.py:223
  13.5 7.9 %collective-permute-start.5 = (bf16[528,128]{1,0:T(8,128)(2,1)S(1)}, bf16[528,128]{1,0:T(8,128)(2,1)S(1)}, u32[]{:S(2)}, u32[]{:S(2)}) collective-permute-start(bf16[528,128]{1,0:T(8,128)(2,1)S(1)} %gate.7.refs_1_), channel_id=1, source_target_pairs={{0,8},{4,12},{8,0},{12,4},{1,9},{5,13},{9,1},{13,5},{2,10},{6,14},... | collective-permute-start | bytes 405512 | tf_op jit(solution)/shard_map/ppermute | solution.py:226
  18.1 5.1 %collective-permute-start.6 = (bf16[528,128]{1,0:T(8,128)(2,1)S(1)}, bf16[528,128]{1,0:T(8,128)(2,1)S(1)}, u32[]{:S(2)}, u32[]{:S(2)}) collective-permute-start(bf16[528,128]{1,0:T(8,128)(2,1)S(1)} %gate.11), channel_id=1, source_target_pairs={{0,8},{4,12},{8,0},{12,4},{1,9},{5,13},{9,1},{13,5},{2,10},{6,14},... | collective-permute-start | bytes 405512 | tf_op jit(solution)/shard_map/ppermute | solution.py:226
  21.3 2.0 %collective-permute-start.7 = (bf16[4,528,128]{2,1,0:T(8,128)(2,1)S(1)}, bf16[4,528,128]{2,1,0:T(8,128)(2,1)S(1)}, u32[]{:S(2)}, u32[]{:S(2)}) collective-permute-start(bf16[4,528,128]{2,1,0:T(8,128)(2,1)S(1)} %get-tuple-element.14.refs_0_), channel_id=1, source_target_pairs={{0,4},{4,0},{8,12},{12,8},{1,5},{5,1},{9,13},{13,9},{2,6},{6,2},{1... | collective-permute-start | bytes 1622024 | tf_op jit(solution)/shard_map/ppermute | solution.py:300
  23.2 2.0 %collective-permute-start.8 = (bf16[4,528,128]{2,1,0:T(8,128)(2,1)S(1)}, bf16[4,528,128]{2,1,0:T(8,128)(2,1)S(1)}, u32[]{:S(2)}, u32[]{:S(2)}) collective-permute-start(bf16[4,528,128]{2,1,0:T(8,128)(2,1)S(1)} %gather.1.refs_1_), channel_id=1, source_target_pairs={{0,4},{4,0},{8,12},{12,8},{1,5},{5,1},{9,13},{13,9},{2,6},{6,2},{1... | collective-permute-start | bytes 1622024 | tf_op jit(solution)/shard_map/ppermute | solution.py:300
  26.9 12.4 %collective-permute-start.10 = (s32[264,128]{1,0:T(8,128)S(1)}, s32[264,128]{1,0:T(8,128)S(1)}, u32[]{:S(2)}, u32[]{:S(2)}) collective-permute-start(s32[264,128]{1,0:T(8,128)S(1)} %get-tuple-element.17), channel_id=1, source_target_pairs={{0,2},{1,3},{2,0},{3,1},{4,6},{5,7},{6,4},{7,5},{8,10},{9,11},{10,... | collective-permute-start | bytes 405512 | tf_op jit(solution)/shard_map/ppermute | solution.py:324
  28.0 13.8 %copy-start.1 = (bf16[2,256,256]{2,1,0:T(8,128)(2,1)S(1)}, bf16[2,256,256]{2,1,0:T(8,128)(2,1)}, u32[]{:S(2)}) copy-start(bf16[2,256,256]{2,1,0:T(8,128)(2,1)} %core_ref.1) | copy-start | bytes 786436
  28.0 11.3 %collective-permute-start.11 = (s32[264,128]{1,0:T(8,128)S(1)}, s32[264,128]{1,0:T(8,128)S(1)}, u32[]{:S(2)}, u32[]{:S(2)}) collective-permute-start(s32[264,128]{1,0:T(8,128)S(1)} %get-tuple-element.18), channel_id=1, source_target_pairs={{0,3},{1,2},{2,1},{3,0},{4,7},{5,6},{6,5},{7,4},{8,11},{9,10},{10,... | collective-permute-start | bytes 405512 | tf_op jit(solution)/shard_map/ppermute | solution.py:324
  31.5 10.3 %collective-permute-start.9 = (s32[264,128]{1,0:T(8,128)S(1)}, s32[264,128]{1,0:T(8,128)S(1)}, u32[]{:S(2)}, u32[]{:S(2)}) collective-permute-start(s32[264,128]{1,0:T(8,128)S(1)} %get-tuple-element.16), channel_id=1, source_target_pairs={{0,1},{1,0},{2,3},{3,2},{4,5},{5,4},{6,7},{7,6},{8,9},{9,8},{10,11... | collective-permute-start | bytes 405512 | tf_op jit(solution)/shard_map/ppermute | solution.py:326

commit v6 on v5

--- a/solution.py
+++ b/solution.py
@@ -74,7 +74,7 @@
     return jnp.max(jnp.abs(x), axis=0, keepdims=True)
 
 
-def fold_kernel(dens_ref, out_ref):
+def fold_kernel(dens_ref, out_ref, far_ref):
     mono_dev, basis, _ = dens_ref.shape
     half = basis // 2
     diags = []
@@ -91,10 +91,12 @@
     for m in range(mono_dev):
         tail = jnp.where(row == m, diags[m], tail)
     out_ref[pl.ds(mono_dev * basis, rows)] = tail.astype(out_ref.dtype)
+    far_ref[...] = jnp.zeros_like(far_ref)
+    far_ref[pl.ds(0, out_ref.shape[0])] = out_ref[...]
 
 
 def gate_kernel(piece_ref, *refs):
-    refs[-1][...] = piece_ref[...]
+    refs[-1][...] = piece_ref[: refs[-1].shape[0]]
 
 
 def gather_kernel(*refs):
@@ -157,26 +159,56 @@
         mixed, diag = fold(total[:half, :half], total[half:, half:])
         return total[:half, half:], mixed, diag
 
-    for k, out in zip(units, outs):
-        if k == 0:
-            for m in range(mono_dev):
-                off, mixed, diag = partial_of((my_lane ^ k) * mono_dev + m)
-                out[m, :half] = off
-                out[m, half : 2 * half] = mixed
-                out[m, 2 * half :] = jnp.broadcast_to(diag, (8, half))
-            continue
-        tail = []
-        for m in range(mono_dev):
-            off, mixed, diag = partial_of((my_lane ^ k) * mono_dev + m)
-            off_code = scale_code(peak_of(off))
-            mixed_code = scale_code(jnp.maximum(peak_of(mixed), jnp.abs(diag)))
-            out[pl.ds(m * half, half)] = pack(encode(off, off_code), encode(mixed, mixed_code))
-            tail += [pack(off_code, mixed_code), encode(diag, mixed_code)]
-        row = lax.broadcasted_iota(jnp.int32, (out.shape[0] - mono_dev * half, half), 0)
-        last = jnp.zeros(row.shape, jnp.int32)
-        for i, values in enumerate(tail):
-            last = jnp.where(row == i, values, last)
-        out[pl.ds(mono_dev * half, row.shape[0])] = last
+    for (k, coded), out in zip(units, outs):
+        write = write_coded if coded else write_plain
+        write(out, [partial_of((my_lane ^ k) * mono_dev + m) for m in range(mono_dev)])
+
+
+def write_plain(out, parts):
+    half = out.shape[2]
+    for m, (off, mixed, diag) in enumerate(parts):
+        out[m, :half] = off
+        out[m, half : 2 * half] = mixed
+        out[m, 2 * half :] = jnp.broadcast_to(diag, (8, half))
+
+
+def read_plain(ref, m):
+    half = ref.shape[2]
+    return ref[m, :half], ref[m, half : 2 * half], ref[m, 2 * half : 2 * half + 1]
+
+
+def write_coded(out, parts):
+    half = out.shape[1]
+    tail = []
+    for m, (off, mixed, diag) in enumerate(parts):
+        off_code = scale_code(peak_of(off))
+        mixed_code = scale_code(jnp.maximum(peak_of(mixed), jnp.abs(diag)))
+        out[pl.ds(m * half, half)] = pack(encode(off, off_code), encode(mixed, mixed_code))
+        tail += [pack(off_code, mixed_code), encode(diag, mixed_code)]
+    row = lax.broadcasted_iota(jnp.int32, (out.shape[0] - len(parts) * half, half), 0)
+    last = jnp.zeros(row.shape, jnp.int32)
+    for i, values in enumerate(tail):
+        last = jnp.where(row == i, values, last)
+    out[pl.ds(len(parts) * half, row.shape[0])] = last
+
+
+def read_coded(ref, m, mono_dev):
+    half = ref.shape[1]
+    tail = mono_dev * half + 2 * m
+    off_code, mixed_code = unpack(ref[tail : tail + 1])
+    off_q, mixed_q = unpack(ref[m * half : (m + 1) * half])
+    return decode(off_q, off_code), decode(mixed_q, mixed_code), decode(ref[tail + 1 : tail + 2], mixed_code)
+
+
+def summed(plain_ref, coded_refs, m):
+    total = read_plain(plain_ref, m)
+    for ref in coded_refs:
+        total = [a + b for a, b in zip(total, read_coded(ref, m, plain_ref.shape[0]))]
+    return total
+
+
+def merge_kernel(plain_ref, *refs):
+    write_coded(refs[-1], [summed(plain_ref, refs[:-1], m) for m in range(plain_ref.shape[0])])
 
 
 def finish_kernel(core_ref, own_ref, *refs):
@@ -184,16 +216,7 @@
     mono_dev, basis, _ = out_ref.shape
     half = basis // 2
     for m in range(mono_dev):
-        off = own_ref[m, :half]
-        mixed = own_ref[m, half : 2 * half]
-        diag = own_ref[m, 2 * half : 2 * half + 1]
-        for part in parts:
-            tail = mono_dev * half + 2 * m
-            off_code, mixed_code = unpack(part[tail : tail + 1])
-            off_q, mixed_q = unpack(part[m * half : (m + 1) * half])
-            off = off + decode(off_q, off_code)
-            mixed = mixed + decode(mixed_q, mixed_code)
-            diag = diag + decode(part[tail + 1 : tail + 2], mixed_code)
+        off, mixed, diag = summed(own_ref, parts, m)
         first, second = unfold(mixed, diag)
         core = core_ref[m].astype(jnp.float32)
         out_ref[m, :half, :half] = core[:half, :half] + first
@@ -211,11 +234,11 @@
     small = pltpu.CompilerParams(vmem_limit_bytes=8 * 2**20)
 
     rows = mono_dev * basis + round_up(mono_dev, 16)
-    shard = pl.pallas_call(
+    shard, shard_far = pl.pallas_call(
         fold_kernel,
-        out_shape=jax.ShapeDtypeStruct((rows, half), density.dtype),
+        out_shape=[pltpu.VMEM((rows, half), density.dtype), pltpu.VMEM((rows + 16, half), density.dtype)],
         in_specs=[IN_VMEM],
-        out_specs=IN_VMEM,
+        out_specs=[IN_VMEM] * 2,
         compiler_params=small,
         name="fold",
     )(density)
@@ -227,7 +250,7 @@
 
     rows_y = groups // 2
     top = lanes // 2
-    near = {(0, 0): shard, (0, top): along_z(shard, top)}
+    near = {(0, 0): shard, (0, top): along_z(shard_far, top)}
 
     def double(start):
         bit = top // 2
@@ -301,14 +324,14 @@
     places = [[y * lanes + k for y, k in keys] for keys in (early, later)]
     places += [[rows_y * lanes + place for place in keys] for keys in places]
 
-    own = jax.ShapeDtypeStruct((mono_dev, basis + 8, half), jnp.float32)
-    coded = jax.ShapeDtypeStruct((mono_dev * half + round_up(2 * mono_dev, 8), half), jnp.int32)
+    plain = pltpu.VMEM((mono_dev, basis + 8, half), jnp.float32)
+    coded = pltpu.VMEM((mono_dev * half + round_up(2 * mono_dev, 8), half), jnp.int32)
     piece_bytes = groups * lanes * rows * half * 2
 
     def couple(units, name):
         return pl.pallas_call(
             functools.partial(couple_kernel, groups, lanes, mono_dev, units, places),
-            out_shape=[own if k == 0 else coded for k in units],
+            out_shape=[coded if is_coded else plain for _, is_coded in units],
             in_specs=[IN_SMEM] + [IN_VMEM] * (1 + len(pieces)),
             out_specs=[IN_VMEM] * len(units),
             scratch_shapes=[pltpu.VMEM((groups * lanes, rows, half), density.dtype)],
@@ -318,20 +341,27 @@
             name=name,
         )(names, blocks, *pieces)
 
-    far_units = range(lanes // 2, lanes)
-    near_units = range(lanes // 2)
-    far = couple(far_units, "couple_far")
-    far_terms = [lax.ppermute(far[k - lanes // 2], "intra", xor_pairs(lanes, k)) for k in far_units]
-    close = couple(near_units, "couple_near")
-    close_terms = [lax.ppermute(close[k], "intra", xor_pairs(lanes, k)) for k in near_units[1:]]
+    steps = range(1, top)
+    relayed = couple([(top ^ k, True) for k in steps], "couple_relay") if top > 1 else []
+    relayed = [along_z(unit, k) for k, unit in zip(steps, relayed)]
+    own, across, *close = couple([(0, False), (top, False)] + [(k, True) for k in steps], "couple")
+    close = [along_z(unit, k) for k, unit in zip(steps, close)]
+    across = pl.pallas_call(
+        merge_kernel,
+        out_shape=coded,
+        in_specs=[IN_VMEM] * (1 + len(relayed)),
+        out_specs=IN_VMEM,
+        compiler_params=small,
+        name="merge",
+    )(across, *relayed)
     return pl.pallas_call(
         finish_kernel,
         out_shape=jax.ShapeDtypeStruct((mono_dev, basis, basis), jnp.float32),
-        in_specs=[IN_VMEM] * (1 + lanes),
+        in_specs=[IN_VMEM] * (3 + len(close)),
         out_specs=IN_VMEM,
         compiler_params=small,
         name="finish",
-    )(h_core, close[0], *close_terms, *far_terms)
+    )(h_core, own, *close, along_z(across, top))
 
 
 def solution(mesh):

time: 43 us -> 42.6 us (level)
  starting transfers between devices: 16.4 us -> 15.6 us
    ppermute x3 -> x0, waiting for transfers between devices: 9.59 us -> none  [the longest x2 7.1 us: local(): lax.ppermute(far[k - lanes // 2], 'intra', xor_pairs(lanes, k))]
    ppermute x3 -> x6, waiting for transfers between devices: 5.92 us -> 13 us  [along_z(): return lax.ppermute(piece, 'intra', xor_pairs(lanes, bit))]
    ppermute x3 -> x6, starting transfers between devices: 6.19 us -> 10.7 us  [along_z(): return lax.ppermute(piece, 'intra', xor_pairs(lanes, bit))]
    ppermute x3 -> x0, starting transfers between devices: 3.62 us -> none  [the longest x2 2.86 us: local(): lax.ppermute(far[k - lanes // 2], 'intra', xor_pairs(lanes, k))]
    ppermute x4, waiting for transfers between devices: 1.79 us -> 4.53 us  [along_y(): return lax.ppermute(piece, 'gddi', xor_pairs(groups, 2 * y))]
    ppermute x4, starting transfers between devices: 6.47 us -> 4.81 us  [along_y(): return lax.ppermute(piece, 'gddi', xor_pairs(groups, 2 * y))]
  transfers between devices with their start and end apart: 12 -> 12, of which waited for: 7 -> 8; matrix products, arithmetic and copies ran while one was open for 0% -> 0% of each run, Pallas kernels for 8% -> 10%
where the time goes in v6:
time: 42.6 us; the launch traced here: 42.5 us
  waiting for transfers between devices  19.4 us (46%)
  starting transfers between devices  15.6 us (37%)
  Pallas kernels  6.31 us (15%)
  local copies, waits for them, and re-layouts  0.96 us (2%)
    ppermute x6, waiting for transfers between devices, along_z(): return lax.ppermute(piece, 'intra', xor_pairs(lanes, bit))  13 us
    ppermute x6, starting transfers between devices, along_z(): return lax.ppermute(piece, 'intra', xor_pairs(lanes, bit))  10.7 us
    ppermute x4, starting transfers between devices, along_y(): return lax.ppermute(piece, 'gddi', xor_pairs(groups, 2 * y))  4.81 us
    ppermute x4, waiting for transfers between devices, along_y(): return lax.ppermute(piece, 'gddi', xor_pairs(groups, 2 * y))  4.53 us
    pallas_call x2, Pallas kernels, couple(): pl.pallas_call(functools.partial(couple_kernel, groups, lanes, mono_dev,...  3.36 us
    ppermute x2, waiting for transfers between devices, local(): lax.ppermute(piece, 'gddi', xor_pairs(groups, 1))  1.91 us
    pallas_call x1, Pallas kernels, local(): pl.pallas_call(stage_kernel, out_shape=[pltpu.SMEM((nbr.shape[1], nbr.sha...  1.62 us
    pallas_call x1, Pallas kernels, local(): pl.pallas_call(finish_kernel, out_shape=jax.ShapeDtypeStruct((mono_dev, b...  0.98 us
  transfers between devices with their start and end apart: 12, of which 8 were waited for; matrix products, arithmetic and copies ran while one was open for 0% of the time, Pallas kernels for 10%

profile of v6, /device:TPU:0, one launch (start us, length us, event | category | flops | bytes accessed | tf_op | source)
XLA Modules:
  0.0 42.5 jit_solution(14308146885950244249)
XLA Ops:
  0.0 0.9 %copy-done = bf16[2,256,256]{2,1,0:T(8,128)(2,1)S(1)} copy-done((bf16[2,256,256]{2,1,0:T(8,128)(2,1)S(1)}, bf16[2,256,256]{2,1,0:T(8,128)(2,1)}, u32[]{:S(2)}) %copy-start) | copy-done | bytes 262168
  1.0 4.1 %collective-permute-start = (bf16[544,128]{1,0:T(8,128)(2,1)S(1)}, bf16[544,128]{1,0:T(8,128)(2,1)S(1)}, u32[]{:S(2)}, u32[]{:S(2)}) collective-permute-start(bf16[544,128]{1,0:T(8,128)(2,1)S(1)} %get-tuple-element.14), channel_id=1, source_target_pairs={{0,2},{1,3},{2,0},{3,1},{4,6},{5,7},{6,4},{7,5},{8,10},{9,11},{10,... | collective-permute-start | bytes 417800 | tf_op jit(solution)/shard_map/ppermute | solution.py:246
  5.1 1.6 %collective-permute-start.1 = (bf16[528,128]{1,0:T(8,128)(2,1)S(1)}, bf16[528,128]{1,0:T(8,128)(2,1)S(1)}, u32[]{:S(2)}, u32[]{:S(2)}) collective-permute-start(bf16[528,128]{1,0:T(8,128)(2,1)S(1)} %get-tuple-element.13.refs_0_), channel_id=1, source_target_pairs={{0,1},{1,0},{2,3},{3,2},{4,5},{5,4},{6,7},{7,6},{8,9},{9,8},{10,11... | collective-permute-start | bytes 405512 | tf_op jit(solution)/shard_map/ppermute | solution.py:246
  6.7 1.5 %collective-permute-start.2 = (bf16[528,128]{1,0:T(8,128)(2,1)S(1)}, bf16[528,128]{1,0:T(8,128)(2,1)S(1)}, u32[]{:S(2)}, u32[]{:S(2)}) collective-permute-start(bf16[528,128]{1,0:T(8,128)(2,1)S(1)} %get-tuple-element.13.refs_0_), channel_id=1, source_target_pairs={{0,8},{4,12},{8,0},{12,4},{1,9},{5,13},{9,1},{13,5},{2,10},{6,14},... | collective-permute-start | bytes 405512 | tf_op jit(solution)/shard_map/ppermute | solution.py:249
  8.2 3.8 %collective-permute-done.1.refs_1_.refs_2_ = bf16[528,128]{1,0:T(8,128)(2,1)S(1)} collective-permute-done((bf16[528,128]{1,0:T(8,128)(2,1)S(1)}, bf16[528,128]{1,0:T(8,128)(2,1)S(1)}, u32[]{:S(2)}, u32[]{:S(2)}) %collective-permute-start.1) | collective-permute-done | bytes 135200 | tf_op jit(solution)/shard_map/ppermute | solution.py:246
  12.0 1.6 %collective-permute-start.3 = (bf16[528,128]{1,0:T(8,128)(2,1)S(1)}, bf16[528,128]{1,0:T(8,128)(2,1)S(1)}, u32[]{:S(2)}, u32[]{:S(2)}) collective-permute-start(bf16[528,128]{1,0:T(8,128)(2,1)S(1)} %collective-permute-done.1.refs_1_.refs_2_), channel_id=1, source_target_pairs={{0,8},{4,12},{8,0},{12,4},{1,9},{5,13},{9,1},{13,5},{2,10},{6,14},... | collective-permute-start | bytes 405512 | tf_op jit(solution)/shard_map/ppermute | solution.py:249
  13.6 1.5 %collective-permute-start.4 = (bf16[528,128]{1,0:T(8,128)(2,1)S(1)}, bf16[528,128]{1,0:T(8,128)(2,1)S(1)}, u32[]{:S(2)}, u32[]{:S(2)}) collective-permute-start(bf16[528,128]{1,0:T(8,128)(2,1)S(1)} %gate.7.refs_1_), channel_id=1, source_target_pairs={{0,1},{1,0},{2,3},{3,2},{4,5},{5,4},{6,7},{7,6},{8,9},{9,8},{10,11... | collective-permute-start | bytes 405512 | tf_op jit(solution)/shard_map/ppermute | solution.py:246
  15.1 0.5 %collective-permute-start.5 = (bf16[528,128]{1,0:T(8,128)(2,1)S(1)}, bf16[528,128]{1,0:T(8,128)(2,1)S(1)}, u32[]{:S(2)}, u32[]{:S(2)}) collective-permute-start(bf16[528,128]{1,0:T(8,128)(2,1)S(1)} %gate.7.refs_1_), channel_id=1, source_target_pairs={{0,8},{4,12},{8,0},{12,4},{1,9},{5,13},{9,1},{13,5},{2,10},{6,14},... | collective-permute-start | bytes 405512 | tf_op jit(solution)/shard_map/ppermute | solution.py:249
  15.6 2.4 %collective-permute-done.3.piece_ref.refs_0_ = bf16[528,128]{1,0:T(8,128)(2,1)S(1)} collective-permute-done((bf16[528,128]{1,0:T(8,128)(2,1)S(1)}, bf16[528,128]{1,0:T(8,128)(2,1)S(1)}, u32[]{:S(2)}, u32[]{:S(2)}) %collective-permute-start.3) | collective-permute-done | bytes 135200 | tf_op jit(solution)/shard_map/ppermute | solution.py:249
  18.0 0.7 %collective-permute-done.4.piece_ref.refs_1_ = bf16[528,128]{1,0:T(8,128)(2,1)S(1)} collective-permute-done((bf16[528,128]{1,0:T(8,128)(2,1)S(1)}, bf16[528,128]{1,0:T(8,128)(2,1)S(1)}, u32[]{:S(2)}, u32[]{:S(2)}) %collective-permute-start.4) | collective-permute-done | bytes 135200 | tf_op jit(solution)/shard_map/ppermute | solution.py:246
  18.7 1.2 %collective-permute-start.6 = (bf16[528,128]{1,0:T(8,128)(2,1)S(1)}, bf16[528,128]{1,0:T(8,128)(2,1)S(1)}, u32[]{:S(2)}, u32[]{:S(2)}) collective-permute-start(bf16[528,128]{1,0:T(8,128)(2,1)S(1)} %gate.11), channel_id=1, source_target_pairs={{0,8},{4,12},{8,0},{12,4},{1,9},{5,13},{9,1},{13,5},{2,10},{6,14},... | collective-permute-start | bytes 405512 | tf_op jit(solution)/shard_map/ppermute | solution.py:249
  19.9 1.6 %stage.1 = (s32[8,32]{1,0:T(8,128)S(4)}, bf16[8,2,256,256]{3,2,1,0:T(8,128)(2,1)S(1)}, bf16[4,528,128]{2,1,0:T(8,128)(2,1)S(1)}) custom-call(s32[8,32]{1,0:T(8,128)} %bitcast.1, bf16[8,2,256,256]{3,2,1,0:T(8,128)(2,1)} %esp_ref.1, bf16[528,128]{1,0:T(8,128)(2,1)S(1)} %get-tuple-element.13.refs_0_, bf16[528,128]{1,0:T(8,128)(2,1)S(1)} %gate.7.refs_1_, ...), custom_call_target="tpu_custom_call" | custom-call | tf_op jit(solution)/shard_map/stage/pallas_call | solution.py:297
  21.6 2.1 %collective-permute-done.6.refs_3_ = bf16[528,128]{1,0:T(8,128)(2,1)S(1)} collective-permute-done((bf16[528,128]{1,0:T(8,128)(2,1)S(1)}, bf16[528,128]{1,0:T(8,128)(2,1)S(1)}, u32[]{:S(2)}, u32[]{:S(2)}) %collective-permute-start.6) | collective-permute-done | bytes 135200 | tf_op jit(solution)/shard_map/ppermute | solution.py:249
  23.9 1.9 %collective-permute-done.8.refs_3_ = bf16[4,528,128]{2,1,0:T(8,128)(2,1)S(1)} collective-permute-done((bf16[4,528,128]{2,1,0:T(8,128)(2,1)S(1)}, bf16[4,528,128]{2,1,0:T(8,128)(2,1)S(1)}, u32[]{:S(2)}, u32[]{:S(2)}) %collective-permute-start.8) | collective-permute-done | bytes 540704 | tf_op jit(solution)/shard_map/ppermute | solution.py:323
  25.8 1.1 %couple_relay.1 = s32[264,128]{1,0:T(8,128)S(1)} custom-call(s32[8,32]{1,0:T(8,128)S(4)} %get-tuple-element.15.nbr_ref, bf16[8,2,256,256]{3,2,1,0:T(8,128)(2,1)S(1)} %get-tuple-element.16.esp_ref, bf16[4,528,128]{2,1,0:T(8,128)(2,1)S(1)} %get-tuple-element.17.refs_0_, bf16[4,528,128]{2,1,0:T(8,128)(2,1)S(1)} %gather.1.refs_1_, ...), custom_call_target="tpu_custom_call" | custom-call | tf_op jit(solution)/shard_map/couple_relay/pallas_call | solution.py:332
  27.0 1.5 %collective-permute-start.10 = (s32[264,128]{1,0:T(8,128)S(1)}, s32[264,128]{1,0:T(8,128)S(1)}, u32[]{:S(2)}, u32[]{:S(2)}) collective-permute-start(s32[264,128]{1,0:T(8,128)S(1)} %couple_relay.1), channel_id=1, source_target_pairs={{0,1},{1,0},{2,3},{3,2},{4,5},{5,4},{6,7},{7,6},{8,9},{9,8},{10,11... | collective-permute-start | bytes 405512 | tf_op jit(solution)/shard_map/ppermute | solution.py:246
  28.5 2.2 %couple.1 = (f32[2,264,128]{2,1,0:T(8,128)S(1)}, f32[2,264,128]{2,1,0:T(8,128)S(1)}, s32[264,128]{1,0:T(8,128)S(1)}) custom-call(s32[8,32]{1,0:T(8,128)S(4)} %get-tuple-element.15.nbr_ref, bf16[8,2,256,256]{3,2,1,0:T(8,128)(2,1)S(1)} %get-tuple-element.16.esp_ref, bf16[4,528,128]{2,1,0:T(8,128)(2,1)S(1)} %get-tuple-element.17.refs_0_, ...), custom_call_target="tpu_custom_call" | custom-call | tf_op jit(solution)/shard_map/couple/pallas_call | solution.py:332
  30.7 0.7 %collective-permute-start.9 = (s32[264,128]{1,0:T(8,128)S(1)}, s32[264,128]{1,0:T(8,128)S(1)}, u32[]{:S(2)}, u32[]{:S(2)}) collective-permute-start(s32[264,128]{1,0:T(8,128)S(1)} %get-tuple-element.19), channel_id=1, source_target_pairs={{0,1},{1,0},{2,3},{3,2},{4,5},{5,4},{6,7},{7,6},{8,9},{9,8},{10,11... | collective-permute-start | bytes 405512 | tf_op jit(solution)/shard_map/ppermute | solution.py:246
  31.4 1.3 %collective-permute-done.10.refs_0_ = s32[264,128]{1,0:T(8,128)S(1)} collective-permute-done((s32[264,128]{1,0:T(8,128)S(1)}, s32[264,128]{1,0:T(8,128)S(1)}, u32[]{:S(2)}, u32[]{:S(2)}) %collective-permute-start.10) | collective-permute-done | bytes 135200 | tf_op jit(solution)/shard_map/ppermute | solution.py:246
  32.7 0.2 merge.1
  32.8 1.4 %collective-permute-start.11 = (s32[264,128]{1,0:T(8,128)S(1)}, s32[264,128]{1,0:T(8,128)S(1)}, u32[]{:S(2)}, u32[]{:S(2)}) collective-permute-start(s32[264,128]{1,0:T(8,128)S(1)} %merge.1), channel_id=1, source_target_pairs={{0,2},{1,3},{2,0},{3,1},{4,6},{5,7},{6,4},{7,5},{8,10},{9,11},{10,... | collective-permute-start | bytes 405512 | tf_op jit(solution)/shard_map/ppermute | solution.py:246
  34.2 3.3 %collective-permute-done.9.refs_0_ = s32[264,128]{1,0:T(8,128)S(1)} collective-permute-done((s32[264,128]{1,0:T(8,128)S(1)}, s32[264,128]{1,0:T(8,128)S(1)}, u32[]{:S(2)}, u32[]{:S(2)}) %collective-permute-start.9) | collective-permute-done | bytes 135200 | tf_op jit(solution)/shard_map/ppermute | solution.py:246
  37.5 4.0 %collective-permute-done.11.refs_1_ = s32[264,128]{1,0:T(8,128)S(1)} collective-permute-done((s32[264,128]{1,0:T(8,128)S(1)}, s32[264,128]{1,0:T(8,128)S(1)}, u32[]{:S(2)}, u32[]{:S(2)}) %collective-permute-start.11) | collective-permute-done | bytes 135200 | tf_op jit(solution)/shard_map/ppermute | solution.py:246
  41.5 1.0 %finish.1 = f32[2,256,256]{2,1,0:T(8,128)} custom-call(bf16[2,256,256]{2,1,0:T(8,128)(2,1)S(1)} %copy-done.1, f32[2,264,128]{2,1,0:T(8,128)S(1)} %get-tuple-element.18.own_ref, s32[264,128]{1,0:T(8,128)S(1)} %collective-permute-done.9.refs_0_, s32[264,128]{1,0:T(8,128)S(1)} %collective-permute-done.11.refs_1_), custom_call_target="tpu_custom_call" | custom-call | tf_op jit(solution)/shard_map/finish/pallas_call | solution.py:357
  (17 shorter events, 0.4 us)
Async XLA Ops:
  0.0 0.9 %copy-start = (bf16[2,256,256]{2,1,0:T(8,128)(2,1)S(1)}, bf16[2,256,256]{2,1,0:T(8,128)(2,1)}, u32[]{:S(2)}) copy-start(bf16[2,256,256]{2,1,0:T(8,128)(2,1)} %dens_ref.1) | copy-start | bytes 786436
  1.0 12.5 %collective-permute-start = (bf16[544,128]{1,0:T(8,128)(2,1)S(1)}, bf16[544,128]{1,0:T(8,128)(2,1)S(1)}, u32[]{:S(2)}, u32[]{:S(2)}) collective-permute-start(bf16[544,128]{1,0:T(8,128)(2,1)S(1)} %get-tuple-element.14), channel_id=1, source_target_pairs={{0,2},{1,3},{2,0},{3,1},{4,6},{5,7},{6,4},{7,5},{8,10},{9,11},{10,... | collective-permute-start | bytes 417800 | tf_op jit(solution)/shard_map/ppermute | solution.py:246
  5.1 6.9 %collective-permute-start.1 = (bf16[528,128]{1,0:T(8,128)(2,1)S(1)}, bf16[528,128]{1,0:T(8,128)(2,1)S(1)}, u32[]{:S(2)}, u32[]{:S(2)}) collective-permute-start(bf16[528,128]{1,0:T(8,128)(2,1)S(1)} %get-tuple-element.13.refs_0_), channel_id=1, source_target_pairs={{0,1},{1,0},{2,3},{3,2},{4,5},{5,4},{6,7},{7,6},{8,9},{9,8},{10,11... | collective-permute-start | bytes 405512 | tf_op jit(solution)/shard_map/ppermute | solution.py:246
  6.7 6.9 %collective-permute-start.2 = (bf16[528,128]{1,0:T(8,128)(2,1)S(1)}, bf16[528,128]{1,0:T(8,128)(2,1)S(1)}, u32[]{:S(2)}, u32[]{:S(2)}) collective-permute-start(bf16[528,128]{1,0:T(8,128)(2,1)S(1)} %get-tuple-element.13.refs_0_), channel_id=1, source_target_pairs={{0,8},{4,12},{8,0},{12,4},{1,9},{5,13},{9,1},{13,5},{2,10},{6,14},... | collective-permute-start | bytes 405512 | tf_op jit(solution)/shard_map/ppermute | solution.py:249
  12.0 6.0 %collective-permute-start.3 = (bf16[528,128]{1,0:T(8,128)(2,1)S(1)}, bf16[528,128]{1,0:T(8,128)(2,1)S(1)}, u32[]{:S(2)}, u32[]{:S(2)}) collective-permute-start(bf16[528,128]{1,0:T(8,128)(2,1)S(1)} %collective-permute-done.1.refs_1_.refs_2_), channel_id=1, source_target_pairs={{0,8},{4,12},{8,0},{12,4},{1,9},{5,13},{9,1},{13,5},{2,10},{6,14},... | collective-permute-start | bytes 405512 | tf_op jit(solution)/shard_map/ppermute | solution.py:249
  13.6 5.1 %collective-permute-start.4 = (bf16[528,128]{1,0:T(8,128)(2,1)S(1)}, bf16[528,128]{1,0:T(8,128)(2,1)S(1)}, u32[]{:S(2)}, u32[]{:S(2)}) collective-permute-start(bf16[528,128]{1,0:T(8,128)(2,1)S(1)} %gate.7.refs_1_), channel_id=1, source_target_pairs={{0,1},{1,0},{2,3},{3,2},{4,5},{5,4},{6,7},{7,6},{8,9},{9,8},{10,11... | collective-permute-start | bytes 405512 | tf_op jit(solution)/shard_map/ppermute | solution.py:246
  15.1 6.5 %collective-permute-start.5 = (bf16[528,128]{1,0:T(8,128)(2,1)S(1)}, bf16[528,128]{1,0:T(8,128)(2,1)S(1)}, u32[]{:S(2)}, u32[]{:S(2)}) collective-permute-start(bf16[528,128]{1,0:T(8,128)(2,1)S(1)} %gate.7.refs_1_), channel_id=1, source_target_pairs={{0,8},{4,12},{8,0},{12,4},{1,9},{5,13},{9,1},{13,5},{2,10},{6,14},... | collective-permute-start | bytes 405512 | tf_op jit(solution)/shard_map/ppermute | solution.py:249
  18.7 5.1 %collective-permute-start.6 = (bf16[528,128]{1,0:T(8,128)(2,1)S(1)}, bf16[528,128]{1,0:T(8,128)(2,1)S(1)}, u32[]{:S(2)}, u32[]{:S(2)}) collective-permute-start(bf16[528,128]{1,0:T(8,128)(2,1)S(1)} %gate.11), channel_id=1, source_target_pairs={{0,8},{4,12},{8,0},{12,4},{1,9},{5,13},{9,1},{13,5},{2,10},{6,14},... | collective-permute-start | bytes 405512 | tf_op jit(solution)/shard_map/ppermute | solution.py:249
  21.6 2.4 %collective-permute-start.7 = (bf16[4,528,128]{2,1,0:T(8,128)(2,1)S(1)}, bf16[4,528,128]{2,1,0:T(8,128)(2,1)S(1)}, u32[]{:S(2)}, u32[]{:S(2)}) collective-permute-start(bf16[4,528,128]{2,1,0:T(8,128)(2,1)S(1)} %get-tuple-element.17.refs_0_), channel_id=1, source_target_pairs={{0,4},{4,0},{8,12},{12,8},{1,5},{5,1},{9,13},{13,9},{2,6},{6,2},{1... | collective-permute-start | bytes 1622024 | tf_op jit(solution)/shard_map/ppermute | solution.py:323
  23.8 2.0 %collective-permute-start.8 = (bf16[4,528,128]{2,1,0:T(8,128)(2,1)S(1)}, bf16[4,528,128]{2,1,0:T(8,128)(2,1)S(1)}, u32[]{:S(2)}, u32[]{:S(2)}) collective-permute-start(bf16[4,528,128]{2,1,0:T(8,128)(2,1)S(1)} %gather.1.refs_1_), channel_id=1, source_target_pairs={{0,4},{4,0},{8,12},{12,8},{1,5},{5,1},{9,13},{13,9},{2,6},{6,2},{1... | collective-permute-start | bytes 1622024 | tf_op jit(solution)/shard_map/ppermute | solution.py:323
  27.0 14.5 %copy-start.1 = (bf16[2,256,256]{2,1,0:T(8,128)(2,1)S(1)}, bf16[2,256,256]{2,1,0:T(8,128)(2,1)}, u32[]{:S(2)}) copy-start(bf16[2,256,256]{2,1,0:T(8,128)(2,1)} %core_ref.1) | copy-start | bytes 786436
  27.0 5.7 %collective-permute-start.10 = (s32[264,128]{1,0:T(8,128)S(1)}, s32[264,128]{1,0:T(8,128)S(1)}, u32[]{:S(2)}, u32[]{:S(2)}) collective-permute-start(s32[264,128]{1,0:T(8,128)S(1)} %couple_relay.1), channel_id=1, source_target_pairs={{0,1},{1,0},{2,3},{3,2},{4,5},{5,4},{6,7},{7,6},{8,9},{9,8},{10,11... | collective-permute-start | bytes 405512 | tf_op jit(solution)/shard_map/ppermute | solution.py:246
  30.7 6.8 %collective-permute-start.9 = (s32[264,128]{1,0:T(8,128)S(1)}, s32[264,128]{1,0:T(8,128)S(1)}, u32[]{:S(2)}, u32[]{:S(2)}) collective-permute-start(s32[264,128]{1,0:T(8,128)S(1)} %get-tuple-element.19), channel_id=1, source_target_pairs={{0,1},{1,0},{2,3},{3,2},{4,5},{5,4},{6,7},{7,6},{8,9},{9,8},{10,11... | collective-permute-start | bytes 405512 | tf_op jit(solution)/shard_map/ppermute | solution.py:246
  32.8 8.7 %collective-permute-start.11 = (s32[264,128]{1,0:T(8,128)S(1)}, s32[264,128]{1,0:T(8,128)S(1)}, u32[]{:S(2)}, u32[]{:S(2)}) collective-permute-start(s32[264,128]{1,0:T(8,128)S(1)} %merge.1), channel_id=1, source_target_pairs={{0,2},{1,3},{2,0},{3,1},{4,6},{5,7},{6,4},{7,5},{8,10},{9,11},{10,... | collective-permute-start | bytes 405512 | tf_op jit(solution)/shard_map/ppermute | solution.py:246

commit v7 on v6

--- a/solution.py
+++ b/solution.py
@@ -74,7 +74,7 @@
     return jnp.max(jnp.abs(x), axis=0, keepdims=True)
 
 
-def fold_kernel(dens_ref, out_ref, far_ref):
+def fold_kernel(dens_ref, out_ref):
     mono_dev, basis, _ = dens_ref.shape
     half = basis // 2
     diags = []
@@ -91,44 +91,40 @@
     for m in range(mono_dev):
         tail = jnp.where(row == m, diags[m], tail)
     out_ref[pl.ds(mono_dev * basis, rows)] = tail.astype(out_ref.dtype)
-    far_ref[...] = jnp.zeros_like(far_ref)
-    far_ref[pl.ds(0, out_ref.shape[0])] = out_ref[...]
 
 
 def gate_kernel(piece_ref, *refs):
-    refs[-1][...] = piece_ref[: refs[-1].shape[0]]
-
-
-def gather_kernel(*refs):
-    for i, piece in enumerate(refs[:-1]):
-        refs[-1][i] = piece[...]
-
-
-def stage_kernel(nbr_ref, esp_ref, *refs):
-    nbr_out, esp_out, row_out, sems = refs[-4:]
+    out_ref = refs[-1]
+    out_ref[pl.ds(0, piece_ref.shape[0])] = piece_ref[...]
+    extra = out_ref.shape[0] - piece_ref.shape[0]
+    if extra:
+        out_ref[pl.ds(piece_ref.shape[0], extra)] = jnp.zeros((extra, out_ref.shape[1]), out_ref.dtype)
+
+
+def stage_kernel(nbr_ref, esp_ref, piece_ref, *refs):
+    nbr_out, esp_out, piece_out, sems = refs[-4:]
     copies = [
         pltpu.make_async_copy(esp_ref, esp_out, sems.at[0]),
         pltpu.make_async_copy(nbr_ref, nbr_out, sems.at[1]),
     ]
     for copy in copies:
         copy.start()
-    for i, piece in enumerate(refs[:-4]):
-        row_out[i] = piece[...]
+    piece_out[...] = piece_ref[...]
     for copy in copies:
         copy.wait()
 
 
-def couple_kernel(groups, lanes, mono_dev, units, places, nbr_ref, esp_ref, *refs):
-    pieces, outs, store = refs[: len(places)], refs[len(places) : -1], refs[-1]
+def couple_kernel(groups, lanes, mono_dev, units, nbr_ref, esp_ref, *refs):
+    n_pieces = groups * lanes
+    pieces, outs, store = refs[:n_pieces], refs[n_pieces:-1], refs[-1]
     my_group = lax.axis_index("gddi")
     my_lane = lax.axis_index("intra")
     _, slot_dev, basis, _ = esp_ref.shape
     mono_grp = mono_dev * lanes
     half = basis // 2
     tail_rows = store.shape[1] - mono_dev * basis
-    for piece, where in zip(pieces, places):
-        for i, place in enumerate(where):
-            store[place] = piece[i]
+    for i, piece in enumerate(pieces):
+        store[i] = piece[pl.ds(0, store.shape[1])]
 
     def near_density(fragment):
         apart = (fragment // mono_grp) ^ my_group
@@ -234,11 +230,11 @@
     small = pltpu.CompilerParams(vmem_limit_bytes=8 * 2**20)
 
     rows = mono_dev * basis + round_up(mono_dev, 16)
-    shard, shard_far = pl.pallas_call(
+    shard = pl.pallas_call(
         fold_kernel,
-        out_shape=[pltpu.VMEM((rows, half), density.dtype), pltpu.VMEM((rows + 16, half), density.dtype)],
+        out_shape=pltpu.VMEM((rows, half), density.dtype),
         in_specs=[IN_VMEM],
-        out_specs=[IN_VMEM] * 2,
+        out_specs=IN_VMEM,
         compiler_params=small,
         name="fold",
     )(density)
@@ -250,7 +246,7 @@
 
     rows_y = groups // 2
     top = lanes // 2
-    near = {(0, 0): shard, (0, top): along_z(shard_far, top)}
+    near = {(0, 0): shard, (0, top): along_z(shard, top)}
 
     def double(start):
         bit = top // 2
@@ -264,10 +260,10 @@
     for y in range(1, rows_y):
         near[y, 0] = along_y(shard, y)
 
-    def gate(piece, *after):
+    def gate(piece, *after, extra=0):
         return pl.pallas_call(
             gate_kernel,
-            out_shape=pltpu.VMEM(shard.shape, shard.dtype),
+            out_shape=pltpu.VMEM((piece.shape[0] + extra,) + piece.shape[1:], piece.dtype),
             in_specs=[IN_VMEM] + [hbm] * len(after),
             out_specs=IN_VMEM,
             compiler_params=small,
@@ -285,23 +281,18 @@
         ahead = [gate(ahead[0], *ahead[1:])]
     for y in range(1, rows_y):
         near[y, top] = along_y(near[0, top], y)
+        near[y, top] = gate(near[y, top])
         for k in range(top + 1, lanes):
             near[y, k] = along_y(gate(near[0, k], *ahead), y)
 
-    early = [(y, k) for y, k in near if (y > 0) + bin(k).count("1") <= 1]
-    later = [key for key in near if key not in early]
-
-    def shape(count):
-        return pltpu.VMEM((count, rows, half), density.dtype)
-
-    names, blocks, first = pl.pallas_call(
+    names, blocks, near[rows_y - 1, 0] = pl.pallas_call(
         stage_kernel,
         out_shape=[
             pltpu.SMEM((nbr.shape[1], nbr.shape[0]), nbr.dtype),
             pltpu.VMEM(esp_block.shape, esp_block.dtype),
-            shape(len(early)),
+            pltpu.VMEM(shard.shape, shard.dtype),
         ],
-        in_specs=[hbm, hbm] + [IN_VMEM] * len(early),
+        in_specs=[hbm, hbm, IN_VMEM, hbm],
         out_specs=[IN_SMEM, IN_VMEM, IN_VMEM],
         scratch_shapes=[pltpu.SemaphoreType.DMA((2,))],
         compiler_params=small,
@@ -309,20 +300,11 @@
     )(
         pltpu.with_memory_space_constraint(nbr.T, pltpu.HBM),
         pltpu.with_memory_space_constraint(esp_block, pltpu.HBM),
-        *[near[key] for key in early],
+        near[rows_y - 1, 0],
+        near[0, lanes - 1],
     )
-    second = pl.pallas_call(
-        gather_kernel,
-        out_shape=shape(len(later)),
-        in_specs=[IN_VMEM] * len(later),
-        out_specs=IN_VMEM,
-        compiler_params=pltpu.CompilerParams(vmem_limit_bytes=2 * len(later) * rows * half * 2 + 4 * 2**20),
-        name="gather",
-    )(*[near[key] for key in later])
-    mine = [first, second]
+    mine = [near[y, k] for y in range(rows_y) for k in range(lanes)]
     pieces = mine + [lax.ppermute(piece, "gddi", xor_pairs(groups, 1)) for piece in mine]
-    places = [[y * lanes + k for y, k in keys] for keys in (early, later)]
-    places += [[rows_y * lanes + place for place in keys] for keys in places]
 
     plain = pltpu.VMEM((mono_dev, basis + 8, half), jnp.float32)
     coded = pltpu.VMEM((mono_dev * half + round_up(2 * mono_dev, 8), half), jnp.int32)
@@ -330,7 +312,7 @@
 
     def couple(units, name):
         return pl.pallas_call(
-            functools.partial(couple_kernel, groups, lanes, mono_dev, units, places),
+            functools.partial(couple_kernel, groups, lanes, mono_dev, units),
             out_shape=[coded if is_coded else plain for _, is_coded in units],
             in_specs=[IN_SMEM] + [IN_VMEM] * (1 + len(pieces)),
             out_specs=[IN_VMEM] * len(units),
@@ -345,15 +327,15 @@
     relayed = couple([(top ^ k, True) for k in steps], "couple_relay") if top > 1 else []
     relayed = [along_z(unit, k) for k, unit in zip(steps, relayed)]
     own, across, *close = couple([(0, False), (top, False)] + [(k, True) for k in steps], "couple")
-    close = [along_z(unit, k) for k, unit in zip(steps, close)]
     across = pl.pallas_call(
         merge_kernel,
-        out_shape=coded,
+        out_shape=pltpu.VMEM((coded.shape[0] + 8, half), jnp.int32),
         in_specs=[IN_VMEM] * (1 + len(relayed)),
         out_specs=IN_VMEM,
         compiler_params=small,
         name="merge",
     )(across, *relayed)
+    close = [along_z(gate(unit, across), k) for k, unit in zip(steps, close)]
     return pl.pallas_call(
         finish_kernel,
         out_shape=jax.ShapeDtypeStruct((mono_dev, basis, basis), jnp.float32),

time: 42.6 us -> 41.8 us (0.981)
  waiting for transfers between devices: 19.4 us -> 16.3 us
  starting transfers between devices: 15.6 us -> 18 us
    ppermute x4, waiting for transfers between devices: 4.53 us -> 0.68 us  [along_y(): return lax.ppermute(piece, 'gddi', xor_pairs(groups, 2 * y))]
    ppermute x4, starting transfers between devices: 4.81 us -> 6.47 us  [along_y(): return lax.ppermute(piece, 'gddi', xor_pairs(groups, 2 * y))]
    ppermute x2 -> x8, starting transfers between devices: 0.14 us -> 1.65 us  [local(): lax.ppermute(piece, 'gddi', xor_pairs(groups, 1))]
    ppermute x6, waiting for transfers between devices: 13 us -> 14.3 us  [along_z(): return lax.ppermute(piece, 'intra', xor_pairs(lanes, bit))]
    ppermute x6, starting transfers between devices: 10.7 us -> 9.86 us  [along_z(): return lax.ppermute(piece, 'intra', xor_pairs(lanes, bit))]
    ppermute x2 -> x8, waiting for transfers between devices: 1.91 us -> 1.36 us  [local(): lax.ppermute(piece, 'gddi', xor_pairs(groups, 1))]
  transfers between devices with their start and end apart: 12 -> 18, of which waited for: 8 -> 9; matrix products, arithmetic and copies ran while one was open for 0% -> 0% of each run, Pallas kernels for 10% -> 9%
where the time goes in v7:
time: 41.8 us; the launch traced here: 41.7 us
  starting transfers between devices  18 us (43%)
  waiting for transfers between devices  16.3 us (39%)
  Pallas kernels  6.27 us (15%)
  local copies, waits for them, and re-layouts  0.96 us (2%)
    ppermute x6, waiting for transfers between devices, along_z(): return lax.ppermute(piece, 'intra', xor_pairs(lanes, bit))  14.3 us
    ppermute x6, starting transfers between devices, along_z(): return lax.ppermute(piece, 'intra', xor_pairs(lanes, bit))  9.86 us
    ppermute x4, starting transfers between devices, along_y(): return lax.ppermute(piece, 'gddi', xor_pairs(groups, 2 * y))  6.47 us
    pallas_call x2, Pallas kernels, couple(): pl.pallas_call(functools.partial(couple_kernel, groups, lanes, mono_dev,...  3.37 us
    ppermute x8, starting transfers between devices, local(): lax.ppermute(piece, 'gddi', xor_pairs(groups, 1))  1.65 us
    pallas_call x1, Pallas kernels, local(): pl.pallas_call(stage_kernel, out_shape=[pltpu.SMEM((nbr.shape[1], nbr.sha...  1.62 us
    ppermute x8, waiting for transfers between devices, local(): lax.ppermute(piece, 'gddi', xor_pairs(groups, 1))  1.36 us
    pallas_call x1, Pallas kernels, local(): pl.pallas_call(finish_kernel, out_shape=jax.ShapeDtypeStruct((mono_dev, b...  0.99 us
  transfers between devices with their start and end apart: 18, of which 9 were waited for; matrix products, arithmetic and copies ran while one was open for 0% of the time, Pallas kernels for 9%

profile of v7, /device:TPU:0, one launch (start us, length us, event | category | flops | bytes accessed | tf_op | source)
XLA Modules:
  0.0 41.7 jit_solution(10807525324014283349)
XLA Ops:
  0.0 0.9 %copy-done = bf16[2,256,256]{2,1,0:T(8,128)(2,1)S(1)} copy-done((bf16[2,256,256]{2,1,0:T(8,128)(2,1)S(1)}, bf16[2,256,256]{2,1,0:T(8,128)(2,1)}, u32[]{:S(2)}) %copy-start) | copy-done | bytes 262168
  1.0 3.1 %collective-permute-start.2 = (bf16[528,128]{1,0:T(8,128)(2,1)S(1)}, bf16[528,128]{1,0:T(8,128)(2,1)S(1)}, u32[]{:S(2)}, u32[]{:S(2)}) collective-permute-start(bf16[528,128]{1,0:T(8,128)(2,1)S(1)} %fold.1.refs_0_), channel_id=1, source_target_pairs={{0,1},{1,0},{2,3},{3,2},{4,5},{5,4},{6,7},{7,6},{8,9},{9,8},{10,11... | collective-permute-start | bytes 405512 | tf_op jit(solution)/shard_map/ppermute | solution.py:242
  4.1 2.6 %collective-permute-start.1 = (bf16[528,128]{1,0:T(8,128)(2,1)S(1)}, bf16[528,128]{1,0:T(8,128)(2,1)S(1)}, u32[]{:S(2)}, u32[]{:S(2)}) collective-permute-start(bf16[528,128]{1,0:T(8,128)(2,1)S(1)} %fold.1.refs_0_), channel_id=1, source_target_pairs={{0,2},{1,3},{2,0},{3,1},{4,6},{5,7},{6,4},{7,5},{8,10},{9,11},{10,... | collective-permute-start | bytes 405512 | tf_op jit(solution)/shard_map/ppermute | solution.py:242
  6.7 1.5 %collective-permute-start = (bf16[528,128]{1,0:T(8,128)(2,1)S(1)}, bf16[528,128]{1,0:T(8,128)(2,1)S(1)}, u32[]{:S(2)}, u32[]{:S(2)}) collective-permute-start(bf16[528,128]{1,0:T(8,128)(2,1)S(1)} %fold.1.refs_0_), channel_id=1, source_target_pairs={{0,8},{4,12},{8,0},{12,4},{1,9},{5,13},{9,1},{13,5},{2,10},{6,14},... | collective-permute-start | bytes 405512 | tf_op jit(solution)/shard_map/ppermute | solution.py:245
  8.2 1.5 %collective-permute-done.2.refs_1_ = bf16[528,128]{1,0:T(8,128)(2,1)S(1)} collective-permute-done((bf16[528,128]{1,0:T(8,128)(2,1)S(1)}, bf16[528,128]{1,0:T(8,128)(2,1)S(1)}, u32[]{:S(2)}, u32[]{:S(2)}) %collective-permute-start.2) | collective-permute-done | bytes 135200 | tf_op jit(solution)/shard_map/ppermute | solution.py:242
  9.7 1.8 %collective-permute-start.4 = (bf16[528,128]{1,0:T(8,128)(2,1)S(1)}, bf16[528,128]{1,0:T(8,128)(2,1)S(1)}, u32[]{:S(2)}, u32[]{:S(2)}) collective-permute-start(bf16[528,128]{1,0:T(8,128)(2,1)S(1)} %collective-permute-done.2.refs_1_), channel_id=1, source_target_pairs={{0,8},{4,12},{8,0},{12,4},{1,9},{5,13},{9,1},{13,5},{2,10},{6,14},... | collective-permute-start | bytes 405512 | tf_op jit(solution)/shard_map/ppermute | solution.py:245
  11.5 1.4 %collective-permute-done.1.piece_ref = bf16[528,128]{1,0:T(8,128)(2,1)S(1)} collective-permute-done((bf16[528,128]{1,0:T(8,128)(2,1)S(1)}, bf16[528,128]{1,0:T(8,128)(2,1)S(1)}, u32[]{:S(2)}, u32[]{:S(2)}) %collective-permute-start.1) | collective-permute-done | bytes 135200 | tf_op jit(solution)/shard_map/ppermute | solution.py:242
  13.0 0.5 %collective-permute-start.3 = (bf16[528,128]{1,0:T(8,128)(2,1)S(1)}, bf16[528,128]{1,0:T(8,128)(2,1)S(1)}, u32[]{:S(2)}, u32[]{:S(2)}) collective-permute-start(bf16[528,128]{1,0:T(8,128)(2,1)S(1)} %gate.9.refs_2_), channel_id=1, source_target_pairs={{0,1},{1,0},{2,3},{3,2},{4,5},{5,4},{6,7},{7,6},{8,9},{9,8},{10,11... | collective-permute-start | bytes 405512 | tf_op jit(solution)/shard_map/ppermute | solution.py:242
  13.5 1.5 %collective-permute-start.5 = (bf16[528,128]{1,0:T(8,128)(2,1)S(1)}, bf16[528,128]{1,0:T(8,128)(2,1)S(1)}, u32[]{:S(2)}, u32[]{:S(2)}) collective-permute-start(bf16[528,128]{1,0:T(8,128)(2,1)S(1)} %gate.9.refs_2_), channel_id=1, source_target_pairs={{0,8},{4,12},{8,0},{12,4},{1,9},{5,13},{9,1},{13,5},{2,10},{6,14},... | collective-permute-start | bytes 405512 | tf_op jit(solution)/shard_map/ppermute | solution.py:245
  15.1 0.5 %collective-permute-start.9 = (bf16[528,128]{1,0:T(8,128)(2,1)S(1)}, bf16[528,128]{1,0:T(8,128)(2,1)S(1)}, u32[]{:S(2)}, u32[]{:S(2)}) collective-permute-start(bf16[528,128]{1,0:T(8,128)(2,1)S(1)} %gate.9.refs_2_), channel_id=1, source_target_pairs={{0,4},{4,0},{8,12},{12,8},{1,5},{5,1},{9,13},{13,9},{2,6},{6,2},{1... | collective-permute-start | bytes 405512 | tf_op jit(solution)/shard_map/ppermute | solution.py:307
  15.6 2.5 %collective-permute-done.3.refs_0_.piece_ref.refs_3_ = bf16[528,128]{1,0:T(8,128)(2,1)S(1)} collective-permute-done((bf16[528,128]{1,0:T(8,128)(2,1)S(1)}, bf16[528,128]{1,0:T(8,128)(2,1)S(1)}, u32[]{:S(2)}, u32[]{:S(2)}) %collective-permute-start.3) | collective-permute-done | bytes 135200 | tf_op jit(solution)/shard_map/ppermute | solution.py:242
  18.1 1.6 %collective-permute-start.6 = (bf16[528,128]{1,0:T(8,128)(2,1)S(1)}, bf16[528,128]{1,0:T(8,128)(2,1)S(1)}, u32[]{:S(2)}, u32[]{:S(2)}) collective-permute-start(bf16[528,128]{1,0:T(8,128)(2,1)S(1)} %gate.14), channel_id=1, source_target_pairs={{0,8},{4,12},{8,0},{12,4},{1,9},{5,13},{9,1},{13,5},{2,10},{6,14},... | collective-permute-start | bytes 405512 | tf_op jit(solution)/shard_map/ppermute | solution.py:245
  19.7 1.6 %stage.1 = (s32[8,32]{1,0:T(8,128)S(4)}, bf16[8,2,256,256]{3,2,1,0:T(8,128)(2,1)S(1)}, bf16[528,128]{1,0:T(8,128)(2,1)S(1)}) custom-call(s32[8,32]{1,0:T(8,128)} %bitcast.1, bf16[8,2,256,256]{3,2,1,0:T(8,128)(2,1)} %esp_ref.1, bf16[528,128]{1,0:T(8,128)(2,1)S(1)} %collective-permute-done.refs_2_.piece_ref, ...), custom_call_target="tpu_custom_call" | custom-call | tf_op jit(solution)/shard_map/stage/pallas_call | solution.py:288
  21.4 0.6 %collective-permute-start.13 = (bf16[528,128]{1,0:T(8,128)(2,1)S(1)}, bf16[528,128]{1,0:T(8,128)(2,1)S(1)}, u32[]{:S(2)}, u32[]{:S(2)}) collective-permute-start(bf16[528,128]{1,0:T(8,128)(2,1)S(1)} %gate.10.refs_6_), channel_id=1, source_target_pairs={{0,4},{4,0},{8,12},{12,8},{1,5},{5,1},{9,13},{13,9},{2,6},{6,2},{1... | collective-permute-start | bytes 405512 | tf_op jit(solution)/shard_map/ppermute | solution.py:307
  22.5 0.7 %collective-permute-done.6.refs_7_ = bf16[528,128]{1,0:T(8,128)(2,1)S(1)} collective-permute-done((bf16[528,128]{1,0:T(8,128)(2,1)S(1)}, bf16[528,128]{1,0:T(8,128)(2,1)S(1)}, u32[]{:S(2)}, u32[]{:S(2)}) %collective-permute-start.6) | collective-permute-done | bytes 135200 | tf_op jit(solution)/shard_map/ppermute | solution.py:245
  23.6 1.0 %collective-permute-done.14.refs_15_ = bf16[528,128]{1,0:T(8,128)(2,1)S(1)} collective-permute-done((bf16[528,128]{1,0:T(8,128)(2,1)S(1)}, bf16[528,128]{1,0:T(8,128)(2,1)S(1)}, u32[]{:S(2)}, u32[]{:S(2)}) %collective-permute-start.14) | collective-permute-done | bytes 135200 | tf_op jit(solution)/shard_map/ppermute | solution.py:307
  24.6 1.1 %couple_relay.1 = s32[264,128]{1,0:T(8,128)S(1)} custom-call(s32[8,32]{1,0:T(8,128)S(4)} %get-tuple-element.11.nbr_ref, bf16[8,2,256,256]{3,2,1,0:T(8,128)(2,1)S(1)} %get-tuple-element.12.esp_ref, bf16[528,128]{1,0:T(8,128)(2,1)S(1)} %fold.1.refs_0_, bf16[528,128]{1,0:T(8,128)(2,1)S(1)} %collective-permute-done.2.refs_1_, bf16[528,128]{1,0:T(8,128)(2,1)S(1)} %gate.9.refs_2_, ...), custom_call_target="tpu_custom_call" | custom-call | tf_op jit(solution)/shard_map/couple_relay/pallas_call | solution.py:314
  25.7 0.5 %collective-permute-start.15 = (s32[264,128]{1,0:T(8,128)S(1)}, s32[264,128]{1,0:T(8,128)S(1)}, u32[]{:S(2)}, u32[]{:S(2)}) collective-permute-start(s32[264,128]{1,0:T(8,128)S(1)} %couple_relay.1), channel_id=1, source_target_pairs={{0,1},{1,0},{2,3},{3,2},{4,5},{5,4},{6,7},{7,6},{8,9},{9,8},{10,11... | collective-permute-start | bytes 405512 | tf_op jit(solution)/shard_map/ppermute | solution.py:242
  26.2 2.2 %couple.1 = (f32[2,264,128]{2,1,0:T(8,128)S(1)}, f32[2,264,128]{2,1,0:T(8,128)S(1)}, s32[264,128]{1,0:T(8,128)S(1)}) custom-call(s32[8,32]{1,0:T(8,128)S(4)} %get-tuple-element.11.nbr_ref, bf16[8,2,256,256]{3,2,1,0:T(8,128)(2,1)S(1)} %get-tuple-element.12.esp_ref, bf16[528,128]{1,0:T(8,128)(2,1)S(1)} %fold.1.refs_0_, ...), custom_call_target="tpu_custom_call" | custom-call | tf_op jit(solution)/shard_map/couple/pallas_call | solution.py:314
  28.5 2.9 %collective-permute-done.15.refs_0_ = s32[264,128]{1,0:T(8,128)S(1)} collective-permute-done((s32[264,128]{1,0:T(8,128)S(1)}, s32[264,128]{1,0:T(8,128)S(1)}, u32[]{:S(2)}, u32[]{:S(2)}) %collective-permute-start.15) | collective-permute-done | bytes 135200 | tf_op jit(solution)/shard_map/ppermute | solution.py:242
  31.6 1.4 %collective-permute-start.17 = (s32[272,128]{1,0:T(8,128)S(1)}, s32[272,128]{1,0:T(8,128)S(1)}, u32[]{:S(2)}, u32[]{:S(2)}) collective-permute-start(s32[272,128]{1,0:T(8,128)S(1)} %merge.1.refs_0_), channel_id=1, source_target_pairs={{0,2},{1,3},{2,0},{3,1},{4,6},{5,7},{6,4},{7,5},{8,10},{9,11},{10,... | collective-permute-start | bytes 417800 | tf_op jit(solution)/shard_map/ppermute | solution.py:242
  32.9 1.8 %collective-permute-start.16 = (s32[264,128]{1,0:T(8,128)S(1)}, s32[264,128]{1,0:T(8,128)S(1)}, u32[]{:S(2)}, u32[]{:S(2)}) collective-permute-start(s32[264,128]{1,0:T(8,128)S(1)} %gate.15), channel_id=1, source_target_pairs={{0,1},{1,0},{2,3},{3,2},{4,5},{5,4},{6,7},{7,6},{8,9},{9,8},{10,11... | collective-permute-start | bytes 405512 | tf_op jit(solution)/shard_map/ppermute | solution.py:242
  34.7 5.9 %collective-permute-done.16.refs_0_ = s32[264,128]{1,0:T(8,128)S(1)} collective-permute-done((s32[264,128]{1,0:T(8,128)S(1)}, s32[264,128]{1,0:T(8,128)S(1)}, u32[]{:S(2)}, u32[]{:S(2)}) %collective-permute-start.16) | collective-permute-done | bytes 135200 | tf_op jit(solution)/shard_map/ppermute | solution.py:242
  40.7 1.0 %finish.1 = f32[2,256,256]{2,1,0:T(8,128)} custom-call(bf16[2,256,256]{2,1,0:T(8,128)(2,1)S(1)} %copy-done.1, f32[2,264,128]{2,1,0:T(8,128)S(1)} %get-tuple-element.14.own_ref, s32[264,128]{1,0:T(8,128)S(1)} %collective-permute-done.16.refs_0_, s32[272,128]{1,0:T(8,128)S(1)} %collective-permute-done.17.refs_1_), custom_call_target="tpu_custom_call" | custom-call | tf_op jit(solution)/shard_map/finish/pallas_call | solution.py:339
  (30 shorter events, 1.3 us)
Async XLA Ops:
  0.0 0.9 %copy-start = (bf16[2,256,256]{2,1,0:T(8,128)(2,1)S(1)}, bf16[2,256,256]{2,1,0:T(8,128)(2,1)}, u32[]{:S(2)}) copy-start(bf16[2,256,256]{2,1,0:T(8,128)(2,1)} %dens_ref.1) | copy-start | bytes 786436
  1.0 8.7 %collective-permute-start.2 = (bf16[528,128]{1,0:T(8,128)(2,1)S(1)}, bf16[528,128]{1,0:T(8,128)(2,1)S(1)}, u32[]{:S(2)}, u32[]{:S(2)}) collective-permute-start(bf16[528,128]{1,0:T(8,128)(2,1)S(1)} %fold.1.refs_0_), channel_id=1, source_target_pairs={{0,1},{1,0},{2,3},{3,2},{4,5},{5,4},{6,7},{7,6},{8,9},{9,8},{10,11... | collective-permute-start | bytes 405512 | tf_op jit(solution)/shard_map/ppermute | solution.py:242
  4.1 8.9 %collective-permute-start.1 = (bf16[528,128]{1,0:T(8,128)(2,1)S(1)}, bf16[528,128]{1,0:T(8,128)(2,1)S(1)}, u32[]{:S(2)}, u32[]{:S(2)}) collective-permute-start(bf16[528,128]{1,0:T(8,128)(2,1)S(1)} %fold.1.refs_0_), channel_id=1, source_target_pairs={{0,2},{1,3},{2,0},{3,1},{4,6},{5,7},{6,4},{7,5},{8,10},{9,11},{10,... | collective-permute-start | bytes 405512 | tf_op jit(solution)/shard_map/ppermute | solution.py:242
  6.7 6.3 %collective-permute-start = (bf16[528,128]{1,0:T(8,128)(2,1)S(1)}, bf16[528,128]{1,0:T(8,128)(2,1)S(1)}, u32[]{:S(2)}, u32[]{:S(2)}) collective-permute-start(bf16[528,128]{1,0:T(8,128)(2,1)S(1)} %fold.1.refs_0_), channel_id=1, source_target_pairs={{0,8},{4,12},{8,0},{12,4},{1,9},{5,13},{9,1},{13,5},{2,10},{6,14},... | collective-permute-start | bytes 405512 | tf_op jit(solution)/shard_map/ppermute | solution.py:245
  9.7 5.9 %collective-permute-start.4 = (bf16[528,128]{1,0:T(8,128)(2,1)S(1)}, bf16[528,128]{1,0:T(8,128)(2,1)S(1)}, u32[]{:S(2)}, u32[]{:S(2)}) collective-permute-start(bf16[528,128]{1,0:T(8,128)(2,1)S(1)} %collective-permute-done.2.refs_1_), channel_id=1, source_target_pairs={{0,8},{4,12},{8,0},{12,4},{1,9},{5,13},{9,1},{13,5},{2,10},{6,14},... | collective-permute-start | bytes 405512 | tf_op jit(solution)/shard_map/ppermute | solution.py:245
  13.0 5.1 %collective-permute-start.3 = (bf16[528,128]{1,0:T(8,128)(2,1)S(1)}, bf16[528,128]{1,0:T(8,128)(2,1)S(1)}, u32[]{:S(2)}, u32[]{:S(2)}) collective-permute-start(bf16[528,128]{1,0:T(8,128)(2,1)S(1)} %gate.9.refs_2_), channel_id=1, source_target_pairs={{0,1},{1,0},{2,3},{3,2},{4,5},{5,4},{6,7},{7,6},{8,9},{9,8},{10,11... | collective-permute-start | bytes 405512 | tf_op jit(solution)/shard_map/ppermute | solution.py:242
  13.5 7.8 %collective-permute-start.5 = (bf16[528,128]{1,0:T(8,128)(2,1)S(1)}, bf16[528,128]{1,0:T(8,128)(2,1)S(1)}, u32[]{:S(2)}, u32[]{:S(2)}) collective-permute-start(bf16[528,128]{1,0:T(8,128)(2,1)S(1)} %gate.9.refs_2_), channel_id=1, source_target_pairs={{0,8},{4,12},{8,0},{12,4},{1,9},{5,13},{9,1},{13,5},{2,10},{6,14},... | collective-permute-start | bytes 405512 | tf_op jit(solution)/shard_map/ppermute | solution.py:245
  15.1 6.4 %collective-permute-start.7 = (bf16[528,128]{1,0:T(8,128)(2,1)S(1)}, bf16[528,128]{1,0:T(8,128)(2,1)S(1)}, u32[]{:S(2)}, u32[]{:S(2)}) collective-permute-start(bf16[528,128]{1,0:T(8,128)(2,1)S(1)} %fold.1.refs_0_), channel_id=1, source_target_pairs={{0,4},{4,0},{8,12},{12,8},{1,5},{5,1},{9,13},{13,9},{2,6},{6,2},{1... | collective-permute-start | bytes 405512 | tf_op jit(solution)/shard_map/ppermute | solution.py:307
  15.1 7.0 %collective-permute-start.9 = (bf16[528,128]{1,0:T(8,128)(2,1)S(1)}, bf16[528,128]{1,0:T(8,128)(2,1)S(1)}, u32[]{:S(2)}, u32[]{:S(2)}) collective-permute-start(bf16[528,128]{1,0:T(8,128)(2,1)S(1)} %gate.9.refs_2_), channel_id=1, source_target_pairs={{0,4},{4,0},{8,12},{12,8},{1,5},{5,1},{9,13},{13,9},{2,6},{6,2},{1... | collective-permute-start | bytes 405512 | tf_op jit(solution)/shard_map/ppermute | solution.py:307
  15.6 6.4 %collective-permute-start.8 = (bf16[528,128]{1,0:T(8,128)(2,1)S(1)}, bf16[528,128]{1,0:T(8,128)(2,1)S(1)}, u32[]{:S(2)}, u32[]{:S(2)}) collective-permute-start(bf16[528,128]{1,0:T(8,128)(2,1)S(1)} %collective-permute-done.2.refs_1_), channel_id=1, source_target_pairs={{0,4},{4,0},{8,12},{12,8},{1,5},{5,1},{9,13},{13,9},{2,6},{6,2},{1... | collective-permute-start | bytes 405512 | tf_op jit(solution)/shard_map/ppermute | solution.py:307
  18.1 5.1 %collective-permute-start.6 = (bf16[528,128]{1,0:T(8,128)(2,1)S(1)}, bf16[528,128]{1,0:T(8,128)(2,1)S(1)}, u32[]{:S(2)}, u32[]{:S(2)}) collective-permute-start(bf16[528,128]{1,0:T(8,128)(2,1)S(1)} %gate.14), channel_id=1, source_target_pairs={{0,8},{4,12},{8,0},{12,4},{1,9},{5,13},{9,1},{13,5},{2,10},{6,14},... | collective-permute-start | bytes 405512 | tf_op jit(solution)/shard_map/ppermute | solution.py:245
  21.3 2.0 %collective-permute-start.11 = (bf16[528,128]{1,0:T(8,128)(2,1)S(1)}, bf16[528,128]{1,0:T(8,128)(2,1)S(1)}, u32[]{:S(2)}, u32[]{:S(2)}) collective-permute-start(bf16[528,128]{1,0:T(8,128)(2,1)S(1)} %get-tuple-element.13.refs_4_), channel_id=1, source_target_pairs={{0,4},{4,0},{8,12},{12,8},{1,5},{5,1},{9,13},{13,9},{2,6},{6,2},{1... | collective-permute-start | bytes 405512 | tf_op jit(solution)/shard_map/ppermute | solution.py:307
  21.4 2.1 %collective-permute-start.13 = (bf16[528,128]{1,0:T(8,128)(2,1)S(1)}, bf16[528,128]{1,0:T(8,128)(2,1)S(1)}, u32[]{:S(2)}, u32[]{:S(2)}) collective-permute-start(bf16[528,128]{1,0:T(8,128)(2,1)S(1)} %gate.10.refs_6_), channel_id=1, source_target_pairs={{0,4},{4,0},{8,12},{12,8},{1,5},{5,1},{9,13},{13,9},{2,6},{6,2},{1... | collective-permute-start | bytes 405512 | tf_op jit(solution)/shard_map/ppermute | solution.py:307
  22.0 1.4 %collective-permute-start.10 = (bf16[528,128]{1,0:T(8,128)(2,1)S(1)}, bf16[528,128]{1,0:T(8,128)(2,1)S(1)}, u32[]{:S(2)}, u32[]{:S(2)}) collective-permute-start(bf16[528,128]{1,0:T(8,128)(2,1)S(1)} %collective-permute-done.3.refs_0_.piece_ref.refs_3_), channel_id=1, source_target_pairs={{0,4},{4,0},{8,12},{12,8},{1,5},{5,1},{9,13},{13,9},{2,6},{6,2},{1... | collective-permute-start | bytes 405512 | tf_op jit(solution)/shard_map/ppermute | solution.py:307
  22.1 1.5 %collective-permute-start.12 = (bf16[528,128]{1,0:T(8,128)(2,1)S(1)}, bf16[528,128]{1,0:T(8,128)(2,1)S(1)}, u32[]{:S(2)}, u32[]{:S(2)}) collective-permute-start(bf16[528,128]{1,0:T(8,128)(2,1)S(1)} %collective-permute-done.4.piece_ref.refs_5_), channel_id=1, source_target_pairs={{0,4},{4,0},{8,12},{12,8},{1,5},{5,1},{9,13},{13,9},{2,6},{6,2},{1... | collective-permute-start | bytes 405512 | tf_op jit(solution)/shard_map/ppermute | solution.py:307
  23.2 1.4 %collective-permute-start.14 = (bf16[528,128]{1,0:T(8,128)(2,1)S(1)}, bf16[528,128]{1,0:T(8,128)(2,1)S(1)}, u32[]{:S(2)}, u32[]{:S(2)}) collective-permute-start(bf16[528,128]{1,0:T(8,128)(2,1)S(1)} %collective-permute-done.6.refs_7_), channel_id=1, source_target_pairs={{0,4},{4,0},{8,12},{12,8},{1,5},{5,1},{9,13},{13,9},{2,6},{6,2},{1... | collective-permute-start | bytes 405512 | tf_op jit(solution)/shard_map/ppermute | solution.py:307
  25.7 15.0 %copy-start.1 = (bf16[2,256,256]{2,1,0:T(8,128)(2,1)S(1)}, bf16[2,256,256]{2,1,0:T(8,128)(2,1)}, u32[]{:S(2)}) copy-start(bf16[2,256,256]{2,1,0:T(8,128)(2,1)} %core_ref.1) | copy-start | bytes 786436
  25.7 5.7 %collective-permute-start.15 = (s32[264,128]{1,0:T(8,128)S(1)}, s32[264,128]{1,0:T(8,128)S(1)}, u32[]{:S(2)}, u32[]{:S(2)}) collective-permute-start(s32[264,128]{1,0:T(8,128)S(1)} %couple_relay.1), channel_id=1, source_target_pairs={{0,1},{1,0},{2,3},{3,2},{4,5},{5,4},{6,7},{7,6},{8,9},{9,8},{10,11... | collective-permute-start | bytes 405512 | tf_op jit(solution)/shard_map/ppermute | solution.py:242
  31.6 9.1 %collective-permute-start.17 = (s32[272,128]{1,0:T(8,128)S(1)}, s32[272,128]{1,0:T(8,128)S(1)}, u32[]{:S(2)}, u32[]{:S(2)}) collective-permute-start(s32[272,128]{1,0:T(8,128)S(1)} %merge.1.refs_0_), channel_id=1, source_target_pairs={{0,2},{1,3},{2,0},{3,1},{4,6},{5,7},{6,4},{7,5},{8,10},{9,11},{10,... | collective-permute-start | bytes 417800 | tf_op jit(solution)/shard_map/ppermute | solution.py:242
  32.9 7.7 %collective-permute-start.16 = (s32[264,128]{1,0:T(8,128)S(1)}, s32[264,128]{1,0:T(8,128)S(1)}, u32[]{:S(2)}, u32[]{:S(2)}) collective-permute-start(s32[264,128]{1,0:T(8,128)S(1)} %gate.15), channel_id=1, source_target_pairs={{0,1},{1,0},{2,3},{3,2},{4,5},{5,4},{6,7},{7,6},{8,9},{9,8},{10,11... | collective-permute-start | bytes 405512 | tf_op jit(solution)/shard_map/ppermute | solution.py:242

commit v8 on v7

--- a/solution.py
+++ b/solution.py
@@ -94,11 +94,7 @@
 
 
 def gate_kernel(piece_ref, *refs):
-    out_ref = refs[-1]
-    out_ref[pl.ds(0, piece_ref.shape[0])] = piece_ref[...]
-    extra = out_ref.shape[0] - piece_ref.shape[0]
-    if extra:
-        out_ref[pl.ds(piece_ref.shape[0], extra)] = jnp.zeros((extra, out_ref.shape[1]), out_ref.dtype)
+    refs[-1][...] = piece_ref[...]
 
 
 def stage_kernel(nbr_ref, esp_ref, piece_ref, *refs):
@@ -115,16 +111,19 @@
 
 
 def couple_kernel(groups, lanes, mono_dev, units, nbr_ref, esp_ref, *refs):
-    n_pieces = groups * lanes
-    pieces, outs, store = refs[:n_pieces], refs[n_pieces:-1], refs[-1]
+    outs = refs[len(refs) - len(units) :]
+    if len(refs) > len(units) + 1:
+        pieces, store = refs[: -1 - len(units)], refs[-1 - len(units)]
+        for i, piece in enumerate(pieces):
+            store[i] = piece[...]
+    else:
+        store = refs[0]
     my_group = lax.axis_index("gddi")
     my_lane = lax.axis_index("intra")
     _, slot_dev, basis, _ = esp_ref.shape
     mono_grp = mono_dev * lanes
     half = basis // 2
     tail_rows = store.shape[1] - mono_dev * basis
-    for i, piece in enumerate(pieces):
-        store[i] = piece[pl.ds(0, store.shape[1])]
 
     def near_density(fragment):
         apart = (fragment // mono_grp) ^ my_group
@@ -260,10 +259,10 @@
     for y in range(1, rows_y):
         near[y, 0] = along_y(shard, y)
 
-    def gate(piece, *after, extra=0):
+    def gate(piece, *after):
         return pl.pallas_call(
             gate_kernel,
-            out_shape=pltpu.VMEM((piece.shape[0] + extra,) + piece.shape[1:], piece.dtype),
+            out_shape=pltpu.VMEM(piece.shape, piece.dtype),
             in_specs=[IN_VMEM] + [hbm] * len(after),
             out_specs=IN_VMEM,
             compiler_params=small,
@@ -310,13 +309,15 @@
     coded = pltpu.VMEM((mono_dev * half + round_up(2 * mono_dev, 8), half), jnp.int32)
     piece_bytes = groups * lanes * rows * half * 2
 
-    def couple(units, name):
+    keep = pltpu.VMEM if piece_bytes <= 4 * 2**20 else jax.ShapeDtypeStruct
+    store = keep((groups * lanes, rows, half), density.dtype)
+
+    def couple(units, name, pieces, fill=False):
         return pl.pallas_call(
             functools.partial(couple_kernel, groups, lanes, mono_dev, units),
-            out_shape=[coded if is_coded else plain for _, is_coded in units],
+            out_shape=[store] * fill + [coded if is_coded else plain for _, is_coded in units],
             in_specs=[IN_SMEM] + [IN_VMEM] * (1 + len(pieces)),
-            out_specs=[IN_VMEM] * len(units),
-            scratch_shapes=[pltpu.VMEM((groups * lanes, rows, half), density.dtype)],
+            out_specs=[IN_VMEM] * (fill + len(units)),
             compiler_params=pltpu.CompilerParams(
                 vmem_limit_bytes=2 * (piece_bytes + esp_block.size * 2) + 8 * 2**20
             ),
@@ -324,18 +325,21 @@
         )(names, blocks, *pieces)
 
     steps = range(1, top)
-    relayed = couple([(top ^ k, True) for k in steps], "couple_relay") if top > 1 else []
+    filled, *relayed = couple([(top ^ k, True) for k in steps], "couple_relay", pieces, fill=True)
     relayed = [along_z(unit, k) for k, unit in zip(steps, relayed)]
-    own, across, *close = couple([(0, False), (top, False)] + [(k, True) for k in steps], "couple")
+    close = couple([(k, True) for k in steps], "couple_near", [filled])
+    close = [along_z(unit, k) for k, unit in zip(steps, close)]
+    for _ in range(5):
+        close = [gate(unit) for unit in close]
+    across, own = couple([(top, False), (0, False)], "couple_far", [filled])
     across = pl.pallas_call(
         merge_kernel,
-        out_shape=pltpu.VMEM((coded.shape[0] + 8, half), jnp.int32),
+        out_shape=coded,
         in_specs=[IN_VMEM] * (1 + len(relayed)),
         out_specs=IN_VMEM,
         compiler_params=small,
         name="merge",
     )(across, *relayed)
-    close = [along_z(gate(unit, across), k) for k, unit in zip(steps, close)]
     return pl.pallas_call(
         finish_kernel,
         out_shape=jax.ShapeDtypeStruct((mono_dev, basis, basis), jnp.float32),

time: 41.8 us -> 41.3 us (0.988)
  starting transfers between devices: 18 us -> 17.3 us
    ppermute x6, starting transfers between devices: 9.86 us -> 9.22 us  [along_z(): return lax.ppermute(piece, 'intra', xor_pairs(lanes, bit))]
    pallas_call x2 -> x3, Pallas kernels: 3.37 us -> 3.57 us  [couple(): pl.pallas_call(functools.partial(couple_kernel, groups, lanes, mono_dev,...]
  transfers between devices with their start and end apart: 18 -> 18, of which waited for: 9 -> 10; matrix products, arithmetic and copies ran while one was open for 0% -> 0% of each run, Pallas kernels for 9% -> 11%
where the time goes in v8:
time: 41.3 us; the launch traced here: 41.2 us
  starting transfers between devices  17.3 us (42%)
  waiting for transfers between devices  16.2 us (39%)
  Pallas kernels  6.51 us (16%)
  local copies, waits for them, and re-layouts  0.96 us (2%)
    ppermute x6, waiting for transfers between devices, along_z(): return lax.ppermute(piece, 'intra', xor_pairs(lanes, bit))  14.1 us
    ppermute x6, starting transfers between devices, along_z(): return lax.ppermute(piece, 'intra', xor_pairs(lanes, bit))  9.22 us
    ppermute x4, starting transfers between devices, along_y(): return lax.ppermute(piece, 'gddi', xor_pairs(groups, 2 * y))  6.47 us
    pallas_call x3, Pallas kernels, couple(): pl.pallas_call(functools.partial(couple_kernel, groups, lanes, mono_dev,...  3.57 us
    ppermute x8, starting transfers between devices, local(): lax.ppermute(piece, 'gddi', xor_pairs(groups, 1))  1.66 us
    pallas_call x1, Pallas kernels, local(): pl.pallas_call(stage_kernel, out_shape=[pltpu.SMEM((nbr.shape[1], nbr.sha...  1.62 us
    ppermute x8, waiting for transfers between devices, local(): lax.ppermute(piece, 'gddi', xor_pairs(groups, 1))  1.36 us
    pallas_call x1, Pallas kernels, local(): pl.pallas_call(finish_kernel, out_shape=jax.ShapeDtypeStruct((mono_dev, b...  0.98 us
  transfers between devices with their start and end apart: 18, of which 10 were waited for; matrix products, arithmetic and copies ran while one was open for 0% of the time, Pallas kernels for 11%

profile of v8, /device:TPU:0, one launch (start us, length us, event | category | flops | bytes accessed | tf_op | source)
XLA Modules:
  0.0 41.2 jit_solution(6331875122070337258)
XLA Ops:
  0.0 0.9 %copy-done = bf16[2,256,256]{2,1,0:T(8,128)(2,1)S(1)} copy-done((bf16[2,256,256]{2,1,0:T(8,128)(2,1)S(1)}, bf16[2,256,256]{2,1,0:T(8,128)(2,1)}, u32[]{:S(2)}) %copy-start) | copy-done | bytes 262168
  1.0 3.1 %collective-permute-start.2 = (bf16[528,128]{1,0:T(8,128)(2,1)S(1)}, bf16[528,128]{1,0:T(8,128)(2,1)S(1)}, u32[]{:S(2)}, u32[]{:S(2)}) collective-permute-start(bf16[528,128]{1,0:T(8,128)(2,1)S(1)} %fold.1.refs_0_), channel_id=1, source_target_pairs={{0,1},{1,0},{2,3},{3,2},{4,5},{5,4},{6,7},{7,6},{8,9},{9,8},{10,11... | collective-permute-start | bytes 405512 | tf_op jit(solution)/shard_map/ppermute | solution.py:241
  4.1 2.6 %collective-permute-start.1 = (bf16[528,128]{1,0:T(8,128)(2,1)S(1)}, bf16[528,128]{1,0:T(8,128)(2,1)S(1)}, u32[]{:S(2)}, u32[]{:S(2)}) collective-permute-start(bf16[528,128]{1,0:T(8,128)(2,1)S(1)} %fold.1.refs_0_), channel_id=1, source_target_pairs={{0,2},{1,3},{2,0},{3,1},{4,6},{5,7},{6,4},{7,5},{8,10},{9,11},{10,... | collective-permute-start | bytes 405512 | tf_op jit(solution)/shard_map/ppermute | solution.py:241
  6.7 1.5 %collective-permute-start = (bf16[528,128]{1,0:T(8,128)(2,1)S(1)}, bf16[528,128]{1,0:T(8,128)(2,1)S(1)}, u32[]{:S(2)}, u32[]{:S(2)}) collective-permute-start(bf16[528,128]{1,0:T(8,128)(2,1)S(1)} %fold.1.refs_0_), channel_id=1, source_target_pairs={{0,8},{4,12},{8,0},{12,4},{1,9},{5,13},{9,1},{13,5},{2,10},{6,14},... | collective-permute-start | bytes 405512 | tf_op jit(solution)/shard_map/ppermute | solution.py:244
  8.2 1.5 %collective-permute-done.2.refs_1_ = bf16[528,128]{1,0:T(8,128)(2,1)S(1)} collective-permute-done((bf16[528,128]{1,0:T(8,128)(2,1)S(1)}, bf16[528,128]{1,0:T(8,128)(2,1)S(1)}, u32[]{:S(2)}, u32[]{:S(2)}) %collective-permute-start.2) | collective-permute-done | bytes 135200 | tf_op jit(solution)/shard_map/ppermute | solution.py:241
  9.7 1.8 %collective-permute-start.4 = (bf16[528,128]{1,0:T(8,128)(2,1)S(1)}, bf16[528,128]{1,0:T(8,128)(2,1)S(1)}, u32[]{:S(2)}, u32[]{:S(2)}) collective-permute-start(bf16[528,128]{1,0:T(8,128)(2,1)S(1)} %collective-permute-done.2.refs_1_), channel_id=1, source_target_pairs={{0,8},{4,12},{8,0},{12,4},{1,9},{5,13},{9,1},{13,5},{2,10},{6,14},... | collective-permute-start | bytes 405512 | tf_op jit(solution)/shard_map/ppermute | solution.py:244
  11.5 1.4 %collective-permute-done.1.piece_ref = bf16[528,128]{1,0:T(8,128)(2,1)S(1)} collective-permute-done((bf16[528,128]{1,0:T(8,128)(2,1)S(1)}, bf16[528,128]{1,0:T(8,128)(2,1)S(1)}, u32[]{:S(2)}, u32[]{:S(2)}) %collective-permute-start.1) | collective-permute-done | bytes 135200 | tf_op jit(solution)/shard_map/ppermute | solution.py:241
  13.0 0.5 %collective-permute-start.3 = (bf16[528,128]{1,0:T(8,128)(2,1)S(1)}, bf16[528,128]{1,0:T(8,128)(2,1)S(1)}, u32[]{:S(2)}, u32[]{:S(2)}) collective-permute-start(bf16[528,128]{1,0:T(8,128)(2,1)S(1)} %gate.13.refs_2_), channel_id=1, source_target_pairs={{0,1},{1,0},{2,3},{3,2},{4,5},{5,4},{6,7},{7,6},{8,9},{9,8},{10,11... | collective-permute-start | bytes 405512 | tf_op jit(solution)/shard_map/ppermute | solution.py:241
  13.5 1.5 %collective-permute-start.5 = (bf16[528,128]{1,0:T(8,128)(2,1)S(1)}, bf16[528,128]{1,0:T(8,128)(2,1)S(1)}, u32[]{:S(2)}, u32[]{:S(2)}) collective-permute-start(bf16[528,128]{1,0:T(8,128)(2,1)S(1)} %gate.13.refs_2_), channel_id=1, source_target_pairs={{0,8},{4,12},{8,0},{12,4},{1,9},{5,13},{9,1},{13,5},{2,10},{6,14},... | collective-permute-start | bytes 405512 | tf_op jit(solution)/shard_map/ppermute | solution.py:244
  15.6 2.5 %collective-permute-done.3.refs_0_.piece_ref.refs_3_ = bf16[528,128]{1,0:T(8,128)(2,1)S(1)} collective-permute-done((bf16[528,128]{1,0:T(8,128)(2,1)S(1)}, bf16[528,128]{1,0:T(8,128)(2,1)S(1)}, u32[]{:S(2)}, u32[]{:S(2)}) %collective-permute-start.3) | collective-permute-done | bytes 135200 | tf_op jit(solution)/shard_map/ppermute | solution.py:241
  18.1 1.6 %collective-permute-start.6 = (bf16[528,128]{1,0:T(8,128)(2,1)S(1)}, bf16[528,128]{1,0:T(8,128)(2,1)S(1)}, u32[]{:S(2)}, u32[]{:S(2)}) collective-permute-start(bf16[528,128]{1,0:T(8,128)(2,1)S(1)} %gate.18), channel_id=1, source_target_pairs={{0,8},{4,12},{8,0},{12,4},{1,9},{5,13},{9,1},{13,5},{2,10},{6,14},... | collective-permute-start | bytes 405512 | tf_op jit(solution)/shard_map/ppermute | solution.py:244
  19.8 1.6 %stage.1 = (s32[8,32]{1,0:T(8,128)S(4)}, bf16[8,2,256,256]{3,2,1,0:T(8,128)(2,1)S(1)}, bf16[528,128]{1,0:T(8,128)(2,1)S(1)}) custom-call(s32[8,32]{1,0:T(8,128)} %bitcast.1, bf16[8,2,256,256]{3,2,1,0:T(8,128)(2,1)} %esp_ref.1, bf16[528,128]{1,0:T(8,128)(2,1)S(1)} %collective-permute-done.refs_2_.piece_ref, ...), custom_call_target="tpu_custom_call" | custom-call | tf_op jit(solution)/shard_map/stage/pallas_call | solution.py:287
  21.4 0.6 %collective-permute-start.11 = (bf16[528,128]{1,0:T(8,128)(2,1)S(1)}, bf16[528,128]{1,0:T(8,128)(2,1)S(1)}, u32[]{:S(2)}, u32[]{:S(2)}) collective-permute-start(bf16[528,128]{1,0:T(8,128)(2,1)S(1)} %get-tuple-element.14.refs_4_), channel_id=1, source_target_pairs={{0,4},{4,0},{8,12},{12,8},{1,5},{5,1},{9,13},{13,9},{2,6},{6,2},{1... | collective-permute-start | bytes 405512 | tf_op jit(solution)/shard_map/ppermute | solution.py:306
  22.5 0.7 %collective-permute-done.6.refs_7_ = bf16[528,128]{1,0:T(8,128)(2,1)S(1)} collective-permute-done((bf16[528,128]{1,0:T(8,128)(2,1)S(1)}, bf16[528,128]{1,0:T(8,128)(2,1)S(1)}, u32[]{:S(2)}, u32[]{:S(2)}) %collective-permute-start.6) | collective-permute-done | bytes 135200 | tf_op jit(solution)/shard_map/ppermute | solution.py:244
  23.6 1.0 %collective-permute-done.14.refs_15_ = bf16[528,128]{1,0:T(8,128)(2,1)S(1)} collective-permute-done((bf16[528,128]{1,0:T(8,128)(2,1)S(1)}, bf16[528,128]{1,0:T(8,128)(2,1)S(1)}, u32[]{:S(2)}, u32[]{:S(2)}) %collective-permute-start.14) | collective-permute-done | bytes 135200 | tf_op jit(solution)/shard_map/ppermute | solution.py:306
  24.6 1.1 %couple_relay.1 = (bf16[16,528,128]{2,1,0:T(8,128)(2,1)S(1)}, s32[264,128]{1,0:T(8,128)S(1)}) custom-call(s32[8,32]{1,0:T(8,128)S(4)} %get-tuple-element.12.nbr_ref, bf16[8,2,256,256]{3,2,1,0:T(8,128)(2,1)S(1)} %get-tuple-element.13.esp_ref, bf16[528,128]{1,0:T(8,128)(2,1)S(1)} %fold.1.refs_0_, bf16[528,128]{1,0:T(8,128)(2,1)S(1)} %collective-permute-done.2.refs_1_, ...), custom_call_target="tpu_custom_call" | custom-call | tf_op jit(solution)/shard_map/couple_relay/pallas_call | solution.py:316
  26.2 1.0 %couple_near.1 = s32[264,128]{1,0:T(8,128)S(1)} custom-call(s32[8,32]{1,0:T(8,128)S(4)} %get-tuple-element.12.nbr_ref, bf16[8,2,256,256]{3,2,1,0:T(8,128)(2,1)S(1)} %get-tuple-element.13.esp_ref, bf16[16,528,128]{2,1,0:T(8,128)(2,1)S(1)} %get-tuple-element.15.refs_0_), custom_call_target="tpu_custom_call" | custom-call | tf_op jit(solution)/shard_map/couple_near/pallas_call | solution.py:316
  27.2 1.7 %collective-permute-start.15 = (s32[264,128]{1,0:T(8,128)S(1)}, s32[264,128]{1,0:T(8,128)S(1)}, u32[]{:S(2)}, u32[]{:S(2)}) collective-permute-start(s32[264,128]{1,0:T(8,128)S(1)} %couple_near.1), channel_id=1, source_target_pairs={{0,1},{1,0},{2,3},{3,2},{4,5},{5,4},{6,7},{7,6},{8,9},{9,8},{10,11... | collective-permute-start | bytes 405512 | tf_op jit(solution)/shard_map/ppermute | solution.py:241
  28.8 1.5 %couple_far.1 = (f32[2,264,128]{2,1,0:T(8,128)S(1)}, f32[2,264,128]{2,1,0:T(8,128)S(1)}) custom-call(s32[8,32]{1,0:T(8,128)S(4)} %get-tuple-element.12.nbr_ref, bf16[8,2,256,256]{3,2,1,0:T(8,128)(2,1)S(1)} %get-tuple-element.13.esp_ref, bf16[16,528,128]{2,1,0:T(8,128)(2,1)S(1)} %get-tuple-element.15.refs_0_), custom_call_target="tpu_custom_call" | custom-call | tf_op jit(solution)/shard_map/couple_far/pallas_call | solution.py:316
  30.3 1.9 %collective-permute-done.16.refs_0_ = s32[264,128]{1,0:T(8,128)S(1)} collective-permute-done((s32[264,128]{1,0:T(8,128)S(1)}, s32[264,128]{1,0:T(8,128)S(1)}, u32[]{:S(2)}, u32[]{:S(2)}) %collective-permute-start.16) | collective-permute-done | bytes 135200 | tf_op jit(solution)/shard_map/ppermute | solution.py:241
  32.3 0.9 %collective-permute-start.17 = (s32[264,128]{1,0:T(8,128)S(1)}, s32[264,128]{1,0:T(8,128)S(1)}, u32[]{:S(2)}, u32[]{:S(2)}) collective-permute-start(s32[264,128]{1,0:T(8,128)S(1)} %merge.1), channel_id=1, source_target_pairs={{0,2},{1,3},{2,0},{3,1},{4,6},{5,7},{6,4},{7,5},{8,10},{9,11},{10,... | collective-permute-start | bytes 405512 | tf_op jit(solution)/shard_map/ppermute | solution.py:241
  33.2 1.1 %collective-permute-done.15.piece_ref = s32[264,128]{1,0:T(8,128)S(1)} collective-permute-done((s32[264,128]{1,0:T(8,128)S(1)}, s32[264,128]{1,0:T(8,128)S(1)}, u32[]{:S(2)}, u32[]{:S(2)}) %collective-permute-start.15) | collective-permute-done | bytes 135200 | tf_op jit(solution)/shard_map/ppermute | solution.py:241
  34.4 5.8 %collective-permute-done.17.refs_1_ = s32[264,128]{1,0:T(8,128)S(1)} collective-permute-done((s32[264,128]{1,0:T(8,128)S(1)}, s32[264,128]{1,0:T(8,128)S(1)}, u32[]{:S(2)}, u32[]{:S(2)}) %collective-permute-start.17) | collective-permute-done | bytes 135200 | tf_op jit(solution)/shard_map/ppermute | solution.py:241
  40.2 1.0 %finish.1 = f32[2,256,256]{2,1,0:T(8,128)} custom-call(bf16[2,256,256]{2,1,0:T(8,128)(2,1)S(1)} %copy-done.1, f32[2,264,128]{2,1,0:T(8,128)S(1)} %get-tuple-element.16.own_ref, s32[264,128]{1,0:T(8,128)S(1)} %gate.23.refs_0_, s32[264,128]{1,0:T(8,128)S(1)} %collective-permute-done.17.refs_1_), custom_call_target="tpu_custom_call" | custom-call | tf_op jit(solution)/shard_map/finish/pallas_call | solution.py:343
  (35 shorter events, 2.3 us)
Async XLA Ops:
  0.0 0.9 %copy-start = (bf16[2,256,256]{2,1,0:T(8,128)(2,1)S(1)}, bf16[2,256,256]{2,1,0:T(8,128)(2,1)}, u32[]{:S(2)}) copy-start(bf16[2,256,256]{2,1,0:T(8,128)(2,1)} %dens_ref.1) | copy-start | bytes 786436
  1.0 8.7 %collective-permute-start.2 = (bf16[528,128]{1,0:T(8,128)(2,1)S(1)}, bf16[528,128]{1,0:T(8,128)(2,1)S(1)}, u32[]{:S(2)}, u32[]{:S(2)}) collective-permute-start(bf16[528,128]{1,0:T(8,128)(2,1)S(1)} %fold.1.refs_0_), channel_id=1, source_target_pairs={{0,1},{1,0},{2,3},{3,2},{4,5},{5,4},{6,7},{7,6},{8,9},{9,8},{10,11... | collective-permute-start | bytes 405512 | tf_op jit(solution)/shard_map/ppermute | solution.py:241
  4.1 8.9 %collective-permute-start.1 = (bf16[528,128]{1,0:T(8,128)(2,1)S(1)}, bf16[528,128]{1,0:T(8,128)(2,1)S(1)}, u32[]{:S(2)}, u32[]{:S(2)}) collective-permute-start(bf16[528,128]{1,0:T(8,128)(2,1)S(1)} %fold.1.refs_0_), channel_id=1, source_target_pairs={{0,2},{1,3},{2,0},{3,1},{4,6},{5,7},{6,4},{7,5},{8,10},{9,11},{10,... | collective-permute-start | bytes 405512 | tf_op jit(solution)/shard_map/ppermute | solution.py:241
  6.7 6.3 %collective-permute-start = (bf16[528,128]{1,0:T(8,128)(2,1)S(1)}, bf16[528,128]{1,0:T(8,128)(2,1)S(1)}, u32[]{:S(2)}, u32[]{:S(2)}) collective-permute-start(bf16[528,128]{1,0:T(8,128)(2,1)S(1)} %fold.1.refs_0_), channel_id=1, source_target_pairs={{0,8},{4,12},{8,0},{12,4},{1,9},{5,13},{9,1},{13,5},{2,10},{6,14},... | collective-permute-start | bytes 405512 | tf_op jit(solution)/shard_map/ppermute | solution.py:244
  9.7 5.9 %collective-permute-start.4 = (bf16[528,128]{1,0:T(8,128)(2,1)S(1)}, bf16[528,128]{1,0:T(8,128)(2,1)S(1)}, u32[]{:S(2)}, u32[]{:S(2)}) collective-permute-start(bf16[528,128]{1,0:T(8,128)(2,1)S(1)} %collective-permute-done.2.refs_1_), channel_id=1, source_target_pairs={{0,8},{4,12},{8,0},{12,4},{1,9},{5,13},{9,1},{13,5},{2,10},{6,14},... | collective-permute-start | bytes 405512 | tf_op jit(solution)/shard_map/ppermute | solution.py:244
  13.0 5.1 %collective-permute-start.3 = (bf16[528,128]{1,0:T(8,128)(2,1)S(1)}, bf16[528,128]{1,0:T(8,128)(2,1)S(1)}, u32[]{:S(2)}, u32[]{:S(2)}) collective-permute-start(bf16[528,128]{1,0:T(8,128)(2,1)S(1)} %gate.13.refs_2_), channel_id=1, source_target_pairs={{0,1},{1,0},{2,3},{3,2},{4,5},{5,4},{6,7},{7,6},{8,9},{9,8},{10,11... | collective-permute-start | bytes 405512 | tf_op jit(solution)/shard_map/ppermute | solution.py:241
  13.5 6.2 %collective-permute-start.5 = (bf16[528,128]{1,0:T(8,128)(2,1)S(1)}, bf16[528,128]{1,0:T(8,128)(2,1)S(1)}, u32[]{:S(2)}, u32[]{:S(2)}) collective-permute-start(bf16[528,128]{1,0:T(8,128)(2,1)S(1)} %gate.13.refs_2_), channel_id=1, source_target_pairs={{0,8},{4,12},{8,0},{12,4},{1,9},{5,13},{9,1},{13,5},{2,10},{6,14},... | collective-permute-start | bytes 405512 | tf_op jit(solution)/shard_map/ppermute | solution.py:244
  15.1 6.4 %collective-permute-start.7 = (bf16[528,128]{1,0:T(8,128)(2,1)S(1)}, bf16[528,128]{1,0:T(8,128)(2,1)S(1)}, u32[]{:S(2)}, u32[]{:S(2)}) collective-permute-start(bf16[528,128]{1,0:T(8,128)(2,1)S(1)} %fold.1.refs_0_), channel_id=1, source_target_pairs={{0,4},{4,0},{8,12},{12,8},{1,5},{5,1},{9,13},{13,9},{2,6},{6,2},{1... | collective-permute-start | bytes 405512 | tf_op jit(solution)/shard_map/ppermute | solution.py:306
  15.1 7.0 %collective-permute-start.9 = (bf16[528,128]{1,0:T(8,128)(2,1)S(1)}, bf16[528,128]{1,0:T(8,128)(2,1)S(1)}, u32[]{:S(2)}, u32[]{:S(2)}) collective-permute-start(bf16[528,128]{1,0:T(8,128)(2,1)S(1)} %gate.13.refs_2_), channel_id=1, source_target_pairs={{0,4},{4,0},{8,12},{12,8},{1,5},{5,1},{9,13},{13,9},{2,6},{6,2},{1... | collective-permute-start | bytes 405512 | tf_op jit(solution)/shard_map/ppermute | solution.py:306
  15.6 6.4 %collective-permute-start.8 = (bf16[528,128]{1,0:T(8,128)(2,1)S(1)}, bf16[528,128]{1,0:T(8,128)(2,1)S(1)}, u32[]{:S(2)}, u32[]{:S(2)}) collective-permute-start(bf16[528,128]{1,0:T(8,128)(2,1)S(1)} %collective-permute-done.2.refs_1_), channel_id=1, source_target_pairs={{0,4},{4,0},{8,12},{12,8},{1,5},{5,1},{9,13},{13,9},{2,6},{6,2},{1... | collective-permute-start | bytes 405512 | tf_op jit(solution)/shard_map/ppermute | solution.py:306
  18.1 5.1 %collective-permute-start.6 = (bf16[528,128]{1,0:T(8,128)(2,1)S(1)}, bf16[528,128]{1,0:T(8,128)(2,1)S(1)}, u32[]{:S(2)}, u32[]{:S(2)}) collective-permute-start(bf16[528,128]{1,0:T(8,128)(2,1)S(1)} %gate.18), channel_id=1, source_target_pairs={{0,8},{4,12},{8,0},{12,4},{1,9},{5,13},{9,1},{13,5},{2,10},{6,14},... | collective-permute-start | bytes 405512 | tf_op jit(solution)/shard_map/ppermute | solution.py:244
  19.7 3.6 %collective-permute-start.13 = (bf16[528,128]{1,0:T(8,128)(2,1)S(1)}, bf16[528,128]{1,0:T(8,128)(2,1)S(1)}, u32[]{:S(2)}, u32[]{:S(2)}) collective-permute-start(bf16[528,128]{1,0:T(8,128)(2,1)S(1)} %gate.14.refs_6_), channel_id=1, source_target_pairs={{0,4},{4,0},{8,12},{12,8},{1,5},{5,1},{9,13},{13,9},{2,6},{6,2},{1... | collective-permute-start | bytes 405512 | tf_op jit(solution)/shard_map/ppermute | solution.py:306
  21.4 2.1 %collective-permute-start.11 = (bf16[528,128]{1,0:T(8,128)(2,1)S(1)}, bf16[528,128]{1,0:T(8,128)(2,1)S(1)}, u32[]{:S(2)}, u32[]{:S(2)}) collective-permute-start(bf16[528,128]{1,0:T(8,128)(2,1)S(1)} %get-tuple-element.14.refs_4_), channel_id=1, source_target_pairs={{0,4},{4,0},{8,12},{12,8},{1,5},{5,1},{9,13},{13,9},{2,6},{6,2},{1... | collective-permute-start | bytes 405512 | tf_op jit(solution)/shard_map/ppermute | solution.py:306
  22.0 1.4 %collective-permute-start.12 = (bf16[528,128]{1,0:T(8,128)(2,1)S(1)}, bf16[528,128]{1,0:T(8,128)(2,1)S(1)}, u32[]{:S(2)}, u32[]{:S(2)}) collective-permute-start(bf16[528,128]{1,0:T(8,128)(2,1)S(1)} %collective-permute-done.4.piece_ref.refs_5_), channel_id=1, source_target_pairs={{0,4},{4,0},{8,12},{12,8},{1,5},{5,1},{9,13},{13,9},{2,6},{6,2},{1... | collective-permute-start | bytes 405512 | tf_op jit(solution)/shard_map/ppermute | solution.py:306
  22.1 1.5 %collective-permute-start.10 = (bf16[528,128]{1,0:T(8,128)(2,1)S(1)}, bf16[528,128]{1,0:T(8,128)(2,1)S(1)}, u32[]{:S(2)}, u32[]{:S(2)}) collective-permute-start(bf16[528,128]{1,0:T(8,128)(2,1)S(1)} %collective-permute-done.3.refs_0_.piece_ref.refs_3_), channel_id=1, source_target_pairs={{0,4},{4,0},{8,12},{12,8},{1,5},{5,1},{9,13},{13,9},{2,6},{6,2},{1... | collective-permute-start | bytes 405512 | tf_op jit(solution)/shard_map/ppermute | solution.py:306
  23.2 1.4 %collective-permute-start.14 = (bf16[528,128]{1,0:T(8,128)(2,1)S(1)}, bf16[528,128]{1,0:T(8,128)(2,1)S(1)}, u32[]{:S(2)}, u32[]{:S(2)}) collective-permute-start(bf16[528,128]{1,0:T(8,128)(2,1)S(1)} %collective-permute-done.6.refs_7_), channel_id=1, source_target_pairs={{0,4},{4,0},{8,12},{12,8},{1,5},{5,1},{9,13},{13,9},{2,6},{6,2},{1... | collective-permute-start | bytes 405512 | tf_op jit(solution)/shard_map/ppermute | solution.py:306
  25.7 6.5 %collective-permute-start.16 = (s32[264,128]{1,0:T(8,128)S(1)}, s32[264,128]{1,0:T(8,128)S(1)}, u32[]{:S(2)}, u32[]{:S(2)}) collective-permute-start(s32[264,128]{1,0:T(8,128)S(1)} %get-tuple-element.18), channel_id=1, source_target_pairs={{0,1},{1,0},{2,3},{3,2},{4,5},{5,4},{6,7},{7,6},{8,9},{9,8},{10,11... | collective-permute-start | bytes 405512 | tf_op jit(solution)/shard_map/ppermute | solution.py:241
  27.2 13.0 %copy-start.1 = (bf16[2,256,256]{2,1,0:T(8,128)(2,1)S(1)}, bf16[2,256,256]{2,1,0:T(8,128)(2,1)}, u32[]{:S(2)}) copy-start(bf16[2,256,256]{2,1,0:T(8,128)(2,1)} %core_ref.1) | copy-start | bytes 786436
  27.2 7.1 %collective-permute-start.15 = (s32[264,128]{1,0:T(8,128)S(1)}, s32[264,128]{1,0:T(8,128)S(1)}, u32[]{:S(2)}, u32[]{:S(2)}) collective-permute-start(s32[264,128]{1,0:T(8,128)S(1)} %couple_near.1), channel_id=1, source_target_pairs={{0,1},{1,0},{2,3},{3,2},{4,5},{5,4},{6,7},{7,6},{8,9},{9,8},{10,11... | collective-permute-start | bytes 405512 | tf_op jit(solution)/shard_map/ppermute | solution.py:241
  32.3 7.8 %collective-permute-start.17 = (s32[264,128]{1,0:T(8,128)S(1)}, s32[264,128]{1,0:T(8,128)S(1)}, u32[]{:S(2)}, u32[]{:S(2)}) collective-permute-start(s32[264,128]{1,0:T(8,128)S(1)} %merge.1), channel_id=1, source_target_pairs={{0,2},{1,3},{2,0},{3,1},{4,6},{5,7},{6,4},{7,5},{8,10},{9,11},{10,... | collective-permute-start | bytes 405512 | tf_op jit(solution)/shard_map/ppermute | solution.py:241

commit v9 on v8

--- a/solution.py
+++ b/solution.py
@@ -97,8 +97,12 @@
     refs[-1][...] = piece_ref[...]
 
 
-def stage_kernel(nbr_ref, esp_ref, piece_ref, *refs):
-    nbr_out, esp_out, piece_out, sems = refs[-4:]
+def gather_kernel(*refs):
+    for i, piece in enumerate(refs[:-1]):
+        refs[-1][i] = piece[...]
+
+
+def stage_kernel(nbr_ref, esp_ref, piece_ref, nbr_out, esp_out, piece_out, sems):
     copies = [
         pltpu.make_async_copy(esp_ref, esp_out, sems.at[0]),
         pltpu.make_async_copy(nbr_ref, nbr_out, sems.at[1]),
@@ -110,12 +114,15 @@
         copy.wait()
 
 
-def couple_kernel(groups, lanes, mono_dev, units, nbr_ref, esp_ref, *refs):
+def couple_kernel(groups, lanes, mono_dev, units, places, nbr_ref, esp_ref, *refs):
     outs = refs[len(refs) - len(units) :]
     if len(refs) > len(units) + 1:
         pieces, store = refs[: -1 - len(units)], refs[-1 - len(units)]
-        for i, piece in enumerate(pieces):
-            store[i] = piece[...]
+        at = 0
+        for piece in pieces:
+            for part in [piece] if len(piece.shape) == 2 else [piece.at[i] for i in range(piece.shape[0])]:
+                store[places[at]] = part[...]
+                at += 1
     else:
         store = refs[0]
     my_group = lax.axis_index("gddi")
@@ -269,29 +276,29 @@
             name="gate",
         )(piece, *after)
 
+    def across(piece, y, k):
+        pairs = [(g * lanes + i, (g ^ 2 * y) * lanes + (i ^ k)) for g in range(groups) for i in range(lanes)]
+        return lax.ppermute(piece, ("gddi", "intra"), pairs)
+
     others = [piece for key, piece in near.items() if key != (0, top)]
     near[0, top] = gate(gate(near[0, top]), *others)
     for y in range(1, rows_y):
         for k in range(1, top):
             near[y, k] = along_y(near[0, k], y)
+            near[y, k] = gate(gate(near[y, k]))
     double(top)
-    ahead = [near[y, k] for y in range(1, rows_y) for k in range(1, top)]
-    for _ in range(3):
-        ahead = [gate(ahead[0], *ahead[1:])]
     for y in range(1, rows_y):
-        near[y, top] = along_y(near[0, top], y)
-        near[y, top] = gate(near[y, top])
-        for k in range(top + 1, lanes):
-            near[y, k] = along_y(gate(near[0, k], *ahead), y)
-
-    names, blocks, near[rows_y - 1, 0] = pl.pallas_call(
+        for k in range(top):
+            near[y, top ^ k] = across(near[0, top], y, k)
+
+    names, blocks, near[rows_y - 1, top - 1] = pl.pallas_call(
         stage_kernel,
         out_shape=[
             pltpu.SMEM((nbr.shape[1], nbr.shape[0]), nbr.dtype),
             pltpu.VMEM(esp_block.shape, esp_block.dtype),
             pltpu.VMEM(shard.shape, shard.dtype),
         ],
-        in_specs=[hbm, hbm, IN_VMEM, hbm],
+        in_specs=[hbm, hbm, IN_VMEM],
         out_specs=[IN_SMEM, IN_VMEM, IN_VMEM],
         scratch_shapes=[pltpu.SemaphoreType.DMA((2,))],
         compiler_params=small,
@@ -299,11 +306,28 @@
     )(
         pltpu.with_memory_space_constraint(nbr.T, pltpu.HBM),
         pltpu.with_memory_space_constraint(esp_block, pltpu.HBM),
-        near[rows_y - 1, 0],
-        near[0, lanes - 1],
+        near[rows_y - 1, top - 1],
     )
-    mine = [near[y, k] for y in range(rows_y) for k in range(lanes)]
-    pieces = mine + [lax.ppermute(piece, "gddi", xor_pairs(groups, 1)) for piece in mine]
+    def to_mate(piece):
+        return lax.ppermute(piece, "gddi", xor_pairs(groups, 1))
+
+    keys = [(y, k) for y in range(rows_y) for k in range(lanes)]
+    batch = [key for key in keys if key[0] == 0 and bin(key[1]).count("1") <= 1]
+    batched = pl.pallas_call(
+        gather_kernel,
+        out_shape=pltpu.VMEM((len(batch),) + shard.shape, shard.dtype),
+        in_specs=[IN_VMEM] * len(batch),
+        out_specs=IN_VMEM,
+        compiler_params=small,
+        name="gather",
+    )(*[near[key] for key in batch])
+    single = [key for key in keys if key not in batch]
+    pieces = [near[key] for key in keys] + [to_mate(batched)] + [to_mate(near[key]) for key in single]
+    for i, (y, k) in enumerate(single):
+        if 0 < k < top:
+            pieces[len(keys) + 1 + i] = gate(pieces[len(keys) + 1 + i])
+    places = [y * lanes + k for y, k in keys]
+    places += [rows_y * lanes + y * lanes + k for y, k in batch + single]
 
     plain = pltpu.VMEM((mono_dev, basis + 8, half), jnp.float32)
     coded = pltpu.VMEM((mono_dev * half + round_up(2 * mono_dev, 8), half), jnp.int32)
@@ -314,7 +338,7 @@
 
     def couple(units, name, pieces, fill=False):
         return pl.pallas_call(
-            functools.partial(couple_kernel, groups, lanes, mono_dev, units),
+            functools.partial(couple_kernel, groups, lanes, mono_dev, units, places),
             out_shape=[store] * fill + [coded if is_coded else plain for _, is_coded in units],
             in_specs=[IN_SMEM] + [IN_VMEM] * (1 + len(pieces)),
             out_specs=[IN_VMEM] * (fill + len(units)),
@@ -331,15 +355,15 @@
     close = [along_z(unit, k) for k, unit in zip(steps, close)]
     for _ in range(5):
         close = [gate(unit) for unit in close]
-    across, own = couple([(top, False), (0, False)], "couple_far", [filled])
-    across = pl.pallas_call(
+    beyond, own = couple([(top, False), (0, False)], "couple_far", [filled])
+    beyond = pl.pallas_call(
         merge_kernel,
         out_shape=coded,
         in_specs=[IN_VMEM] * (1 + len(relayed)),
         out_specs=IN_VMEM,
         compiler_params=small,
         name="merge",
-    )(across, *relayed)
+    )(beyond, *relayed)
     return pl.pallas_call(
         finish_kernel,
         out_shape=jax.ShapeDtypeStruct((mono_dev, basis, basis), jnp.float32),
@@ -347,7 +371,7 @@
         out_specs=IN_VMEM,
         compiler_params=small,
         name="finish",
-    )(h_core, own, *close, along_z(across, top))
+    )(h_core, own, *close, along_z(beyond, top))
 
 
 def solution(mesh):

time: 41.3 us -> 41.7 us (level)
  waiting for transfers between devices: 16.2 us -> 17.4 us
  starting transfers between devices: 17.3 us -> 16.5 us
    ppermute x8, waiting for transfers between devices: 1.36 us -> 5.73 us  [the longest x2 4.49 us: across(): return lax.ppermute(piece, ('gddi', 'intra'), pairs)]
    ppermute x4 -> x2, starting transfers between devices: 6.47 us -> 3.37 us  [along_y(): return lax.ppermute(piece, 'gddi', xor_pairs(groups, 2 * y))]
    ppermute x6, waiting for transfers between devices: 14.1 us -> 11.7 us  [along_z(): return lax.ppermute(piece, 'intra', xor_pairs(lanes, bit))]
    ppermute x6, starting transfers between devices: 9.22 us -> 10.5 us  [along_z(): return lax.ppermute(piece, 'intra', xor_pairs(lanes, bit))]
    ppermute x8, starting transfers between devices: 1.66 us -> 2.67 us  [the longest x2 1.98 us: across(): return lax.ppermute(piece, ('gddi', 'intra'), pairs)]
    ppermute x4 -> x2, waiting for transfers between devices: 0.69 us -> 0.01 us  [along_y(): return lax.ppermute(piece, 'gddi', xor_pairs(groups, 2 * y))]
  transfers between devices with their start and end apart: 18 -> 16, of which waited for: 10 -> 11; matrix products, arithmetic and copies ran while one was open for 0% -> 0% of each run, Pallas kernels for 11% -> 10%
where the time goes in v9:
time: 41.7 us; the launch traced here: 41.6 us
  waiting for transfers between devices  17.4 us (42%)
  starting transfers between devices  16.5 us (40%)
  Pallas kernels  6.52 us (16%)
  local copies, waits for them, and re-layouts  0.96 us (2%)
    ppermute x6, waiting for transfers between devices, along_z(): return lax.ppermute(piece, 'intra', xor_pairs(lanes, bit))  11.7 us
    ppermute x6, starting transfers between devices, along_z(): return lax.ppermute(piece, 'intra', xor_pairs(lanes, bit))  10.5 us
    ppermute x2, waiting for transfers between devices, across(): return lax.ppermute(piece, ('gddi', 'intra'), pairs)  4.49 us
    pallas_call x3, Pallas kernels, couple(): pl.pallas_call(functools.partial(couple_kernel, groups, lanes, mono_dev,...  3.57 us
    ppermute x2, starting transfers between devices, along_y(): return lax.ppermute(piece, 'gddi', xor_pairs(groups, 2 * y))  3.37 us
    ppermute x2, starting transfers between devices, across(): return lax.ppermute(piece, ('gddi', 'intra'), pairs)  1.98 us
    pallas_call x1, Pallas kernels, local(): pl.pallas_call(stage_kernel, out_shape=[pltpu.SMEM((nbr.shape[1], nbr.sha...  1.62 us
    ppermute x6, waiting for transfers between devices, to_mate(): return lax.ppermute(piece, 'gddi', xor_pairs(groups, 1))  1.24 us
  transfers between devices with their start and end apart: 16, of which 11 were waited for; matrix products, arithmetic and copies ran while one was open for 0% of the time, Pallas kernels for 10%

profile of v9, /device:TPU:0, one launch (start us, length us, event | category | flops | bytes accessed | tf_op | source)
XLA Modules:
  0.0 41.6 jit_solution(11814249584447348523)
XLA Ops:
  0.0 0.9 %copy-done = bf16[2,256,256]{2,1,0:T(8,128)(2,1)S(1)} copy-done((bf16[2,256,256]{2,1,0:T(8,128)(2,1)S(1)}, bf16[2,256,256]{2,1,0:T(8,128)(2,1)}, u32[]{:S(2)}) %copy-start) | copy-done | bytes 262168
  1.0 3.1 %collective-permute-start = (bf16[528,128]{1,0:T(8,128)(2,1)S(1)}, bf16[528,128]{1,0:T(8,128)(2,1)S(1)}, u32[]{:S(2)}, u32[]{:S(2)}) collective-permute-start(bf16[528,128]{1,0:T(8,128)(2,1)S(1)} %fold.1.refs_0_), channel_id=1, source_target_pairs={{0,1},{1,0},{2,3},{3,2},{4,5},{5,4},{6,7},{7,6},{8,9},{9,8},{10,11... | collective-permute-start | bytes 405512 | tf_op jit(solution)/shard_map/ppermute | solution.py:248
  4.1 2.6 %collective-permute-start.2 = (bf16[528,128]{1,0:T(8,128)(2,1)S(1)}, bf16[528,128]{1,0:T(8,128)(2,1)S(1)}, u32[]{:S(2)}, u32[]{:S(2)}) collective-permute-start(bf16[528,128]{1,0:T(8,128)(2,1)S(1)} %fold.1.refs_0_), channel_id=1, source_target_pairs={{0,2},{1,3},{2,0},{3,1},{4,6},{5,7},{6,4},{7,5},{8,10},{9,11},{10,... | collective-permute-start | bytes 405512 | tf_op jit(solution)/shard_map/ppermute | solution.py:248
  6.7 1.5 %collective-permute-start.3 = (bf16[528,128]{1,0:T(8,128)(2,1)S(1)}, bf16[528,128]{1,0:T(8,128)(2,1)S(1)}, u32[]{:S(2)}, u32[]{:S(2)}) collective-permute-start(bf16[528,128]{1,0:T(8,128)(2,1)S(1)} %fold.1.refs_0_), channel_id=1, source_target_pairs={{0,8},{4,12},{8,0},{12,4},{1,9},{5,13},{9,1},{13,5},{2,10},{6,14},... | collective-permute-start | bytes 405512 | tf_op jit(solution)/shard_map/ppermute | solution.py:251
  8.2 1.5 %collective-permute-done.refs_1_ = bf16[528,128]{1,0:T(8,128)(2,1)S(1)} collective-permute-done((bf16[528,128]{1,0:T(8,128)(2,1)S(1)}, bf16[528,128]{1,0:T(8,128)(2,1)S(1)}, u32[]{:S(2)}, u32[]{:S(2)}) %collective-permute-start) | collective-permute-done | bytes 135200 | tf_op jit(solution)/shard_map/ppermute | solution.py:248
  9.7 1.8 %collective-permute-start.1 = (bf16[528,128]{1,0:T(8,128)(2,1)S(1)}, bf16[528,128]{1,0:T(8,128)(2,1)S(1)}, u32[]{:S(2)}, u32[]{:S(2)}) collective-permute-start(bf16[528,128]{1,0:T(8,128)(2,1)S(1)} %collective-permute-done.refs_1_), channel_id=1, source_target_pairs={{0,8},{4,12},{8,0},{12,4},{1,9},{5,13},{9,1},{13,5},{2,10},{6,14},... | collective-permute-start | bytes 405512 | tf_op jit(solution)/shard_map/ppermute | solution.py:251
  11.5 1.4 %collective-permute-done.2.piece_ref = bf16[528,128]{1,0:T(8,128)(2,1)S(1)} collective-permute-done((bf16[528,128]{1,0:T(8,128)(2,1)S(1)}, bf16[528,128]{1,0:T(8,128)(2,1)S(1)}, u32[]{:S(2)}, u32[]{:S(2)}) %collective-permute-start.2) | collective-permute-done | bytes 135200 | tf_op jit(solution)/shard_map/ppermute | solution.py:248
  13.1 1.5 %collective-permute-start.6 = (bf16[528,128]{1,0:T(8,128)(2,1)S(1)}, bf16[528,128]{1,0:T(8,128)(2,1)S(1)}, u32[]{:S(2)}, u32[]{:S(2)}) collective-permute-start(bf16[528,128]{1,0:T(8,128)(2,1)S(1)} %gate.13.refs_2_), channel_id=1, source_target_pairs={{0,9},{1,8},{2,11},{3,10},{4,13},{5,12},{6,15},{7,14},{8,1},{9,0},... | collective-permute-start | bytes 405512 | tf_op jit(solution)/shard_map/ppermute | solution.py:281
  14.6 0.5 %collective-permute-start.5 = (bf16[528,128]{1,0:T(8,128)(2,1)S(1)}, bf16[528,128]{1,0:T(8,128)(2,1)S(1)}, u32[]{:S(2)}, u32[]{:S(2)}) collective-permute-start(bf16[528,128]{1,0:T(8,128)(2,1)S(1)} %gate.13.refs_2_), channel_id=1, source_target_pairs={{0,8},{1,9},{2,10},{3,11},{4,12},{5,13},{6,14},{7,15},{8,0},{9,1},... | collective-permute-start | bytes 405512 | tf_op jit(solution)/shard_map/ppermute | solution.py:281
  15.1 1.6 %collective-permute-start.4 = (bf16[528,128]{1,0:T(8,128)(2,1)S(1)}, bf16[528,128]{1,0:T(8,128)(2,1)S(1)}, u32[]{:S(2)}, u32[]{:S(2)}) collective-permute-start(bf16[528,128]{1,0:T(8,128)(2,1)S(1)} %gate.13.refs_2_), channel_id=1, source_target_pairs={{0,1},{1,0},{2,3},{3,2},{4,5},{5,4},{6,7},{7,6},{8,9},{9,8},{10,11... | collective-permute-start | bytes 405512 | tf_op jit(solution)/shard_map/ppermute | solution.py:248
  16.7 1.6 %stage.1 = (s32[8,32]{1,0:T(8,128)S(4)}, bf16[8,2,256,256]{3,2,1,0:T(8,128)(2,1)S(1)}, bf16[528,128]{1,0:T(8,128)(2,1)S(1)}) custom-call(s32[8,32]{1,0:T(8,128)} %bitcast.1, bf16[8,2,256,256]{3,2,1,0:T(8,128)(2,1)} %esp_ref.1, bf16[528,128]{1,0:T(8,128)(2,1)S(1)} %gate.11.piece_ref), custom_call_target="tpu_custom_call" | custom-call | tf_op jit(solution)/shard_map/stage/pallas_call | solution.py:294
  18.4 2.1 %collective-permute-done.6.refs_7_ = bf16[528,128]{1,0:T(8,128)(2,1)S(1)} collective-permute-done((bf16[528,128]{1,0:T(8,128)(2,1)S(1)}, bf16[528,128]{1,0:T(8,128)(2,1)S(1)}, u32[]{:S(2)}, u32[]{:S(2)}) %collective-permute-start.6) | collective-permute-done | bytes 135200 | tf_op jit(solution)/shard_map/ppermute | solution.py:281
  20.5 2.4 %collective-permute-done.5.refs_6_ = bf16[528,128]{1,0:T(8,128)(2,1)S(1)} collective-permute-done((bf16[528,128]{1,0:T(8,128)(2,1)S(1)}, bf16[528,128]{1,0:T(8,128)(2,1)S(1)}, u32[]{:S(2)}, u32[]{:S(2)}) %collective-permute-start.5) | collective-permute-done | bytes 135200 | tf_op jit(solution)/shard_map/ppermute | solution.py:281
  23.6 0.7 %collective-permute-done.12.refs_13_ = bf16[528,128]{1,0:T(8,128)(2,1)S(1)} collective-permute-done((bf16[528,128]{1,0:T(8,128)(2,1)S(1)}, bf16[528,128]{1,0:T(8,128)(2,1)S(1)}, u32[]{:S(2)}, u32[]{:S(2)}) %collective-permute-start.12) | collective-permute-done | bytes 135200 | tf_op jit(solution)/shard_map/ppermute | solution.py:312
  24.8 1.1 %couple_relay.1 = (bf16[16,528,128]{2,1,0:T(8,128)(2,1)S(1)}, s32[264,128]{1,0:T(8,128)S(1)}) custom-call(s32[8,32]{1,0:T(8,128)S(4)} %get-tuple-element.12.nbr_ref, bf16[8,2,256,256]{3,2,1,0:T(8,128)(2,1)S(1)} %get-tuple-element.13.esp_ref, bf16[528,128]{1,0:T(8,128)(2,1)S(1)} %fold.1.refs_0_, bf16[528,128]{1,0:T(8,128)(2,1)S(1)} %collective-permute-done.refs_1_, ...), custom_call_target="tpu_custom_call" | custom-call | tf_op jit(solution)/shard_map/couple_relay/pallas_call | solution.py:340
  25.9 0.5 %collective-permute-start.14 = (s32[264,128]{1,0:T(8,128)S(1)}, s32[264,128]{1,0:T(8,128)S(1)}, u32[]{:S(2)}, u32[]{:S(2)}) collective-permute-start(s32[264,128]{1,0:T(8,128)S(1)} %get-tuple-element.18), channel_id=1, source_target_pairs={{0,1},{1,0},{2,3},{3,2},{4,5},{5,4},{6,7},{7,6},{8,9},{9,8},{10,11... | collective-permute-start | bytes 405512 | tf_op jit(solution)/shard_map/ppermute | solution.py:248
  26.5 1.0 %couple_near.1 = s32[264,128]{1,0:T(8,128)S(1)} custom-call(s32[8,32]{1,0:T(8,128)S(4)} %get-tuple-element.12.nbr_ref, bf16[8,2,256,256]{3,2,1,0:T(8,128)(2,1)S(1)} %get-tuple-element.13.esp_ref, bf16[16,528,128]{2,1,0:T(8,128)(2,1)S(1)} %get-tuple-element.15.refs_0_), custom_call_target="tpu_custom_call" | custom-call | tf_op jit(solution)/shard_map/couple_near/pallas_call | solution.py:340
  27.5 1.6 %collective-permute-start.13 = (s32[264,128]{1,0:T(8,128)S(1)}, s32[264,128]{1,0:T(8,128)S(1)}, u32[]{:S(2)}, u32[]{:S(2)}) collective-permute-start(s32[264,128]{1,0:T(8,128)S(1)} %couple_near.1), channel_id=1, source_target_pairs={{0,1},{1,0},{2,3},{3,2},{4,5},{5,4},{6,7},{7,6},{8,9},{9,8},{10,11... | collective-permute-start | bytes 405512 | tf_op jit(solution)/shard_map/ppermute | solution.py:248
  29.1 1.5 %couple_far.1 = (f32[2,264,128]{2,1,0:T(8,128)S(1)}, f32[2,264,128]{2,1,0:T(8,128)S(1)}) custom-call(s32[8,32]{1,0:T(8,128)S(4)} %get-tuple-element.12.nbr_ref, bf16[8,2,256,256]{3,2,1,0:T(8,128)(2,1)S(1)} %get-tuple-element.13.esp_ref, bf16[16,528,128]{2,1,0:T(8,128)(2,1)S(1)} %get-tuple-element.15.refs_0_), custom_call_target="tpu_custom_call" | custom-call | tf_op jit(solution)/shard_map/couple_far/pallas_call | solution.py:340
  30.6 1.9 %collective-permute-done.14.refs_0_ = s32[264,128]{1,0:T(8,128)S(1)} collective-permute-done((s32[264,128]{1,0:T(8,128)S(1)}, s32[264,128]{1,0:T(8,128)S(1)}, u32[]{:S(2)}, u32[]{:S(2)}) %collective-permute-start.14) | collective-permute-done | bytes 135200 | tf_op jit(solution)/shard_map/ppermute | solution.py:248
  32.6 1.1 %collective-permute-start.15 = (s32[264,128]{1,0:T(8,128)S(1)}, s32[264,128]{1,0:T(8,128)S(1)}, u32[]{:S(2)}, u32[]{:S(2)}) collective-permute-start(s32[264,128]{1,0:T(8,128)S(1)} %merge.1), channel_id=1, source_target_pairs={{0,2},{1,3},{2,0},{3,1},{4,6},{5,7},{6,4},{7,5},{8,10},{9,11},{10,... | collective-permute-start | bytes 405512 | tf_op jit(solution)/shard_map/ppermute | solution.py:248
  33.7 0.9 %collective-permute-done.13.piece_ref = s32[264,128]{1,0:T(8,128)S(1)} collective-permute-done((s32[264,128]{1,0:T(8,128)S(1)}, s32[264,128]{1,0:T(8,128)S(1)}, u32[]{:S(2)}, u32[]{:S(2)}) %collective-permute-start.13) | collective-permute-done | bytes 135200 | tf_op jit(solution)/shard_map/ppermute | solution.py:248
  34.7 5.9 %collective-permute-done.15.refs_1_ = s32[264,128]{1,0:T(8,128)S(1)} collective-permute-done((s32[264,128]{1,0:T(8,128)S(1)}, s32[264,128]{1,0:T(8,128)S(1)}, u32[]{:S(2)}, u32[]{:S(2)}) %collective-permute-start.15) | collective-permute-done | bytes 135200 | tf_op jit(solution)/shard_map/ppermute | solution.py:248
  40.6 1.0 %finish.1 = f32[2,256,256]{2,1,0:T(8,128)} custom-call(bf16[2,256,256]{2,1,0:T(8,128)(2,1)S(1)} %copy-done.1, f32[2,264,128]{2,1,0:T(8,128)S(1)} %get-tuple-element.16.own_ref, s32[264,128]{1,0:T(8,128)S(1)} %gate.19.refs_0_, s32[264,128]{1,0:T(8,128)S(1)} %collective-permute-done.15.refs_1_), custom_call_target="tpu_custom_call" | custom-call | tf_op jit(solution)/shard_map/finish/pallas_call | solution.py:367
  (30 shorter events, 1.6 us)
Async XLA Ops:
  0.0 0.9 %copy-start = (bf16[2,256,256]{2,1,0:T(8,128)(2,1)S(1)}, bf16[2,256,256]{2,1,0:T(8,128)(2,1)}, u32[]{:S(2)}) copy-start(bf16[2,256,256]{2,1,0:T(8,128)(2,1)} %dens_ref.1) | copy-start | bytes 786436
  1.0 8.7 %collective-permute-start = (bf16[528,128]{1,0:T(8,128)(2,1)S(1)}, bf16[528,128]{1,0:T(8,128)(2,1)S(1)}, u32[]{:S(2)}, u32[]{:S(2)}) collective-permute-start(bf16[528,128]{1,0:T(8,128)(2,1)S(1)} %fold.1.refs_0_), channel_id=1, source_target_pairs={{0,1},{1,0},{2,3},{3,2},{4,5},{5,4},{6,7},{7,6},{8,9},{9,8},{10,11... | collective-permute-start | bytes 405512 | tf_op jit(solution)/shard_map/ppermute | solution.py:248
  4.1 8.9 %collective-permute-start.2 = (bf16[528,128]{1,0:T(8,128)(2,1)S(1)}, bf16[528,128]{1,0:T(8,128)(2,1)S(1)}, u32[]{:S(2)}, u32[]{:S(2)}) collective-permute-start(bf16[528,128]{1,0:T(8,128)(2,1)S(1)} %fold.1.refs_0_), channel_id=1, source_target_pairs={{0,2},{1,3},{2,0},{3,1},{4,6},{5,7},{6,4},{7,5},{8,10},{9,11},{10,... | collective-permute-start | bytes 405512 | tf_op jit(solution)/shard_map/ppermute | solution.py:248
  6.7 6.3 %collective-permute-start.3 = (bf16[528,128]{1,0:T(8,128)(2,1)S(1)}, bf16[528,128]{1,0:T(8,128)(2,1)S(1)}, u32[]{:S(2)}, u32[]{:S(2)}) collective-permute-start(bf16[528,128]{1,0:T(8,128)(2,1)S(1)} %fold.1.refs_0_), channel_id=1, source_target_pairs={{0,8},{4,12},{8,0},{12,4},{1,9},{5,13},{9,1},{13,5},{2,10},{6,14},... | collective-permute-start | bytes 405512 | tf_op jit(solution)/shard_map/ppermute | solution.py:251
  9.7 7.0 %collective-permute-start.1 = (bf16[528,128]{1,0:T(8,128)(2,1)S(1)}, bf16[528,128]{1,0:T(8,128)(2,1)S(1)}, u32[]{:S(2)}, u32[]{:S(2)}) collective-permute-start(bf16[528,128]{1,0:T(8,128)(2,1)S(1)} %collective-permute-done.refs_1_), channel_id=1, source_target_pairs={{0,8},{4,12},{8,0},{12,4},{1,9},{5,13},{9,1},{13,5},{2,10},{6,14},... | collective-permute-start | bytes 405512 | tf_op jit(solution)/shard_map/ppermute | solution.py:251
  13.1 11.8 %collective-permute-start.7 = (bf16[3,528,128]{2,1,0:T(8,128)(2,1)S(1)}, bf16[3,528,128]{2,1,0:T(8,128)(2,1)S(1)}, u32[]{:S(2)}, u32[]{:S(2)}) collective-permute-start(bf16[3,528,128]{2,1,0:T(8,128)(2,1)S(1)} %gather.1), channel_id=1, source_target_pairs={{0,4},{4,0},{8,12},{12,8},{1,5},{5,1},{9,13},{13,9},{2,6},{6,2},{1... | collective-permute-start | bytes 1216520 | tf_op jit(solution)/shard_map/ppermute | solution.py:312
  13.1 7.4 %collective-permute-start.6 = (bf16[528,128]{1,0:T(8,128)(2,1)S(1)}, bf16[528,128]{1,0:T(8,128)(2,1)S(1)}, u32[]{:S(2)}, u32[]{:S(2)}) collective-permute-start(bf16[528,128]{1,0:T(8,128)(2,1)S(1)} %gate.13.refs_2_), channel_id=1, source_target_pairs={{0,9},{1,8},{2,11},{3,10},{4,13},{5,12},{6,15},{7,14},{8,1},{9,0},... | collective-permute-start | bytes 405512 | tf_op jit(solution)/shard_map/ppermute | solution.py:281
  14.6 8.3 %collective-permute-start.5 = (bf16[528,128]{1,0:T(8,128)(2,1)S(1)}, bf16[528,128]{1,0:T(8,128)(2,1)S(1)}, u32[]{:S(2)}, u32[]{:S(2)}) collective-permute-start(bf16[528,128]{1,0:T(8,128)(2,1)S(1)} %gate.13.refs_2_), channel_id=1, source_target_pairs={{0,8},{1,9},{2,10},{3,11},{4,12},{5,13},{6,14},{7,15},{8,0},{9,1},... | collective-permute-start | bytes 405512 | tf_op jit(solution)/shard_map/ppermute | solution.py:281
  15.1 7.9 %collective-permute-start.4 = (bf16[528,128]{1,0:T(8,128)(2,1)S(1)}, bf16[528,128]{1,0:T(8,128)(2,1)S(1)}, u32[]{:S(2)}, u32[]{:S(2)}) collective-permute-start(bf16[528,128]{1,0:T(8,128)(2,1)S(1)} %gate.13.refs_2_), channel_id=1, source_target_pairs={{0,1},{1,0},{2,3},{3,2},{4,5},{5,4},{6,7},{7,6},{8,9},{9,8},{10,11... | collective-permute-start | bytes 405512 | tf_op jit(solution)/shard_map/ppermute | solution.py:248
  18.4 5.1 %collective-permute-start.10 = (bf16[528,128]{1,0:T(8,128)(2,1)S(1)}, bf16[528,128]{1,0:T(8,128)(2,1)S(1)}, u32[]{:S(2)}, u32[]{:S(2)}) collective-permute-start(bf16[528,128]{1,0:T(8,128)(2,1)S(1)} %get-tuple-element.14.refs_5_), channel_id=1, source_target_pairs={{0,4},{4,0},{8,12},{12,8},{1,5},{5,1},{9,13},{13,9},{2,6},{6,2},{1... | collective-permute-start | bytes 405512 | tf_op jit(solution)/shard_map/ppermute | solution.py:312
  20.5 3.0 %collective-permute-start.9 = (bf16[528,128]{1,0:T(8,128)(2,1)S(1)}, bf16[528,128]{1,0:T(8,128)(2,1)S(1)}, u32[]{:S(2)}, u32[]{:S(2)}) collective-permute-start(bf16[528,128]{1,0:T(8,128)(2,1)S(1)} %collective-permute-done.3.refs_2_.refs_4_), channel_id=1, source_target_pairs={{0,4},{4,0},{8,12},{12,8},{1,5},{5,1},{9,13},{13,9},{2,6},{6,2},{1... | collective-permute-start | bytes 405512 | tf_op jit(solution)/shard_map/ppermute | solution.py:312
  22.9 1.4 %collective-permute-start.12 = (bf16[528,128]{1,0:T(8,128)(2,1)S(1)}, bf16[528,128]{1,0:T(8,128)(2,1)S(1)}, u32[]{:S(2)}, u32[]{:S(2)}) collective-permute-start(bf16[528,128]{1,0:T(8,128)(2,1)S(1)} %collective-permute-done.6.refs_7_), channel_id=1, source_target_pairs={{0,4},{4,0},{8,12},{12,8},{1,5},{5,1},{9,13},{13,9},{2,6},{6,2},{1... | collective-permute-start | bytes 405512 | tf_op jit(solution)/shard_map/ppermute | solution.py:312
  23.0 1.4 %collective-permute-start.11 = (bf16[528,128]{1,0:T(8,128)(2,1)S(1)}, bf16[528,128]{1,0:T(8,128)(2,1)S(1)}, u32[]{:S(2)}, u32[]{:S(2)}) collective-permute-start(bf16[528,128]{1,0:T(8,128)(2,1)S(1)} %collective-permute-done.5.refs_6_), channel_id=1, source_target_pairs={{0,4},{4,0},{8,12},{12,8},{1,5},{5,1},{9,13},{13,9},{2,6},{6,2},{1... | collective-permute-start | bytes 405512 | tf_op jit(solution)/shard_map/ppermute | solution.py:312
  23.5 1.4 %collective-permute-start.8 = (bf16[528,128]{1,0:T(8,128)(2,1)S(1)}, bf16[528,128]{1,0:T(8,128)(2,1)S(1)}, u32[]{:S(2)}, u32[]{:S(2)}) collective-permute-start(bf16[528,128]{1,0:T(8,128)(2,1)S(1)} %collective-permute-done.4.refs_3_), channel_id=1, source_target_pairs={{0,4},{4,0},{8,12},{12,8},{1,5},{5,1},{9,13},{13,9},{2,6},{6,2},{1... | collective-permute-start | bytes 405512 | tf_op jit(solution)/shard_map/ppermute | solution.py:312
  25.9 6.5 %collective-permute-start.14 = (s32[264,128]{1,0:T(8,128)S(1)}, s32[264,128]{1,0:T(8,128)S(1)}, u32[]{:S(2)}, u32[]{:S(2)}) collective-permute-start(s32[264,128]{1,0:T(8,128)S(1)} %get-tuple-element.18), channel_id=1, source_target_pairs={{0,1},{1,0},{2,3},{3,2},{4,5},{5,4},{6,7},{7,6},{8,9},{9,8},{10,11... | collective-permute-start | bytes 405512 | tf_op jit(solution)/shard_map/ppermute | solution.py:248
  27.5 13.1 %copy-start.1 = (bf16[2,256,256]{2,1,0:T(8,128)(2,1)S(1)}, bf16[2,256,256]{2,1,0:T(8,128)(2,1)}, u32[]{:S(2)}) copy-start(bf16[2,256,256]{2,1,0:T(8,128)(2,1)} %core_ref.1) | copy-start | bytes 786436
  27.5 7.1 %collective-permute-start.13 = (s32[264,128]{1,0:T(8,128)S(1)}, s32[264,128]{1,0:T(8,128)S(1)}, u32[]{:S(2)}, u32[]{:S(2)}) collective-permute-start(s32[264,128]{1,0:T(8,128)S(1)} %couple_near.1), channel_id=1, source_target_pairs={{0,1},{1,0},{2,3},{3,2},{4,5},{5,4},{6,7},{7,6},{8,9},{9,8},{10,11... | collective-permute-start | bytes 405512 | tf_op jit(solution)/shard_map/ppermute | solution.py:248
  32.6 8.0 %collective-permute-start.15 = (s32[264,128]{1,0:T(8,128)S(1)}, s32[264,128]{1,0:T(8,128)S(1)}, u32[]{:S(2)}, u32[]{:S(2)}) collective-permute-start(s32[264,128]{1,0:T(8,128)S(1)} %merge.1), channel_id=1, source_target_pairs={{0,2},{1,3},{2,0},{3,1},{4,6},{5,7},{6,4},{7,5},{8,10},{9,11},{10,... | collective-permute-start | bytes 405512 | tf_op jit(solution)/shard_map/ppermute | solution.py:248

commit v10 on v8

--- a/solution.py
+++ b/solution.py
@@ -142,15 +142,17 @@
         return jnp.concatenate([top, bottom], axis=0)
 
     def partial_of(fragment):
-        total = None
+        high, low, blocks = [], [], []
         for s in range(slot_dev):
             name = nbr_ref[my_lane * slot_dev + s, my_group * mono_grp + fragment]
             block = esp_ref[fragment, s]
             half_term = jnp.dot(block, near_density(name), preferred_element_type=jnp.float32)
-            high = half_term.astype(jnp.bfloat16)
-            low = (half_term - high.astype(jnp.float32)).astype(jnp.bfloat16)
-            term = transposed_dot(high, block) + transposed_dot(low, block)
-            total = term if total is None else total + term
+            high.append(half_term.astype(jnp.bfloat16))
+            low.append((half_term - high[-1].astype(jnp.float32)).astype(jnp.bfloat16))
+            blocks.append(block)
+        both = jnp.concatenate([jnp.concatenate(high, axis=1), jnp.concatenate(low, axis=1)], axis=0)
+        both = transposed_dot(both, jnp.concatenate(blocks, axis=1))
+        total = both[:basis] + both[basis:]
         mixed, diag = fold(total[:half, :half], total[half:, half:])
         return total[:half, half:], mixed, diag
 
@@ -271,18 +273,12 @@
 
     others = [piece for key, piece in near.items() if key != (0, top)]
     near[0, top] = gate(gate(near[0, top]), *others)
+    double(top)
     for y in range(1, rows_y):
         for k in range(1, top):
+            near[y, k] = along_z(near[y, k & (k - 1)], k & -k)
+        for k in range(top, lanes):
             near[y, k] = along_y(near[0, k], y)
-    double(top)
-    ahead = [near[y, k] for y in range(1, rows_y) for k in range(1, top)]
-    for _ in range(3):
-        ahead = [gate(ahead[0], *ahead[1:])]
-    for y in range(1, rows_y):
-        near[y, top] = along_y(near[0, top], y)
-        near[y, top] = gate(near[y, top])
-        for k in range(top + 1, lanes):
-            near[y, k] = along_y(gate(near[0, k], *ahead), y)
 
     names, blocks, near[rows_y - 1, 0] = pl.pallas_call(
         stage_kernel,
@@ -302,7 +298,8 @@
         near[rows_y - 1, 0],
         near[0, lanes - 1],
     )
-    mine = [near[y, k] for y in range(rows_y) for k in range(lanes)]
+    keys = [(y, k) for y in range(rows_y) for k in range(lanes)]
+    mine = [near[key] for key in keys]
     pieces = mine + [lax.ppermute(piece, "gddi", xor_pairs(groups, 1)) for piece in mine]
 
     plain = pltpu.VMEM((mono_dev, basis + 8, half), jnp.float32)

time: 41.3 us -> 41.1 us (level)
  starting transfers between devices: 17.3 us -> 19.6 us
  waiting for transfers between devices: 16.2 us -> 14.6 us
  Pallas kernels: 6.51 us -> 5.69 us
    ppermute x6 -> x7, starting transfers between devices: 9.22 us -> 13.1 us  [along_z(): return lax.ppermute(piece, 'intra', xor_pairs(lanes, bit))]
    ppermute x6 -> x7, waiting for transfers between devices: 14.1 us -> 12.4 us  [along_z(): return lax.ppermute(piece, 'intra', xor_pairs(lanes, bit))]
    ppermute x4 -> x3, starting transfers between devices: 6.47 us -> 4.85 us  [along_y(): return lax.ppermute(piece, 'gddi', xor_pairs(groups, 2 * y))]
    pallas_call x3, Pallas kernels: 3.57 us -> 2.81 us  [couple(): pl.pallas_call(functools.partial(couple_kernel, groups, lanes, mono_dev,...]
  transfers between devices with their start and end apart: 18 -> 18, of which waited for: 10 -> 8; matrix products, arithmetic and copies ran while one was open for 0% -> 0% of each run, Pallas kernels for 11% -> 9%
where the time goes in v10:
time: 41.1 us; the launch traced here: 40.9 us
  starting transfers between devices  19.6 us (48%)
  waiting for transfers between devices  14.6 us (36%)
  Pallas kernels  5.69 us (14%)
  local copies, waits for them, and re-layouts  0.96 us (2%)
    ppermute x7, starting transfers between devices, along_z(): return lax.ppermute(piece, 'intra', xor_pairs(lanes, bit))  13.1 us
    ppermute x7, waiting for transfers between devices, along_z(): return lax.ppermute(piece, 'intra', xor_pairs(lanes, bit))  12.4 us
    ppermute x3, starting transfers between devices, along_y(): return lax.ppermute(piece, 'gddi', xor_pairs(groups, 2 * y))  4.85 us
    pallas_call x3, Pallas kernels, couple(): pl.pallas_call(functools.partial(couple_kernel, groups, lanes, mono_dev,...  2.81 us
    pallas_call x1, Pallas kernels, local(): pl.pallas_call(stage_kernel, out_shape=[pltpu.SMEM((nbr.shape[1], nbr.sha...  1.62 us
    ppermute x8, starting transfers between devices, local(): lax.ppermute(piece, 'gddi', xor_pairs(groups, 1))  1.59 us
    ppermute x8, waiting for transfers between devices, local(): lax.ppermute(piece, 'gddi', xor_pairs(groups, 1))  1.36 us
    pallas_call x1, Pallas kernels, local(): pl.pallas_call(finish_kernel, out_shape=jax.ShapeDtypeStruct((mono_dev, b...  0.98 us
  transfers between devices with their start and end apart: 18, of which 8 were waited for; matrix products, arithmetic and copies ran while one was open for 0% of the time, Pallas kernels for 9%

profile of v10, /device:TPU:0, one launch (start us, length us, event | category | flops | bytes accessed | tf_op | source)
XLA Modules:
  0.0 40.9 jit_solution(4769103815179749578)
XLA Ops:
  0.0 0.9 %copy-done = bf16[2,256,256]{2,1,0:T(8,128)(2,1)S(1)} copy-done((bf16[2,256,256]{2,1,0:T(8,128)(2,1)S(1)}, bf16[2,256,256]{2,1,0:T(8,128)(2,1)}, u32[]{:S(2)}) %copy-start) | copy-done | bytes 262168
  1.0 4.1 %collective-permute-start.1 = (bf16[528,128]{1,0:T(8,128)(2,1)S(1)}, bf16[528,128]{1,0:T(8,128)(2,1)S(1)}, u32[]{:S(2)}, u32[]{:S(2)}) collective-permute-start(bf16[528,128]{1,0:T(8,128)(2,1)S(1)} %fold.1.refs_0_), channel_id=1, source_target_pairs={{0,2},{1,3},{2,0},{3,1},{4,6},{5,7},{6,4},{7,5},{8,10},{9,11},{10,... | collective-permute-start | bytes 405512 | tf_op jit(solution)/shard_map/ppermute | solution.py:243
  5.1 1.6 %collective-permute-start.2 = (bf16[528,128]{1,0:T(8,128)(2,1)S(1)}, bf16[528,128]{1,0:T(8,128)(2,1)S(1)}, u32[]{:S(2)}, u32[]{:S(2)}) collective-permute-start(bf16[528,128]{1,0:T(8,128)(2,1)S(1)} %fold.1.refs_0_), channel_id=1, source_target_pairs={{0,1},{1,0},{2,3},{3,2},{4,5},{5,4},{6,7},{7,6},{8,9},{9,8},{10,11... | collective-permute-start | bytes 405512 | tf_op jit(solution)/shard_map/ppermute | solution.py:243
  6.7 1.5 %collective-permute-start = (bf16[528,128]{1,0:T(8,128)(2,1)S(1)}, bf16[528,128]{1,0:T(8,128)(2,1)S(1)}, u32[]{:S(2)}, u32[]{:S(2)}) collective-permute-start(bf16[528,128]{1,0:T(8,128)(2,1)S(1)} %fold.1.refs_0_), channel_id=1, source_target_pairs={{0,8},{4,12},{8,0},{12,4},{1,9},{5,13},{9,1},{13,5},{2,10},{6,14},... | collective-permute-start | bytes 405512 | tf_op jit(solution)/shard_map/ppermute | solution.py:246
  8.2 3.5 %collective-permute-done.1.piece_ref = bf16[528,128]{1,0:T(8,128)(2,1)S(1)} collective-permute-done((bf16[528,128]{1,0:T(8,128)(2,1)S(1)}, bf16[528,128]{1,0:T(8,128)(2,1)S(1)}, u32[]{:S(2)}, u32[]{:S(2)}) %collective-permute-start.1) | collective-permute-done | bytes 135200 | tf_op jit(solution)/shard_map/ppermute | solution.py:243
  11.9 1.5 %collective-permute-start.3 = (bf16[528,128]{1,0:T(8,128)(2,1)S(1)}, bf16[528,128]{1,0:T(8,128)(2,1)S(1)}, u32[]{:S(2)}, u32[]{:S(2)}) collective-permute-start(bf16[528,128]{1,0:T(8,128)(2,1)S(1)} %gate.8.refs_2_), channel_id=1, source_target_pairs={{0,1},{1,0},{2,3},{3,2},{4,5},{5,4},{6,7},{7,6},{8,9},{9,8},{10,11... | collective-permute-start | bytes 405512 | tf_op jit(solution)/shard_map/ppermute | solution.py:243
  13.4 0.5 %collective-permute-start.9 = (bf16[528,128]{1,0:T(8,128)(2,1)S(1)}, bf16[528,128]{1,0:T(8,128)(2,1)S(1)}, u32[]{:S(2)}, u32[]{:S(2)}) collective-permute-start(bf16[528,128]{1,0:T(8,128)(2,1)S(1)} %gate.8.refs_2_), channel_id=1, source_target_pairs={{0,4},{4,0},{8,12},{12,8},{1,5},{5,1},{9,13},{13,9},{2,6},{6,2},{1... | collective-permute-start | bytes 405512 | tf_op jit(solution)/shard_map/ppermute | solution.py:303
  13.9 1.5 %collective-permute-start.5 = (bf16[528,128]{1,0:T(8,128)(2,1)S(1)}, bf16[528,128]{1,0:T(8,128)(2,1)S(1)}, u32[]{:S(2)}, u32[]{:S(2)}) collective-permute-start(bf16[528,128]{1,0:T(8,128)(2,1)S(1)} %gate.8.refs_2_), channel_id=1, source_target_pairs={{0,8},{4,12},{8,0},{12,4},{1,9},{5,13},{9,1},{13,5},{2,10},{6,14},... | collective-permute-start | bytes 405512 | tf_op jit(solution)/shard_map/ppermute | solution.py:246
  15.5 0.6 %collective-permute-start.4 = (bf16[528,128]{1,0:T(8,128)(2,1)S(1)}, bf16[528,128]{1,0:T(8,128)(2,1)S(1)}, u32[]{:S(2)}, u32[]{:S(2)}) collective-permute-start(bf16[528,128]{1,0:T(8,128)(2,1)S(1)} %collective-permute-done.refs_2_.piece_ref), channel_id=1, source_target_pairs={{0,1},{1,0},{2,3},{3,2},{4,5},{5,4},{6,7},{7,6},{8,9},{9,8},{10,11... | collective-permute-start | bytes 405512 | tf_op jit(solution)/shard_map/ppermute | solution.py:243
  16.1 0.9 %collective-permute-done.3.refs_0_.refs_3_ = bf16[528,128]{1,0:T(8,128)(2,1)S(1)} collective-permute-done((bf16[528,128]{1,0:T(8,128)(2,1)S(1)}, bf16[528,128]{1,0:T(8,128)(2,1)S(1)}, u32[]{:S(2)}, u32[]{:S(2)}) %collective-permute-start.3) | collective-permute-done | bytes 135200 | tf_op jit(solution)/shard_map/ppermute | solution.py:243
  17.0 1.8 %collective-permute-start.6 = (bf16[528,128]{1,0:T(8,128)(2,1)S(1)}, bf16[528,128]{1,0:T(8,128)(2,1)S(1)}, u32[]{:S(2)}, u32[]{:S(2)}) collective-permute-start(bf16[528,128]{1,0:T(8,128)(2,1)S(1)} %collective-permute-done.3.refs_0_.refs_3_), channel_id=1, source_target_pairs={{0,8},{4,12},{8,0},{12,4},{1,9},{5,13},{9,1},{13,5},{2,10},{6,14},... | collective-permute-start | bytes 405512 | tf_op jit(solution)/shard_map/ppermute | solution.py:246
  18.8 1.6 %stage.1 = (s32[8,32]{1,0:T(8,128)S(4)}, bf16[8,2,256,256]{3,2,1,0:T(8,128)(2,1)S(1)}, bf16[528,128]{1,0:T(8,128)(2,1)S(1)}) custom-call(s32[8,32]{1,0:T(8,128)} %bitcast.1, bf16[8,2,256,256]{3,2,1,0:T(8,128)(2,1)} %esp_ref.1, bf16[528,128]{1,0:T(8,128)(2,1)S(1)} %collective-permute-done.refs_2_.piece_ref, ...), custom_call_target="tpu_custom_call" | custom-call | tf_op jit(solution)/shard_map/stage/pallas_call | solution.py:283
  20.5 0.5 %collective-permute-start.10 = (bf16[528,128]{1,0:T(8,128)(2,1)S(1)}, bf16[528,128]{1,0:T(8,128)(2,1)S(1)}, u32[]{:S(2)}, u32[]{:S(2)}) collective-permute-start(bf16[528,128]{1,0:T(8,128)(2,1)S(1)} %collective-permute-done.3.refs_0_.refs_3_), channel_id=1, source_target_pairs={{0,4},{4,0},{8,12},{12,8},{1,5},{5,1},{9,13},{13,9},{2,6},{6,2},{1... | collective-permute-start | bytes 405512 | tf_op jit(solution)/shard_map/ppermute | solution.py:303
  21.1 0.4 %collective-permute-start.12 = (bf16[528,128]{1,0:T(8,128)(2,1)S(1)}, bf16[528,128]{1,0:T(8,128)(2,1)S(1)}, u32[]{:S(2)}, u32[]{:S(2)}) collective-permute-start(bf16[528,128]{1,0:T(8,128)(2,1)S(1)} %collective-permute-done.4.refs_5_), channel_id=1, source_target_pairs={{0,4},{4,0},{8,12},{12,8},{1,5},{5,1},{9,13},{13,9},{2,6},{6,2},{1... | collective-permute-start | bytes 405512 | tf_op jit(solution)/shard_map/ppermute | solution.py:303
  21.5 0.8 %collective-permute-done.6.refs_7_ = bf16[528,128]{1,0:T(8,128)(2,1)S(1)} collective-permute-done((bf16[528,128]{1,0:T(8,128)(2,1)S(1)}, bf16[528,128]{1,0:T(8,128)(2,1)S(1)}, u32[]{:S(2)}, u32[]{:S(2)}) %collective-permute-start.6) | collective-permute-done | bytes 135200 | tf_op jit(solution)/shard_map/ppermute | solution.py:246
  22.6 1.1 %collective-permute-done.14.refs_15_ = bf16[528,128]{1,0:T(8,128)(2,1)S(1)} collective-permute-done((bf16[528,128]{1,0:T(8,128)(2,1)S(1)}, bf16[528,128]{1,0:T(8,128)(2,1)S(1)}, u32[]{:S(2)}, u32[]{:S(2)}) %collective-permute-start.14) | collective-permute-done | bytes 135200 | tf_op jit(solution)/shard_map/ppermute | solution.py:303
  23.7 0.9 %couple_relay.1 = (bf16[16,528,128]{2,1,0:T(8,128)(2,1)S(1)}, s32[264,128]{1,0:T(8,128)S(1)}) custom-call(s32[8,32]{1,0:T(8,128)S(4)} %get-tuple-element.12.nbr_ref, bf16[8,2,256,256]{3,2,1,0:T(8,128)(2,1)S(1)} %get-tuple-element.13.esp_ref, bf16[528,128]{1,0:T(8,128)(2,1)S(1)} %fold.1.refs_0_, bf16[528,128]{1,0:T(8,128)(2,1)S(1)} %collective-permute-done.2.refs_1_, ...), custom_call_target="tpu_custom_call" | custom-call | tf_op jit(solution)/shard_map/couple_relay/pallas_call | solution.py:313
  24.6 1.8 %collective-permute-start.16 = (s32[264,128]{1,0:T(8,128)S(1)}, s32[264,128]{1,0:T(8,128)S(1)}, u32[]{:S(2)}, u32[]{:S(2)}) collective-permute-start(s32[264,128]{1,0:T(8,128)S(1)} %get-tuple-element.18), channel_id=1, source_target_pairs={{0,1},{1,0},{2,3},{3,2},{4,5},{5,4},{6,7},{7,6},{8,9},{9,8},{10,11... | collective-permute-start | bytes 405512 | tf_op jit(solution)/shard_map/ppermute | solution.py:243
  26.4 0.8 %couple_near.1 = s32[264,128]{1,0:T(8,128)S(1)} custom-call(s32[8,32]{1,0:T(8,128)S(4)} %get-tuple-element.12.nbr_ref, bf16[8,2,256,256]{3,2,1,0:T(8,128)(2,1)S(1)} %get-tuple-element.13.esp_ref, bf16[16,528,128]{2,1,0:T(8,128)(2,1)S(1)} %get-tuple-element.15.refs_0_), custom_call_target="tpu_custom_call" | custom-call | tf_op jit(solution)/shard_map/couple_near/pallas_call | solution.py:313
  27.6 1.1 %couple_far.1 = (f32[2,264,128]{2,1,0:T(8,128)S(1)}, f32[2,264,128]{2,1,0:T(8,128)S(1)}) custom-call(s32[8,32]{1,0:T(8,128)S(4)} %get-tuple-element.12.nbr_ref, bf16[8,2,256,256]{3,2,1,0:T(8,128)(2,1)S(1)} %get-tuple-element.13.esp_ref, bf16[16,528,128]{2,1,0:T(8,128)(2,1)S(1)} %get-tuple-element.15.refs_0_), custom_call_target="tpu_custom_call" | custom-call | tf_op jit(solution)/shard_map/couple_far/pallas_call | solution.py:313
  28.7 2.1 %collective-permute-done.16.refs_0_ = s32[264,128]{1,0:T(8,128)S(1)} collective-permute-done((s32[264,128]{1,0:T(8,128)S(1)}, s32[264,128]{1,0:T(8,128)S(1)}, u32[]{:S(2)}, u32[]{:S(2)}) %collective-permute-start.16) | collective-permute-done | bytes 135200 | tf_op jit(solution)/shard_map/ppermute | solution.py:243
  31.0 3.1 %collective-permute-start.17 = (s32[264,128]{1,0:T(8,128)S(1)}, s32[264,128]{1,0:T(8,128)S(1)}, u32[]{:S(2)}, u32[]{:S(2)}) collective-permute-start(s32[264,128]{1,0:T(8,128)S(1)} %merge.1), channel_id=1, source_target_pairs={{0,2},{1,3},{2,0},{3,1},{4,6},{5,7},{6,4},{7,5},{8,10},{9,11},{10,... | collective-permute-start | bytes 405512 | tf_op jit(solution)/shard_map/ppermute | solution.py:243
  34.2 5.7 %collective-permute-done.17.refs_1_ = s32[264,128]{1,0:T(8,128)S(1)} collective-permute-done((s32[264,128]{1,0:T(8,128)S(1)}, s32[264,128]{1,0:T(8,128)S(1)}, u32[]{:S(2)}, u32[]{:S(2)}) %collective-permute-start.17) | collective-permute-done | bytes 135200 | tf_op jit(solution)/shard_map/ppermute | solution.py:243
  39.9 1.0 %finish.1 = f32[2,256,256]{2,1,0:T(8,128)} custom-call(bf16[2,256,256]{2,1,0:T(8,128)(2,1)S(1)} %copy-done.1, f32[2,264,128]{2,1,0:T(8,128)S(1)} %get-tuple-element.16.own_ref, s32[264,128]{1,0:T(8,128)S(1)} %gate.13.refs_0_, s32[264,128]{1,0:T(8,128)S(1)} %collective-permute-done.17.refs_1_), custom_call_target="tpu_custom_call" | custom-call | tf_op jit(solution)/shard_map/finish/pallas_call | solution.py:340
  (30 shorter events, 1.2 us)
Async XLA Ops:
  0.0 0.9 %copy-start = (bf16[2,256,256]{2,1,0:T(8,128)(2,1)S(1)}, bf16[2,256,256]{2,1,0:T(8,128)(2,1)}, u32[]{:S(2)}) copy-start(bf16[2,256,256]{2,1,0:T(8,128)(2,1)} %dens_ref.1) | copy-start | bytes 786436
  1.0 10.7 %collective-permute-start.1 = (bf16[528,128]{1,0:T(8,128)(2,1)S(1)}, bf16[528,128]{1,0:T(8,128)(2,1)S(1)}, u32[]{:S(2)}, u32[]{:S(2)}) collective-permute-start(bf16[528,128]{1,0:T(8,128)(2,1)S(1)} %fold.1.refs_0_), channel_id=1, source_target_pairs={{0,2},{1,3},{2,0},{3,1},{4,6},{5,7},{6,4},{7,5},{8,10},{9,11},{10,... | collective-permute-start | bytes 405512 | tf_op jit(solution)/shard_map/ppermute | solution.py:243
  5.1 6.8 %collective-permute-start.2 = (bf16[528,128]{1,0:T(8,128)(2,1)S(1)}, bf16[528,128]{1,0:T(8,128)(2,1)S(1)}, u32[]{:S(2)}, u32[]{:S(2)}) collective-permute-start(bf16[528,128]{1,0:T(8,128)(2,1)S(1)} %fold.1.refs_0_), channel_id=1, source_target_pairs={{0,1},{1,0},{2,3},{3,2},{4,5},{5,4},{6,7},{7,6},{8,9},{9,8},{10,11... | collective-permute-start | bytes 405512 | tf_op jit(solution)/shard_map/ppermute | solution.py:243
  6.7 5.2 %collective-permute-start = (bf16[528,128]{1,0:T(8,128)(2,1)S(1)}, bf16[528,128]{1,0:T(8,128)(2,1)S(1)}, u32[]{:S(2)}, u32[]{:S(2)}) collective-permute-start(bf16[528,128]{1,0:T(8,128)(2,1)S(1)} %fold.1.refs_0_), channel_id=1, source_target_pairs={{0,8},{4,12},{8,0},{12,4},{1,9},{5,13},{9,1},{13,5},{2,10},{6,14},... | collective-permute-start | bytes 405512 | tf_op jit(solution)/shard_map/ppermute | solution.py:246
  8.2 7.3 %collective-permute-start.7 = (bf16[528,128]{1,0:T(8,128)(2,1)S(1)}, bf16[528,128]{1,0:T(8,128)(2,1)S(1)}, u32[]{:S(2)}, u32[]{:S(2)}) collective-permute-start(bf16[528,128]{1,0:T(8,128)(2,1)S(1)} %fold.1.refs_0_), channel_id=1, source_target_pairs={{0,4},{4,0},{8,12},{12,8},{1,5},{5,1},{9,13},{13,9},{2,6},{6,2},{1... | collective-permute-start | bytes 405512 | tf_op jit(solution)/shard_map/ppermute | solution.py:303
  11.9 5.1 %collective-permute-start.3 = (bf16[528,128]{1,0:T(8,128)(2,1)S(1)}, bf16[528,128]{1,0:T(8,128)(2,1)S(1)}, u32[]{:S(2)}, u32[]{:S(2)}) collective-permute-start(bf16[528,128]{1,0:T(8,128)(2,1)S(1)} %gate.8.refs_2_), channel_id=1, source_target_pairs={{0,1},{1,0},{2,3},{3,2},{4,5},{5,4},{6,7},{7,6},{8,9},{9,8},{10,11... | collective-permute-start | bytes 405512 | tf_op jit(solution)/shard_map/ppermute | solution.py:243
  13.4 7.0 %collective-permute-start.8 = (bf16[528,128]{1,0:T(8,128)(2,1)S(1)}, bf16[528,128]{1,0:T(8,128)(2,1)S(1)}, u32[]{:S(2)}, u32[]{:S(2)}) collective-permute-start(bf16[528,128]{1,0:T(8,128)(2,1)S(1)} %collective-permute-done.2.refs_1_), channel_id=1, source_target_pairs={{0,4},{4,0},{8,12},{12,8},{1,5},{5,1},{9,13},{13,9},{2,6},{6,2},{1... | collective-permute-start | bytes 405512 | tf_op jit(solution)/shard_map/ppermute | solution.py:303
  13.4 7.1 %collective-permute-start.9 = (bf16[528,128]{1,0:T(8,128)(2,1)S(1)}, bf16[528,128]{1,0:T(8,128)(2,1)S(1)}, u32[]{:S(2)}, u32[]{:S(2)}) collective-permute-start(bf16[528,128]{1,0:T(8,128)(2,1)S(1)} %gate.8.refs_2_), channel_id=1, source_target_pairs={{0,4},{4,0},{8,12},{12,8},{1,5},{5,1},{9,13},{13,9},{2,6},{6,2},{1... | collective-permute-start | bytes 405512 | tf_op jit(solution)/shard_map/ppermute | solution.py:303
  13.9 7.1 %collective-permute-start.5 = (bf16[528,128]{1,0:T(8,128)(2,1)S(1)}, bf16[528,128]{1,0:T(8,128)(2,1)S(1)}, u32[]{:S(2)}, u32[]{:S(2)}) collective-permute-start(bf16[528,128]{1,0:T(8,128)(2,1)S(1)} %gate.8.refs_2_), channel_id=1, source_target_pairs={{0,8},{4,12},{8,0},{12,4},{1,9},{5,13},{9,1},{13,5},{2,10},{6,14},... | collective-permute-start | bytes 405512 | tf_op jit(solution)/shard_map/ppermute | solution.py:246
  15.5 5.6 %collective-permute-start.4 = (bf16[528,128]{1,0:T(8,128)(2,1)S(1)}, bf16[528,128]{1,0:T(8,128)(2,1)S(1)}, u32[]{:S(2)}, u32[]{:S(2)}) collective-permute-start(bf16[528,128]{1,0:T(8,128)(2,1)S(1)} %collective-permute-done.refs_2_.piece_ref), channel_id=1, source_target_pairs={{0,1},{1,0},{2,3},{3,2},{4,5},{5,4},{6,7},{7,6},{8,9},{9,8},{10,11... | collective-permute-start | bytes 405512 | tf_op jit(solution)/shard_map/ppermute | solution.py:243
  17.0 5.3 %collective-permute-start.6 = (bf16[528,128]{1,0:T(8,128)(2,1)S(1)}, bf16[528,128]{1,0:T(8,128)(2,1)S(1)}, u32[]{:S(2)}, u32[]{:S(2)}) collective-permute-start(bf16[528,128]{1,0:T(8,128)(2,1)S(1)} %collective-permute-done.3.refs_0_.refs_3_), channel_id=1, source_target_pairs={{0,8},{4,12},{8,0},{12,4},{1,9},{5,13},{9,1},{13,5},{2,10},{6,14},... | collective-permute-start | bytes 405512 | tf_op jit(solution)/shard_map/ppermute | solution.py:246
  20.4 2.1 %collective-permute-start.11 = (bf16[528,128]{1,0:T(8,128)(2,1)S(1)}, bf16[528,128]{1,0:T(8,128)(2,1)S(1)}, u32[]{:S(2)}, u32[]{:S(2)}) collective-permute-start(bf16[528,128]{1,0:T(8,128)(2,1)S(1)} %get-tuple-element.14.refs_4_), channel_id=1, source_target_pairs={{0,4},{4,0},{8,12},{12,8},{1,5},{5,1},{9,13},{13,9},{2,6},{6,2},{1... | collective-permute-start | bytes 405512 | tf_op jit(solution)/shard_map/ppermute | solution.py:303
  20.5 1.9 %collective-permute-start.10 = (bf16[528,128]{1,0:T(8,128)(2,1)S(1)}, bf16[528,128]{1,0:T(8,128)(2,1)S(1)}, u32[]{:S(2)}, u32[]{:S(2)}) collective-permute-start(bf16[528,128]{1,0:T(8,128)(2,1)S(1)} %collective-permute-done.3.refs_0_.refs_3_), channel_id=1, source_target_pairs={{0,4},{4,0},{8,12},{12,8},{1,5},{5,1},{9,13},{13,9},{2,6},{6,2},{1... | collective-permute-start | bytes 405512 | tf_op jit(solution)/shard_map/ppermute | solution.py:303
  21.0 1.4 %collective-permute-start.13 = (bf16[528,128]{1,0:T(8,128)(2,1)S(1)}, bf16[528,128]{1,0:T(8,128)(2,1)S(1)}, u32[]{:S(2)}, u32[]{:S(2)}) collective-permute-start(bf16[528,128]{1,0:T(8,128)(2,1)S(1)} %collective-permute-done.5.refs_6_), channel_id=1, source_target_pairs={{0,4},{4,0},{8,12},{12,8},{1,5},{5,1},{9,13},{13,9},{2,6},{6,2},{1... | collective-permute-start | bytes 405512 | tf_op jit(solution)/shard_map/ppermute | solution.py:303
  21.1 1.5 %collective-permute-start.12 = (bf16[528,128]{1,0:T(8,128)(2,1)S(1)}, bf16[528,128]{1,0:T(8,128)(2,1)S(1)}, u32[]{:S(2)}, u32[]{:S(2)}) collective-permute-start(bf16[528,128]{1,0:T(8,128)(2,1)S(1)} %collective-permute-done.4.refs_5_), channel_id=1, source_target_pairs={{0,4},{4,0},{8,12},{12,8},{1,5},{5,1},{9,13},{13,9},{2,6},{6,2},{1... | collective-permute-start | bytes 405512 | tf_op jit(solution)/shard_map/ppermute | solution.py:303
  22.3 1.4 %collective-permute-start.14 = (bf16[528,128]{1,0:T(8,128)(2,1)S(1)}, bf16[528,128]{1,0:T(8,128)(2,1)S(1)}, u32[]{:S(2)}, u32[]{:S(2)}) collective-permute-start(bf16[528,128]{1,0:T(8,128)(2,1)S(1)} %collective-permute-done.6.refs_7_), channel_id=1, source_target_pairs={{0,4},{4,0},{8,12},{12,8},{1,5},{5,1},{9,13},{13,9},{2,6},{6,2},{1... | collective-permute-start | bytes 405512 | tf_op jit(solution)/shard_map/ppermute | solution.py:303
  24.6 6.2 %collective-permute-start.16 = (s32[264,128]{1,0:T(8,128)S(1)}, s32[264,128]{1,0:T(8,128)S(1)}, u32[]{:S(2)}, u32[]{:S(2)}) collective-permute-start(s32[264,128]{1,0:T(8,128)S(1)} %get-tuple-element.18), channel_id=1, source_target_pairs={{0,1},{1,0},{2,3},{3,2},{4,5},{5,4},{6,7},{7,6},{8,9},{9,8},{10,11... | collective-permute-start | bytes 405512 | tf_op jit(solution)/shard_map/ppermute | solution.py:243
  27.2 12.7 %copy-start.1 = (bf16[2,256,256]{2,1,0:T(8,128)(2,1)S(1)}, bf16[2,256,256]{2,1,0:T(8,128)(2,1)}, u32[]{:S(2)}) copy-start(bf16[2,256,256]{2,1,0:T(8,128)(2,1)} %core_ref.1) | copy-start | bytes 786436
  27.2 6.9 %collective-permute-start.15 = (s32[264,128]{1,0:T(8,128)S(1)}, s32[264,128]{1,0:T(8,128)S(1)}, u32[]{:S(2)}, u32[]{:S(2)}) collective-permute-start(s32[264,128]{1,0:T(8,128)S(1)} %couple_near.1), channel_id=1, source_target_pairs={{0,1},{1,0},{2,3},{3,2},{4,5},{5,4},{6,7},{7,6},{8,9},{9,8},{10,11... | collective-permute-start | bytes 405512 | tf_op jit(solution)/shard_map/ppermute | solution.py:243
  31.0 8.9 %collective-permute-start.17 = (s32[264,128]{1,0:T(8,128)S(1)}, s32[264,128]{1,0:T(8,128)S(1)}, u32[]{:S(2)}, u32[]{:S(2)}) collective-permute-start(s32[264,128]{1,0:T(8,128)S(1)} %merge.1), channel_id=1, source_target_pairs={{0,2},{1,3},{2,0},{3,1},{4,6},{5,7},{6,4},{7,5},{8,10},{9,11},{10,... | collective-permute-start | bytes 405512 | tf_op jit(solution)/shard_map/ppermute | solution.py:243

commit v11 on v10

--- a/solution.py
+++ b/solution.py
@@ -324,19 +324,16 @@
     steps = range(1, top)
     filled, *relayed = couple([(top ^ k, True) for k in steps], "couple_relay", pieces, fill=True)
     relayed = [along_z(unit, k) for k, unit in zip(steps, relayed)]
-    close = couple([(k, True) for k in steps], "couple_near", [filled])
-    close = [along_z(unit, k) for k, unit in zip(steps, close)]
-    for _ in range(5):
-        close = [gate(unit) for unit in close]
-    across, own = couple([(top, False), (0, False)], "couple_far", [filled])
-    across = pl.pallas_call(
+    beyond, own, *close = couple([(top, False), (0, False)] + [(k, True) for k in steps], "couple_rest", [filled])
+    beyond = pl.pallas_call(
         merge_kernel,
-        out_shape=coded,
+        out_shape=pltpu.VMEM((coded.shape[0] + 8, half), jnp.int32),
         in_specs=[IN_VMEM] * (1 + len(relayed)),
         out_specs=IN_VMEM,
         compiler_params=small,
         name="merge",
-    )(across, *relayed)
+    )(beyond, *relayed)
+    close = [along_z(gate(unit, beyond), k) for k, unit in zip(steps, close)]
     return pl.pallas_call(
         finish_kernel,
         out_shape=jax.ShapeDtypeStruct((mono_dev, basis, basis), jnp.float32),
@@ -344,7 +341,7 @@
         out_specs=IN_VMEM,
         compiler_params=small,
         name="finish",
-    )(h_core, own, *close, along_z(across, top))
+    )(h_core, own, *close, along_z(beyond, top))
 
 
 def solution(mesh):

time: 41.1 us -> 41.8 us (1.017)
  starting transfers between devices: 19.6 us -> 21 us
  waiting for transfers between devices: 14.6 us -> 14.1 us
    ppermute x7, starting transfers between devices: 13.1 us -> 14.6 us  [along_z(): return lax.ppermute(piece, 'intra', xor_pairs(lanes, bit))]
    ppermute x7, waiting for transfers between devices: 12.4 us -> 12 us  [along_z(): return lax.ppermute(piece, 'intra', xor_pairs(lanes, bit))]
    pallas_call x3 -> x2, Pallas kernels: 2.81 us -> 2.55 us  [couple(): pl.pallas_call(functools.partial(couple_kernel, groups, lanes, mono_dev,...]
  transfers between devices with their start and end apart: 18 -> 18, of which waited for: 8 -> 8; matrix products, arithmetic and copies ran while one was open for 0% -> 0% of each run, Pallas kernels for 9% -> 8%
where the time goes in v11:
time: 41.8 us; the launch traced here: 41.6 us
  starting transfers between devices  21 us (50%)
  waiting for transfers between devices  14.1 us (34%)
  Pallas kernels  5.39 us (13%)
  local copies, waits for them, and re-layouts  0.95 us (2%)
    ppermute x7, starting transfers between devices, along_z(): return lax.ppermute(piece, 'intra', xor_pairs(lanes, bit))  14.6 us
    ppermute x7, waiting for transfers between devices, along_z(): return lax.ppermute(piece, 'intra', xor_pairs(lanes, bit))  12 us
    ppermute x3, starting transfers between devices, along_y(): return lax.ppermute(piece, 'gddi', xor_pairs(groups, 2 * y))  4.85 us
    pallas_call x2, Pallas kernels, couple(): pl.pallas_call(functools.partial(couple_kernel, groups, lanes, mono_dev,...  2.55 us
    pallas_call x1, Pallas kernels, local(): pl.pallas_call(stage_kernel, out_shape=[pltpu.SMEM((nbr.shape[1], nbr.sha...  1.62 us
    ppermute x8, starting transfers between devices, local(): lax.ppermute(piece, 'gddi', xor_pairs(groups, 1))  1.59 us
    ppermute x8, waiting for transfers between devices, local(): lax.ppermute(piece, 'gddi', xor_pairs(groups, 1))  1.36 us
    pallas_call x1, Pallas kernels, local(): pl.pallas_call(finish_kernel, out_shape=jax.ShapeDtypeStruct((mono_dev, b...  0.98 us
  transfers between devices with their start and end apart: 18, of which 8 were waited for; matrix products, arithmetic and copies ran while one was open for 0% of the time, Pallas kernels for 8%

profile of v11, /device:TPU:0, one launch (start us, length us, event | category | flops | bytes accessed | tf_op | source)
XLA Modules:
  0.0 41.6 jit_solution(3453700355732018642)
XLA Ops:
  0.0 0.9 %copy-done = bf16[2,256,256]{2,1,0:T(8,128)(2,1)S(1)} copy-done((bf16[2,256,256]{2,1,0:T(8,128)(2,1)S(1)}, bf16[2,256,256]{2,1,0:T(8,128)(2,1)}, u32[]{:S(2)}) %copy-start) | copy-done | bytes 262168
  1.0 4.1 %collective-permute-start.1 = (bf16[528,128]{1,0:T(8,128)(2,1)S(1)}, bf16[528,128]{1,0:T(8,128)(2,1)S(1)}, u32[]{:S(2)}, u32[]{:S(2)}) collective-permute-start(bf16[528,128]{1,0:T(8,128)(2,1)S(1)} %fold.1.refs_0_), channel_id=1, source_target_pairs={{0,2},{1,3},{2,0},{3,1},{4,6},{5,7},{6,4},{7,5},{8,10},{9,11},{10,... | collective-permute-start | bytes 405512 | tf_op jit(solution)/shard_map/ppermute | solution.py:243
  5.1 1.6 %collective-permute-start.2 = (bf16[528,128]{1,0:T(8,128)(2,1)S(1)}, bf16[528,128]{1,0:T(8,128)(2,1)S(1)}, u32[]{:S(2)}, u32[]{:S(2)}) collective-permute-start(bf16[528,128]{1,0:T(8,128)(2,1)S(1)} %fold.1.refs_0_), channel_id=1, source_target_pairs={{0,1},{1,0},{2,3},{3,2},{4,5},{5,4},{6,7},{7,6},{8,9},{9,8},{10,11... | collective-permute-start | bytes 405512 | tf_op jit(solution)/shard_map/ppermute | solution.py:243
  6.7 1.5 %collective-permute-start = (bf16[528,128]{1,0:T(8,128)(2,1)S(1)}, bf16[528,128]{1,0:T(8,128)(2,1)S(1)}, u32[]{:S(2)}, u32[]{:S(2)}) collective-permute-start(bf16[528,128]{1,0:T(8,128)(2,1)S(1)} %fold.1.refs_0_), channel_id=1, source_target_pairs={{0,8},{4,12},{8,0},{12,4},{1,9},{5,13},{9,1},{13,5},{2,10},{6,14},... | collective-permute-start | bytes 405512 | tf_op jit(solution)/shard_map/ppermute | solution.py:246
  8.2 3.5 %collective-permute-done.1.piece_ref = bf16[528,128]{1,0:T(8,128)(2,1)S(1)} collective-permute-done((bf16[528,128]{1,0:T(8,128)(2,1)S(1)}, bf16[528,128]{1,0:T(8,128)(2,1)S(1)}, u32[]{:S(2)}, u32[]{:S(2)}) %collective-permute-start.1) | collective-permute-done | bytes 135200 | tf_op jit(solution)/shard_map/ppermute | solution.py:243
  11.9 1.5 %collective-permute-start.3 = (bf16[528,128]{1,0:T(8,128)(2,1)S(1)}, bf16[528,128]{1,0:T(8,128)(2,1)S(1)}, u32[]{:S(2)}, u32[]{:S(2)}) collective-permute-start(bf16[528,128]{1,0:T(8,128)(2,1)S(1)} %gate.4.refs_2_), channel_id=1, source_target_pairs={{0,1},{1,0},{2,3},{3,2},{4,5},{5,4},{6,7},{7,6},{8,9},{9,8},{10,11... | collective-permute-start | bytes 405512 | tf_op jit(solution)/shard_map/ppermute | solution.py:243
  13.4 0.5 %collective-permute-start.9 = (bf16[528,128]{1,0:T(8,128)(2,1)S(1)}, bf16[528,128]{1,0:T(8,128)(2,1)S(1)}, u32[]{:S(2)}, u32[]{:S(2)}) collective-permute-start(bf16[528,128]{1,0:T(8,128)(2,1)S(1)} %gate.4.refs_2_), channel_id=1, source_target_pairs={{0,4},{4,0},{8,12},{12,8},{1,5},{5,1},{9,13},{13,9},{2,6},{6,2},{1... | collective-permute-start | bytes 405512 | tf_op jit(solution)/shard_map/ppermute | solution.py:303
  13.9 1.5 %collective-permute-start.5 = (bf16[528,128]{1,0:T(8,128)(2,1)S(1)}, bf16[528,128]{1,0:T(8,128)(2,1)S(1)}, u32[]{:S(2)}, u32[]{:S(2)}) collective-permute-start(bf16[528,128]{1,0:T(8,128)(2,1)S(1)} %gate.4.refs_2_), channel_id=1, source_target_pairs={{0,8},{4,12},{8,0},{12,4},{1,9},{5,13},{9,1},{13,5},{2,10},{6,14},... | collective-permute-start | bytes 405512 | tf_op jit(solution)/shard_map/ppermute | solution.py:246
  15.5 0.6 %collective-permute-start.4 = (bf16[528,128]{1,0:T(8,128)(2,1)S(1)}, bf16[528,128]{1,0:T(8,128)(2,1)S(1)}, u32[]{:S(2)}, u32[]{:S(2)}) collective-permute-start(bf16[528,128]{1,0:T(8,128)(2,1)S(1)} %collective-permute-done.refs_2_.piece_ref), channel_id=1, source_target_pairs={{0,1},{1,0},{2,3},{3,2},{4,5},{5,4},{6,7},{7,6},{8,9},{9,8},{10,11... | collective-permute-start | bytes 405512 | tf_op jit(solution)/shard_map/ppermute | solution.py:243
  16.1 0.9 %collective-permute-done.3.refs_0_.refs_3_ = bf16[528,128]{1,0:T(8,128)(2,1)S(1)} collective-permute-done((bf16[528,128]{1,0:T(8,128)(2,1)S(1)}, bf16[528,128]{1,0:T(8,128)(2,1)S(1)}, u32[]{:S(2)}, u32[]{:S(2)}) %collective-permute-start.3) | collective-permute-done | bytes 135200 | tf_op jit(solution)/shard_map/ppermute | solution.py:243
  17.0 1.8 %collective-permute-start.6 = (bf16[528,128]{1,0:T(8,128)(2,1)S(1)}, bf16[528,128]{1,0:T(8,128)(2,1)S(1)}, u32[]{:S(2)}, u32[]{:S(2)}) collective-permute-start(bf16[528,128]{1,0:T(8,128)(2,1)S(1)} %collective-permute-done.3.refs_0_.refs_3_), channel_id=1, source_target_pairs={{0,8},{4,12},{8,0},{12,4},{1,9},{5,13},{9,1},{13,5},{2,10},{6,14},... | collective-permute-start | bytes 405512 | tf_op jit(solution)/shard_map/ppermute | solution.py:246
  18.8 1.6 %stage.1 = (s32[8,32]{1,0:T(8,128)S(4)}, bf16[8,2,256,256]{3,2,1,0:T(8,128)(2,1)S(1)}, bf16[528,128]{1,0:T(8,128)(2,1)S(1)}) custom-call(s32[8,32]{1,0:T(8,128)} %bitcast.1, bf16[8,2,256,256]{3,2,1,0:T(8,128)(2,1)} %esp_ref.1, bf16[528,128]{1,0:T(8,128)(2,1)S(1)} %collective-permute-done.refs_2_.piece_ref, ...), custom_call_target="tpu_custom_call" | custom-call | tf_op jit(solution)/shard_map/stage/pallas_call | solution.py:283
  20.5 0.5 %collective-permute-start.10 = (bf16[528,128]{1,0:T(8,128)(2,1)S(1)}, bf16[528,128]{1,0:T(8,128)(2,1)S(1)}, u32[]{:S(2)}, u32[]{:S(2)}) collective-permute-start(bf16[528,128]{1,0:T(8,128)(2,1)S(1)} %collective-permute-done.3.refs_0_.refs_3_), channel_id=1, source_target_pairs={{0,4},{4,0},{8,12},{12,8},{1,5},{5,1},{9,13},{13,9},{2,6},{6,2},{1... | collective-permute-start | bytes 405512 | tf_op jit(solution)/shard_map/ppermute | solution.py:303
  21.1 0.4 %collective-permute-start.12 = (bf16[528,128]{1,0:T(8,128)(2,1)S(1)}, bf16[528,128]{1,0:T(8,128)(2,1)S(1)}, u32[]{:S(2)}, u32[]{:S(2)}) collective-permute-start(bf16[528,128]{1,0:T(8,128)(2,1)S(1)} %collective-permute-done.4.refs_5_), channel_id=1, source_target_pairs={{0,4},{4,0},{8,12},{12,8},{1,5},{5,1},{9,13},{13,9},{2,6},{6,2},{1... | collective-permute-start | bytes 405512 | tf_op jit(solution)/shard_map/ppermute | solution.py:303
  21.5 0.8 %collective-permute-done.6.refs_7_ = bf16[528,128]{1,0:T(8,128)(2,1)S(1)} collective-permute-done((bf16[528,128]{1,0:T(8,128)(2,1)S(1)}, bf16[528,128]{1,0:T(8,128)(2,1)S(1)}, u32[]{:S(2)}, u32[]{:S(2)}) %collective-permute-start.6) | collective-permute-done | bytes 135200 | tf_op jit(solution)/shard_map/ppermute | solution.py:246
  22.6 1.1 %collective-permute-done.14.refs_15_ = bf16[528,128]{1,0:T(8,128)(2,1)S(1)} collective-permute-done((bf16[528,128]{1,0:T(8,128)(2,1)S(1)}, bf16[528,128]{1,0:T(8,128)(2,1)S(1)}, u32[]{:S(2)}, u32[]{:S(2)}) %collective-permute-start.14) | collective-permute-done | bytes 135200 | tf_op jit(solution)/shard_map/ppermute | solution.py:303
  23.7 0.9 %couple_relay.1 = (bf16[16,528,128]{2,1,0:T(8,128)(2,1)S(1)}, s32[264,128]{1,0:T(8,128)S(1)}) custom-call(s32[8,32]{1,0:T(8,128)S(4)} %get-tuple-element.13.nbr_ref, bf16[8,2,256,256]{3,2,1,0:T(8,128)(2,1)S(1)} %get-tuple-element.14.esp_ref, bf16[528,128]{1,0:T(8,128)(2,1)S(1)} %fold.1.refs_0_, bf16[528,128]{1,0:T(8,128)(2,1)S(1)} %collective-permute-done.2.refs_1_, ...), custom_call_target="tpu_custom_call" | custom-call | tf_op jit(solution)/shard_map/couple_relay/pallas_call | solution.py:313
  24.6 1.8 %collective-permute-start.15 = (s32[264,128]{1,0:T(8,128)S(1)}, s32[264,128]{1,0:T(8,128)S(1)}, u32[]{:S(2)}, u32[]{:S(2)}) collective-permute-start(s32[264,128]{1,0:T(8,128)S(1)} %get-tuple-element.20), channel_id=1, source_target_pairs={{0,1},{1,0},{2,3},{3,2},{4,5},{5,4},{6,7},{7,6},{8,9},{9,8},{10,11... | collective-permute-start | bytes 405512 | tf_op jit(solution)/shard_map/ppermute | solution.py:243
  26.4 1.6 %couple_rest.1 = (f32[2,264,128]{2,1,0:T(8,128)S(1)}, f32[2,264,128]{2,1,0:T(8,128)S(1)}, s32[264,128]{1,0:T(8,128)S(1)}) custom-call(s32[8,32]{1,0:T(8,128)S(4)} %get-tuple-element.13.nbr_ref, bf16[8,2,256,256]{3,2,1,0:T(8,128)(2,1)S(1)} %get-tuple-element.14.esp_ref, bf16[16,528,128]{2,1,0:T(8,128)(2,1)S(1)} %get-tuple-element.16.refs_0_), custom_call_target="tpu_custom_call" | custom-call | tf_op jit(solution)/shard_map/couple_rest/pallas_call | solution.py:313
  28.0 2.3 %collective-permute-done.15.refs_0_ = s32[264,128]{1,0:T(8,128)S(1)} collective-permute-done((s32[264,128]{1,0:T(8,128)S(1)}, s32[264,128]{1,0:T(8,128)S(1)}, u32[]{:S(2)}, u32[]{:S(2)}) %collective-permute-start.15) | collective-permute-done | bytes 135200 | tf_op jit(solution)/shard_map/ppermute | solution.py:243
  30.5 3.2 %collective-permute-start.17 = (s32[272,128]{1,0:T(8,128)S(1)}, s32[272,128]{1,0:T(8,128)S(1)}, u32[]{:S(2)}, u32[]{:S(2)}) collective-permute-start(s32[272,128]{1,0:T(8,128)S(1)} %merge.1.refs_0_), channel_id=1, source_target_pairs={{0,2},{1,3},{2,0},{3,1},{4,6},{5,7},{6,4},{7,5},{8,10},{9,11},{10,... | collective-permute-start | bytes 417800 | tf_op jit(solution)/shard_map/ppermute | solution.py:243
  33.7 1.8 %collective-permute-start.16 = (s32[264,128]{1,0:T(8,128)S(1)}, s32[264,128]{1,0:T(8,128)S(1)}, u32[]{:S(2)}, u32[]{:S(2)}) collective-permute-start(s32[264,128]{1,0:T(8,128)S(1)} %gate.5), channel_id=1, source_target_pairs={{0,1},{1,0},{2,3},{3,2},{4,5},{5,4},{6,7},{7,6},{8,9},{9,8},{10,11... | collective-permute-start | bytes 405512 | tf_op jit(solution)/shard_map/ppermute | solution.py:243
  35.5 5.1 %collective-permute-done.16.refs_0_ = s32[264,128]{1,0:T(8,128)S(1)} collective-permute-done((s32[264,128]{1,0:T(8,128)S(1)}, s32[264,128]{1,0:T(8,128)S(1)}, u32[]{:S(2)}, u32[]{:S(2)}) %collective-permute-start.16) | collective-permute-done | bytes 135200 | tf_op jit(solution)/shard_map/ppermute | solution.py:243
  40.6 1.0 %finish.1 = f32[2,256,256]{2,1,0:T(8,128)} custom-call(bf16[2,256,256]{2,1,0:T(8,128)(2,1)S(1)} %copy-done.1, f32[2,264,128]{2,1,0:T(8,128)S(1)} %get-tuple-element.17.own_ref, s32[264,128]{1,0:T(8,128)S(1)} %collective-permute-done.16.refs_0_, s32[272,128]{1,0:T(8,128)S(1)} %collective-permute-done.17.refs_1_), custom_call_target="tpu_custom_call" | custom-call | tf_op jit(solution)/shard_map/finish/pallas_call | solution.py:337
  (25 shorter events, 0.8 us)
Async XLA Ops:
  0.0 0.9 %copy-start = (bf16[2,256,256]{2,1,0:T(8,128)(2,1)S(1)}, bf16[2,256,256]{2,1,0:T(8,128)(2,1)}, u32[]{:S(2)}) copy-start(bf16[2,256,256]{2,1,0:T(8,128)(2,1)} %dens_ref.1) | copy-start | bytes 786436
  1.0 10.7 %collective-permute-start.1 = (bf16[528,128]{1,0:T(8,128)(2,1)S(1)}, bf16[528,128]{1,0:T(8,128)(2,1)S(1)}, u32[]{:S(2)}, u32[]{:S(2)}) collective-permute-start(bf16[528,128]{1,0:T(8,128)(2,1)S(1)} %fold.1.refs_0_), channel_id=1, source_target_pairs={{0,2},{1,3},{2,0},{3,1},{4,6},{5,7},{6,4},{7,5},{8,10},{9,11},{10,... | collective-permute-start | bytes 405512 | tf_op jit(solution)/shard_map/ppermute | solution.py:243
  5.1 6.8 %collective-permute-start.2 = (bf16[528,128]{1,0:T(8,128)(2,1)S(1)}, bf16[528,128]{1,0:T(8,128)(2,1)S(1)}, u32[]{:S(2)}, u32[]{:S(2)}) collective-permute-start(bf16[528,128]{1,0:T(8,128)(2,1)S(1)} %fold.1.refs_0_), channel_id=1, source_target_pairs={{0,1},{1,0},{2,3},{3,2},{4,5},{5,4},{6,7},{7,6},{8,9},{9,8},{10,11... | collective-permute-start | bytes 405512 | tf_op jit(solution)/shard_map/ppermute | solution.py:243
  6.7 5.2 %collective-permute-start = (bf16[528,128]{1,0:T(8,128)(2,1)S(1)}, bf16[528,128]{1,0:T(8,128)(2,1)S(1)}, u32[]{:S(2)}, u32[]{:S(2)}) collective-permute-start(bf16[528,128]{1,0:T(8,128)(2,1)S(1)} %fold.1.refs_0_), channel_id=1, source_target_pairs={{0,8},{4,12},{8,0},{12,4},{1,9},{5,13},{9,1},{13,5},{2,10},{6,14},... | collective-permute-start | bytes 405512 | tf_op jit(solution)/shard_map/ppermute | solution.py:246
  8.2 7.3 %collective-permute-start.7 = (bf16[528,128]{1,0:T(8,128)(2,1)S(1)}, bf16[528,128]{1,0:T(8,128)(2,1)S(1)}, u32[]{:S(2)}, u32[]{:S(2)}) collective-permute-start(bf16[528,128]{1,0:T(8,128)(2,1)S(1)} %fold.1.refs_0_), channel_id=1, source_target_pairs={{0,4},{4,0},{8,12},{12,8},{1,5},{5,1},{9,13},{13,9},{2,6},{6,2},{1... | collective-permute-start | bytes 405512 | tf_op jit(solution)/shard_map/ppermute | solution.py:303
  11.9 5.1 %collective-permute-start.3 = (bf16[528,128]{1,0:T(8,128)(2,1)S(1)}, bf16[528,128]{1,0:T(8,128)(2,1)S(1)}, u32[]{:S(2)}, u32[]{:S(2)}) collective-permute-start(bf16[528,128]{1,0:T(8,128)(2,1)S(1)} %gate.4.refs_2_), channel_id=1, source_target_pairs={{0,1},{1,0},{2,3},{3,2},{4,5},{5,4},{6,7},{7,6},{8,9},{9,8},{10,11... | collective-permute-start | bytes 405512 | tf_op jit(solution)/shard_map/ppermute | solution.py:243
  13.4 7.0 %collective-permute-start.8 = (bf16[528,128]{1,0:T(8,128)(2,1)S(1)}, bf16[528,128]{1,0:T(8,128)(2,1)S(1)}, u32[]{:S(2)}, u32[]{:S(2)}) collective-permute-start(bf16[528,128]{1,0:T(8,128)(2,1)S(1)} %collective-permute-done.2.refs_1_), channel_id=1, source_target_pairs={{0,4},{4,0},{8,12},{12,8},{1,5},{5,1},{9,13},{13,9},{2,6},{6,2},{1... | collective-permute-start | bytes 405512 | tf_op jit(solution)/shard_map/ppermute | solution.py:303
  13.4 7.1 %collective-permute-start.9 = (bf16[528,128]{1,0:T(8,128)(2,1)S(1)}, bf16[528,128]{1,0:T(8,128)(2,1)S(1)}, u32[]{:S(2)}, u32[]{:S(2)}) collective-permute-start(bf16[528,128]{1,0:T(8,128)(2,1)S(1)} %gate.4.refs_2_), channel_id=1, source_target_pairs={{0,4},{4,0},{8,12},{12,8},{1,5},{5,1},{9,13},{13,9},{2,6},{6,2},{1... | collective-permute-start | bytes 405512 | tf_op jit(solution)/shard_map/ppermute | solution.py:303
  13.9 7.1 %collective-permute-start.5 = (bf16[528,128]{1,0:T(8,128)(2,1)S(1)}, bf16[528,128]{1,0:T(8,128)(2,1)S(1)}, u32[]{:S(2)}, u32[]{:S(2)}) collective-permute-start(bf16[528,128]{1,0:T(8,128)(2,1)S(1)} %gate.4.refs_2_), channel_id=1, source_target_pairs={{0,8},{4,12},{8,0},{12,4},{1,9},{5,13},{9,1},{13,5},{2,10},{6,14},... | collective-permute-start | bytes 405512 | tf_op jit(solution)/shard_map/ppermute | solution.py:246
  15.5 5.6 %collective-permute-start.4 = (bf16[528,128]{1,0:T(8,128)(2,1)S(1)}, bf16[528,128]{1,0:T(8,128)(2,1)S(1)}, u32[]{:S(2)}, u32[]{:S(2)}) collective-permute-start(bf16[528,128]{1,0:T(8,128)(2,1)S(1)} %collective-permute-done.refs_2_.piece_ref), channel_id=1, source_target_pairs={{0,1},{1,0},{2,3},{3,2},{4,5},{5,4},{6,7},{7,6},{8,9},{9,8},{10,11... | collective-permute-start | bytes 405512 | tf_op jit(solution)/shard_map/ppermute | solution.py:243
  17.0 5.3 %collective-permute-start.6 = (bf16[528,128]{1,0:T(8,128)(2,1)S(1)}, bf16[528,128]{1,0:T(8,128)(2,1)S(1)}, u32[]{:S(2)}, u32[]{:S(2)}) collective-permute-start(bf16[528,128]{1,0:T(8,128)(2,1)S(1)} %collective-permute-done.3.refs_0_.refs_3_), channel_id=1, source_target_pairs={{0,8},{4,12},{8,0},{12,4},{1,9},{5,13},{9,1},{13,5},{2,10},{6,14},... | collective-permute-start | bytes 405512 | tf_op jit(solution)/shard_map/ppermute | solution.py:246
  20.4 2.1 %collective-permute-start.11 = (bf16[528,128]{1,0:T(8,128)(2,1)S(1)}, bf16[528,128]{1,0:T(8,128)(2,1)S(1)}, u32[]{:S(2)}, u32[]{:S(2)}) collective-permute-start(bf16[528,128]{1,0:T(8,128)(2,1)S(1)} %get-tuple-element.15.refs_4_), channel_id=1, source_target_pairs={{0,4},{4,0},{8,12},{12,8},{1,5},{5,1},{9,13},{13,9},{2,6},{6,2},{1... | collective-permute-start | bytes 405512 | tf_op jit(solution)/shard_map/ppermute | solution.py:303
  20.5 1.9 %collective-permute-start.10 = (bf16[528,128]{1,0:T(8,128)(2,1)S(1)}, bf16[528,128]{1,0:T(8,128)(2,1)S(1)}, u32[]{:S(2)}, u32[]{:S(2)}) collective-permute-start(bf16[528,128]{1,0:T(8,128)(2,1)S(1)} %collective-permute-done.3.refs_0_.refs_3_), channel_id=1, source_target_pairs={{0,4},{4,0},{8,12},{12,8},{1,5},{5,1},{9,13},{13,9},{2,6},{6,2},{1... | collective-permute-start | bytes 405512 | tf_op jit(solution)/shard_map/ppermute | solution.py:303
  21.0 1.4 %collective-permute-start.13 = (bf16[528,128]{1,0:T(8,128)(2,1)S(1)}, bf16[528,128]{1,0:T(8,128)(2,1)S(1)}, u32[]{:S(2)}, u32[]{:S(2)}) collective-permute-start(bf16[528,128]{1,0:T(8,128)(2,1)S(1)} %collective-permute-done.5.refs_6_), channel_id=1, source_target_pairs={{0,4},{4,0},{8,12},{12,8},{1,5},{5,1},{9,13},{13,9},{2,6},{6,2},{1... | collective-permute-start | bytes 405512 | tf_op jit(solution)/shard_map/ppermute | solution.py:303
  21.1 1.5 %collective-permute-start.12 = (bf16[528,128]{1,0:T(8,128)(2,1)S(1)}, bf16[528,128]{1,0:T(8,128)(2,1)S(1)}, u32[]{:S(2)}, u32[]{:S(2)}) collective-permute-start(bf16[528,128]{1,0:T(8,128)(2,1)S(1)} %collective-permute-done.4.refs_5_), channel_id=1, source_target_pairs={{0,4},{4,0},{8,12},{12,8},{1,5},{5,1},{9,13},{13,9},{2,6},{6,2},{1... | collective-permute-start | bytes 405512 | tf_op jit(solution)/shard_map/ppermute | solution.py:303
  22.3 1.4 %collective-permute-start.14 = (bf16[528,128]{1,0:T(8,128)(2,1)S(1)}, bf16[528,128]{1,0:T(8,128)(2,1)S(1)}, u32[]{:S(2)}, u32[]{:S(2)}) collective-permute-start(bf16[528,128]{1,0:T(8,128)(2,1)S(1)} %collective-permute-done.6.refs_7_), channel_id=1, source_target_pairs={{0,4},{4,0},{8,12},{12,8},{1,5},{5,1},{9,13},{13,9},{2,6},{6,2},{1... | collective-permute-start | bytes 405512 | tf_op jit(solution)/shard_map/ppermute | solution.py:303
  24.6 5.7 %collective-permute-start.15 = (s32[264,128]{1,0:T(8,128)S(1)}, s32[264,128]{1,0:T(8,128)S(1)}, u32[]{:S(2)}, u32[]{:S(2)}) collective-permute-start(s32[264,128]{1,0:T(8,128)S(1)} %get-tuple-element.20), channel_id=1, source_target_pairs={{0,1},{1,0},{2,3},{3,2},{4,5},{5,4},{6,7},{7,6},{8,9},{9,8},{10,11... | collective-permute-start | bytes 405512 | tf_op jit(solution)/shard_map/ppermute | solution.py:243
  26.4 14.2 %copy-start.1 = (bf16[2,256,256]{2,1,0:T(8,128)(2,1)S(1)}, bf16[2,256,256]{2,1,0:T(8,128)(2,1)}, u32[]{:S(2)}) copy-start(bf16[2,256,256]{2,1,0:T(8,128)(2,1)} %core_ref.1) | copy-start | bytes 786436
  30.5 10.1 %collective-permute-start.17 = (s32[272,128]{1,0:T(8,128)S(1)}, s32[272,128]{1,0:T(8,128)S(1)}, u32[]{:S(2)}, u32[]{:S(2)}) collective-permute-start(s32[272,128]{1,0:T(8,128)S(1)} %merge.1.refs_0_), channel_id=1, source_target_pairs={{0,2},{1,3},{2,0},{3,1},{4,6},{5,7},{6,4},{7,5},{8,10},{9,11},{10,... | collective-permute-start | bytes 417800 | tf_op jit(solution)/shard_map/ppermute | solution.py:243
  33.7 6.9 %collective-permute-start.16 = (s32[264,128]{1,0:T(8,128)S(1)}, s32[264,128]{1,0:T(8,128)S(1)}, u32[]{:S(2)}, u32[]{:S(2)}) collective-permute-start(s32[264,128]{1,0:T(8,128)S(1)} %gate.5), channel_id=1, source_target_pairs={{0,1},{1,0},{2,3},{3,2},{4,5},{5,4},{6,7},{7,6},{8,9},{9,8},{10,11... | collective-permute-start | bytes 405512 | tf_op jit(solution)/shard_map/ppermute | solution.py:243

commit v12 on v11

--- a/solution.py
+++ b/solution.py
@@ -202,10 +202,6 @@
     for ref in coded_refs:
         total = [a + b for a, b in zip(total, read_coded(ref, m, plain_ref.shape[0]))]
     return total
-
-
-def merge_kernel(plain_ref, *refs):
-    write_coded(refs[-1], [summed(plain_ref, refs[:-1], m) for m in range(plain_ref.shape[0])])
 
 
 def finish_kernel(core_ref, own_ref, *refs):
@@ -321,27 +317,22 @@
             name=name,
         )(names, blocks, *pieces)
 
-    steps = range(1, top)
-    filled, *relayed = couple([(top ^ k, True) for k in steps], "couple_relay", pieces, fill=True)
-    relayed = [along_z(unit, k) for k, unit in zip(steps, relayed)]
-    beyond, own, *close = couple([(top, False), (0, False)] + [(k, True) for k in steps], "couple_rest", [filled])
-    beyond = pl.pallas_call(
-        merge_kernel,
-        out_shape=pltpu.VMEM((coded.shape[0] + 8, half), jnp.int32),
-        in_specs=[IN_VMEM] * (1 + len(relayed)),
-        out_specs=IN_VMEM,
-        compiler_params=small,
-        name="merge",
-    )(beyond, *relayed)
-    close = [along_z(gate(unit, beyond), k) for k, unit in zip(steps, close)]
+    filled, beyond = couple([(top, True)], "couple_first", pieces, fill=True)
+    beyond = {top: along_z(beyond, top)}
+    for _ in range(5):
+        beyond[top] = gate(beyond[top])
+    rest = [k for k in range(1, lanes) if k != top]
+    own, *units = couple([(0, False)] + [(k, True) for k in rest], "couple_rest", [filled])
+    for k, unit in zip(rest, units):
+        beyond[k] = along_z(unit, k)
     return pl.pallas_call(
         finish_kernel,
         out_shape=jax.ShapeDtypeStruct((mono_dev, basis, basis), jnp.float32),
-        in_specs=[IN_VMEM] * (3 + len(close)),
+        in_specs=[IN_VMEM] * (1 + lanes),
         out_specs=IN_VMEM,
         compiler_params=small,
         name="finish",
-    )(h_core, own, *close, along_z(beyond, top))
+    )(h_core, own, *[beyond[k] for k in range(1, lanes)])
 
 
 def solution(mesh):

time: 41.8 us -> 40.2 us (0.962)
  starting transfers between devices: 21 us -> 19.2 us
    ppermute x7, starting transfers between devices: 14.6 us -> 12.8 us  [along_z(): return lax.ppermute(piece, 'intra', xor_pairs(lanes, bit))]
  transfers between devices with their start and end apart: 18 -> 18, of which waited for: 8 -> 8; matrix products, arithmetic and copies ran while one was open for 0% -> 0% of each run, Pallas kernels for 8% -> 9%
where the time goes in v12:
time: 40.2 us; the launch traced here: 40 us
  starting transfers between devices  19.2 us (48%)
  waiting for transfers between devices  14.3 us (36%)
  Pallas kernels  5.42 us (13%)
  local copies, waits for them, and re-layouts  0.95 us (2%)
    ppermute x7, starting transfers between devices, along_z(): return lax.ppermute(piece, 'intra', xor_pairs(lanes, bit))  12.8 us
    ppermute x7, waiting for transfers between devices, along_z(): return lax.ppermute(piece, 'intra', xor_pairs(lanes, bit))  12.1 us
    ppermute x3, starting transfers between devices, along_y(): return lax.ppermute(piece, 'gddi', xor_pairs(groups, 2 * y))  4.85 us
    pallas_call x2, Pallas kernels, couple(): pl.pallas_call(functools.partial(couple_kernel, groups, lanes, mono_dev,...  2.63 us
    pallas_call x1, Pallas kernels, local(): pl.pallas_call(stage_kernel, out_shape=[pltpu.SMEM((nbr.shape[1], nbr.sha...  1.62 us
    ppermute x8, starting transfers between devices, local(): lax.ppermute(piece, 'gddi', xor_pairs(groups, 1))  1.59 us
    ppermute x8, waiting for transfers between devices, local(): lax.ppermute(piece, 'gddi', xor_pairs(groups, 1))  1.36 us
    pallas_call x1, Pallas kernels, local(): pl.pallas_call(finish_kernel, out_shape=jax.ShapeDtypeStruct((mono_dev, b...  1.04 us
  transfers between devices with their start and end apart: 18, of which 8 were waited for; matrix products, arithmetic and copies ran while one was open for 0% of the time, Pallas kernels for 9%

profile of v12, /device:TPU:0, one launch (start us, length us, event | category | flops | bytes accessed | tf_op | source)
XLA Modules:
  0.0 40.0 jit_solution(3677442509379460001)
XLA Ops:
  0.0 0.9 %copy-done = bf16[2,256,256]{2,1,0:T(8,128)(2,1)S(1)} copy-done((bf16[2,256,256]{2,1,0:T(8,128)(2,1)S(1)}, bf16[2,256,256]{2,1,0:T(8,128)(2,1)}, u32[]{:S(2)}) %copy-start) | copy-done | bytes 262168
  1.0 4.1 %collective-permute-start.1 = (bf16[528,128]{1,0:T(8,128)(2,1)S(1)}, bf16[528,128]{1,0:T(8,128)(2,1)S(1)}, u32[]{:S(2)}, u32[]{:S(2)}) collective-permute-start(bf16[528,128]{1,0:T(8,128)(2,1)S(1)} %fold.1.refs_0_), channel_id=1, source_target_pairs={{0,2},{1,3},{2,0},{3,1},{4,6},{5,7},{6,4},{7,5},{8,10},{9,11},{10,... | collective-permute-start | bytes 405512 | tf_op jit(solution)/shard_map/ppermute | solution.py:239
  5.1 1.6 %collective-permute-start.2 = (bf16[528,128]{1,0:T(8,128)(2,1)S(1)}, bf16[528,128]{1,0:T(8,128)(2,1)S(1)}, u32[]{:S(2)}, u32[]{:S(2)}) collective-permute-start(bf16[528,128]{1,0:T(8,128)(2,1)S(1)} %fold.1.refs_0_), channel_id=1, source_target_pairs={{0,1},{1,0},{2,3},{3,2},{4,5},{5,4},{6,7},{7,6},{8,9},{9,8},{10,11... | collective-permute-start | bytes 405512 | tf_op jit(solution)/shard_map/ppermute | solution.py:239
  6.7 1.5 %collective-permute-start = (bf16[528,128]{1,0:T(8,128)(2,1)S(1)}, bf16[528,128]{1,0:T(8,128)(2,1)S(1)}, u32[]{:S(2)}, u32[]{:S(2)}) collective-permute-start(bf16[528,128]{1,0:T(8,128)(2,1)S(1)} %fold.1.refs_0_), channel_id=1, source_target_pairs={{0,8},{4,12},{8,0},{12,4},{1,9},{5,13},{9,1},{13,5},{2,10},{6,14},... | collective-permute-start | bytes 405512 | tf_op jit(solution)/shard_map/ppermute | solution.py:242
  8.2 3.5 %collective-permute-done.1.piece_ref = bf16[528,128]{1,0:T(8,128)(2,1)S(1)} collective-permute-done((bf16[528,128]{1,0:T(8,128)(2,1)S(1)}, bf16[528,128]{1,0:T(8,128)(2,1)S(1)}, u32[]{:S(2)}, u32[]{:S(2)}) %collective-permute-start.1) | collective-permute-done | bytes 135200 | tf_op jit(solution)/shard_map/ppermute | solution.py:239
  11.9 1.5 %collective-permute-start.3 = (bf16[528,128]{1,0:T(8,128)(2,1)S(1)}, bf16[528,128]{1,0:T(8,128)(2,1)S(1)}, u32[]{:S(2)}, u32[]{:S(2)}) collective-permute-start(bf16[528,128]{1,0:T(8,128)(2,1)S(1)} %gate.8.refs_2_), channel_id=1, source_target_pairs={{0,1},{1,0},{2,3},{3,2},{4,5},{5,4},{6,7},{7,6},{8,9},{9,8},{10,11... | collective-permute-start | bytes 405512 | tf_op jit(solution)/shard_map/ppermute | solution.py:239
  13.4 0.5 %collective-permute-start.9 = (bf16[528,128]{1,0:T(8,128)(2,1)S(1)}, bf16[528,128]{1,0:T(8,128)(2,1)S(1)}, u32[]{:S(2)}, u32[]{:S(2)}) collective-permute-start(bf16[528,128]{1,0:T(8,128)(2,1)S(1)} %gate.8.refs_2_), channel_id=1, source_target_pairs={{0,4},{4,0},{8,12},{12,8},{1,5},{5,1},{9,13},{13,9},{2,6},{6,2},{1... | collective-permute-start | bytes 405512 | tf_op jit(solution)/shard_map/ppermute | solution.py:299
  13.9 1.5 %collective-permute-start.5 = (bf16[528,128]{1,0:T(8,128)(2,1)S(1)}, bf16[528,128]{1,0:T(8,128)(2,1)S(1)}, u32[]{:S(2)}, u32[]{:S(2)}) collective-permute-start(bf16[528,128]{1,0:T(8,128)(2,1)S(1)} %gate.8.refs_2_), channel_id=1, source_target_pairs={{0,8},{4,12},{8,0},{12,4},{1,9},{5,13},{9,1},{13,5},{2,10},{6,14},... | collective-permute-start | bytes 405512 | tf_op jit(solution)/shard_map/ppermute | solution.py:242
  15.5 0.6 %collective-permute-start.4 = (bf16[528,128]{1,0:T(8,128)(2,1)S(1)}, bf16[528,128]{1,0:T(8,128)(2,1)S(1)}, u32[]{:S(2)}, u32[]{:S(2)}) collective-permute-start(bf16[528,128]{1,0:T(8,128)(2,1)S(1)} %collective-permute-done.refs_2_.piece_ref), channel_id=1, source_target_pairs={{0,1},{1,0},{2,3},{3,2},{4,5},{5,4},{6,7},{7,6},{8,9},{9,8},{10,11... | collective-permute-start | bytes 405512 | tf_op jit(solution)/shard_map/ppermute | solution.py:239
  16.1 0.9 %collective-permute-done.3.refs_0_.refs_3_ = bf16[528,128]{1,0:T(8,128)(2,1)S(1)} collective-permute-done((bf16[528,128]{1,0:T(8,128)(2,1)S(1)}, bf16[528,128]{1,0:T(8,128)(2,1)S(1)}, u32[]{:S(2)}, u32[]{:S(2)}) %collective-permute-start.3) | collective-permute-done | bytes 135200 | tf_op jit(solution)/shard_map/ppermute | solution.py:239
  17.0 1.8 %collective-permute-start.6 = (bf16[528,128]{1,0:T(8,128)(2,1)S(1)}, bf16[528,128]{1,0:T(8,128)(2,1)S(1)}, u32[]{:S(2)}, u32[]{:S(2)}) collective-permute-start(bf16[528,128]{1,0:T(8,128)(2,1)S(1)} %collective-permute-done.3.refs_0_.refs_3_), channel_id=1, source_target_pairs={{0,8},{4,12},{8,0},{12,4},{1,9},{5,13},{9,1},{13,5},{2,10},{6,14},... | collective-permute-start | bytes 405512 | tf_op jit(solution)/shard_map/ppermute | solution.py:242
  18.8 1.6 %stage.1 = (s32[8,32]{1,0:T(8,128)S(4)}, bf16[8,2,256,256]{3,2,1,0:T(8,128)(2,1)S(1)}, bf16[528,128]{1,0:T(8,128)(2,1)S(1)}) custom-call(s32[8,32]{1,0:T(8,128)} %bitcast.1, bf16[8,2,256,256]{3,2,1,0:T(8,128)(2,1)} %esp_ref.1, bf16[528,128]{1,0:T(8,128)(2,1)S(1)} %collective-permute-done.refs_2_.piece_ref, ...), custom_call_target="tpu_custom_call" | custom-call | tf_op jit(solution)/shard_map/stage/pallas_call | solution.py:279
  20.5 0.5 %collective-permute-start.10 = (bf16[528,128]{1,0:T(8,128)(2,1)S(1)}, bf16[528,128]{1,0:T(8,128)(2,1)S(1)}, u32[]{:S(2)}, u32[]{:S(2)}) collective-permute-start(bf16[528,128]{1,0:T(8,128)(2,1)S(1)} %collective-permute-done.3.refs_0_.refs_3_), channel_id=1, source_target_pairs={{0,4},{4,0},{8,12},{12,8},{1,5},{5,1},{9,13},{13,9},{2,6},{6,2},{1... | collective-permute-start | bytes 405512 | tf_op jit(solution)/shard_map/ppermute | solution.py:299
  21.1 0.4 %collective-permute-start.12 = (bf16[528,128]{1,0:T(8,128)(2,1)S(1)}, bf16[528,128]{1,0:T(8,128)(2,1)S(1)}, u32[]{:S(2)}, u32[]{:S(2)}) collective-permute-start(bf16[528,128]{1,0:T(8,128)(2,1)S(1)} %collective-permute-done.4.refs_5_), channel_id=1, source_target_pairs={{0,4},{4,0},{8,12},{12,8},{1,5},{5,1},{9,13},{13,9},{2,6},{6,2},{1... | collective-permute-start | bytes 405512 | tf_op jit(solution)/shard_map/ppermute | solution.py:299
  21.5 0.8 %collective-permute-done.6.refs_7_ = bf16[528,128]{1,0:T(8,128)(2,1)S(1)} collective-permute-done((bf16[528,128]{1,0:T(8,128)(2,1)S(1)}, bf16[528,128]{1,0:T(8,128)(2,1)S(1)}, u32[]{:S(2)}, u32[]{:S(2)}) %collective-permute-start.6) | collective-permute-done | bytes 135200 | tf_op jit(solution)/shard_map/ppermute | solution.py:242
  22.4 0.2 collective-permute-done.12.refs_13_
  22.6 1.1 %collective-permute-done.14.refs_15_ = bf16[528,128]{1,0:T(8,128)(2,1)S(1)} collective-permute-done((bf16[528,128]{1,0:T(8,128)(2,1)S(1)}, bf16[528,128]{1,0:T(8,128)(2,1)S(1)}, u32[]{:S(2)}, u32[]{:S(2)}) %collective-permute-start.14) | collective-permute-done | bytes 135200 | tf_op jit(solution)/shard_map/ppermute | solution.py:299
  23.7 0.9 %couple_first.1 = (bf16[16,528,128]{2,1,0:T(8,128)(2,1)S(1)}, s32[264,128]{1,0:T(8,128)S(1)}) custom-call(s32[8,32]{1,0:T(8,128)S(4)} %get-tuple-element.13.nbr_ref, bf16[8,2,256,256]{3,2,1,0:T(8,128)(2,1)S(1)} %get-tuple-element.14.esp_ref, bf16[528,128]{1,0:T(8,128)(2,1)S(1)} %fold.1.refs_0_, bf16[528,128]{1,0:T(8,128)(2,1)S(1)} %collective-permute-done.2.refs_1_, ...), custom_call_target="tpu_custom_call" | custom-call | tf_op jit(solution)/shard_map/couple_first/pallas_call | solution.py:309
  24.6 2.5 %collective-permute-start.16 = (s32[264,128]{1,0:T(8,128)S(1)}, s32[264,128]{1,0:T(8,128)S(1)}, u32[]{:S(2)}, u32[]{:S(2)}) collective-permute-start(s32[264,128]{1,0:T(8,128)S(1)} %get-tuple-element.19), channel_id=1, source_target_pairs={{0,2},{1,3},{2,0},{3,1},{4,6},{5,7},{6,4},{7,5},{8,10},{9,11},{10,... | collective-permute-start | bytes 405512 | tf_op jit(solution)/shard_map/ppermute | solution.py:239
  27.1 1.7 %couple_rest.1 = (f32[2,264,128]{2,1,0:T(8,128)S(1)}, s32[264,128]{1,0:T(8,128)S(1)}, s32[264,128]{1,0:T(8,128)S(1)}) custom-call(s32[8,32]{1,0:T(8,128)S(4)} %get-tuple-element.13.nbr_ref, bf16[8,2,256,256]{3,2,1,0:T(8,128)(2,1)S(1)} %get-tuple-element.14.esp_ref, bf16[16,528,128]{2,1,0:T(8,128)(2,1)S(1)} %get-tuple-element.16.refs_0_), custom_call_target="tpu_custom_call" | custom-call | tf_op jit(solution)/shard_map/couple_rest/pallas_call | solution.py:309
  28.8 2.5 %collective-permute-start.15 = (s32[264,128]{1,0:T(8,128)S(1)}, s32[264,128]{1,0:T(8,128)S(1)}, u32[]{:S(2)}, u32[]{:S(2)}) collective-permute-start(s32[264,128]{1,0:T(8,128)S(1)} %get-tuple-element.18), channel_id=1, source_target_pairs={{0,1},{1,0},{2,3},{3,2},{4,5},{5,4},{6,7},{7,6},{8,9},{9,8},{10,11... | collective-permute-start | bytes 405512 | tf_op jit(solution)/shard_map/ppermute | solution.py:239
  31.3 3.5 %collective-permute-done.16.piece_ref = s32[264,128]{1,0:T(8,128)S(1)} collective-permute-done((s32[264,128]{1,0:T(8,128)S(1)}, s32[264,128]{1,0:T(8,128)S(1)}, u32[]{:S(2)}, u32[]{:S(2)}) %collective-permute-start.16) | collective-permute-done | bytes 135200 | tf_op jit(solution)/shard_map/ppermute | solution.py:239
  34.9 4.1 %collective-permute-done.15.refs_0_ = s32[264,128]{1,0:T(8,128)S(1)} collective-permute-done((s32[264,128]{1,0:T(8,128)S(1)}, s32[264,128]{1,0:T(8,128)S(1)}, u32[]{:S(2)}, u32[]{:S(2)}) %collective-permute-start.15) | collective-permute-done | bytes 135200 | tf_op jit(solution)/shard_map/ppermute | solution.py:239
  39.0 1.0 %finish.1 = f32[2,256,256]{2,1,0:T(8,128)} custom-call(bf16[2,256,256]{2,1,0:T(8,128)(2,1)S(1)} %copy-done.1, f32[2,264,128]{2,1,0:T(8,128)S(1)} %get-tuple-element.17.own_ref, s32[264,128]{1,0:T(8,128)S(1)} %collective-permute-done.15.refs_0_, s32[264,128]{1,0:T(8,128)S(1)} %gate.13.refs_1_, s32[264,128]{1,0:T(8,128)S(1)} %collective-permute-done.17.refs_2_), custom_call_target="tpu_custom_call" | custom-call | tf_op jit(solution)/shard_map/finish/pallas_call | solution.py:328
  (28 shorter events, 0.5 us)
Async XLA Ops:
  0.0 0.9 %copy-start = (bf16[2,256,256]{2,1,0:T(8,128)(2,1)S(1)}, bf16[2,256,256]{2,1,0:T(8,128)(2,1)}, u32[]{:S(2)}) copy-start(bf16[2,256,256]{2,1,0:T(8,128)(2,1)} %dens_ref.1) | copy-start | bytes 786436
  1.0 10.7 %collective-permute-start.1 = (bf16[528,128]{1,0:T(8,128)(2,1)S(1)}, bf16[528,128]{1,0:T(8,128)(2,1)S(1)}, u32[]{:S(2)}, u32[]{:S(2)}) collective-permute-start(bf16[528,128]{1,0:T(8,128)(2,1)S(1)} %fold.1.refs_0_), channel_id=1, source_target_pairs={{0,2},{1,3},{2,0},{3,1},{4,6},{5,7},{6,4},{7,5},{8,10},{9,11},{10,... | collective-permute-start | bytes 405512 | tf_op jit(solution)/shard_map/ppermute | solution.py:239
  5.1 6.8 %collective-permute-start.2 = (bf16[528,128]{1,0:T(8,128)(2,1)S(1)}, bf16[528,128]{1,0:T(8,128)(2,1)S(1)}, u32[]{:S(2)}, u32[]{:S(2)}) collective-permute-start(bf16[528,128]{1,0:T(8,128)(2,1)S(1)} %fold.1.refs_0_), channel_id=1, source_target_pairs={{0,1},{1,0},{2,3},{3,2},{4,5},{5,4},{6,7},{7,6},{8,9},{9,8},{10,11... | collective-permute-start | bytes 405512 | tf_op jit(solution)/shard_map/ppermute | solution.py:239
  6.7 5.2 %collective-permute-start = (bf16[528,128]{1,0:T(8,128)(2,1)S(1)}, bf16[528,128]{1,0:T(8,128)(2,1)S(1)}, u32[]{:S(2)}, u32[]{:S(2)}) collective-permute-start(bf16[528,128]{1,0:T(8,128)(2,1)S(1)} %fold.1.refs_0_), channel_id=1, source_target_pairs={{0,8},{4,12},{8,0},{12,4},{1,9},{5,13},{9,1},{13,5},{2,10},{6,14},... | collective-permute-start | bytes 405512 | tf_op jit(solution)/shard_map/ppermute | solution.py:242
  8.2 7.3 %collective-permute-start.7 = (bf16[528,128]{1,0:T(8,128)(2,1)S(1)}, bf16[528,128]{1,0:T(8,128)(2,1)S(1)}, u32[]{:S(2)}, u32[]{:S(2)}) collective-permute-start(bf16[528,128]{1,0:T(8,128)(2,1)S(1)} %fold.1.refs_0_), channel_id=1, source_target_pairs={{0,4},{4,0},{8,12},{12,8},{1,5},{5,1},{9,13},{13,9},{2,6},{6,2},{1... | collective-permute-start | bytes 405512 | tf_op jit(solution)/shard_map/ppermute | solution.py:299
  11.9 5.1 %collective-permute-start.3 = (bf16[528,128]{1,0:T(8,128)(2,1)S(1)}, bf16[528,128]{1,0:T(8,128)(2,1)S(1)}, u32[]{:S(2)}, u32[]{:S(2)}) collective-permute-start(bf16[528,128]{1,0:T(8,128)(2,1)S(1)} %gate.8.refs_2_), channel_id=1, source_target_pairs={{0,1},{1,0},{2,3},{3,2},{4,5},{5,4},{6,7},{7,6},{8,9},{9,8},{10,11... | collective-permute-start | bytes 405512 | tf_op jit(solution)/shard_map/ppermute | solution.py:239
  13.4 7.0 %collective-permute-start.8 = (bf16[528,128]{1,0:T(8,128)(2,1)S(1)}, bf16[528,128]{1,0:T(8,128)(2,1)S(1)}, u32[]{:S(2)}, u32[]{:S(2)}) collective-permute-start(bf16[528,128]{1,0:T(8,128)(2,1)S(1)} %collective-permute-done.2.refs_1_), channel_id=1, source_target_pairs={{0,4},{4,0},{8,12},{12,8},{1,5},{5,1},{9,13},{13,9},{2,6},{6,2},{1... | collective-permute-start | bytes 405512 | tf_op jit(solution)/shard_map/ppermute | solution.py:299
  13.4 7.1 %collective-permute-start.9 = (bf16[528,128]{1,0:T(8,128)(2,1)S(1)}, bf16[528,128]{1,0:T(8,128)(2,1)S(1)}, u32[]{:S(2)}, u32[]{:S(2)}) collective-permute-start(bf16[528,128]{1,0:T(8,128)(2,1)S(1)} %gate.8.refs_2_), channel_id=1, source_target_pairs={{0,4},{4,0},{8,12},{12,8},{1,5},{5,1},{9,13},{13,9},{2,6},{6,2},{1... | collective-permute-start | bytes 405512 | tf_op jit(solution)/shard_map/ppermute | solution.py:299
  13.9 7.1 %collective-permute-start.5 = (bf16[528,128]{1,0:T(8,128)(2,1)S(1)}, bf16[528,128]{1,0:T(8,128)(2,1)S(1)}, u32[]{:S(2)}, u32[]{:S(2)}) collective-permute-start(bf16[528,128]{1,0:T(8,128)(2,1)S(1)} %gate.8.refs_2_), channel_id=1, source_target_pairs={{0,8},{4,12},{8,0},{12,4},{1,9},{5,13},{9,1},{13,5},{2,10},{6,14},... | collective-permute-start | bytes 405512 | tf_op jit(solution)/shard_map/ppermute | solution.py:242
  15.5 5.6 %collective-permute-start.4 = (bf16[528,128]{1,0:T(8,128)(2,1)S(1)}, bf16[528,128]{1,0:T(8,128)(2,1)S(1)}, u32[]{:S(2)}, u32[]{:S(2)}) collective-permute-start(bf16[528,128]{1,0:T(8,128)(2,1)S(1)} %collective-permute-done.refs_2_.piece_ref), channel_id=1, source_target_pairs={{0,1},{1,0},{2,3},{3,2},{4,5},{5,4},{6,7},{7,6},{8,9},{9,8},{10,11... | collective-permute-start | bytes 405512 | tf_op jit(solution)/shard_map/ppermute | solution.py:239
  17.0 5.3 %collective-permute-start.6 = (bf16[528,128]{1,0:T(8,128)(2,1)S(1)}, bf16[528,128]{1,0:T(8,128)(2,1)S(1)}, u32[]{:S(2)}, u32[]{:S(2)}) collective-permute-start(bf16[528,128]{1,0:T(8,128)(2,1)S(1)} %collective-permute-done.3.refs_0_.refs_3_), channel_id=1, source_target_pairs={{0,8},{4,12},{8,0},{12,4},{1,9},{5,13},{9,1},{13,5},{2,10},{6,14},... | collective-permute-start | bytes 405512 | tf_op jit(solution)/shard_map/ppermute | solution.py:242
  20.4 2.1 %collective-permute-start.11 = (bf16[528,128]{1,0:T(8,128)(2,1)S(1)}, bf16[528,128]{1,0:T(8,128)(2,1)S(1)}, u32[]{:S(2)}, u32[]{:S(2)}) collective-permute-start(bf16[528,128]{1,0:T(8,128)(2,1)S(1)} %get-tuple-element.15.refs_4_), channel_id=1, source_target_pairs={{0,4},{4,0},{8,12},{12,8},{1,5},{5,1},{9,13},{13,9},{2,6},{6,2},{1... | collective-permute-start | bytes 405512 | tf_op jit(solution)/shard_map/ppermute | solution.py:299
  20.5 1.9 %collective-permute-start.10 = (bf16[528,128]{1,0:T(8,128)(2,1)S(1)}, bf16[528,128]{1,0:T(8,128)(2,1)S(1)}, u32[]{:S(2)}, u32[]{:S(2)}) collective-permute-start(bf16[528,128]{1,0:T(8,128)(2,1)S(1)} %collective-permute-done.3.refs_0_.refs_3_), channel_id=1, source_target_pairs={{0,4},{4,0},{8,12},{12,8},{1,5},{5,1},{9,13},{13,9},{2,6},{6,2},{1... | collective-permute-start | bytes 405512 | tf_op jit(solution)/shard_map/ppermute | solution.py:299
  21.0 1.4 %collective-permute-start.13 = (bf16[528,128]{1,0:T(8,128)(2,1)S(1)}, bf16[528,128]{1,0:T(8,128)(2,1)S(1)}, u32[]{:S(2)}, u32[]{:S(2)}) collective-permute-start(bf16[528,128]{1,0:T(8,128)(2,1)S(1)} %collective-permute-done.5.refs_6_), channel_id=1, source_target_pairs={{0,4},{4,0},{8,12},{12,8},{1,5},{5,1},{9,13},{13,9},{2,6},{6,2},{1... | collective-permute-start | bytes 405512 | tf_op jit(solution)/shard_map/ppermute | solution.py:299
  21.1 1.5 %collective-permute-start.12 = (bf16[528,128]{1,0:T(8,128)(2,1)S(1)}, bf16[528,128]{1,0:T(8,128)(2,1)S(1)}, u32[]{:S(2)}, u32[]{:S(2)}) collective-permute-start(bf16[528,128]{1,0:T(8,128)(2,1)S(1)} %collective-permute-done.4.refs_5_), channel_id=1, source_target_pairs={{0,4},{4,0},{8,12},{12,8},{1,5},{5,1},{9,13},{13,9},{2,6},{6,2},{1... | collective-permute-start | bytes 405512 | tf_op jit(solution)/shard_map/ppermute | solution.py:299
  22.3 1.4 %collective-permute-start.14 = (bf16[528,128]{1,0:T(8,128)(2,1)S(1)}, bf16[528,128]{1,0:T(8,128)(2,1)S(1)}, u32[]{:S(2)}, u32[]{:S(2)}) collective-permute-start(bf16[528,128]{1,0:T(8,128)(2,1)S(1)} %collective-permute-done.6.refs_7_), channel_id=1, source_target_pairs={{0,4},{4,0},{8,12},{12,8},{1,5},{5,1},{9,13},{13,9},{2,6},{6,2},{1... | collective-permute-start | bytes 405512 | tf_op jit(solution)/shard_map/ppermute | solution.py:299
  24.6 10.2 %collective-permute-start.16 = (s32[264,128]{1,0:T(8,128)S(1)}, s32[264,128]{1,0:T(8,128)S(1)}, u32[]{:S(2)}, u32[]{:S(2)}) collective-permute-start(s32[264,128]{1,0:T(8,128)S(1)} %get-tuple-element.19), channel_id=1, source_target_pairs={{0,2},{1,3},{2,0},{3,1},{4,6},{5,7},{6,4},{7,5},{8,10},{9,11},{10,... | collective-permute-start | bytes 405512 | tf_op jit(solution)/shard_map/ppermute | solution.py:239
  27.1 11.9 %copy-start.1 = (bf16[2,256,256]{2,1,0:T(8,128)(2,1)S(1)}, bf16[2,256,256]{2,1,0:T(8,128)(2,1)}, u32[]{:S(2)}) copy-start(bf16[2,256,256]{2,1,0:T(8,128)(2,1)} %core_ref.1) | copy-start | bytes 786436
  28.8 10.2 %collective-permute-start.15 = (s32[264,128]{1,0:T(8,128)S(1)}, s32[264,128]{1,0:T(8,128)S(1)}, u32[]{:S(2)}, u32[]{:S(2)}) collective-permute-start(s32[264,128]{1,0:T(8,128)S(1)} %get-tuple-element.18), channel_id=1, source_target_pairs={{0,1},{1,0},{2,3},{3,2},{4,5},{5,4},{6,7},{7,6},{8,9},{9,8},{10,11... | collective-permute-start | bytes 405512 | tf_op jit(solution)/shard_map/ppermute | solution.py:239
  31.3 7.7 %collective-permute-start.17 = (s32[264,128]{1,0:T(8,128)S(1)}, s32[264,128]{1,0:T(8,128)S(1)}, u32[]{:S(2)}, u32[]{:S(2)}) collective-permute-start(s32[264,128]{1,0:T(8,128)S(1)} %get-tuple-element.20), channel_id=1, source_target_pairs={{0,3},{1,2},{2,1},{3,0},{4,7},{5,6},{6,5},{7,4},{8,11},{9,10},{10,... | collective-permute-start | bytes 405512 | tf_op jit(solution)/shard_map/ppermute | solution.py:239

commit v13 on v12

--- a/solution.py
+++ b/solution.py
@@ -272,7 +272,7 @@
     double(top)
     for y in range(1, rows_y):
         for k in range(1, top):
-            near[y, k] = along_z(near[y, k & (k - 1)], k & -k)
+            near[y, k] = along_z(gate(near[y, k & (k - 1)], near[0, lanes - 1]), k & -k)
         for k in range(top, lanes):
             near[y, k] = along_y(near[0, k], y)
 
@@ -297,6 +297,8 @@
     keys = [(y, k) for y in range(rows_y) for k in range(lanes)]
     mine = [near[key] for key in keys]
     pieces = mine + [lax.ppermute(piece, "gddi", xor_pairs(groups, 1)) for piece in mine]
+    least = len(mine) + (rows_y - 1) * lanes + top - 1
+    pieces = [gate(piece) if i >= len(mine) and i != least else piece for i, piece in enumerate(pieces)]
 
     plain = pltpu.VMEM((mono_dev, basis + 8, half), jnp.float32)
     coded = pltpu.VMEM((mono_dev * half + round_up(2 * mono_dev, 8), half), jnp.int32)

time: 40.2 us -> 41.5 us (1.032)
  waiting for transfers between devices: 14.3 us -> 15.3 us
    ppermute x7, waiting for transfers between devices: 12.1 us -> 14.1 us  [along_z(): return lax.ppermute(piece, 'intra', xor_pairs(lanes, bit))]
    ppermute x3, waiting for transfers between devices: 0.81 us -> 0.01 us  [along_y(): return lax.ppermute(piece, 'gddi', xor_pairs(groups, 2 * y))]
  transfers between devices with their start and end apart: 18 -> 18, of which waited for: 8 -> 7; matrix products, arithmetic and copies ran while one was open for 0% -> 0% of each run, Pallas kernels for 9% -> 8%
where the time goes in v13:
time: 41.5 us; the launch traced here: 41.3 us
  starting transfers between devices  19.4 us (47%)
  waiting for transfers between devices  15.3 us (37%)
  Pallas kernels  5.51 us (13%)
  local copies, waits for them, and re-layouts  0.95 us (2%)
    ppermute x7, waiting for transfers between devices, along_z(): return lax.ppermute(piece, 'intra', xor_pairs(lanes, bit))  14.1 us
    ppermute x7, starting transfers between devices, along_z(): return lax.ppermute(piece, 'intra', xor_pairs(lanes, bit))  13.1 us
    ppermute x3, starting transfers between devices, along_y(): return lax.ppermute(piece, 'gddi', xor_pairs(groups, 2 * y))  4.67 us
    pallas_call x2, Pallas kernels, couple(): pl.pallas_call(functools.partial(couple_kernel, groups, lanes, mono_dev,...  2.63 us
    pallas_call x1, Pallas kernels, local(): pl.pallas_call(stage_kernel, out_shape=[pltpu.SMEM((nbr.shape[1], nbr.sha...  1.62 us
    ppermute x8, starting transfers between devices, local(): lax.ppermute(piece, 'gddi', xor_pairs(groups, 1))  1.59 us
    ppermute x8, waiting for transfers between devices, local(): lax.ppermute(piece, 'gddi', xor_pairs(groups, 1))  1.21 us
    pallas_call x1, Pallas kernels, local(): pl.pallas_call(finish_kernel, out_shape=jax.ShapeDtypeStruct((mono_dev, b...  1.04 us
  transfers between devices with their start and end apart: 18, of which 7 were waited for; matrix products, arithmetic and copies ran while one was open for 0% of the time, Pallas kernels for 8%

profile of v13, /device:TPU:0, one launch (start us, length us, event | category | flops | bytes accessed | tf_op | source)
XLA Modules:
  0.0 41.3 jit_solution(14789947469985386352)
XLA Ops:
  0.0 0.9 %copy-done = bf16[2,256,256]{2,1,0:T(8,128)(2,1)S(1)} copy-done((bf16[2,256,256]{2,1,0:T(8,128)(2,1)S(1)}, bf16[2,256,256]{2,1,0:T(8,128)(2,1)}, u32[]{:S(2)}) %copy-start) | copy-done | bytes 262168
  1.0 4.1 %collective-permute-start.1 = (bf16[528,128]{1,0:T(8,128)(2,1)S(1)}, bf16[528,128]{1,0:T(8,128)(2,1)S(1)}, u32[]{:S(2)}, u32[]{:S(2)}) collective-permute-start(bf16[528,128]{1,0:T(8,128)(2,1)S(1)} %fold.1.refs_0_), channel_id=1, source_target_pairs={{0,2},{1,3},{2,0},{3,1},{4,6},{5,7},{6,4},{7,5},{8,10},{9,11},{10,... | collective-permute-start | bytes 405512 | tf_op jit(solution)/shard_map/ppermute | solution.py:239
  5.1 1.6 %collective-permute-start.2 = (bf16[528,128]{1,0:T(8,128)(2,1)S(1)}, bf16[528,128]{1,0:T(8,128)(2,1)S(1)}, u32[]{:S(2)}, u32[]{:S(2)}) collective-permute-start(bf16[528,128]{1,0:T(8,128)(2,1)S(1)} %fold.1.refs_0_), channel_id=1, source_target_pairs={{0,1},{1,0},{2,3},{3,2},{4,5},{5,4},{6,7},{7,6},{8,9},{9,8},{10,11... | collective-permute-start | bytes 405512 | tf_op jit(solution)/shard_map/ppermute | solution.py:239
  6.7 1.5 %collective-permute-start = (bf16[528,128]{1,0:T(8,128)(2,1)S(1)}, bf16[528,128]{1,0:T(8,128)(2,1)S(1)}, u32[]{:S(2)}, u32[]{:S(2)}) collective-permute-start(bf16[528,128]{1,0:T(8,128)(2,1)S(1)} %fold.1.refs_0_), channel_id=1, source_target_pairs={{0,8},{4,12},{8,0},{12,4},{1,9},{5,13},{9,1},{13,5},{2,10},{6,14},... | collective-permute-start | bytes 405512 | tf_op jit(solution)/shard_map/ppermute | solution.py:242
  8.2 3.5 %collective-permute-done.1.piece_ref = bf16[528,128]{1,0:T(8,128)(2,1)S(1)} collective-permute-done((bf16[528,128]{1,0:T(8,128)(2,1)S(1)}, bf16[528,128]{1,0:T(8,128)(2,1)S(1)}, u32[]{:S(2)}, u32[]{:S(2)}) %collective-permute-start.1) | collective-permute-done | bytes 135200 | tf_op jit(solution)/shard_map/ppermute | solution.py:239
  11.9 1.5 %collective-permute-start.3 = (bf16[528,128]{1,0:T(8,128)(2,1)S(1)}, bf16[528,128]{1,0:T(8,128)(2,1)S(1)}, u32[]{:S(2)}, u32[]{:S(2)}) collective-permute-start(bf16[528,128]{1,0:T(8,128)(2,1)S(1)} %gate.16.refs_2_), channel_id=1, source_target_pairs={{0,1},{1,0},{2,3},{3,2},{4,5},{5,4},{6,7},{7,6},{8,9},{9,8},{10,11... | collective-permute-start | bytes 405512 | tf_op jit(solution)/shard_map/ppermute | solution.py:239
  13.4 1.5 %collective-permute-start.5 = (bf16[528,128]{1,0:T(8,128)(2,1)S(1)}, bf16[528,128]{1,0:T(8,128)(2,1)S(1)}, u32[]{:S(2)}, u32[]{:S(2)}) collective-permute-start(bf16[528,128]{1,0:T(8,128)(2,1)S(1)} %gate.16.refs_2_), channel_id=1, source_target_pairs={{0,8},{4,12},{8,0},{12,4},{1,9},{5,13},{9,1},{13,5},{2,10},{6,14},... | collective-permute-start | bytes 405512 | tf_op jit(solution)/shard_map/ppermute | solution.py:242
  15.0 0.2 collective-permute-start.8
  15.2 0.3 collective-permute-start.9
  15.5 1.5 %collective-permute-done.3.refs_0_.refs_3_ = bf16[528,128]{1,0:T(8,128)(2,1)S(1)} collective-permute-done((bf16[528,128]{1,0:T(8,128)(2,1)S(1)}, bf16[528,128]{1,0:T(8,128)(2,1)S(1)}, u32[]{:S(2)}, u32[]{:S(2)}) %collective-permute-start.3) | collective-permute-done | bytes 135200 | tf_op jit(solution)/shard_map/ppermute | solution.py:239
  17.0 1.6 %collective-permute-start.6 = (bf16[528,128]{1,0:T(8,128)(2,1)S(1)}, bf16[528,128]{1,0:T(8,128)(2,1)S(1)}, u32[]{:S(2)}, u32[]{:S(2)}) collective-permute-start(bf16[528,128]{1,0:T(8,128)(2,1)S(1)} %collective-permute-done.3.refs_0_.refs_3_), channel_id=1, source_target_pairs={{0,8},{4,12},{8,0},{12,4},{1,9},{5,13},{9,1},{13,5},{2,10},{6,14},... | collective-permute-start | bytes 405512 | tf_op jit(solution)/shard_map/ppermute | solution.py:242
  18.6 1.4 %collective-permute-start.4 = (bf16[528,128]{1,0:T(8,128)(2,1)S(1)}, bf16[528,128]{1,0:T(8,128)(2,1)S(1)}, u32[]{:S(2)}, u32[]{:S(2)}) collective-permute-start(bf16[528,128]{1,0:T(8,128)(2,1)S(1)} %gate.17), channel_id=1, source_target_pairs={{0,1},{1,0},{2,3},{3,2},{4,5},{5,4},{6,7},{7,6},{8,9},{9,8},{10,11... | collective-permute-start | bytes 405512 | tf_op jit(solution)/shard_map/ppermute | solution.py:239
  20.0 1.6 %stage.1 = (s32[8,32]{1,0:T(8,128)S(4)}, bf16[8,2,256,256]{3,2,1,0:T(8,128)(2,1)S(1)}, bf16[528,128]{1,0:T(8,128)(2,1)S(1)}) custom-call(s32[8,32]{1,0:T(8,128)} %bitcast.1, bf16[8,2,256,256]{3,2,1,0:T(8,128)(2,1)} %esp_ref.1, bf16[528,128]{1,0:T(8,128)(2,1)S(1)} %collective-permute-done.refs_2_.piece_ref, ...), custom_call_target="tpu_custom_call" | custom-call | tf_op jit(solution)/shard_map/stage/pallas_call | solution.py:279
  21.8 0.5 %collective-permute-start.10 = (bf16[528,128]{1,0:T(8,128)(2,1)S(1)}, bf16[528,128]{1,0:T(8,128)(2,1)S(1)}, u32[]{:S(2)}, u32[]{:S(2)}) collective-permute-start(bf16[528,128]{1,0:T(8,128)(2,1)S(1)} %collective-permute-done.3.refs_0_.refs_3_), channel_id=1, source_target_pairs={{0,4},{4,0},{8,12},{12,8},{1,5},{5,1},{9,13},{13,9},{2,6},{6,2},{1... | collective-permute-start | bytes 405512 | tf_op jit(solution)/shard_map/ppermute | solution.py:299
  22.3 0.4 %collective-permute-start.14 = (bf16[528,128]{1,0:T(8,128)(2,1)S(1)}, bf16[528,128]{1,0:T(8,128)(2,1)S(1)}, u32[]{:S(2)}, u32[]{:S(2)}) collective-permute-start(bf16[528,128]{1,0:T(8,128)(2,1)S(1)} %collective-permute-done.6.refs_7_), channel_id=1, source_target_pairs={{0,4},{4,0},{8,12},{12,8},{1,5},{5,1},{9,13},{13,9},{2,6},{6,2},{1... | collective-permute-start | bytes 405512 | tf_op jit(solution)/shard_map/ppermute | solution.py:299
  22.8 0.9 %collective-permute-done.4.refs_5_ = bf16[528,128]{1,0:T(8,128)(2,1)S(1)} collective-permute-done((bf16[528,128]{1,0:T(8,128)(2,1)S(1)}, bf16[528,128]{1,0:T(8,128)(2,1)S(1)}, u32[]{:S(2)}, u32[]{:S(2)}) %collective-permute-start.4) | collective-permute-done | bytes 135200 | tf_op jit(solution)/shard_map/ppermute | solution.py:239
  23.8 1.2 %collective-permute-done.12.refs_13_ = bf16[528,128]{1,0:T(8,128)(2,1)S(1)} collective-permute-done((bf16[528,128]{1,0:T(8,128)(2,1)S(1)}, bf16[528,128]{1,0:T(8,128)(2,1)S(1)}, u32[]{:S(2)}, u32[]{:S(2)}) %collective-permute-start.12) | collective-permute-done | bytes 135200 | tf_op jit(solution)/shard_map/ppermute | solution.py:299
  25.0 0.9 %couple_first.1 = (bf16[16,528,128]{2,1,0:T(8,128)(2,1)S(1)}, s32[264,128]{1,0:T(8,128)S(1)}) custom-call(s32[8,32]{1,0:T(8,128)S(4)} %get-tuple-element.13.nbr_ref, bf16[8,2,256,256]{3,2,1,0:T(8,128)(2,1)S(1)} %get-tuple-element.14.esp_ref, bf16[528,128]{1,0:T(8,128)(2,1)S(1)} %fold.1.refs_0_, bf16[528,128]{1,0:T(8,128)(2,1)S(1)} %collective-permute-done.2.refs_1_, ...), custom_call_target="tpu_custom_call" | custom-call | tf_op jit(solution)/shard_map/couple_first/pallas_call | solution.py:311
  25.9 2.6 %collective-permute-start.16 = (s32[264,128]{1,0:T(8,128)S(1)}, s32[264,128]{1,0:T(8,128)S(1)}, u32[]{:S(2)}, u32[]{:S(2)}) collective-permute-start(s32[264,128]{1,0:T(8,128)S(1)} %get-tuple-element.19), channel_id=1, source_target_pairs={{0,2},{1,3},{2,0},{3,1},{4,6},{5,7},{6,4},{7,5},{8,10},{9,11},{10,... | collective-permute-start | bytes 405512 | tf_op jit(solution)/shard_map/ppermute | solution.py:239
  28.5 1.7 %couple_rest.1 = (f32[2,264,128]{2,1,0:T(8,128)S(1)}, s32[264,128]{1,0:T(8,128)S(1)}, s32[264,128]{1,0:T(8,128)S(1)}) custom-call(s32[8,32]{1,0:T(8,128)S(4)} %get-tuple-element.13.nbr_ref, bf16[8,2,256,256]{3,2,1,0:T(8,128)(2,1)S(1)} %get-tuple-element.14.esp_ref, bf16[16,528,128]{2,1,0:T(8,128)(2,1)S(1)} %get-tuple-element.16.refs_0_), custom_call_target="tpu_custom_call" | custom-call | tf_op jit(solution)/shard_map/couple_rest/pallas_call | solution.py:311
  30.2 1.8 %collective-permute-start.15 = (s32[264,128]{1,0:T(8,128)S(1)}, s32[264,128]{1,0:T(8,128)S(1)}, u32[]{:S(2)}, u32[]{:S(2)}) collective-permute-start(s32[264,128]{1,0:T(8,128)S(1)} %get-tuple-element.18), channel_id=1, source_target_pairs={{0,1},{1,0},{2,3},{3,2},{4,5},{5,4},{6,7},{7,6},{8,9},{9,8},{10,11... | collective-permute-start | bytes 405512 | tf_op jit(solution)/shard_map/ppermute | solution.py:239
  32.2 4.1 %collective-permute-done.16.piece_ref = s32[264,128]{1,0:T(8,128)S(1)} collective-permute-done((s32[264,128]{1,0:T(8,128)S(1)}, s32[264,128]{1,0:T(8,128)S(1)}, u32[]{:S(2)}, u32[]{:S(2)}) %collective-permute-start.16) | collective-permute-done | bytes 135200 | tf_op jit(solution)/shard_map/ppermute | solution.py:239
  36.4 3.9 %collective-permute-done.15.refs_0_ = s32[264,128]{1,0:T(8,128)S(1)} collective-permute-done((s32[264,128]{1,0:T(8,128)S(1)}, s32[264,128]{1,0:T(8,128)S(1)}, u32[]{:S(2)}, u32[]{:S(2)}) %collective-permute-start.15) | collective-permute-done | bytes 135200 | tf_op jit(solution)/shard_map/ppermute | solution.py:239
  40.3 1.0 %finish.1 = f32[2,256,256]{2,1,0:T(8,128)} custom-call(bf16[2,256,256]{2,1,0:T(8,128)(2,1)S(1)} %copy-done.1, f32[2,264,128]{2,1,0:T(8,128)S(1)} %get-tuple-element.17.own_ref, s32[264,128]{1,0:T(8,128)S(1)} %collective-permute-done.15.refs_0_, s32[264,128]{1,0:T(8,128)S(1)} %gate.29.refs_1_, s32[264,128]{1,0:T(8,128)S(1)} %collective-permute-done.17.refs_2_), custom_call_target="tpu_custom_call" | custom-call | tf_op jit(solution)/shard_map/finish/pallas_call | solution.py:330
  (36 shorter events, 0.7 us)
Async XLA Ops:
  0.0 0.9 %copy-start = (bf16[2,256,256]{2,1,0:T(8,128)(2,1)S(1)}, bf16[2,256,256]{2,1,0:T(8,128)(2,1)}, u32[]{:S(2)}) copy-start(bf16[2,256,256]{2,1,0:T(8,128)(2,1)} %dens_ref.1) | copy-start | bytes 786436
  1.0 10.7 %collective-permute-start.1 = (bf16[528,128]{1,0:T(8,128)(2,1)S(1)}, bf16[528,128]{1,0:T(8,128)(2,1)S(1)}, u32[]{:S(2)}, u32[]{:S(2)}) collective-permute-start(bf16[528,128]{1,0:T(8,128)(2,1)S(1)} %fold.1.refs_0_), channel_id=1, source_target_pairs={{0,2},{1,3},{2,0},{3,1},{4,6},{5,7},{6,4},{7,5},{8,10},{9,11},{10,... | collective-permute-start | bytes 405512 | tf_op jit(solution)/shard_map/ppermute | solution.py:239
  5.1 6.8 %collective-permute-start.2 = (bf16[528,128]{1,0:T(8,128)(2,1)S(1)}, bf16[528,128]{1,0:T(8,128)(2,1)S(1)}, u32[]{:S(2)}, u32[]{:S(2)}) collective-permute-start(bf16[528,128]{1,0:T(8,128)(2,1)S(1)} %fold.1.refs_0_), channel_id=1, source_target_pairs={{0,1},{1,0},{2,3},{3,2},{4,5},{5,4},{6,7},{7,6},{8,9},{9,8},{10,11... | collective-permute-start | bytes 405512 | tf_op jit(solution)/shard_map/ppermute | solution.py:239
  6.7 5.2 %collective-permute-start = (bf16[528,128]{1,0:T(8,128)(2,1)S(1)}, bf16[528,128]{1,0:T(8,128)(2,1)S(1)}, u32[]{:S(2)}, u32[]{:S(2)}) collective-permute-start(bf16[528,128]{1,0:T(8,128)(2,1)S(1)} %fold.1.refs_0_), channel_id=1, source_target_pairs={{0,8},{4,12},{8,0},{12,4},{1,9},{5,13},{9,1},{13,5},{2,10},{6,14},... | collective-permute-start | bytes 405512 | tf_op jit(solution)/shard_map/ppermute | solution.py:242
  11.9 5.1 %collective-permute-start.3 = (bf16[528,128]{1,0:T(8,128)(2,1)S(1)}, bf16[528,128]{1,0:T(8,128)(2,1)S(1)}, u32[]{:S(2)}, u32[]{:S(2)}) collective-permute-start(bf16[528,128]{1,0:T(8,128)(2,1)S(1)} %gate.16.refs_2_), channel_id=1, source_target_pairs={{0,1},{1,0},{2,3},{3,2},{4,5},{5,4},{6,7},{7,6},{8,9},{9,8},{10,11... | collective-permute-start | bytes 405512 | tf_op jit(solution)/shard_map/ppermute | solution.py:239
  13.4 5.2 %collective-permute-start.7 = (bf16[528,128]{1,0:T(8,128)(2,1)S(1)}, bf16[528,128]{1,0:T(8,128)(2,1)S(1)}, u32[]{:S(2)}, u32[]{:S(2)}) collective-permute-start(bf16[528,128]{1,0:T(8,128)(2,1)S(1)} %fold.1.refs_0_), channel_id=1, source_target_pairs={{0,4},{4,0},{8,12},{12,8},{1,5},{5,1},{9,13},{13,9},{2,6},{6,2},{1... | collective-permute-start | bytes 405512 | tf_op jit(solution)/shard_map/ppermute | solution.py:299
  13.4 8.2 %collective-permute-start.5 = (bf16[528,128]{1,0:T(8,128)(2,1)S(1)}, bf16[528,128]{1,0:T(8,128)(2,1)S(1)}, u32[]{:S(2)}, u32[]{:S(2)}) collective-permute-start(bf16[528,128]{1,0:T(8,128)(2,1)S(1)} %gate.16.refs_2_), channel_id=1, source_target_pairs={{0,8},{4,12},{8,0},{12,4},{1,9},{5,13},{9,1},{13,5},{2,10},{6,14},... | collective-permute-start | bytes 405512 | tf_op jit(solution)/shard_map/ppermute | solution.py:242
  15.0 6.8 %collective-permute-start.8 = (bf16[528,128]{1,0:T(8,128)(2,1)S(1)}, bf16[528,128]{1,0:T(8,128)(2,1)S(1)}, u32[]{:S(2)}, u32[]{:S(2)}) collective-permute-start(bf16[528,128]{1,0:T(8,128)(2,1)S(1)} %collective-permute-done.2.refs_1_), channel_id=1, source_target_pairs={{0,4},{4,0},{8,12},{12,8},{1,5},{5,1},{9,13},{13,9},{2,6},{6,2},{1... | collective-permute-start | bytes 405512 | tf_op jit(solution)/shard_map/ppermute | solution.py:299
  15.2 7.1 %collective-permute-start.9 = (bf16[528,128]{1,0:T(8,128)(2,1)S(1)}, bf16[528,128]{1,0:T(8,128)(2,1)S(1)}, u32[]{:S(2)}, u32[]{:S(2)}) collective-permute-start(bf16[528,128]{1,0:T(8,128)(2,1)S(1)} %gate.16.refs_2_), channel_id=1, source_target_pairs={{0,4},{4,0},{8,12},{12,8},{1,5},{5,1},{9,13},{13,9},{2,6},{6,2},{1... | collective-permute-start | bytes 405512 | tf_op jit(solution)/shard_map/ppermute | solution.py:299
  17.0 5.4 %collective-permute-start.6 = (bf16[528,128]{1,0:T(8,128)(2,1)S(1)}, bf16[528,128]{1,0:T(8,128)(2,1)S(1)}, u32[]{:S(2)}, u32[]{:S(2)}) collective-permute-start(bf16[528,128]{1,0:T(8,128)(2,1)S(1)} %collective-permute-done.3.refs_0_.refs_3_), channel_id=1, source_target_pairs={{0,8},{4,12},{8,0},{12,4},{1,9},{5,13},{9,1},{13,5},{2,10},{6,14},... | collective-permute-start | bytes 405512 | tf_op jit(solution)/shard_map/ppermute | solution.py:242
  18.6 5.0 %collective-permute-start.4 = (bf16[528,128]{1,0:T(8,128)(2,1)S(1)}, bf16[528,128]{1,0:T(8,128)(2,1)S(1)}, u32[]{:S(2)}, u32[]{:S(2)}) collective-permute-start(bf16[528,128]{1,0:T(8,128)(2,1)S(1)} %gate.17), channel_id=1, source_target_pairs={{0,1},{1,0},{2,3},{3,2},{4,5},{5,4},{6,7},{7,6},{8,9},{9,8},{10,11... | collective-permute-start | bytes 405512 | tf_op jit(solution)/shard_map/ppermute | solution.py:239
  21.7 2.0 %collective-permute-start.13 = (bf16[528,128]{1,0:T(8,128)(2,1)S(1)}, bf16[528,128]{1,0:T(8,128)(2,1)S(1)}, u32[]{:S(2)}, u32[]{:S(2)}) collective-permute-start(bf16[528,128]{1,0:T(8,128)(2,1)S(1)} %collective-permute-done.5.refs_6_), channel_id=1, source_target_pairs={{0,4},{4,0},{8,12},{12,8},{1,5},{5,1},{9,13},{13,9},{2,6},{6,2},{1... | collective-permute-start | bytes 405512 | tf_op jit(solution)/shard_map/ppermute | solution.py:299
  21.8 2.0 %collective-permute-start.10 = (bf16[528,128]{1,0:T(8,128)(2,1)S(1)}, bf16[528,128]{1,0:T(8,128)(2,1)S(1)}, u32[]{:S(2)}, u32[]{:S(2)}) collective-permute-start(bf16[528,128]{1,0:T(8,128)(2,1)S(1)} %collective-permute-done.3.refs_0_.refs_3_), channel_id=1, source_target_pairs={{0,4},{4,0},{8,12},{12,8},{1,5},{5,1},{9,13},{13,9},{2,6},{6,2},{1... | collective-permute-start | bytes 405512 | tf_op jit(solution)/shard_map/ppermute | solution.py:299
  22.3 1.5 %collective-permute-start.11 = (bf16[528,128]{1,0:T(8,128)(2,1)S(1)}, bf16[528,128]{1,0:T(8,128)(2,1)S(1)}, u32[]{:S(2)}, u32[]{:S(2)}) collective-permute-start(bf16[528,128]{1,0:T(8,128)(2,1)S(1)} %get-tuple-element.15.refs_4_), channel_id=1, source_target_pairs={{0,4},{4,0},{8,12},{12,8},{1,5},{5,1},{9,13},{13,9},{2,6},{6,2},{1... | collective-permute-start | bytes 405512 | tf_op jit(solution)/shard_map/ppermute | solution.py:299
  22.3 1.5 %collective-permute-start.14 = (bf16[528,128]{1,0:T(8,128)(2,1)S(1)}, bf16[528,128]{1,0:T(8,128)(2,1)S(1)}, u32[]{:S(2)}, u32[]{:S(2)}) collective-permute-start(bf16[528,128]{1,0:T(8,128)(2,1)S(1)} %collective-permute-done.6.refs_7_), channel_id=1, source_target_pairs={{0,4},{4,0},{8,12},{12,8},{1,5},{5,1},{9,13},{13,9},{2,6},{6,2},{1... | collective-permute-start | bytes 405512 | tf_op jit(solution)/shard_map/ppermute | solution.py:299
  23.6 1.4 %collective-permute-start.12 = (bf16[528,128]{1,0:T(8,128)(2,1)S(1)}, bf16[528,128]{1,0:T(8,128)(2,1)S(1)}, u32[]{:S(2)}, u32[]{:S(2)}) collective-permute-start(bf16[528,128]{1,0:T(8,128)(2,1)S(1)} %collective-permute-done.4.refs_5_), channel_id=1, source_target_pairs={{0,4},{4,0},{8,12},{12,8},{1,5},{5,1},{9,13},{13,9},{2,6},{6,2},{1... | collective-permute-start | bytes 405512 | tf_op jit(solution)/shard_map/ppermute | solution.py:299
  25.9 10.4 %collective-permute-start.16 = (s32[264,128]{1,0:T(8,128)S(1)}, s32[264,128]{1,0:T(8,128)S(1)}, u32[]{:S(2)}, u32[]{:S(2)}) collective-permute-start(s32[264,128]{1,0:T(8,128)S(1)} %get-tuple-element.19), channel_id=1, source_target_pairs={{0,2},{1,3},{2,0},{3,1},{4,6},{5,7},{6,4},{7,5},{8,10},{9,11},{10,... | collective-permute-start | bytes 405512 | tf_op jit(solution)/shard_map/ppermute | solution.py:239
  28.5 11.8 %copy-start.1 = (bf16[2,256,256]{2,1,0:T(8,128)(2,1)S(1)}, bf16[2,256,256]{2,1,0:T(8,128)(2,1)}, u32[]{:S(2)}) copy-start(bf16[2,256,256]{2,1,0:T(8,128)(2,1)} %core_ref.1) | copy-start | bytes 786436
  30.2 10.0 %collective-permute-start.15 = (s32[264,128]{1,0:T(8,128)S(1)}, s32[264,128]{1,0:T(8,128)S(1)}, u32[]{:S(2)}, u32[]{:S(2)}) collective-permute-start(s32[264,128]{1,0:T(8,128)S(1)} %get-tuple-element.18), channel_id=1, source_target_pairs={{0,1},{1,0},{2,3},{3,2},{4,5},{5,4},{6,7},{7,6},{8,9},{9,8},{10,11... | collective-permute-start | bytes 405512 | tf_op jit(solution)/shard_map/ppermute | solution.py:239
  32.1 8.2 %collective-permute-start.17 = (s32[264,128]{1,0:T(8,128)S(1)}, s32[264,128]{1,0:T(8,128)S(1)}, u32[]{:S(2)}, u32[]{:S(2)}) collective-permute-start(s32[264,128]{1,0:T(8,128)S(1)} %get-tuple-element.20), channel_id=1, source_target_pairs={{0,3},{1,2},{2,1},{3,0},{4,7},{5,6},{6,5},{7,4},{8,11},{9,10},{10,... | collective-permute-start | bytes 405512 | tf_op jit(solution)/shard_map/ppermute | solution.py:239

commit v14 on v12

--- a/solution.py
+++ b/solution.py
@@ -317,14 +317,16 @@
             name=name,
         )(names, blocks, *pieces)
 
-    filled, beyond = couple([(top, True)], "couple_first", pieces, fill=True)
-    beyond = {top: along_z(beyond, top)}
-    for _ in range(5):
-        beyond[top] = gate(beyond[top])
-    rest = [k for k in range(1, lanes) if k != top]
-    own, *units = couple([(0, False)] + [(k, True) for k in rest], "couple_rest", [filled])
-    for k, unit in zip(rest, units):
+    order = sorted(range(1, lanes), key=lambda k: (k < top, -k))
+    filled, unit = couple([(order[0], True)], "couple_first", pieces, fill=True)
+    beyond = {order[0]: along_z(unit, order[0])}
+    units = couple([(k, True) for k in order[1:]], "couple_second", [filled])
+    for k, unit in zip(order[1:], units):
         beyond[k] = along_z(unit, k)
+    (own,) = couple([(0, False)], "couple_own", [filled])
+    for k, n in zip(order, (5, 1)):
+        for _ in range(n):
+            beyond[k] = gate(beyond[k])
     return pl.pallas_call(
         finish_kernel,
         out_shape=jax.ShapeDtypeStruct((mono_dev, basis, basis), jnp.float32),

time: 40.2 us -> 41.4 us (1.030)
  waiting for transfers between devices: 14.3 us -> 15.1 us
    ppermute x7, waiting for transfers between devices: 12.1 us -> 13 us  [along_z(): return lax.ppermute(piece, 'intra', xor_pairs(lanes, bit))]
    pallas_call x2 -> x3, Pallas kernels: 2.63 us -> 2.91 us  [couple(): pl.pallas_call(functools.partial(couple_kernel, groups, lanes, mono_dev,...]
where the time goes in v14:
time: 41.4 us; the launch traced here: 41.2 us
  starting transfers between devices  19.3 us (47%)
  waiting for transfers between devices  15.1 us (36%)
  Pallas kernels  5.71 us (14%)
  local copies, waits for them, and re-layouts  0.96 us (2%)
    ppermute x7, waiting for transfers between devices, along_z(): return lax.ppermute(piece, 'intra', xor_pairs(lanes, bit))  13 us
    ppermute x7, starting transfers between devices, along_z(): return lax.ppermute(piece, 'intra', xor_pairs(lanes, bit))  12.8 us
    ppermute x3, starting transfers between devices, along_y(): return lax.ppermute(piece, 'gddi', xor_pairs(groups, 2 * y))  4.85 us
    pallas_call x3, Pallas kernels, couple(): pl.pallas_call(functools.partial(couple_kernel, groups, lanes, mono_dev,...  2.91 us
    pallas_call x1, Pallas kernels, local(): pl.pallas_call(stage_kernel, out_shape=[pltpu.SMEM((nbr.shape[1], nbr.sha...  1.62 us
    ppermute x8, starting transfers between devices, local(): lax.ppermute(piece, 'gddi', xor_pairs(groups, 1))  1.59 us
    ppermute x8, waiting for transfers between devices, local(): lax.ppermute(piece, 'gddi', xor_pairs(groups, 1))  1.36 us
    pallas_call x1, Pallas kernels, local(): pl.pallas_call(finish_kernel, out_shape=jax.ShapeDtypeStruct((mono_dev, b...  1.04 us
  transfers between devices with their start and end apart: 18, of which 8 were waited for; matrix products, arithmetic and copies ran while one was open for 0% of the time, Pallas kernels for 9%

profile of v14, /device:TPU:0, one launch (start us, length us, event | category | flops | bytes accessed | tf_op | source)
XLA Modules:
  0.0 41.2 jit_solution(5453786653414719220)
XLA Ops:
  0.0 0.9 %copy-done = bf16[2,256,256]{2,1,0:T(8,128)(2,1)S(1)} copy-done((bf16[2,256,256]{2,1,0:T(8,128)(2,1)S(1)}, bf16[2,256,256]{2,1,0:T(8,128)(2,1)}, u32[]{:S(2)}) %copy-start) | copy-done | bytes 262168
  1.0 4.1 %collective-permute-start.1 = (bf16[528,128]{1,0:T(8,128)(2,1)S(1)}, bf16[528,128]{1,0:T(8,128)(2,1)S(1)}, u32[]{:S(2)}, u32[]{:S(2)}) collective-permute-start(bf16[528,128]{1,0:T(8,128)(2,1)S(1)} %fold.1.refs_0_), channel_id=1, source_target_pairs={{0,2},{1,3},{2,0},{3,1},{4,6},{5,7},{6,4},{7,5},{8,10},{9,11},{10,... | collective-permute-start | bytes 405512 | tf_op jit(solution)/shard_map/ppermute | solution.py:239
  5.1 1.6 %collective-permute-start.2 = (bf16[528,128]{1,0:T(8,128)(2,1)S(1)}, bf16[528,128]{1,0:T(8,128)(2,1)S(1)}, u32[]{:S(2)}, u32[]{:S(2)}) collective-permute-start(bf16[528,128]{1,0:T(8,128)(2,1)S(1)} %fold.1.refs_0_), channel_id=1, source_target_pairs={{0,1},{1,0},{2,3},{3,2},{4,5},{5,4},{6,7},{7,6},{8,9},{9,8},{10,11... | collective-permute-start | bytes 405512 | tf_op jit(solution)/shard_map/ppermute | solution.py:239
  6.7 1.5 %collective-permute-start = (bf16[528,128]{1,0:T(8,128)(2,1)S(1)}, bf16[528,128]{1,0:T(8,128)(2,1)S(1)}, u32[]{:S(2)}, u32[]{:S(2)}) collective-permute-start(bf16[528,128]{1,0:T(8,128)(2,1)S(1)} %fold.1.refs_0_), channel_id=1, source_target_pairs={{0,8},{4,12},{8,0},{12,4},{1,9},{5,13},{9,1},{13,5},{2,10},{6,14},... | collective-permute-start | bytes 405512 | tf_op jit(solution)/shard_map/ppermute | solution.py:242
  8.2 3.5 %collective-permute-done.1.piece_ref = bf16[528,128]{1,0:T(8,128)(2,1)S(1)} collective-permute-done((bf16[528,128]{1,0:T(8,128)(2,1)S(1)}, bf16[528,128]{1,0:T(8,128)(2,1)S(1)}, u32[]{:S(2)}, u32[]{:S(2)}) %collective-permute-start.1) | collective-permute-done | bytes 135200 | tf_op jit(solution)/shard_map/ppermute | solution.py:239
  11.9 1.5 %collective-permute-start.3 = (bf16[528,128]{1,0:T(8,128)(2,1)S(1)}, bf16[528,128]{1,0:T(8,128)(2,1)S(1)}, u32[]{:S(2)}, u32[]{:S(2)}) collective-permute-start(bf16[528,128]{1,0:T(8,128)(2,1)S(1)} %gate.9.refs_2_), channel_id=1, source_target_pairs={{0,1},{1,0},{2,3},{3,2},{4,5},{5,4},{6,7},{7,6},{8,9},{9,8},{10,11... | collective-permute-start | bytes 405512 | tf_op jit(solution)/shard_map/ppermute | solution.py:239
  13.4 0.5 %collective-permute-start.9 = (bf16[528,128]{1,0:T(8,128)(2,1)S(1)}, bf16[528,128]{1,0:T(8,128)(2,1)S(1)}, u32[]{:S(2)}, u32[]{:S(2)}) collective-permute-start(bf16[528,128]{1,0:T(8,128)(2,1)S(1)} %gate.9.refs_2_), channel_id=1, source_target_pairs={{0,4},{4,0},{8,12},{12,8},{1,5},{5,1},{9,13},{13,9},{2,6},{6,2},{1... | collective-permute-start | bytes 405512 | tf_op jit(solution)/shard_map/ppermute | solution.py:299
  13.9 1.5 %collective-permute-start.5 = (bf16[528,128]{1,0:T(8,128)(2,1)S(1)}, bf16[528,128]{1,0:T(8,128)(2,1)S(1)}, u32[]{:S(2)}, u32[]{:S(2)}) collective-permute-start(bf16[528,128]{1,0:T(8,128)(2,1)S(1)} %gate.9.refs_2_), channel_id=1, source_target_pairs={{0,8},{4,12},{8,0},{12,4},{1,9},{5,13},{9,1},{13,5},{2,10},{6,14},... | collective-permute-start | bytes 405512 | tf_op jit(solution)/shard_map/ppermute | solution.py:242
  15.5 0.6 %collective-permute-start.4 = (bf16[528,128]{1,0:T(8,128)(2,1)S(1)}, bf16[528,128]{1,0:T(8,128)(2,1)S(1)}, u32[]{:S(2)}, u32[]{:S(2)}) collective-permute-start(bf16[528,128]{1,0:T(8,128)(2,1)S(1)} %collective-permute-done.refs_2_.piece_ref), channel_id=1, source_target_pairs={{0,1},{1,0},{2,3},{3,2},{4,5},{5,4},{6,7},{7,6},{8,9},{9,8},{10,11... | collective-permute-start | bytes 405512 | tf_op jit(solution)/shard_map/ppermute | solution.py:239
  16.1 0.9 %collective-permute-done.3.refs_0_.refs_3_ = bf16[528,128]{1,0:T(8,128)(2,1)S(1)} collective-permute-done((bf16[528,128]{1,0:T(8,128)(2,1)S(1)}, bf16[528,128]{1,0:T(8,128)(2,1)S(1)}, u32[]{:S(2)}, u32[]{:S(2)}) %collective-permute-start.3) | collective-permute-done | bytes 135200 | tf_op jit(solution)/shard_map/ppermute | solution.py:239
  17.0 1.8 %collective-permute-start.6 = (bf16[528,128]{1,0:T(8,128)(2,1)S(1)}, bf16[528,128]{1,0:T(8,128)(2,1)S(1)}, u32[]{:S(2)}, u32[]{:S(2)}) collective-permute-start(bf16[528,128]{1,0:T(8,128)(2,1)S(1)} %collective-permute-done.3.refs_0_.refs_3_), channel_id=1, source_target_pairs={{0,8},{4,12},{8,0},{12,4},{1,9},{5,13},{9,1},{13,5},{2,10},{6,14},... | collective-permute-start | bytes 405512 | tf_op jit(solution)/shard_map/ppermute | solution.py:242
  18.8 1.6 %stage.1 = (s32[8,32]{1,0:T(8,128)S(4)}, bf16[8,2,256,256]{3,2,1,0:T(8,128)(2,1)S(1)}, bf16[528,128]{1,0:T(8,128)(2,1)S(1)}) custom-call(s32[8,32]{1,0:T(8,128)} %bitcast.1, bf16[8,2,256,256]{3,2,1,0:T(8,128)(2,1)} %esp_ref.1, bf16[528,128]{1,0:T(8,128)(2,1)S(1)} %collective-permute-done.refs_2_.piece_ref, ...), custom_call_target="tpu_custom_call" | custom-call | tf_op jit(solution)/shard_map/stage/pallas_call | solution.py:279
  20.5 0.5 %collective-permute-start.10 = (bf16[528,128]{1,0:T(8,128)(2,1)S(1)}, bf16[528,128]{1,0:T(8,128)(2,1)S(1)}, u32[]{:S(2)}, u32[]{:S(2)}) collective-permute-start(bf16[528,128]{1,0:T(8,128)(2,1)S(1)} %collective-permute-done.3.refs_0_.refs_3_), channel_id=1, source_target_pairs={{0,4},{4,0},{8,12},{12,8},{1,5},{5,1},{9,13},{13,9},{2,6},{6,2},{1... | collective-permute-start | bytes 405512 | tf_op jit(solution)/shard_map/ppermute | solution.py:299
  21.1 0.4 %collective-permute-start.12 = (bf16[528,128]{1,0:T(8,128)(2,1)S(1)}, bf16[528,128]{1,0:T(8,128)(2,1)S(1)}, u32[]{:S(2)}, u32[]{:S(2)}) collective-permute-start(bf16[528,128]{1,0:T(8,128)(2,1)S(1)} %collective-permute-done.4.refs_5_), channel_id=1, source_target_pairs={{0,4},{4,0},{8,12},{12,8},{1,5},{5,1},{9,13},{13,9},{2,6},{6,2},{1... | collective-permute-start | bytes 405512 | tf_op jit(solution)/shard_map/ppermute | solution.py:299
  21.5 0.8 %collective-permute-done.6.refs_7_ = bf16[528,128]{1,0:T(8,128)(2,1)S(1)} collective-permute-done((bf16[528,128]{1,0:T(8,128)(2,1)S(1)}, bf16[528,128]{1,0:T(8,128)(2,1)S(1)}, u32[]{:S(2)}, u32[]{:S(2)}) %collective-permute-start.6) | collective-permute-done | bytes 135200 | tf_op jit(solution)/shard_map/ppermute | solution.py:242
  22.6 1.1 %collective-permute-done.14.refs_15_ = bf16[528,128]{1,0:T(8,128)(2,1)S(1)} collective-permute-done((bf16[528,128]{1,0:T(8,128)(2,1)S(1)}, bf16[528,128]{1,0:T(8,128)(2,1)S(1)}, u32[]{:S(2)}, u32[]{:S(2)}) %collective-permute-start.14) | collective-permute-done | bytes 135200 | tf_op jit(solution)/shard_map/ppermute | solution.py:299
  23.7 0.9 %couple_first.1 = (bf16[16,528,128]{2,1,0:T(8,128)(2,1)S(1)}, s32[264,128]{1,0:T(8,128)S(1)}) custom-call(s32[8,32]{1,0:T(8,128)S(4)} %get-tuple-element.12.nbr_ref, bf16[8,2,256,256]{3,2,1,0:T(8,128)(2,1)S(1)} %get-tuple-element.13.esp_ref, bf16[528,128]{1,0:T(8,128)(2,1)S(1)} %fold.1.refs_0_, bf16[528,128]{1,0:T(8,128)(2,1)S(1)} %collective-permute-done.2.refs_1_, ...), custom_call_target="tpu_custom_call" | custom-call | tf_op jit(solution)/shard_map/couple_first/pallas_call | solution.py:309
  24.6 4.4 %collective-permute-start.17 = (s32[264,128]{1,0:T(8,128)S(1)}, s32[264,128]{1,0:T(8,128)S(1)}, u32[]{:S(2)}, u32[]{:S(2)}) collective-permute-start(s32[264,128]{1,0:T(8,128)S(1)} %get-tuple-element.18), channel_id=1, source_target_pairs={{0,3},{1,2},{2,1},{3,0},{4,7},{5,6},{6,5},{7,4},{8,11},{9,10},{10,... | collective-permute-start | bytes 405512 | tf_op jit(solution)/shard_map/ppermute | solution.py:239
  29.0 1.3 %couple_second.1 = (s32[264,128]{1,0:T(8,128)S(1)}, s32[264,128]{1,0:T(8,128)S(1)}) custom-call(s32[8,32]{1,0:T(8,128)S(4)} %get-tuple-element.12.nbr_ref, bf16[8,2,256,256]{3,2,1,0:T(8,128)(2,1)S(1)} %get-tuple-element.13.esp_ref, bf16[16,528,128]{2,1,0:T(8,128)(2,1)S(1)} %get-tuple-element.15.refs_0_), custom_call_target="tpu_custom_call" | custom-call | tf_op jit(solution)/shard_map/couple_second/pallas_call | solution.py:309
  30.4 0.6 %collective-permute-start.15 = (s32[264,128]{1,0:T(8,128)S(1)}, s32[264,128]{1,0:T(8,128)S(1)}, u32[]{:S(2)}, u32[]{:S(2)}) collective-permute-start(s32[264,128]{1,0:T(8,128)S(1)} %get-tuple-element.16), channel_id=1, source_target_pairs={{0,1},{1,0},{2,3},{3,2},{4,5},{5,4},{6,7},{7,6},{8,9},{9,8},{10,11... | collective-permute-start | bytes 405512 | tf_op jit(solution)/shard_map/ppermute | solution.py:239
  31.0 0.7 %couple_own.1.own_ref = f32[2,264,128]{2,1,0:T(8,128)S(1)} custom-call(s32[8,32]{1,0:T(8,128)S(4)} %get-tuple-element.12.nbr_ref, bf16[8,2,256,256]{3,2,1,0:T(8,128)(2,1)S(1)} %get-tuple-element.13.esp_ref, bf16[16,528,128]{2,1,0:T(8,128)(2,1)S(1)} %get-tuple-element.15.refs_0_), custom_call_target="tpu_custom_call" | custom-call | tf_op jit(solution)/shard_map/couple_own/pallas_call | solution.py:309
  31.7 1.8 %collective-permute-done.17.piece_ref = s32[264,128]{1,0:T(8,128)S(1)} collective-permute-done((s32[264,128]{1,0:T(8,128)S(1)}, s32[264,128]{1,0:T(8,128)S(1)}, u32[]{:S(2)}, u32[]{:S(2)}) %collective-permute-start.17) | collective-permute-done | bytes 135200 | tf_op jit(solution)/shard_map/ppermute | solution.py:239
  33.5 6.6 %collective-permute-done.16.piece_ref = s32[264,128]{1,0:T(8,128)S(1)} collective-permute-done((s32[264,128]{1,0:T(8,128)S(1)}, s32[264,128]{1,0:T(8,128)S(1)}, u32[]{:S(2)}, u32[]{:S(2)}) %collective-permute-start.16) | collective-permute-done | bytes 135200 | tf_op jit(solution)/shard_map/ppermute | solution.py:239
  40.2 1.0 %finish.1 = f32[2,256,256]{2,1,0:T(8,128)} custom-call(bf16[2,256,256]{2,1,0:T(8,128)(2,1)S(1)} %copy-done.1, f32[2,264,128]{2,1,0:T(8,128)S(1)} %couple_own.1.own_ref, s32[264,128]{1,0:T(8,128)S(1)} %collective-permute-done.15.refs_0_, s32[264,128]{1,0:T(8,128)S(1)} %gate.10.refs_1_, s32[264,128]{1,0:T(8,128)S(1)} %gate.15.refs_2_), custom_call_target="tpu_custom_call" | custom-call | tf_op jit(solution)/shard_map/finish/pallas_call | solution.py:330
  (30 shorter events, 0.8 us)
Async XLA Ops:
  0.0 0.9 %copy-start = (bf16[2,256,256]{2,1,0:T(8,128)(2,1)S(1)}, bf16[2,256,256]{2,1,0:T(8,128)(2,1)}, u32[]{:S(2)}) copy-start(bf16[2,256,256]{2,1,0:T(8,128)(2,1)} %dens_ref.1) | copy-start | bytes 786436
  1.0 10.7 %collective-permute-start.1 = (bf16[528,128]{1,0:T(8,128)(2,1)S(1)}, bf16[528,128]{1,0:T(8,128)(2,1)S(1)}, u32[]{:S(2)}, u32[]{:S(2)}) collective-permute-start(bf16[528,128]{1,0:T(8,128)(2,1)S(1)} %fold.1.refs_0_), channel_id=1, source_target_pairs={{0,2},{1,3},{2,0},{3,1},{4,6},{5,7},{6,4},{7,5},{8,10},{9,11},{10,... | collective-permute-start | bytes 405512 | tf_op jit(solution)/shard_map/ppermute | solution.py:239
  5.1 6.8 %collective-permute-start.2 = (bf16[528,128]{1,0:T(8,128)(2,1)S(1)}, bf16[528,128]{1,0:T(8,128)(2,1)S(1)}, u32[]{:S(2)}, u32[]{:S(2)}) collective-permute-start(bf16[528,128]{1,0:T(8,128)(2,1)S(1)} %fold.1.refs_0_), channel_id=1, source_target_pairs={{0,1},{1,0},{2,3},{3,2},{4,5},{5,4},{6,7},{7,6},{8,9},{9,8},{10,11... | collective-permute-start | bytes 405512 | tf_op jit(solution)/shard_map/ppermute | solution.py:239
  6.7 5.2 %collective-permute-start = (bf16[528,128]{1,0:T(8,128)(2,1)S(1)}, bf16[528,128]{1,0:T(8,128)(2,1)S(1)}, u32[]{:S(2)}, u32[]{:S(2)}) collective-permute-start(bf16[528,128]{1,0:T(8,128)(2,1)S(1)} %fold.1.refs_0_), channel_id=1, source_target_pairs={{0,8},{4,12},{8,0},{12,4},{1,9},{5,13},{9,1},{13,5},{2,10},{6,14},... | collective-permute-start | bytes 405512 | tf_op jit(solution)/shard_map/ppermute | solution.py:242
  8.2 7.3 %collective-permute-start.7 = (bf16[528,128]{1,0:T(8,128)(2,1)S(1)}, bf16[528,128]{1,0:T(8,128)(2,1)S(1)}, u32[]{:S(2)}, u32[]{:S(2)}) collective-permute-start(bf16[528,128]{1,0:T(8,128)(2,1)S(1)} %fold.1.refs_0_), channel_id=1, source_target_pairs={{0,4},{4,0},{8,12},{12,8},{1,5},{5,1},{9,13},{13,9},{2,6},{6,2},{1... | collective-permute-start | bytes 405512 | tf_op jit(solution)/shard_map/ppermute | solution.py:299
  11.9 5.1 %collective-permute-start.3 = (bf16[528,128]{1,0:T(8,128)(2,1)S(1)}, bf16[528,128]{1,0:T(8,128)(2,1)S(1)}, u32[]{:S(2)}, u32[]{:S(2)}) collective-permute-start(bf16[528,128]{1,0:T(8,128)(2,1)S(1)} %gate.9.refs_2_), channel_id=1, source_target_pairs={{0,1},{1,0},{2,3},{3,2},{4,5},{5,4},{6,7},{7,6},{8,9},{9,8},{10,11... | collective-permute-start | bytes 405512 | tf_op jit(solution)/shard_map/ppermute | solution.py:239
  13.4 7.0 %collective-permute-start.8 = (bf16[528,128]{1,0:T(8,128)(2,1)S(1)}, bf16[528,128]{1,0:T(8,128)(2,1)S(1)}, u32[]{:S(2)}, u32[]{:S(2)}) collective-permute-start(bf16[528,128]{1,0:T(8,128)(2,1)S(1)} %collective-permute-done.2.refs_1_), channel_id=1, source_target_pairs={{0,4},{4,0},{8,12},{12,8},{1,5},{5,1},{9,13},{13,9},{2,6},{6,2},{1... | collective-permute-start | bytes 405512 | tf_op jit(solution)/shard_map/ppermute | solution.py:299
  13.4 7.1 %collective-permute-start.9 = (bf16[528,128]{1,0:T(8,128)(2,1)S(1)}, bf16[528,128]{1,0:T(8,128)(2,1)S(1)}, u32[]{:S(2)}, u32[]{:S(2)}) collective-permute-start(bf16[528,128]{1,0:T(8,128)(2,1)S(1)} %gate.9.refs_2_), channel_id=1, source_target_pairs={{0,4},{4,0},{8,12},{12,8},{1,5},{5,1},{9,13},{13,9},{2,6},{6,2},{1... | collective-permute-start | bytes 405512 | tf_op jit(solution)/shard_map/ppermute | solution.py:299
  13.9 7.1 %collective-permute-start.5 = (bf16[528,128]{1,0:T(8,128)(2,1)S(1)}, bf16[528,128]{1,0:T(8,128)(2,1)S(1)}, u32[]{:S(2)}, u32[]{:S(2)}) collective-permute-start(bf16[528,128]{1,0:T(8,128)(2,1)S(1)} %gate.9.refs_2_), channel_id=1, source_target_pairs={{0,8},{4,12},{8,0},{12,4},{1,9},{5,13},{9,1},{13,5},{2,10},{6,14},... | collective-permute-start | bytes 405512 | tf_op jit(solution)/shard_map/ppermute | solution.py:242
  15.5 5.6 %collective-permute-start.4 = (bf16[528,128]{1,0:T(8,128)(2,1)S(1)}, bf16[528,128]{1,0:T(8,128)(2,1)S(1)}, u32[]{:S(2)}, u32[]{:S(2)}) collective-permute-start(bf16[528,128]{1,0:T(8,128)(2,1)S(1)} %collective-permute-done.refs_2_.piece_ref), channel_id=1, source_target_pairs={{0,1},{1,0},{2,3},{3,2},{4,5},{5,4},{6,7},{7,6},{8,9},{9,8},{10,11... | collective-permute-start | bytes 405512 | tf_op jit(solution)/shard_map/ppermute | solution.py:239
  17.0 5.3 %collective-permute-start.6 = (bf16[528,128]{1,0:T(8,128)(2,1)S(1)}, bf16[528,128]{1,0:T(8,128)(2,1)S(1)}, u32[]{:S(2)}, u32[]{:S(2)}) collective-permute-start(bf16[528,128]{1,0:T(8,128)(2,1)S(1)} %collective-permute-done.3.refs_0_.refs_3_), channel_id=1, source_target_pairs={{0,8},{4,12},{8,0},{12,4},{1,9},{5,13},{9,1},{13,5},{2,10},{6,14},... | collective-permute-start | bytes 405512 | tf_op jit(solution)/shard_map/ppermute | solution.py:242
  20.4 2.1 %collective-permute-start.11 = (bf16[528,128]{1,0:T(8,128)(2,1)S(1)}, bf16[528,128]{1,0:T(8,128)(2,1)S(1)}, u32[]{:S(2)}, u32[]{:S(2)}) collective-permute-start(bf16[528,128]{1,0:T(8,128)(2,1)S(1)} %get-tuple-element.14.refs_4_), channel_id=1, source_target_pairs={{0,4},{4,0},{8,12},{12,8},{1,5},{5,1},{9,13},{13,9},{2,6},{6,2},{1... | collective-permute-start | bytes 405512 | tf_op jit(solution)/shard_map/ppermute | solution.py:299
  20.5 1.9 %collective-permute-start.10 = (bf16[528,128]{1,0:T(8,128)(2,1)S(1)}, bf16[528,128]{1,0:T(8,128)(2,1)S(1)}, u32[]{:S(2)}, u32[]{:S(2)}) collective-permute-start(bf16[528,128]{1,0:T(8,128)(2,1)S(1)} %collective-permute-done.3.refs_0_.refs_3_), channel_id=1, source_target_pairs={{0,4},{4,0},{8,12},{12,8},{1,5},{5,1},{9,13},{13,9},{2,6},{6,2},{1... | collective-permute-start | bytes 405512 | tf_op jit(solution)/shard_map/ppermute | solution.py:299
  21.0 1.4 %collective-permute-start.13 = (bf16[528,128]{1,0:T(8,128)(2,1)S(1)}, bf16[528,128]{1,0:T(8,128)(2,1)S(1)}, u32[]{:S(2)}, u32[]{:S(2)}) collective-permute-start(bf16[528,128]{1,0:T(8,128)(2,1)S(1)} %collective-permute-done.5.refs_6_), channel_id=1, source_target_pairs={{0,4},{4,0},{8,12},{12,8},{1,5},{5,1},{9,13},{13,9},{2,6},{6,2},{1... | collective-permute-start | bytes 405512 | tf_op jit(solution)/shard_map/ppermute | solution.py:299
  21.1 1.5 %collective-permute-start.12 = (bf16[528,128]{1,0:T(8,128)(2,1)S(1)}, bf16[528,128]{1,0:T(8,128)(2,1)S(1)}, u32[]{:S(2)}, u32[]{:S(2)}) collective-permute-start(bf16[528,128]{1,0:T(8,128)(2,1)S(1)} %collective-permute-done.4.refs_5_), channel_id=1, source_target_pairs={{0,4},{4,0},{8,12},{12,8},{1,5},{5,1},{9,13},{13,9},{2,6},{6,2},{1... | collective-permute-start | bytes 405512 | tf_op jit(solution)/shard_map/ppermute | solution.py:299
  22.3 1.4 %collective-permute-start.14 = (bf16[528,128]{1,0:T(8,128)(2,1)S(1)}, bf16[528,128]{1,0:T(8,128)(2,1)S(1)}, u32[]{:S(2)}, u32[]{:S(2)}) collective-permute-start(bf16[528,128]{1,0:T(8,128)(2,1)S(1)} %collective-permute-done.6.refs_7_), channel_id=1, source_target_pairs={{0,4},{4,0},{8,12},{12,8},{1,5},{5,1},{9,13},{13,9},{2,6},{6,2},{1... | collective-permute-start | bytes 405512 | tf_op jit(solution)/shard_map/ppermute | solution.py:299
  24.6 8.8 %collective-permute-start.17 = (s32[264,128]{1,0:T(8,128)S(1)}, s32[264,128]{1,0:T(8,128)S(1)}, u32[]{:S(2)}, u32[]{:S(2)}) collective-permute-start(s32[264,128]{1,0:T(8,128)S(1)} %get-tuple-element.18), channel_id=1, source_target_pairs={{0,3},{1,2},{2,1},{3,0},{4,7},{5,6},{6,5},{7,4},{8,11},{9,10},{10,... | collective-permute-start | bytes 405512 | tf_op jit(solution)/shard_map/ppermute | solution.py:239
  30.3 9.9 %collective-permute-start.16 = (s32[264,128]{1,0:T(8,128)S(1)}, s32[264,128]{1,0:T(8,128)S(1)}, u32[]{:S(2)}, u32[]{:S(2)}) collective-permute-start(s32[264,128]{1,0:T(8,128)S(1)} %get-tuple-element.17), channel_id=1, source_target_pairs={{0,2},{1,3},{2,0},{3,1},{4,6},{5,7},{6,4},{7,5},{8,10},{9,11},{10,... | collective-permute-start | bytes 405512 | tf_op jit(solution)/shard_map/ppermute | solution.py:239
  30.4 9.8 %copy-start.1 = (bf16[2,256,256]{2,1,0:T(8,128)(2,1)S(1)}, bf16[2,256,256]{2,1,0:T(8,128)(2,1)}, u32[]{:S(2)}) copy-start(bf16[2,256,256]{2,1,0:T(8,128)(2,1)} %core_ref.1) | copy-start | bytes 786436
  30.4 9.8 %collective-permute-start.15 = (s32[264,128]{1,0:T(8,128)S(1)}, s32[264,128]{1,0:T(8,128)S(1)}, u32[]{:S(2)}, u32[]{:S(2)}) collective-permute-start(s32[264,128]{1,0:T(8,128)S(1)} %get-tuple-element.16), channel_id=1, source_target_pairs={{0,1},{1,0},{2,3},{3,2},{4,5},{5,4},{6,7},{7,6},{8,9},{9,8},{10,11... | collective-permute-start | bytes 405512 | tf_op jit(solution)/shard_map/ppermute | solution.py:239

commit v15 on v11

--- a/solution.py
+++ b/solution.py
@@ -156,9 +156,9 @@
         mixed, diag = fold(total[:half, :half], total[half:, half:])
         return total[:half, half:], mixed, diag
 
-    for (k, coded), out in zip(units, outs):
+    for (k, coded, members), out in zip(units, outs):
         write = write_coded if coded else write_plain
-        write(out, [partial_of((my_lane ^ k) * mono_dev + m) for m in range(mono_dev)])
+        write(out, [partial_of((my_lane ^ k) * mono_dev + m) for m in members])
 
 
 def write_plain(out, parts):
@@ -189,31 +189,35 @@
     out[pl.ds(len(parts) * half, row.shape[0])] = last
 
 
-def read_coded(ref, m, mono_dev):
+def read_coded(ref, m, count):
     half = ref.shape[1]
-    tail = mono_dev * half + 2 * m
+    tail = count * half + 2 * m
     off_code, mixed_code = unpack(ref[tail : tail + 1])
     off_q, mixed_q = unpack(ref[m * half : (m + 1) * half])
     return decode(off_q, off_code), decode(mixed_q, mixed_code), decode(ref[tail + 1 : tail + 2], mixed_code)
 
 
-def summed(plain_ref, coded_refs, m):
-    total = read_plain(plain_ref, m)
-    for ref in coded_refs:
-        total = [a + b for a, b in zip(total, read_coded(ref, m, plain_ref.shape[0]))]
-    return total
-
-
 def merge_kernel(plain_ref, *refs):
-    write_coded(refs[-1], [summed(plain_ref, refs[:-1], m) for m in range(plain_ref.shape[0])])
-
-
-def finish_kernel(core_ref, own_ref, *refs):
+    count = plain_ref.shape[0]
+    sums = []
+    for m in range(count):
+        total = read_plain(plain_ref, m)
+        for ref in refs[:-2]:
+            total = [a + b for a, b in zip(total, read_coded(ref, m, count))]
+        sums.append(total)
+    write_coded(refs[-1], sums)
+
+
+def finish_kernel(members, core_ref, own_ref, *refs):
     parts, out_ref = refs[:-1], refs[-1]
     mono_dev, basis, _ = out_ref.shape
     half = basis // 2
     for m in range(mono_dev):
-        off, mixed, diag = summed(own_ref, parts, m)
+        total = read_plain(own_ref, m)
+        for part, held in zip(parts, members):
+            if m in held:
+                total = [a + b for a, b in zip(total, read_coded(part, held.index(m), len(held)))]
+        off, mixed, diag = total
         first, second = unfold(mixed, diag)
         core = core_ref[m].astype(jnp.float32)
         out_ref[m, :half, :half] = core[:half, :half] + first
@@ -302,8 +306,12 @@
     mine = [near[key] for key in keys]
     pieces = mine + [lax.ppermute(piece, "gddi", xor_pairs(groups, 1)) for piece in mine]
 
-    plain = pltpu.VMEM((mono_dev, basis + 8, half), jnp.float32)
-    coded = pltpu.VMEM((mono_dev * half + round_up(2 * mono_dev, 8), half), jnp.int32)
+    def plain(count):
+        return pltpu.VMEM((count, basis + 8, half), jnp.float32)
+
+    def coded(count):
+        return pltpu.VMEM((count * half + round_up(2 * count, 8), half), jnp.int32)
+
     piece_bytes = groups * lanes * rows * half * 2
 
     keep = pltpu.VMEM if piece_bytes <= 4 * 2**20 else jax.ShapeDtypeStruct
@@ -312,7 +320,7 @@
     def couple(units, name, pieces, fill=False):
         return pl.pallas_call(
             functools.partial(couple_kernel, groups, lanes, mono_dev, units),
-            out_shape=[store] * fill + [coded if is_coded else plain for _, is_coded in units],
+            out_shape=[store] * fill + [(coded if is_coded else plain)(len(members)) for _, is_coded, members in units],
             in_specs=[IN_SMEM] + [IN_VMEM] * (1 + len(pieces)),
             out_specs=[IN_VMEM] * (fill + len(units)),
             compiler_params=pltpu.CompilerParams(
@@ -321,27 +329,40 @@
             name=name,
         )(names, blocks, *pieces)
 
+    everyone = list(range(mono_dev))
+    direct, relayed = everyone[: mono_dev // 2], everyone[mono_dev // 2 :]
     steps = range(1, top)
-    filled, *relayed = couple([(top ^ k, True) for k in steps], "couple_relay", pieces, fill=True)
-    relayed = [along_z(unit, k) for k, unit in zip(steps, relayed)]
-    beyond, own, *close = couple([(top, False), (0, False)] + [(k, True) for k in steps], "couple_rest", [filled])
-    beyond = pl.pallas_call(
+    filled, across, *relays = couple(
+        [(top, True, direct)] + [(top ^ k, True, relayed) for k in steps], "couple_first", pieces, fill=True
+    )
+    relays = [along_z(unit, k) for k, unit in zip(steps, relays)]
+    across = along_z(across, top)
+    units = couple(
+        [(top, False, relayed)] + [(top ^ k, True, direct) for k in steps] + [(k, True, everyone) for k in steps],
+        "couple_second",
+        [filled],
+    )
+    merged = pl.pallas_call(
         merge_kernel,
-        out_shape=pltpu.VMEM((coded.shape[0] + 8, half), jnp.int32),
-        in_specs=[IN_VMEM] * (1 + len(relayed)),
+        out_shape=coded(len(relayed)),
+        in_specs=[IN_VMEM] * (1 + len(relays)) + [hbm],
         out_specs=IN_VMEM,
         compiler_params=small,
         name="merge",
-    )(beyond, *relayed)
-    close = [along_z(gate(unit, beyond), k) for k, unit in zip(steps, close)]
+    )(units[0], *relays, across)
+    merged = along_z(merged, top)
+    far = [along_z(unit, top ^ k) for k, unit in zip(steps, units[1:top])]
+    close = [along_z(unit, k) for k, unit in zip(steps, units[top:])]
+    (own,) = couple([(0, False, everyone)], "couple_own", [filled])
+    terms = [(across, direct), (merged, relayed)] + [(x, direct) for x in far] + [(x, everyone) for x in close]
     return pl.pallas_call(
-        finish_kernel,
+        functools.partial(finish_kernel, [held for _, held in terms]),
         out_shape=jax.ShapeDtypeStruct((mono_dev, basis, basis), jnp.float32),
-        in_specs=[IN_VMEM] * (3 + len(close)),
+        in_specs=[IN_VMEM] * (2 + len(terms)),
         out_specs=IN_VMEM,
         compiler_params=small,
         name="finish",
-    )(h_core, own, *close, along_z(beyond, top))
+    )(h_core, own, *[unit for unit, _ in terms])
 
 
 def solution(mesh):

time: 41.8 us -> 41.5 us (level)
  waiting for transfers between devices: 14.1 us -> 11.9 us
  starting transfers between devices: 21 us -> 22.8 us
    ppermute x7 -> x9, waiting for transfers between devices: 12 us -> 9.7 us  [along_z(): return lax.ppermute(piece, 'intra', xor_pairs(lanes, bit))]
    ppermute x7 -> x9, starting transfers between devices: 14.6 us -> 16.4 us  [along_z(): return lax.ppermute(piece, 'intra', xor_pairs(lanes, bit))]
    pallas_call x2 -> x3, Pallas kernels: 2.55 us -> 2.83 us  [couple(): pl.pallas_call(functools.partial(couple_kernel, groups, lanes, mono_dev,...]
  transfers between devices with their start and end apart: 18 -> 20, of which waited for: 8 -> 8; matrix products, arithmetic and copies ran while one was open for 0% -> 0% of each run, Pallas kernels for 8% -> 9%
where the time goes in v15:
time: 41.5 us; the launch traced here: 41.4 us
  starting transfers between devices  22.8 us (55%)
  waiting for transfers between devices  11.9 us (29%)
  Pallas kernels  5.63 us (14%)
  local copies, waits for them, and re-layouts  0.96 us (2%)
    ppermute x9, starting transfers between devices, along_z(): return lax.ppermute(piece, 'intra', xor_pairs(lanes, bit))  16.4 us
    ppermute x9, waiting for transfers between devices, along_z(): return lax.ppermute(piece, 'intra', xor_pairs(lanes, bit))  9.7 us
    ppermute x3, starting transfers between devices, along_y(): return lax.ppermute(piece, 'gddi', xor_pairs(groups, 2 * y))  4.85 us
    pallas_call x3, Pallas kernels, couple(): pl.pallas_call(functools.partial(couple_kernel, groups, lanes, mono_dev,...  2.83 us
    pallas_call x1, Pallas kernels, local(): pl.pallas_call(stage_kernel, out_shape=[pltpu.SMEM((nbr.shape[1], nbr.sha...  1.62 us
    ppermute x8, starting transfers between devices, local(): lax.ppermute(piece, 'gddi', xor_pairs(groups, 1))  1.59 us
    ppermute x8, waiting for transfers between devices, local(): lax.ppermute(piece, 'gddi', xor_pairs(groups, 1))  1.36 us
    pallas_call x1, Pallas kernels, local(): pl.pallas_call(functools.partial(finish_kernel, [held for _, held in term...  1.01 us
  transfers between devices with their start and end apart: 20, of which 8 were waited for; matrix products, arithmetic and copies ran while one was open for 0% of the time, Pallas kernels for 9%

profile of v15, /device:TPU:0, one launch (start us, length us, event | category | flops | bytes accessed | tf_op | source)
XLA Modules:
  0.0 41.4 jit_solution(4267397687134867754)
XLA Ops:
  0.0 0.9 %copy-done = bf16[2,256,256]{2,1,0:T(8,128)(2,1)S(1)} copy-done((bf16[2,256,256]{2,1,0:T(8,128)(2,1)S(1)}, bf16[2,256,256]{2,1,0:T(8,128)(2,1)}, u32[]{:S(2)}) %copy-start) | copy-done | bytes 262168
  1.0 4.1 %collective-permute-start.1 = (bf16[528,128]{1,0:T(8,128)(2,1)S(1)}, bf16[528,128]{1,0:T(8,128)(2,1)S(1)}, u32[]{:S(2)}, u32[]{:S(2)}) collective-permute-start(bf16[528,128]{1,0:T(8,128)(2,1)S(1)} %fold.1.refs_0_), channel_id=1, source_target_pairs={{0,2},{1,3},{2,0},{3,1},{4,6},{5,7},{6,4},{7,5},{8,10},{9,11},{10,... | collective-permute-start | bytes 405512 | tf_op jit(solution)/shard_map/ppermute | solution.py:247
  5.1 1.6 %collective-permute-start.2 = (bf16[528,128]{1,0:T(8,128)(2,1)S(1)}, bf16[528,128]{1,0:T(8,128)(2,1)S(1)}, u32[]{:S(2)}, u32[]{:S(2)}) collective-permute-start(bf16[528,128]{1,0:T(8,128)(2,1)S(1)} %fold.1.refs_0_), channel_id=1, source_target_pairs={{0,1},{1,0},{2,3},{3,2},{4,5},{5,4},{6,7},{7,6},{8,9},{9,8},{10,11... | collective-permute-start | bytes 405512 | tf_op jit(solution)/shard_map/ppermute | solution.py:247
  6.7 1.5 %collective-permute-start = (bf16[528,128]{1,0:T(8,128)(2,1)S(1)}, bf16[528,128]{1,0:T(8,128)(2,1)S(1)}, u32[]{:S(2)}, u32[]{:S(2)}) collective-permute-start(bf16[528,128]{1,0:T(8,128)(2,1)S(1)} %fold.1.refs_0_), channel_id=1, source_target_pairs={{0,8},{4,12},{8,0},{12,4},{1,9},{5,13},{9,1},{13,5},{2,10},{6,14},... | collective-permute-start | bytes 405512 | tf_op jit(solution)/shard_map/ppermute | solution.py:250
  8.2 3.5 %collective-permute-done.1.piece_ref = bf16[528,128]{1,0:T(8,128)(2,1)S(1)} collective-permute-done((bf16[528,128]{1,0:T(8,128)(2,1)S(1)}, bf16[528,128]{1,0:T(8,128)(2,1)S(1)}, u32[]{:S(2)}, u32[]{:S(2)}) %collective-permute-start.1) | collective-permute-done | bytes 135200 | tf_op jit(solution)/shard_map/ppermute | solution.py:247
  11.9 1.5 %collective-permute-start.3 = (bf16[528,128]{1,0:T(8,128)(2,1)S(1)}, bf16[528,128]{1,0:T(8,128)(2,1)S(1)}, u32[]{:S(2)}, u32[]{:S(2)}) collective-permute-start(bf16[528,128]{1,0:T(8,128)(2,1)S(1)} %gate.3.refs_2_), channel_id=1, source_target_pairs={{0,1},{1,0},{2,3},{3,2},{4,5},{5,4},{6,7},{7,6},{8,9},{9,8},{10,11... | collective-permute-start | bytes 405512 | tf_op jit(solution)/shard_map/ppermute | solution.py:247
  13.4 0.5 %collective-permute-start.9 = (bf16[528,128]{1,0:T(8,128)(2,1)S(1)}, bf16[528,128]{1,0:T(8,128)(2,1)S(1)}, u32[]{:S(2)}, u32[]{:S(2)}) collective-permute-start(bf16[528,128]{1,0:T(8,128)(2,1)S(1)} %gate.3.refs_2_), channel_id=1, source_target_pairs={{0,4},{4,0},{8,12},{12,8},{1,5},{5,1},{9,13},{13,9},{2,6},{6,2},{1... | collective-permute-start | bytes 405512 | tf_op jit(solution)/shard_map/ppermute | solution.py:307
  13.9 1.5 %collective-permute-start.5 = (bf16[528,128]{1,0:T(8,128)(2,1)S(1)}, bf16[528,128]{1,0:T(8,128)(2,1)S(1)}, u32[]{:S(2)}, u32[]{:S(2)}) collective-permute-start(bf16[528,128]{1,0:T(8,128)(2,1)S(1)} %gate.3.refs_2_), channel_id=1, source_target_pairs={{0,8},{4,12},{8,0},{12,4},{1,9},{5,13},{9,1},{13,5},{2,10},{6,14},... | collective-permute-start | bytes 405512 | tf_op jit(solution)/shard_map/ppermute | solution.py:250
  15.5 0.6 %collective-permute-start.4 = (bf16[528,128]{1,0:T(8,128)(2,1)S(1)}, bf16[528,128]{1,0:T(8,128)(2,1)S(1)}, u32[]{:S(2)}, u32[]{:S(2)}) collective-permute-start(bf16[528,128]{1,0:T(8,128)(2,1)S(1)} %collective-permute-done.refs_2_.piece_ref), channel_id=1, source_target_pairs={{0,1},{1,0},{2,3},{3,2},{4,5},{5,4},{6,7},{7,6},{8,9},{9,8},{10,11... | collective-permute-start | bytes 405512 | tf_op jit(solution)/shard_map/ppermute | solution.py:247
  16.1 0.9 %collective-permute-done.3.refs_0_.refs_3_ = bf16[528,128]{1,0:T(8,128)(2,1)S(1)} collective-permute-done((bf16[528,128]{1,0:T(8,128)(2,1)S(1)}, bf16[528,128]{1,0:T(8,128)(2,1)S(1)}, u32[]{:S(2)}, u32[]{:S(2)}) %collective-permute-start.3) | collective-permute-done | bytes 135200 | tf_op jit(solution)/shard_map/ppermute | solution.py:247
  17.0 1.8 %collective-permute-start.6 = (bf16[528,128]{1,0:T(8,128)(2,1)S(1)}, bf16[528,128]{1,0:T(8,128)(2,1)S(1)}, u32[]{:S(2)}, u32[]{:S(2)}) collective-permute-start(bf16[528,128]{1,0:T(8,128)(2,1)S(1)} %collective-permute-done.3.refs_0_.refs_3_), channel_id=1, source_target_pairs={{0,8},{4,12},{8,0},{12,4},{1,9},{5,13},{9,1},{13,5},{2,10},{6,14},... | collective-permute-start | bytes 405512 | tf_op jit(solution)/shard_map/ppermute | solution.py:250
  18.8 1.6 %stage.1 = (s32[8,32]{1,0:T(8,128)S(4)}, bf16[8,2,256,256]{3,2,1,0:T(8,128)(2,1)S(1)}, bf16[528,128]{1,0:T(8,128)(2,1)S(1)}) custom-call(s32[8,32]{1,0:T(8,128)} %bitcast.1, bf16[8,2,256,256]{3,2,1,0:T(8,128)(2,1)} %esp_ref.1, bf16[528,128]{1,0:T(8,128)(2,1)S(1)} %collective-permute-done.refs_2_.piece_ref, ...), custom_call_target="tpu_custom_call" | custom-call | tf_op jit(solution)/shard_map/stage/pallas_call | solution.py:287
  21.5 0.8 %collective-permute-done.6.refs_7_ = bf16[528,128]{1,0:T(8,128)(2,1)S(1)} collective-permute-done((bf16[528,128]{1,0:T(8,128)(2,1)S(1)}, bf16[528,128]{1,0:T(8,128)(2,1)S(1)}, u32[]{:S(2)}, u32[]{:S(2)}) %collective-permute-start.6) | collective-permute-done | bytes 135200 | tf_op jit(solution)/shard_map/ppermute | solution.py:250
  22.6 1.1 %collective-permute-done.14.refs_15_ = bf16[528,128]{1,0:T(8,128)(2,1)S(1)} collective-permute-done((bf16[528,128]{1,0:T(8,128)(2,1)S(1)}, bf16[528,128]{1,0:T(8,128)(2,1)S(1)}, u32[]{:S(2)}, u32[]{:S(2)}) %collective-permute-start.14) | collective-permute-done | bytes 135200 | tf_op jit(solution)/shard_map/ppermute | solution.py:307
  23.7 0.9 %couple_first.1 = (bf16[16,528,128]{2,1,0:T(8,128)(2,1)S(1)}, s32[136,128]{1,0:T(8,128)S(1)}, s32[136,128]{1,0:T(8,128)S(1)}) custom-call(s32[8,32]{1,0:T(8,128)S(4)} %get-tuple-element.14.nbr_ref, bf16[8,2,256,256]{3,2,1,0:T(8,128)(2,1)S(1)} %get-tuple-element.15.esp_ref, bf16[528,128]{1,0:T(8,128)(2,1)S(1)} %fold.1.refs_0_, ...), custom_call_target="tpu_custom_call" | custom-call | tf_op jit(solution)/shard_map/couple_first/pallas_call | solution.py:321
  24.6 2.5 %collective-permute-start.15 = (s32[136,128]{1,0:T(8,128)S(1)}, s32[136,128]{1,0:T(8,128)S(1)}, u32[]{:S(2)}, u32[]{:S(2)}) collective-permute-start(s32[136,128]{1,0:T(8,128)S(1)} %get-tuple-element.18), channel_id=1, source_target_pairs={{0,2},{1,3},{2,0},{3,1},{4,6},{5,7},{6,4},{7,5},{8,10},{9,11},{10,... | collective-permute-start | bytes 208904 | tf_op jit(solution)/shard_map/ppermute | solution.py:247
  27.1 2.5 %collective-permute-start.16 = (s32[136,128]{1,0:T(8,128)S(1)}, s32[136,128]{1,0:T(8,128)S(1)}, u32[]{:S(2)}, u32[]{:S(2)}) collective-permute-start(s32[136,128]{1,0:T(8,128)S(1)} %get-tuple-element.20), channel_id=1, source_target_pairs={{0,1},{1,0},{2,3},{3,2},{4,5},{5,4},{6,7},{7,6},{8,9},{9,8},{10,11... | collective-permute-start | bytes 208904 | tf_op jit(solution)/shard_map/ppermute | solution.py:247
  29.5 1.2 %couple_second.1 = (f32[1,264,128]{2,1,0:T(8,128)S(1)}, s32[136,128]{1,0:T(8,128)S(1)}, s32[264,128]{1,0:T(8,128)S(1)}) custom-call(s32[8,32]{1,0:T(8,128)S(4)} %get-tuple-element.14.nbr_ref, bf16[8,2,256,256]{3,2,1,0:T(8,128)(2,1)S(1)} %get-tuple-element.15.esp_ref, bf16[16,528,128]{2,1,0:T(8,128)(2,1)S(1)} %get-tuple-element.17.refs_0_), custom_call_target="tpu_custom_call" | custom-call | tf_op jit(solution)/shard_map/couple_second/pallas_call | solution.py:321
  30.8 1.5 %collective-permute-start.18 = (s32[136,128]{1,0:T(8,128)S(1)}, s32[136,128]{1,0:T(8,128)S(1)}, u32[]{:S(2)}, u32[]{:S(2)}) collective-permute-start(s32[136,128]{1,0:T(8,128)S(1)} %get-tuple-element.21), channel_id=1, source_target_pairs={{0,3},{1,2},{2,1},{3,0},{4,7},{5,6},{6,5},{7,4},{8,11},{9,10},{10,... | collective-permute-start | bytes 208904 | tf_op jit(solution)/shard_map/ppermute | solution.py:247
  32.5 2.0 %collective-permute-start.17 = (s32[136,128]{1,0:T(8,128)S(1)}, s32[136,128]{1,0:T(8,128)S(1)}, u32[]{:S(2)}, u32[]{:S(2)}) collective-permute-start(s32[136,128]{1,0:T(8,128)S(1)} %merge.1), channel_id=1, source_target_pairs={{0,2},{1,3},{2,0},{3,1},{4,6},{5,7},{6,4},{7,5},{8,10},{9,11},{10,... | collective-permute-start | bytes 208904 | tf_op jit(solution)/shard_map/ppermute | solution.py:247
  34.5 0.7 %couple_own.1.own_ref = f32[2,264,128]{2,1,0:T(8,128)S(1)} custom-call(s32[8,32]{1,0:T(8,128)S(4)} %get-tuple-element.14.nbr_ref, bf16[8,2,256,256]{3,2,1,0:T(8,128)(2,1)S(1)} %get-tuple-element.15.esp_ref, bf16[16,528,128]{2,1,0:T(8,128)(2,1)S(1)} %get-tuple-element.17.refs_0_), custom_call_target="tpu_custom_call" | custom-call | tf_op jit(solution)/shard_map/couple_own/pallas_call | solution.py:321
  35.2 2.9 %collective-permute-done.18.refs_2_ = s32[136,128]{1,0:T(8,128)S(1)} collective-permute-done((s32[136,128]{1,0:T(8,128)S(1)}, s32[136,128]{1,0:T(8,128)S(1)}, u32[]{:S(2)}, u32[]{:S(2)}) %collective-permute-start.18) | collective-permute-done | bytes 69664 | tf_op jit(solution)/shard_map/ppermute | solution.py:247
  38.1 2.3 %collective-permute-done.17.refs_1_ = s32[136,128]{1,0:T(8,128)S(1)} collective-permute-done((s32[136,128]{1,0:T(8,128)S(1)}, s32[136,128]{1,0:T(8,128)S(1)}, u32[]{:S(2)}, u32[]{:S(2)}) %collective-permute-start.17) | collective-permute-done | bytes 69664 | tf_op jit(solution)/shard_map/ppermute | solution.py:247
  40.3 1.0 %finish.1 = f32[2,256,256]{2,1,0:T(8,128)} custom-call(bf16[2,256,256]{2,1,0:T(8,128)(2,1)S(1)} %copy-done.1, f32[2,264,128]{2,1,0:T(8,128)S(1)} %couple_own.1.own_ref, s32[136,128]{1,0:T(8,128)S(1)} %collective-permute-done.15.refs_1_.refs_0_, s32[136,128]{1,0:T(8,128)S(1)} %collective-permute-done.17.refs_1_, ...), custom_call_target="tpu_custom_call" | custom-call | tf_op jit(solution)/shard_map/finish/pallas_call | solution.py:358
  (29 shorter events, 1.8 us)
Async XLA Ops:
  0.0 0.9 %copy-start = (bf16[2,256,256]{2,1,0:T(8,128)(2,1)S(1)}, bf16[2,256,256]{2,1,0:T(8,128)(2,1)}, u32[]{:S(2)}) copy-start(bf16[2,256,256]{2,1,0:T(8,128)(2,1)} %dens_ref.1) | copy-start | bytes 786436
  1.0 10.7 %collective-permute-start.1 = (bf16[528,128]{1,0:T(8,128)(2,1)S(1)}, bf16[528,128]{1,0:T(8,128)(2,1)S(1)}, u32[]{:S(2)}, u32[]{:S(2)}) collective-permute-start(bf16[528,128]{1,0:T(8,128)(2,1)S(1)} %fold.1.refs_0_), channel_id=1, source_target_pairs={{0,2},{1,3},{2,0},{3,1},{4,6},{5,7},{6,4},{7,5},{8,10},{9,11},{10,... | collective-permute-start | bytes 405512 | tf_op jit(solution)/shard_map/ppermute | solution.py:247
  5.1 6.8 %collective-permute-start.2 = (bf16[528,128]{1,0:T(8,128)(2,1)S(1)}, bf16[528,128]{1,0:T(8,128)(2,1)S(1)}, u32[]{:S(2)}, u32[]{:S(2)}) collective-permute-start(bf16[528,128]{1,0:T(8,128)(2,1)S(1)} %fold.1.refs_0_), channel_id=1, source_target_pairs={{0,1},{1,0},{2,3},{3,2},{4,5},{5,4},{6,7},{7,6},{8,9},{9,8},{10,11... | collective-permute-start | bytes 405512 | tf_op jit(solution)/shard_map/ppermute | solution.py:247
  6.7 5.2 %collective-permute-start = (bf16[528,128]{1,0:T(8,128)(2,1)S(1)}, bf16[528,128]{1,0:T(8,128)(2,1)S(1)}, u32[]{:S(2)}, u32[]{:S(2)}) collective-permute-start(bf16[528,128]{1,0:T(8,128)(2,1)S(1)} %fold.1.refs_0_), channel_id=1, source_target_pairs={{0,8},{4,12},{8,0},{12,4},{1,9},{5,13},{9,1},{13,5},{2,10},{6,14},... | collective-permute-start | bytes 405512 | tf_op jit(solution)/shard_map/ppermute | solution.py:250
  8.2 7.3 %collective-permute-start.7 = (bf16[528,128]{1,0:T(8,128)(2,1)S(1)}, bf16[528,128]{1,0:T(8,128)(2,1)S(1)}, u32[]{:S(2)}, u32[]{:S(2)}) collective-permute-start(bf16[528,128]{1,0:T(8,128)(2,1)S(1)} %fold.1.refs_0_), channel_id=1, source_target_pairs={{0,4},{4,0},{8,12},{12,8},{1,5},{5,1},{9,13},{13,9},{2,6},{6,2},{1... | collective-permute-start | bytes 405512 | tf_op jit(solution)/shard_map/ppermute | solution.py:307
  11.9 5.1 %collective-permute-start.3 = (bf16[528,128]{1,0:T(8,128)(2,1)S(1)}, bf16[528,128]{1,0:T(8,128)(2,1)S(1)}, u32[]{:S(2)}, u32[]{:S(2)}) collective-permute-start(bf16[528,128]{1,0:T(8,128)(2,1)S(1)} %gate.3.refs_2_), channel_id=1, source_target_pairs={{0,1},{1,0},{2,3},{3,2},{4,5},{5,4},{6,7},{7,6},{8,9},{9,8},{10,11... | collective-permute-start | bytes 405512 | tf_op jit(solution)/shard_map/ppermute | solution.py:247
  13.4 7.0 %collective-permute-start.8 = (bf16[528,128]{1,0:T(8,128)(2,1)S(1)}, bf16[528,128]{1,0:T(8,128)(2,1)S(1)}, u32[]{:S(2)}, u32[]{:S(2)}) collective-permute-start(bf16[528,128]{1,0:T(8,128)(2,1)S(1)} %collective-permute-done.2.refs_1_), channel_id=1, source_target_pairs={{0,4},{4,0},{8,12},{12,8},{1,5},{5,1},{9,13},{13,9},{2,6},{6,2},{1... | collective-permute-start | bytes 405512 | tf_op jit(solution)/shard_map/ppermute | solution.py:307
  13.4 7.1 %collective-permute-start.9 = (bf16[528,128]{1,0:T(8,128)(2,1)S(1)}, bf16[528,128]{1,0:T(8,128)(2,1)S(1)}, u32[]{:S(2)}, u32[]{:S(2)}) collective-permute-start(bf16[528,128]{1,0:T(8,128)(2,1)S(1)} %gate.3.refs_2_), channel_id=1, source_target_pairs={{0,4},{4,0},{8,12},{12,8},{1,5},{5,1},{9,13},{13,9},{2,6},{6,2},{1... | collective-permute-start | bytes 405512 | tf_op jit(solution)/shard_map/ppermute | solution.py:307
  13.9 7.1 %collective-permute-start.5 = (bf16[528,128]{1,0:T(8,128)(2,1)S(1)}, bf16[528,128]{1,0:T(8,128)(2,1)S(1)}, u32[]{:S(2)}, u32[]{:S(2)}) collective-permute-start(bf16[528,128]{1,0:T(8,128)(2,1)S(1)} %gate.3.refs_2_), channel_id=1, source_target_pairs={{0,8},{4,12},{8,0},{12,4},{1,9},{5,13},{9,1},{13,5},{2,10},{6,14},... | collective-permute-start | bytes 405512 | tf_op jit(solution)/shard_map/ppermute | solution.py:250
  15.5 5.6 %collective-permute-start.4 = (bf16[528,128]{1,0:T(8,128)(2,1)S(1)}, bf16[528,128]{1,0:T(8,128)(2,1)S(1)}, u32[]{:S(2)}, u32[]{:S(2)}) collective-permute-start(bf16[528,128]{1,0:T(8,128)(2,1)S(1)} %collective-permute-done.refs_2_.piece_ref), channel_id=1, source_target_pairs={{0,1},{1,0},{2,3},{3,2},{4,5},{5,4},{6,7},{7,6},{8,9},{9,8},{10,11... | collective-permute-start | bytes 405512 | tf_op jit(solution)/shard_map/ppermute | solution.py:247
  17.0 5.3 %collective-permute-start.6 = (bf16[528,128]{1,0:T(8,128)(2,1)S(1)}, bf16[528,128]{1,0:T(8,128)(2,1)S(1)}, u32[]{:S(2)}, u32[]{:S(2)}) collective-permute-start(bf16[528,128]{1,0:T(8,128)(2,1)S(1)} %collective-permute-done.3.refs_0_.refs_3_), channel_id=1, source_target_pairs={{0,8},{4,12},{8,0},{12,4},{1,9},{5,13},{9,1},{13,5},{2,10},{6,14},... | collective-permute-start | bytes 405512 | tf_op jit(solution)/shard_map/ppermute | solution.py:250
  20.4 2.1 %collective-permute-start.11 = (bf16[528,128]{1,0:T(8,128)(2,1)S(1)}, bf16[528,128]{1,0:T(8,128)(2,1)S(1)}, u32[]{:S(2)}, u32[]{:S(2)}) collective-permute-start(bf16[528,128]{1,0:T(8,128)(2,1)S(1)} %get-tuple-element.16.refs_4_), channel_id=1, source_target_pairs={{0,4},{4,0},{8,12},{12,8},{1,5},{5,1},{9,13},{13,9},{2,6},{6,2},{1... | collective-permute-start | bytes 405512 | tf_op jit(solution)/shard_map/ppermute | solution.py:307
  20.5 1.9 %collective-permute-start.10 = (bf16[528,128]{1,0:T(8,128)(2,1)S(1)}, bf16[528,128]{1,0:T(8,128)(2,1)S(1)}, u32[]{:S(2)}, u32[]{:S(2)}) collective-permute-start(bf16[528,128]{1,0:T(8,128)(2,1)S(1)} %collective-permute-done.3.refs_0_.refs_3_), channel_id=1, source_target_pairs={{0,4},{4,0},{8,12},{12,8},{1,5},{5,1},{9,13},{13,9},{2,6},{6,2},{1... | collective-permute-start | bytes 405512 | tf_op jit(solution)/shard_map/ppermute | solution.py:307
  21.0 1.4 %collective-permute-start.13 = (bf16[528,128]{1,0:T(8,128)(2,1)S(1)}, bf16[528,128]{1,0:T(8,128)(2,1)S(1)}, u32[]{:S(2)}, u32[]{:S(2)}) collective-permute-start(bf16[528,128]{1,0:T(8,128)(2,1)S(1)} %collective-permute-done.5.refs_6_), channel_id=1, source_target_pairs={{0,4},{4,0},{8,12},{12,8},{1,5},{5,1},{9,13},{13,9},{2,6},{6,2},{1... | collective-permute-start | bytes 405512 | tf_op jit(solution)/shard_map/ppermute | solution.py:307
  21.1 1.5 %collective-permute-start.12 = (bf16[528,128]{1,0:T(8,128)(2,1)S(1)}, bf16[528,128]{1,0:T(8,128)(2,1)S(1)}, u32[]{:S(2)}, u32[]{:S(2)}) collective-permute-start(bf16[528,128]{1,0:T(8,128)(2,1)S(1)} %collective-permute-done.4.refs_5_), channel_id=1, source_target_pairs={{0,4},{4,0},{8,12},{12,8},{1,5},{5,1},{9,13},{13,9},{2,6},{6,2},{1... | collective-permute-start | bytes 405512 | tf_op jit(solution)/shard_map/ppermute | solution.py:307
  22.3 1.4 %collective-permute-start.14 = (bf16[528,128]{1,0:T(8,128)(2,1)S(1)}, bf16[528,128]{1,0:T(8,128)(2,1)S(1)}, u32[]{:S(2)}, u32[]{:S(2)}) collective-permute-start(bf16[528,128]{1,0:T(8,128)(2,1)S(1)} %collective-permute-done.6.refs_7_), channel_id=1, source_target_pairs={{0,4},{4,0},{8,12},{12,8},{1,5},{5,1},{9,13},{13,9},{2,6},{6,2},{1... | collective-permute-start | bytes 405512 | tf_op jit(solution)/shard_map/ppermute | solution.py:307
  24.6 7.8 %collective-permute-start.15 = (s32[136,128]{1,0:T(8,128)S(1)}, s32[136,128]{1,0:T(8,128)S(1)}, u32[]{:S(2)}, u32[]{:S(2)}) collective-permute-start(s32[136,128]{1,0:T(8,128)S(1)} %get-tuple-element.18), channel_id=1, source_target_pairs={{0,2},{1,3},{2,0},{3,1},{4,6},{5,7},{6,4},{7,5},{8,10},{9,11},{10,... | collective-permute-start | bytes 208904 | tf_op jit(solution)/shard_map/ppermute | solution.py:247
  27.1 5.3 %collective-permute-start.16 = (s32[136,128]{1,0:T(8,128)S(1)}, s32[136,128]{1,0:T(8,128)S(1)}, u32[]{:S(2)}, u32[]{:S(2)}) collective-permute-start(s32[136,128]{1,0:T(8,128)S(1)} %get-tuple-element.20), channel_id=1, source_target_pairs={{0,1},{1,0},{2,3},{3,2},{4,5},{5,4},{6,7},{7,6},{8,9},{9,8},{10,11... | collective-permute-start | bytes 208904 | tf_op jit(solution)/shard_map/ppermute | solution.py:247
  30.8 7.3 %collective-permute-start.19 = (s32[264,128]{1,0:T(8,128)S(1)}, s32[264,128]{1,0:T(8,128)S(1)}, u32[]{:S(2)}, u32[]{:S(2)}) collective-permute-start(s32[264,128]{1,0:T(8,128)S(1)} %get-tuple-element.22), channel_id=1, source_target_pairs={{0,1},{1,0},{2,3},{3,2},{4,5},{5,4},{6,7},{7,6},{8,9},{9,8},{10,11... | collective-permute-start | bytes 405512 | tf_op jit(solution)/shard_map/ppermute | solution.py:247
  30.8 7.2 %collective-permute-start.18 = (s32[136,128]{1,0:T(8,128)S(1)}, s32[136,128]{1,0:T(8,128)S(1)}, u32[]{:S(2)}, u32[]{:S(2)}) collective-permute-start(s32[136,128]{1,0:T(8,128)S(1)} %get-tuple-element.21), channel_id=1, source_target_pairs={{0,3},{1,2},{2,1},{3,0},{4,7},{5,6},{6,5},{7,4},{8,11},{9,10},{10,... | collective-permute-start | bytes 208904 | tf_op jit(solution)/shard_map/ppermute | solution.py:247
  32.5 7.9 %copy-start.1 = (bf16[2,256,256]{2,1,0:T(8,128)(2,1)S(1)}, bf16[2,256,256]{2,1,0:T(8,128)(2,1)}, u32[]{:S(2)}) copy-start(bf16[2,256,256]{2,1,0:T(8,128)(2,1)} %core_ref.1) | copy-start | bytes 786436
  32.5 7.8 %collective-permute-start.17 = (s32[136,128]{1,0:T(8,128)S(1)}, s32[136,128]{1,0:T(8,128)S(1)}, u32[]{:S(2)}, u32[]{:S(2)}) collective-permute-start(s32[136,128]{1,0:T(8,128)S(1)} %merge.1), channel_id=1, source_target_pairs={{0,2},{1,3},{2,0},{3,1},{4,6},{5,7},{6,4},{7,5},{8,10},{9,11},{10,... | collective-permute-start | bytes 208904 | tf_op jit(solution)/shard_map/ppermute | solution.py:247

commit v16 on v9

--- a/solution.py
+++ b/solution.py
@@ -149,15 +149,17 @@
         return jnp.concatenate([top, bottom], axis=0)
 
     def partial_of(fragment):
-        total = None
+        high, low, blocks = [], [], []
         for s in range(slot_dev):
             name = nbr_ref[my_lane * slot_dev + s, my_group * mono_grp + fragment]
             block = esp_ref[fragment, s]
             half_term = jnp.dot(block, near_density(name), preferred_element_type=jnp.float32)
-            high = half_term.astype(jnp.bfloat16)
-            low = (half_term - high.astype(jnp.float32)).astype(jnp.bfloat16)
-            term = transposed_dot(high, block) + transposed_dot(low, block)
-            total = term if total is None else total + term
+            high.append(half_term.astype(jnp.bfloat16))
+            low.append((half_term - high[-1].astype(jnp.float32)).astype(jnp.bfloat16))
+            blocks.append(block)
+        both = jnp.concatenate([jnp.concatenate(high, axis=1), jnp.concatenate(low, axis=1)], axis=0)
+        both = transposed_dot(both, jnp.concatenate(blocks, axis=1))
+        total = both[:basis] + both[basis:]
         mixed, diag = fold(total[:half, :half], total[half:, half:])
         return total[:half, half:], mixed, diag
 
@@ -207,10 +209,6 @@
     for ref in coded_refs:
         total = [a + b for a, b in zip(total, read_coded(ref, m, plain_ref.shape[0]))]
     return total
-
-
-def merge_kernel(plain_ref, *refs):
-    write_coded(refs[-1], [summed(plain_ref, refs[:-1], m) for m in range(plain_ref.shape[0])])
 
 
 def finish_kernel(core_ref, own_ref, *refs):
@@ -348,30 +346,22 @@
             name=name,
         )(names, blocks, *pieces)
 
-    steps = range(1, top)
-    filled, *relayed = couple([(top ^ k, True) for k in steps], "couple_relay", pieces, fill=True)
-    relayed = [along_z(unit, k) for k, unit in zip(steps, relayed)]
-    close = couple([(k, True) for k in steps], "couple_near", [filled])
-    close = [along_z(unit, k) for k, unit in zip(steps, close)]
+    filled, beyond = couple([(top, True)], "couple_first", pieces, fill=True)
+    beyond = {top: along_z(beyond, top)}
     for _ in range(5):
-        close = [gate(unit) for unit in close]
-    beyond, own = couple([(top, False), (0, False)], "couple_far", [filled])
-    beyond = pl.pallas_call(
-        merge_kernel,
-        out_shape=coded,
-        in_specs=[IN_VMEM] * (1 + len(relayed)),
-        out_specs=IN_VMEM,
-        compiler_params=small,
-        name="merge",
-    )(beyond, *relayed)
+        beyond[top] = gate(beyond[top])
+    rest = [k for k in range(1, lanes) if k != top]
+    own, *units = couple([(0, False)] + [(k, True) for k in rest], "couple_rest", [filled])
+    for k, unit in zip(rest, units):
+        beyond[k] = along_z(unit, k)
     return pl.pallas_call(
         finish_kernel,
         out_shape=jax.ShapeDtypeStruct((mono_dev, basis, basis), jnp.float32),
-        in_specs=[IN_VMEM] * (3 + len(close)),
+        in_specs=[IN_VMEM] * (1 + lanes),
         out_specs=IN_VMEM,
         compiler_params=small,
         name="finish",
-    )(h_core, own, *close, along_z(beyond, top))
+    )(h_core, own, *[beyond[k] for k in range(1, lanes)])
 
 
 def solution(mesh):

time: 41.7 us -> 41.2 us (0.988)
  starting transfers between devices: 16.5 us -> 17.8 us
  Pallas kernels: 6.52 us -> 5.49 us
  waiting for transfers between devices: 17.4 us -> 16.7 us
    ppermute x6, starting transfers between devices: 10.5 us -> 11.8 us  [along_z(): return lax.ppermute(piece, 'intra', xor_pairs(lanes, bit))]
    pallas_call x3 -> x2, Pallas kernels: 3.57 us -> 2.64 us  [couple(): pl.pallas_call(functools.partial(couple_kernel, groups, lanes, mono_dev,...]
    ppermute x6, waiting for transfers between devices: 11.7 us -> 10.9 us  [along_z(): return lax.ppermute(piece, 'intra', xor_pairs(lanes, bit))]
  transfers between devices with their start and end apart: 16 -> 16, of which waited for: 11 -> 10; matrix products, arithmetic and copies ran while one was open for 0% -> 0% of each run, Pallas kernels for 10% -> 8%
where the time goes in v16:
time: 41.2 us; the launch traced here: 41.1 us
  starting transfers between devices  17.8 us (43%)
  waiting for transfers between devices  16.7 us (41%)
  Pallas kernels  5.49 us (13%)
  local copies, waits for them, and re-layouts  0.95 us (2%)
    ppermute x6, starting transfers between devices, along_z(): return lax.ppermute(piece, 'intra', xor_pairs(lanes, bit))  11.8 us
    ppermute x6, waiting for transfers between devices, along_z(): return lax.ppermute(piece, 'intra', xor_pairs(lanes, bit))  10.9 us
    ppermute x2, waiting for transfers between devices, across(): return lax.ppermute(piece, ('gddi', 'intra'), pairs)  4.49 us
    ppermute x2, starting transfers between devices, along_y(): return lax.ppermute(piece, 'gddi', xor_pairs(groups, 2 * y))  3.37 us
    pallas_call x2, Pallas kernels, couple(): pl.pallas_call(functools.partial(couple_kernel, groups, lanes, mono_dev,...  2.64 us
    ppermute x2, starting transfers between devices, across(): return lax.ppermute(piece, ('gddi', 'intra'), pairs)  1.98 us
    pallas_call x1, Pallas kernels, local(): pl.pallas_call(stage_kernel, out_shape=[pltpu.SMEM((nbr.shape[1], nbr.sha...  1.62 us
    ppermute x6, waiting for transfers between devices, to_mate(): return lax.ppermute(piece, 'gddi', xor_pairs(groups, 1))  1.24 us
  transfers between devices with their start and end apart: 16, of which 10 were waited for; matrix products, arithmetic and copies ran while one was open for 0% of the time, Pallas kernels for 8%

profile of v16, /device:TPU:0, one launch (start us, length us, event | category | flops | bytes accessed | tf_op | source)
XLA Modules:
  0.0 41.1 jit_solution(10046878209642099841)
XLA Ops:
  0.0 0.9 %copy-done = bf16[2,256,256]{2,1,0:T(8,128)(2,1)S(1)} copy-done((bf16[2,256,256]{2,1,0:T(8,128)(2,1)S(1)}, bf16[2,256,256]{2,1,0:T(8,128)(2,1)}, u32[]{:S(2)}) %copy-start) | copy-done | bytes 262168
  1.0 3.1 %collective-permute-start = (bf16[528,128]{1,0:T(8,128)(2,1)S(1)}, bf16[528,128]{1,0:T(8,128)(2,1)S(1)}, u32[]{:S(2)}, u32[]{:S(2)}) collective-permute-start(bf16[528,128]{1,0:T(8,128)(2,1)S(1)} %fold.1.refs_0_), channel_id=1, source_target_pairs={{0,1},{1,0},{2,3},{3,2},{4,5},{5,4},{6,7},{7,6},{8,9},{9,8},{10,11... | collective-permute-start | bytes 405512 | tf_op jit(solution)/shard_map/ppermute | solution.py:246
  4.1 2.6 %collective-permute-start.2 = (bf16[528,128]{1,0:T(8,128)(2,1)S(1)}, bf16[528,128]{1,0:T(8,128)(2,1)S(1)}, u32[]{:S(2)}, u32[]{:S(2)}) collective-permute-start(bf16[528,128]{1,0:T(8,128)(2,1)S(1)} %fold.1.refs_0_), channel_id=1, source_target_pairs={{0,2},{1,3},{2,0},{3,1},{4,6},{5,7},{6,4},{7,5},{8,10},{9,11},{10,... | collective-permute-start | bytes 405512 | tf_op jit(solution)/shard_map/ppermute | solution.py:246
  6.7 1.5 %collective-permute-start.3 = (bf16[528,128]{1,0:T(8,128)(2,1)S(1)}, bf16[528,128]{1,0:T(8,128)(2,1)S(1)}, u32[]{:S(2)}, u32[]{:S(2)}) collective-permute-start(bf16[528,128]{1,0:T(8,128)(2,1)S(1)} %fold.1.refs_0_), channel_id=1, source_target_pairs={{0,8},{4,12},{8,0},{12,4},{1,9},{5,13},{9,1},{13,5},{2,10},{6,14},... | collective-permute-start | bytes 405512 | tf_op jit(solution)/shard_map/ppermute | solution.py:249
  8.2 1.5 %collective-permute-done.refs_1_ = bf16[528,128]{1,0:T(8,128)(2,1)S(1)} collective-permute-done((bf16[528,128]{1,0:T(8,128)(2,1)S(1)}, bf16[528,128]{1,0:T(8,128)(2,1)S(1)}, u32[]{:S(2)}, u32[]{:S(2)}) %collective-permute-start) | collective-permute-done | bytes 135200 | tf_op jit(solution)/shard_map/ppermute | solution.py:246
  9.7 1.8 %collective-permute-start.1 = (bf16[528,128]{1,0:T(8,128)(2,1)S(1)}, bf16[528,128]{1,0:T(8,128)(2,1)S(1)}, u32[]{:S(2)}, u32[]{:S(2)}) collective-permute-start(bf16[528,128]{1,0:T(8,128)(2,1)S(1)} %collective-permute-done.refs_1_), channel_id=1, source_target_pairs={{0,8},{4,12},{8,0},{12,4},{1,9},{5,13},{9,1},{13,5},{2,10},{6,14},... | collective-permute-start | bytes 405512 | tf_op jit(solution)/shard_map/ppermute | solution.py:249
  11.5 1.4 %collective-permute-done.2.piece_ref = bf16[528,128]{1,0:T(8,128)(2,1)S(1)} collective-permute-done((bf16[528,128]{1,0:T(8,128)(2,1)S(1)}, bf16[528,128]{1,0:T(8,128)(2,1)S(1)}, u32[]{:S(2)}, u32[]{:S(2)}) %collective-permute-start.2) | collective-permute-done | bytes 135200 | tf_op jit(solution)/shard_map/ppermute | solution.py:246
  13.1 1.5 %collective-permute-start.6 = (bf16[528,128]{1,0:T(8,128)(2,1)S(1)}, bf16[528,128]{1,0:T(8,128)(2,1)S(1)}, u32[]{:S(2)}, u32[]{:S(2)}) collective-permute-start(bf16[528,128]{1,0:T(8,128)(2,1)S(1)} %gate.13.refs_2_), channel_id=1, source_target_pairs={{0,9},{1,8},{2,11},{3,10},{4,13},{5,12},{6,15},{7,14},{8,1},{9,0},... | collective-permute-start | bytes 405512 | tf_op jit(solution)/shard_map/ppermute | solution.py:279
  14.6 0.5 %collective-permute-start.5 = (bf16[528,128]{1,0:T(8,128)(2,1)S(1)}, bf16[528,128]{1,0:T(8,128)(2,1)S(1)}, u32[]{:S(2)}, u32[]{:S(2)}) collective-permute-start(bf16[528,128]{1,0:T(8,128)(2,1)S(1)} %gate.13.refs_2_), channel_id=1, source_target_pairs={{0,8},{1,9},{2,10},{3,11},{4,12},{5,13},{6,14},{7,15},{8,0},{9,1},... | collective-permute-start | bytes 405512 | tf_op jit(solution)/shard_map/ppermute | solution.py:279
  15.1 1.6 %collective-permute-start.4 = (bf16[528,128]{1,0:T(8,128)(2,1)S(1)}, bf16[528,128]{1,0:T(8,128)(2,1)S(1)}, u32[]{:S(2)}, u32[]{:S(2)}) collective-permute-start(bf16[528,128]{1,0:T(8,128)(2,1)S(1)} %gate.13.refs_2_), channel_id=1, source_target_pairs={{0,1},{1,0},{2,3},{3,2},{4,5},{5,4},{6,7},{7,6},{8,9},{9,8},{10,11... | collective-permute-start | bytes 405512 | tf_op jit(solution)/shard_map/ppermute | solution.py:246
  16.7 1.6 %stage.1 = (s32[8,32]{1,0:T(8,128)S(4)}, bf16[8,2,256,256]{3,2,1,0:T(8,128)(2,1)S(1)}, bf16[528,128]{1,0:T(8,128)(2,1)S(1)}) custom-call(s32[8,32]{1,0:T(8,128)} %bitcast.1, bf16[8,2,256,256]{3,2,1,0:T(8,128)(2,1)} %esp_ref.1, bf16[528,128]{1,0:T(8,128)(2,1)S(1)} %gate.11.piece_ref), custom_call_target="tpu_custom_call" | custom-call | tf_op jit(solution)/shard_map/stage/pallas_call | solution.py:292
  18.4 2.1 %collective-permute-done.6.refs_7_ = bf16[528,128]{1,0:T(8,128)(2,1)S(1)} collective-permute-done((bf16[528,128]{1,0:T(8,128)(2,1)S(1)}, bf16[528,128]{1,0:T(8,128)(2,1)S(1)}, u32[]{:S(2)}, u32[]{:S(2)}) %collective-permute-start.6) | collective-permute-done | bytes 135200 | tf_op jit(solution)/shard_map/ppermute | solution.py:279
  20.5 2.4 %collective-permute-done.5.refs_6_ = bf16[528,128]{1,0:T(8,128)(2,1)S(1)} collective-permute-done((bf16[528,128]{1,0:T(8,128)(2,1)S(1)}, bf16[528,128]{1,0:T(8,128)(2,1)S(1)}, u32[]{:S(2)}, u32[]{:S(2)}) %collective-permute-start.5) | collective-permute-done | bytes 135200 | tf_op jit(solution)/shard_map/ppermute | solution.py:279
  23.0 0.4 collective-permute-start.11
  23.6 0.7 %collective-permute-done.12.refs_13_ = bf16[528,128]{1,0:T(8,128)(2,1)S(1)} collective-permute-done((bf16[528,128]{1,0:T(8,128)(2,1)S(1)}, bf16[528,128]{1,0:T(8,128)(2,1)S(1)}, u32[]{:S(2)}, u32[]{:S(2)}) %collective-permute-start.12) | collective-permute-done | bytes 135200 | tf_op jit(solution)/shard_map/ppermute | solution.py:310
  24.5 0.3 collective-permute-done.8.refs_9_
  24.8 0.9 %couple_first.1 = (bf16[16,528,128]{2,1,0:T(8,128)(2,1)S(1)}, s32[264,128]{1,0:T(8,128)S(1)}) custom-call(s32[8,32]{1,0:T(8,128)S(4)} %get-tuple-element.13.nbr_ref, bf16[8,2,256,256]{3,2,1,0:T(8,128)(2,1)S(1)} %get-tuple-element.14.esp_ref, bf16[528,128]{1,0:T(8,128)(2,1)S(1)} %fold.1.refs_0_, bf16[528,128]{1,0:T(8,128)(2,1)S(1)} %collective-permute-done.refs_1_, ...), custom_call_target="tpu_custom_call" | custom-call | tf_op jit(solution)/shard_map/couple_first/pallas_call | solution.py:338
  25.7 1.4 %collective-permute-start.14 = (s32[264,128]{1,0:T(8,128)S(1)}, s32[264,128]{1,0:T(8,128)S(1)}, u32[]{:S(2)}, u32[]{:S(2)}) collective-permute-start(s32[264,128]{1,0:T(8,128)S(1)} %get-tuple-element.19), channel_id=1, source_target_pairs={{0,2},{1,3},{2,0},{3,1},{4,6},{5,7},{6,4},{7,5},{8,10},{9,11},{10,... | collective-permute-start | bytes 405512 | tf_op jit(solution)/shard_map/ppermute | solution.py:246
  27.1 1.7 %couple_rest.1 = (f32[2,264,128]{2,1,0:T(8,128)S(1)}, s32[264,128]{1,0:T(8,128)S(1)}, s32[264,128]{1,0:T(8,128)S(1)}) custom-call(s32[8,32]{1,0:T(8,128)S(4)} %get-tuple-element.13.nbr_ref, bf16[8,2,256,256]{3,2,1,0:T(8,128)(2,1)S(1)} %get-tuple-element.14.esp_ref, bf16[16,528,128]{2,1,0:T(8,128)(2,1)S(1)} %get-tuple-element.16.refs_0_), custom_call_target="tpu_custom_call" | custom-call | tf_op jit(solution)/shard_map/couple_rest/pallas_call | solution.py:338
  28.9 1.6 %collective-permute-start.13 = (s32[264,128]{1,0:T(8,128)S(1)}, s32[264,128]{1,0:T(8,128)S(1)}, u32[]{:S(2)}, u32[]{:S(2)}) collective-permute-start(s32[264,128]{1,0:T(8,128)S(1)} %get-tuple-element.18), channel_id=1, source_target_pairs={{0,1},{1,0},{2,3},{3,2},{4,5},{5,4},{6,7},{7,6},{8,9},{9,8},{10,11... | collective-permute-start | bytes 405512 | tf_op jit(solution)/shard_map/ppermute | solution.py:246
  30.4 1.6 %collective-permute-start.15 = (s32[264,128]{1,0:T(8,128)S(1)}, s32[264,128]{1,0:T(8,128)S(1)}, u32[]{:S(2)}, u32[]{:S(2)}) collective-permute-start(s32[264,128]{1,0:T(8,128)S(1)} %get-tuple-element.20), channel_id=1, source_target_pairs={{0,3},{1,2},{2,1},{3,0},{4,7},{5,6},{6,5},{7,4},{8,11},{9,10},{10,... | collective-permute-start | bytes 405512 | tf_op jit(solution)/shard_map/ppermute | solution.py:246
  32.0 4.0 %collective-permute-done.14.piece_ref = s32[264,128]{1,0:T(8,128)S(1)} collective-permute-done((s32[264,128]{1,0:T(8,128)S(1)}, s32[264,128]{1,0:T(8,128)S(1)}, u32[]{:S(2)}, u32[]{:S(2)}) %collective-permute-start.14) | collective-permute-done | bytes 135200 | tf_op jit(solution)/shard_map/ppermute | solution.py:246
  36.1 3.9 %collective-permute-done.13.refs_0_ = s32[264,128]{1,0:T(8,128)S(1)} collective-permute-done((s32[264,128]{1,0:T(8,128)S(1)}, s32[264,128]{1,0:T(8,128)S(1)}, u32[]{:S(2)}, u32[]{:S(2)}) %collective-permute-start.13) | collective-permute-done | bytes 135200 | tf_op jit(solution)/shard_map/ppermute | solution.py:246
  40.0 1.0 %finish.1 = f32[2,256,256]{2,1,0:T(8,128)} custom-call(bf16[2,256,256]{2,1,0:T(8,128)(2,1)S(1)} %copy-done.1, f32[2,264,128]{2,1,0:T(8,128)S(1)} %get-tuple-element.17.own_ref, s32[264,128]{1,0:T(8,128)S(1)} %collective-permute-done.13.refs_0_, s32[264,128]{1,0:T(8,128)S(1)} %gate.19.refs_1_, s32[264,128]{1,0:T(8,128)S(1)} %collective-permute-done.15.refs_2_), custom_call_target="tpu_custom_call" | custom-call | tf_op jit(solution)/shard_map/finish/pallas_call | solution.py:357
  (28 shorter events, 0.8 us)
Async XLA Ops:
  0.0 0.9 %copy-start = (bf16[2,256,256]{2,1,0:T(8,128)(2,1)S(1)}, bf16[2,256,256]{2,1,0:T(8,128)(2,1)}, u32[]{:S(2)}) copy-start(bf16[2,256,256]{2,1,0:T(8,128)(2,1)} %dens_ref.1) | copy-start | bytes 786436
  1.0 8.7 %collective-permute-start = (bf16[528,128]{1,0:T(8,128)(2,1)S(1)}, bf16[528,128]{1,0:T(8,128)(2,1)S(1)}, u32[]{:S(2)}, u32[]{:S(2)}) collective-permute-start(bf16[528,128]{1,0:T(8,128)(2,1)S(1)} %fold.1.refs_0_), channel_id=1, source_target_pairs={{0,1},{1,0},{2,3},{3,2},{4,5},{5,4},{6,7},{7,6},{8,9},{9,8},{10,11... | collective-permute-start | bytes 405512 | tf_op jit(solution)/shard_map/ppermute | solution.py:246
  4.1 8.9 %collective-permute-start.2 = (bf16[528,128]{1,0:T(8,128)(2,1)S(1)}, bf16[528,128]{1,0:T(8,128)(2,1)S(1)}, u32[]{:S(2)}, u32[]{:S(2)}) collective-permute-start(bf16[528,128]{1,0:T(8,128)(2,1)S(1)} %fold.1.refs_0_), channel_id=1, source_target_pairs={{0,2},{1,3},{2,0},{3,1},{4,6},{5,7},{6,4},{7,5},{8,10},{9,11},{10,... | collective-permute-start | bytes 405512 | tf_op jit(solution)/shard_map/ppermute | solution.py:246
  6.7 6.3 %collective-permute-start.3 = (bf16[528,128]{1,0:T(8,128)(2,1)S(1)}, bf16[528,128]{1,0:T(8,128)(2,1)S(1)}, u32[]{:S(2)}, u32[]{:S(2)}) collective-permute-start(bf16[528,128]{1,0:T(8,128)(2,1)S(1)} %fold.1.refs_0_), channel_id=1, source_target_pairs={{0,8},{4,12},{8,0},{12,4},{1,9},{5,13},{9,1},{13,5},{2,10},{6,14},... | collective-permute-start | bytes 405512 | tf_op jit(solution)/shard_map/ppermute | solution.py:249
  9.7 7.0 %collective-permute-start.1 = (bf16[528,128]{1,0:T(8,128)(2,1)S(1)}, bf16[528,128]{1,0:T(8,128)(2,1)S(1)}, u32[]{:S(2)}, u32[]{:S(2)}) collective-permute-start(bf16[528,128]{1,0:T(8,128)(2,1)S(1)} %collective-permute-done.refs_1_), channel_id=1, source_target_pairs={{0,8},{4,12},{8,0},{12,4},{1,9},{5,13},{9,1},{13,5},{2,10},{6,14},... | collective-permute-start | bytes 405512 | tf_op jit(solution)/shard_map/ppermute | solution.py:249
  13.1 11.8 %collective-permute-start.7 = (bf16[3,528,128]{2,1,0:T(8,128)(2,1)S(1)}, bf16[3,528,128]{2,1,0:T(8,128)(2,1)S(1)}, u32[]{:S(2)}, u32[]{:S(2)}) collective-permute-start(bf16[3,528,128]{2,1,0:T(8,128)(2,1)S(1)} %gather.1), channel_id=1, source_target_pairs={{0,4},{4,0},{8,12},{12,8},{1,5},{5,1},{9,13},{13,9},{2,6},{6,2},{1... | collective-permute-start | bytes 1216520 | tf_op jit(solution)/shard_map/ppermute | solution.py:310
  13.1 7.4 %collective-permute-start.6 = (bf16[528,128]{1,0:T(8,128)(2,1)S(1)}, bf16[528,128]{1,0:T(8,128)(2,1)S(1)}, u32[]{:S(2)}, u32[]{:S(2)}) collective-permute-start(bf16[528,128]{1,0:T(8,128)(2,1)S(1)} %gate.13.refs_2_), channel_id=1, source_target_pairs={{0,9},{1,8},{2,11},{3,10},{4,13},{5,12},{6,15},{7,14},{8,1},{9,0},... | collective-permute-start | bytes 405512 | tf_op jit(solution)/shard_map/ppermute | solution.py:279
  14.6 8.3 %collective-permute-start.5 = (bf16[528,128]{1,0:T(8,128)(2,1)S(1)}, bf16[528,128]{1,0:T(8,128)(2,1)S(1)}, u32[]{:S(2)}, u32[]{:S(2)}) collective-permute-start(bf16[528,128]{1,0:T(8,128)(2,1)S(1)} %gate.13.refs_2_), channel_id=1, source_target_pairs={{0,8},{1,9},{2,10},{3,11},{4,12},{5,13},{6,14},{7,15},{8,0},{9,1},... | collective-permute-start | bytes 405512 | tf_op jit(solution)/shard_map/ppermute | solution.py:279
  15.1 7.9 %collective-permute-start.4 = (bf16[528,128]{1,0:T(8,128)(2,1)S(1)}, bf16[528,128]{1,0:T(8,128)(2,1)S(1)}, u32[]{:S(2)}, u32[]{:S(2)}) collective-permute-start(bf16[528,128]{1,0:T(8,128)(2,1)S(1)} %gate.13.refs_2_), channel_id=1, source_target_pairs={{0,1},{1,0},{2,3},{3,2},{4,5},{5,4},{6,7},{7,6},{8,9},{9,8},{10,11... | collective-permute-start | bytes 405512 | tf_op jit(solution)/shard_map/ppermute | solution.py:246
  18.4 5.1 %collective-permute-start.10 = (bf16[528,128]{1,0:T(8,128)(2,1)S(1)}, bf16[528,128]{1,0:T(8,128)(2,1)S(1)}, u32[]{:S(2)}, u32[]{:S(2)}) collective-permute-start(bf16[528,128]{1,0:T(8,128)(2,1)S(1)} %get-tuple-element.15.refs_5_), channel_id=1, source_target_pairs={{0,4},{4,0},{8,12},{12,8},{1,5},{5,1},{9,13},{13,9},{2,6},{6,2},{1... | collective-permute-start | bytes 405512 | tf_op jit(solution)/shard_map/ppermute | solution.py:310
  20.5 3.0 %collective-permute-start.9 = (bf16[528,128]{1,0:T(8,128)(2,1)S(1)}, bf16[528,128]{1,0:T(8,128)(2,1)S(1)}, u32[]{:S(2)}, u32[]{:S(2)}) collective-permute-start(bf16[528,128]{1,0:T(8,128)(2,1)S(1)} %collective-permute-done.3.refs_2_.refs_4_), channel_id=1, source_target_pairs={{0,4},{4,0},{8,12},{12,8},{1,5},{5,1},{9,13},{13,9},{2,6},{6,2},{1... | collective-permute-start | bytes 405512 | tf_op jit(solution)/shard_map/ppermute | solution.py:310
  22.9 1.4 %collective-permute-start.12 = (bf16[528,128]{1,0:T(8,128)(2,1)S(1)}, bf16[528,128]{1,0:T(8,128)(2,1)S(1)}, u32[]{:S(2)}, u32[]{:S(2)}) collective-permute-start(bf16[528,128]{1,0:T(8,128)(2,1)S(1)} %collective-permute-done.6.refs_7_), channel_id=1, source_target_pairs={{0,4},{4,0},{8,12},{12,8},{1,5},{5,1},{9,13},{13,9},{2,6},{6,2},{1... | collective-permute-start | bytes 405512 | tf_op jit(solution)/shard_map/ppermute | solution.py:310
  23.0 1.4 %collective-permute-start.11 = (bf16[528,128]{1,0:T(8,128)(2,1)S(1)}, bf16[528,128]{1,0:T(8,128)(2,1)S(1)}, u32[]{:S(2)}, u32[]{:S(2)}) collective-permute-start(bf16[528,128]{1,0:T(8,128)(2,1)S(1)} %collective-permute-done.5.refs_6_), channel_id=1, source_target_pairs={{0,4},{4,0},{8,12},{12,8},{1,5},{5,1},{9,13},{13,9},{2,6},{6,2},{1... | collective-permute-start | bytes 405512 | tf_op jit(solution)/shard_map/ppermute | solution.py:310
  23.5 1.4 %collective-permute-start.8 = (bf16[528,128]{1,0:T(8,128)(2,1)S(1)}, bf16[528,128]{1,0:T(8,128)(2,1)S(1)}, u32[]{:S(2)}, u32[]{:S(2)}) collective-permute-start(bf16[528,128]{1,0:T(8,128)(2,1)S(1)} %collective-permute-done.4.refs_3_), channel_id=1, source_target_pairs={{0,4},{4,0},{8,12},{12,8},{1,5},{5,1},{9,13},{13,9},{2,6},{6,2},{1... | collective-permute-start | bytes 405512 | tf_op jit(solution)/shard_map/ppermute | solution.py:310
  25.7 10.3 %collective-permute-start.14 = (s32[264,128]{1,0:T(8,128)S(1)}, s32[264,128]{1,0:T(8,128)S(1)}, u32[]{:S(2)}, u32[]{:S(2)}) collective-permute-start(s32[264,128]{1,0:T(8,128)S(1)} %get-tuple-element.19), channel_id=1, source_target_pairs={{0,2},{1,3},{2,0},{3,1},{4,6},{5,7},{6,4},{7,5},{8,10},{9,11},{10,... | collective-permute-start | bytes 405512 | tf_op jit(solution)/shard_map/ppermute | solution.py:246
  27.1 12.9 %copy-start.1 = (bf16[2,256,256]{2,1,0:T(8,128)(2,1)S(1)}, bf16[2,256,256]{2,1,0:T(8,128)(2,1)}, u32[]{:S(2)}) copy-start(bf16[2,256,256]{2,1,0:T(8,128)(2,1)} %core_ref.1) | copy-start | bytes 786436
  28.9 11.2 %collective-permute-start.13 = (s32[264,128]{1,0:T(8,128)S(1)}, s32[264,128]{1,0:T(8,128)S(1)}, u32[]{:S(2)}, u32[]{:S(2)}) collective-permute-start(s32[264,128]{1,0:T(8,128)S(1)} %get-tuple-element.18), channel_id=1, source_target_pairs={{0,1},{1,0},{2,3},{3,2},{4,5},{5,4},{6,7},{7,6},{8,9},{9,8},{10,11... | collective-permute-start | bytes 405512 | tf_op jit(solution)/shard_map/ppermute | solution.py:246
  30.4 9.6 %collective-permute-start.15 = (s32[264,128]{1,0:T(8,128)S(1)}, s32[264,128]{1,0:T(8,128)S(1)}, u32[]{:S(2)}, u32[]{:S(2)}) collective-permute-start(s32[264,128]{1,0:T(8,128)S(1)} %get-tuple-element.20), channel_id=1, source_target_pairs={{0,3},{1,2},{2,1},{3,0},{4,7},{5,6},{6,5},{7,4},{8,11},{9,10},{10,... | collective-permute-start | bytes 405512 | tf_op jit(solution)/shard_map/ppermute | solution.py:246

commit v17 on v12

--- a/solution.py
+++ b/solution.py
@@ -204,18 +204,27 @@
     return total
 
 
+def add_kernel(plain_ref, *refs):
+    write_plain(refs[-1], [summed(plain_ref, refs[:-1], m) for m in range(plain_ref.shape[0])])
+
+
 def finish_kernel(core_ref, own_ref, *refs):
-    parts, out_ref = refs[:-1], refs[-1]
-    mono_dev, basis, _ = out_ref.shape
+    parts, (out_ref, ready, sems) = refs[:-3], refs[-3:]
+    mono_dev, basis, _ = ready.shape
     half = basis // 2
+    copies = []
     for m in range(mono_dev):
         off, mixed, diag = summed(own_ref, parts, m)
         first, second = unfold(mixed, diag)
         core = core_ref[m].astype(jnp.float32)
-        out_ref[m, :half, :half] = core[:half, :half] + first
-        out_ref[m, :half, half:] = core[:half, half:] + off
-        out_ref[m, half:, :half] = core[half:, :half] + off.T
-        out_ref[m, half:, half:] = core[half:, half:] + second
+        ready[m, :half, :half] = core[:half, :half] + first
+        ready[m, :half, half:] = core[:half, half:] + off
+        ready[m, half:, :half] = core[half:, :half] + off.T
+        ready[m, half:, half:] = core[half:, half:] + second
+        copies.append(pltpu.make_async_copy(ready.at[m], out_ref.at[m], sems.at[m]))
+        copies[-1].start()
+    for copy in copies:
+        copy.wait()
 
 
 def local(density, h_core, esp_block, nbr):
@@ -234,7 +243,7 @@
         out_specs=IN_VMEM,
         compiler_params=small,
         name="fold",
-    )(density)
+    )(pltpu.with_memory_space_constraint(density, pltpu.HBM))
     def along_z(piece, bit):
         return lax.ppermute(piece, "intra", xor_pairs(lanes, bit))
 
@@ -325,14 +334,26 @@
     own, *units = couple([(0, False)] + [(k, True) for k in rest], "couple_rest", [filled])
     for k, unit in zip(rest, units):
         beyond[k] = along_z(unit, k)
+    own = pl.pallas_call(
+        add_kernel,
+        out_shape=plain,
+        in_specs=[IN_VMEM] * 2,
+        out_specs=IN_VMEM,
+        compiler_params=small,
+        name="add",
+    )(own, beyond[top])
     return pl.pallas_call(
         finish_kernel,
         out_shape=jax.ShapeDtypeStruct((mono_dev, basis, basis), jnp.float32),
-        in_specs=[IN_VMEM] * (1 + lanes),
-        out_specs=IN_VMEM,
+        in_specs=[IN_VMEM] * (2 + len(rest)),
+        out_specs=hbm,
+        scratch_shapes=[
+            pltpu.VMEM((mono_dev, basis, basis), jnp.float32),
+            pltpu.SemaphoreType.DMA((mono_dev,)),
+        ],
         compiler_params=small,
         name="finish",
-    )(h_core, own, *[beyond[k] for k in range(1, lanes)])
+    )(h_core, own, *[beyond[k] for k in rest])
 
 
 def solution(mesh):

time: 40.2 us -> 40.1 us (level)
  local copies, waits for them, and re-layouts: 0.95 us -> 0.01 us
  Pallas kernels: 5.42 us -> 6.34 us
    unnamed x4 -> x2, local copies, waits for them, and re-layouts: 0.95 us -> 0.01 us
    pallas_call x1, Pallas kernels: 0.06 us -> 1 us  [local(): pl.pallas_call(fold_kernel, out_shape=pltpu.VMEM((rows, half), density.dt...]
where the time goes in v17:
time: 40.1 us; the launch traced here: 39.9 us
  starting transfers between devices  19.3 us (48%)
  waiting for transfers between devices  14.2 us (35%)
  Pallas kernels  6.34 us (16%)
    ppermute x7, starting transfers between devices, along_z(): return lax.ppermute(piece, 'intra', xor_pairs(lanes, bit))  12.8 us
    ppermute x7, waiting for transfers between devices, along_z(): return lax.ppermute(piece, 'intra', xor_pairs(lanes, bit))  12 us
    ppermute x3, starting transfers between devices, along_y(): return lax.ppermute(piece, 'gddi', xor_pairs(groups, 2 * y))  4.85 us
    pallas_call x2, Pallas kernels, couple(): pl.pallas_call(functools.partial(couple_kernel, groups, lanes, mono_dev,...  2.63 us
    pallas_call x1, Pallas kernels, local(): pl.pallas_call(stage_kernel, out_shape=[pltpu.SMEM((nbr.shape[1], nbr.sha...  1.62 us
    ppermute x8, starting transfers between devices, local(): lax.ppermute(piece, 'gddi', xor_pairs(groups, 1))  1.59 us
    ppermute x8, waiting for transfers between devices, local(): lax.ppermute(piece, 'gddi', xor_pairs(groups, 1))  1.36 us
    pallas_call x1, Pallas kernels, local(): pl.pallas_call(fold_kernel, out_shape=pltpu.VMEM((rows, half), density.dt...  1 us
  transfers between devices with their start and end apart: 18, of which 8 were waited for; matrix products, arithmetic and copies ran while one was open for 0% of the time, Pallas kernels for 9%

profile of v17, /device:TPU:0, one launch (start us, length us, event | category | flops | bytes accessed | tf_op | source)
XLA Modules:
  0.0 39.9 jit_solution(636571821789729904)
XLA Ops:
  0.0 1.0 %fold.1.refs_0_ = bf16[528,128]{1,0:T(8,128)(2,1)S(1)} custom-call(bf16[2,256,256]{2,1,0:T(8,128)(2,1)} %dens_ref.1), custom_call_target="tpu_custom_call" | custom-call | tf_op jit(solution)/shard_map/fold/pallas_call | solution.py:239
  1.0 4.1 %collective-permute-start.1 = (bf16[528,128]{1,0:T(8,128)(2,1)S(1)}, bf16[528,128]{1,0:T(8,128)(2,1)S(1)}, u32[]{:S(2)}, u32[]{:S(2)}) collective-permute-start(bf16[528,128]{1,0:T(8,128)(2,1)S(1)} %fold.1.refs_0_), channel_id=1, source_target_pairs={{0,2},{1,3},{2,0},{3,1},{4,6},{5,7},{6,4},{7,5},{8,10},{9,11},{10,... | collective-permute-start | bytes 405512 | tf_op jit(solution)/shard_map/ppermute | solution.py:248
  5.1 1.6 %collective-permute-start.2 = (bf16[528,128]{1,0:T(8,128)(2,1)S(1)}, bf16[528,128]{1,0:T(8,128)(2,1)S(1)}, u32[]{:S(2)}, u32[]{:S(2)}) collective-permute-start(bf16[528,128]{1,0:T(8,128)(2,1)S(1)} %fold.1.refs_0_), channel_id=1, source_target_pairs={{0,1},{1,0},{2,3},{3,2},{4,5},{5,4},{6,7},{7,6},{8,9},{9,8},{10,11... | collective-permute-start | bytes 405512 | tf_op jit(solution)/shard_map/ppermute | solution.py:248
  6.7 1.5 %collective-permute-start = (bf16[528,128]{1,0:T(8,128)(2,1)S(1)}, bf16[528,128]{1,0:T(8,128)(2,1)S(1)}, u32[]{:S(2)}, u32[]{:S(2)}) collective-permute-start(bf16[528,128]{1,0:T(8,128)(2,1)S(1)} %fold.1.refs_0_), channel_id=1, source_target_pairs={{0,8},{4,12},{8,0},{12,4},{1,9},{5,13},{9,1},{13,5},{2,10},{6,14},... | collective-permute-start | bytes 405512 | tf_op jit(solution)/shard_map/ppermute | solution.py:251
  8.2 3.5 %collective-permute-done.1.piece_ref = bf16[528,128]{1,0:T(8,128)(2,1)S(1)} collective-permute-done((bf16[528,128]{1,0:T(8,128)(2,1)S(1)}, bf16[528,128]{1,0:T(8,128)(2,1)S(1)}, u32[]{:S(2)}, u32[]{:S(2)}) %collective-permute-start.1) | collective-permute-done | bytes 135200 | tf_op jit(solution)/shard_map/ppermute | solution.py:248
  11.9 1.5 %collective-permute-start.3 = (bf16[528,128]{1,0:T(8,128)(2,1)S(1)}, bf16[528,128]{1,0:T(8,128)(2,1)S(1)}, u32[]{:S(2)}, u32[]{:S(2)}) collective-permute-start(bf16[528,128]{1,0:T(8,128)(2,1)S(1)} %gate.8.refs_2_), channel_id=1, source_target_pairs={{0,1},{1,0},{2,3},{3,2},{4,5},{5,4},{6,7},{7,6},{8,9},{9,8},{10,11... | collective-permute-start | bytes 405512 | tf_op jit(solution)/shard_map/ppermute | solution.py:248
  13.4 0.5 %collective-permute-start.9 = (bf16[528,128]{1,0:T(8,128)(2,1)S(1)}, bf16[528,128]{1,0:T(8,128)(2,1)S(1)}, u32[]{:S(2)}, u32[]{:S(2)}) collective-permute-start(bf16[528,128]{1,0:T(8,128)(2,1)S(1)} %gate.8.refs_2_), channel_id=1, source_target_pairs={{0,4},{4,0},{8,12},{12,8},{1,5},{5,1},{9,13},{13,9},{2,6},{6,2},{1... | collective-permute-start | bytes 405512 | tf_op jit(solution)/shard_map/ppermute | solution.py:308
  13.9 1.5 %collective-permute-start.5 = (bf16[528,128]{1,0:T(8,128)(2,1)S(1)}, bf16[528,128]{1,0:T(8,128)(2,1)S(1)}, u32[]{:S(2)}, u32[]{:S(2)}) collective-permute-start(bf16[528,128]{1,0:T(8,128)(2,1)S(1)} %gate.8.refs_2_), channel_id=1, source_target_pairs={{0,8},{4,12},{8,0},{12,4},{1,9},{5,13},{9,1},{13,5},{2,10},{6,14},... | collective-permute-start | bytes 405512 | tf_op jit(solution)/shard_map/ppermute | solution.py:251
  15.5 0.6 %collective-permute-start.4 = (bf16[528,128]{1,0:T(8,128)(2,1)S(1)}, bf16[528,128]{1,0:T(8,128)(2,1)S(1)}, u32[]{:S(2)}, u32[]{:S(2)}) collective-permute-start(bf16[528,128]{1,0:T(8,128)(2,1)S(1)} %collective-permute-done.refs_2_.piece_ref), channel_id=1, source_target_pairs={{0,1},{1,0},{2,3},{3,2},{4,5},{5,4},{6,7},{7,6},{8,9},{9,8},{10,11... | collective-permute-start | bytes 405512 | tf_op jit(solution)/shard_map/ppermute | solution.py:248
  16.1 0.9 %collective-permute-done.3.refs_0_.refs_3_ = bf16[528,128]{1,0:T(8,128)(2,1)S(1)} collective-permute-done((bf16[528,128]{1,0:T(8,128)(2,1)S(1)}, bf16[528,128]{1,0:T(8,128)(2,1)S(1)}, u32[]{:S(2)}, u32[]{:S(2)}) %collective-permute-start.3) | collective-permute-done | bytes 135200 | tf_op jit(solution)/shard_map/ppermute | solution.py:248
  17.0 1.8 %collective-permute-start.6 = (bf16[528,128]{1,0:T(8,128)(2,1)S(1)}, bf16[528,128]{1,0:T(8,128)(2,1)S(1)}, u32[]{:S(2)}, u32[]{:S(2)}) collective-permute-start(bf16[528,128]{1,0:T(8,128)(2,1)S(1)} %collective-permute-done.3.refs_0_.refs_3_), channel_id=1, source_target_pairs={{0,8},{4,12},{8,0},{12,4},{1,9},{5,13},{9,1},{13,5},{2,10},{6,14},... | collective-permute-start | bytes 405512 | tf_op jit(solution)/shard_map/ppermute | solution.py:251
  18.8 1.6 %stage.1 = (s32[8,32]{1,0:T(8,128)S(4)}, bf16[8,2,256,256]{3,2,1,0:T(8,128)(2,1)S(1)}, bf16[528,128]{1,0:T(8,128)(2,1)S(1)}) custom-call(s32[8,32]{1,0:T(8,128)} %bitcast.1, bf16[8,2,256,256]{3,2,1,0:T(8,128)(2,1)} %esp_ref.1, bf16[528,128]{1,0:T(8,128)(2,1)S(1)} %collective-permute-done.refs_2_.piece_ref, ...), custom_call_target="tpu_custom_call" | custom-call | tf_op jit(solution)/shard_map/stage/pallas_call | solution.py:288
  20.5 0.5 %collective-permute-start.10 = (bf16[528,128]{1,0:T(8,128)(2,1)S(1)}, bf16[528,128]{1,0:T(8,128)(2,1)S(1)}, u32[]{:S(2)}, u32[]{:S(2)}) collective-permute-start(bf16[528,128]{1,0:T(8,128)(2,1)S(1)} %collective-permute-done.3.refs_0_.refs_3_), channel_id=1, source_target_pairs={{0,4},{4,0},{8,12},{12,8},{1,5},{5,1},{9,13},{13,9},{2,6},{6,2},{1... | collective-permute-start | bytes 405512 | tf_op jit(solution)/shard_map/ppermute | solution.py:308
  21.1 0.4 %collective-permute-start.12 = (bf16[528,128]{1,0:T(8,128)(2,1)S(1)}, bf16[528,128]{1,0:T(8,128)(2,1)S(1)}, u32[]{:S(2)}, u32[]{:S(2)}) collective-permute-start(bf16[528,128]{1,0:T(8,128)(2,1)S(1)} %collective-permute-done.4.refs_5_), channel_id=1, source_target_pairs={{0,4},{4,0},{8,12},{12,8},{1,5},{5,1},{9,13},{13,9},{2,6},{6,2},{1... | collective-permute-start | bytes 405512 | tf_op jit(solution)/shard_map/ppermute | solution.py:308
  21.5 0.8 %collective-permute-done.6.refs_7_ = bf16[528,128]{1,0:T(8,128)(2,1)S(1)} collective-permute-done((bf16[528,128]{1,0:T(8,128)(2,1)S(1)}, bf16[528,128]{1,0:T(8,128)(2,1)S(1)}, u32[]{:S(2)}, u32[]{:S(2)}) %collective-permute-start.6) | collective-permute-done | bytes 135200 | tf_op jit(solution)/shard_map/ppermute | solution.py:251
  22.4 0.2 collective-permute-done.12.refs_13_
  22.6 1.1 %collective-permute-done.14.refs_15_ = bf16[528,128]{1,0:T(8,128)(2,1)S(1)} collective-permute-done((bf16[528,128]{1,0:T(8,128)(2,1)S(1)}, bf16[528,128]{1,0:T(8,128)(2,1)S(1)}, u32[]{:S(2)}, u32[]{:S(2)}) %collective-permute-start.14) | collective-permute-done | bytes 135200 | tf_op jit(solution)/shard_map/ppermute | solution.py:308
  23.7 0.9 %couple_first.1 = (bf16[16,528,128]{2,1,0:T(8,128)(2,1)S(1)}, s32[264,128]{1,0:T(8,128)S(1)}) custom-call(s32[8,32]{1,0:T(8,128)S(4)} %get-tuple-element.13.nbr_ref, bf16[8,2,256,256]{3,2,1,0:T(8,128)(2,1)S(1)} %get-tuple-element.14.esp_ref, bf16[528,128]{1,0:T(8,128)(2,1)S(1)} %fold.1.refs_0_, bf16[528,128]{1,0:T(8,128)(2,1)S(1)} %collective-permute-done.2.refs_1_, ...), custom_call_target="tpu_custom_call" | custom-call | tf_op jit(solution)/shard_map/couple_first/pallas_call | solution.py:318
  24.6 2.4 %collective-permute-start.15 = (s32[264,128]{1,0:T(8,128)S(1)}, s32[264,128]{1,0:T(8,128)S(1)}, u32[]{:S(2)}, u32[]{:S(2)}) collective-permute-start(s32[264,128]{1,0:T(8,128)S(1)} %get-tuple-element.18), channel_id=1, source_target_pairs={{0,2},{1,3},{2,0},{3,1},{4,6},{5,7},{6,4},{7,5},{8,10},{9,11},{10,... | collective-permute-start | bytes 405512 | tf_op jit(solution)/shard_map/ppermute | solution.py:248
  27.0 1.7 %couple_rest.1 = (f32[2,264,128]{2,1,0:T(8,128)S(1)}, s32[264,128]{1,0:T(8,128)S(1)}, s32[264,128]{1,0:T(8,128)S(1)}) custom-call(s32[8,32]{1,0:T(8,128)S(4)} %get-tuple-element.13.nbr_ref, bf16[8,2,256,256]{3,2,1,0:T(8,128)(2,1)S(1)} %get-tuple-element.14.esp_ref, bf16[16,528,128]{2,1,0:T(8,128)(2,1)S(1)} %get-tuple-element.16.refs_0_), custom_call_target="tpu_custom_call" | custom-call | tf_op jit(solution)/shard_map/couple_rest/pallas_call | solution.py:318
  28.8 2.6 %collective-permute-start.16 = (s32[264,128]{1,0:T(8,128)S(1)}, s32[264,128]{1,0:T(8,128)S(1)}, u32[]{:S(2)}, u32[]{:S(2)}) collective-permute-start(s32[264,128]{1,0:T(8,128)S(1)} %get-tuple-element.19), channel_id=1, source_target_pairs={{0,1},{1,0},{2,3},{3,2},{4,5},{5,4},{6,7},{7,6},{8,9},{9,8},{10,11... | collective-permute-start | bytes 405512 | tf_op jit(solution)/shard_map/ppermute | solution.py:248
  31.3 3.4 %collective-permute-done.15.piece_ref = s32[264,128]{1,0:T(8,128)S(1)} collective-permute-done((s32[264,128]{1,0:T(8,128)S(1)}, s32[264,128]{1,0:T(8,128)S(1)}, u32[]{:S(2)}, u32[]{:S(2)}) %collective-permute-start.15) | collective-permute-done | bytes 135200 | tf_op jit(solution)/shard_map/ppermute | solution.py:248
  34.9 4.0 %collective-permute-done.16.refs_0_ = s32[264,128]{1,0:T(8,128)S(1)} collective-permute-done((s32[264,128]{1,0:T(8,128)S(1)}, s32[264,128]{1,0:T(8,128)S(1)}, u32[]{:S(2)}, u32[]{:S(2)}) %collective-permute-start.16) | collective-permute-done | bytes 135200 | tf_op jit(solution)/shard_map/ppermute | solution.py:248
  39.0 1.0 %finish.1 = f32[2,256,256]{2,1,0:T(8,128)} custom-call(bf16[2,256,256]{2,1,0:T(8,128)(2,1)S(1)} %copy-done, f32[2,264,128]{2,1,0:T(8,128)S(1)} %add.1.own_ref, s32[264,128]{1,0:T(8,128)S(1)} %collective-permute-done.16.refs_0_, s32[264,128]{1,0:T(8,128)S(1)} %collective-permute-done.17.refs_1_), custom_call_target="tpu_custom_call" | custom-call | tf_op jit(solution)/shard_map/finish/pallas_call | solution.py:345
  (27 shorter events, 0.5 us)
Async XLA Ops:
  1.0 10.7 %collective-permute-start.1 = (bf16[528,128]{1,0:T(8,128)(2,1)S(1)}, bf16[528,128]{1,0:T(8,128)(2,1)S(1)}, u32[]{:S(2)}, u32[]{:S(2)}) collective-permute-start(bf16[528,128]{1,0:T(8,128)(2,1)S(1)} %fold.1.refs_0_), channel_id=1, source_target_pairs={{0,2},{1,3},{2,0},{3,1},{4,6},{5,7},{6,4},{7,5},{8,10},{9,11},{10,... | collective-permute-start | bytes 405512 | tf_op jit(solution)/shard_map/ppermute | solution.py:248
  5.1 6.8 %collective-permute-start.2 = (bf16[528,128]{1,0:T(8,128)(2,1)S(1)}, bf16[528,128]{1,0:T(8,128)(2,1)S(1)}, u32[]{:S(2)}, u32[]{:S(2)}) collective-permute-start(bf16[528,128]{1,0:T(8,128)(2,1)S(1)} %fold.1.refs_0_), channel_id=1, source_target_pairs={{0,1},{1,0},{2,3},{3,2},{4,5},{5,4},{6,7},{7,6},{8,9},{9,8},{10,11... | collective-permute-start | bytes 405512 | tf_op jit(solution)/shard_map/ppermute | solution.py:248
  6.7 5.2 %collective-permute-start = (bf16[528,128]{1,0:T(8,128)(2,1)S(1)}, bf16[528,128]{1,0:T(8,128)(2,1)S(1)}, u32[]{:S(2)}, u32[]{:S(2)}) collective-permute-start(bf16[528,128]{1,0:T(8,128)(2,1)S(1)} %fold.1.refs_0_), channel_id=1, source_target_pairs={{0,8},{4,12},{8,0},{12,4},{1,9},{5,13},{9,1},{13,5},{2,10},{6,14},... | collective-permute-start | bytes 405512 | tf_op jit(solution)/shard_map/ppermute | solution.py:251
  8.2 7.3 %collective-permute-start.7 = (bf16[528,128]{1,0:T(8,128)(2,1)S(1)}, bf16[528,128]{1,0:T(8,128)(2,1)S(1)}, u32[]{:S(2)}, u32[]{:S(2)}) collective-permute-start(bf16[528,128]{1,0:T(8,128)(2,1)S(1)} %fold.1.refs_0_), channel_id=1, source_target_pairs={{0,4},{4,0},{8,12},{12,8},{1,5},{5,1},{9,13},{13,9},{2,6},{6,2},{1... | collective-permute-start | bytes 405512 | tf_op jit(solution)/shard_map/ppermute | solution.py:308
  11.9 5.1 %collective-permute-start.3 = (bf16[528,128]{1,0:T(8,128)(2,1)S(1)}, bf16[528,128]{1,0:T(8,128)(2,1)S(1)}, u32[]{:S(2)}, u32[]{:S(2)}) collective-permute-start(bf16[528,128]{1,0:T(8,128)(2,1)S(1)} %gate.8.refs_2_), channel_id=1, source_target_pairs={{0,1},{1,0},{2,3},{3,2},{4,5},{5,4},{6,7},{7,6},{8,9},{9,8},{10,11... | collective-permute-start | bytes 405512 | tf_op jit(solution)/shard_map/ppermute | solution.py:248
  13.4 7.0 %collective-permute-start.8 = (bf16[528,128]{1,0:T(8,128)(2,1)S(1)}, bf16[528,128]{1,0:T(8,128)(2,1)S(1)}, u32[]{:S(2)}, u32[]{:S(2)}) collective-permute-start(bf16[528,128]{1,0:T(8,128)(2,1)S(1)} %collective-permute-done.2.refs_1_), channel_id=1, source_target_pairs={{0,4},{4,0},{8,12},{12,8},{1,5},{5,1},{9,13},{13,9},{2,6},{6,2},{1... | collective-permute-start | bytes 405512 | tf_op jit(solution)/shard_map/ppermute | solution.py:308
  13.4 7.1 %collective-permute-start.9 = (bf16[528,128]{1,0:T(8,128)(2,1)S(1)}, bf16[528,128]{1,0:T(8,128)(2,1)S(1)}, u32[]{:S(2)}, u32[]{:S(2)}) collective-permute-start(bf16[528,128]{1,0:T(8,128)(2,1)S(1)} %gate.8.refs_2_), channel_id=1, source_target_pairs={{0,4},{4,0},{8,12},{12,8},{1,5},{5,1},{9,13},{13,9},{2,6},{6,2},{1... | collective-permute-start | bytes 405512 | tf_op jit(solution)/shard_map/ppermute | solution.py:308
  13.9 7.1 %collective-permute-start.5 = (bf16[528,128]{1,0:T(8,128)(2,1)S(1)}, bf16[528,128]{1,0:T(8,128)(2,1)S(1)}, u32[]{:S(2)}, u32[]{:S(2)}) collective-permute-start(bf16[528,128]{1,0:T(8,128)(2,1)S(1)} %gate.8.refs_2_), channel_id=1, source_target_pairs={{0,8},{4,12},{8,0},{12,4},{1,9},{5,13},{9,1},{13,5},{2,10},{6,14},... | collective-permute-start | bytes 405512 | tf_op jit(solution)/shard_map/ppermute | solution.py:251
  15.5 5.6 %collective-permute-start.4 = (bf16[528,128]{1,0:T(8,128)(2,1)S(1)}, bf16[528,128]{1,0:T(8,128)(2,1)S(1)}, u32[]{:S(2)}, u32[]{:S(2)}) collective-permute-start(bf16[528,128]{1,0:T(8,128)(2,1)S(1)} %collective-permute-done.refs_2_.piece_ref), channel_id=1, source_target_pairs={{0,1},{1,0},{2,3},{3,2},{4,5},{5,4},{6,7},{7,6},{8,9},{9,8},{10,11... | collective-permute-start | bytes 405512 | tf_op jit(solution)/shard_map/ppermute | solution.py:248
  17.0 5.3 %collective-permute-start.6 = (bf16[528,128]{1,0:T(8,128)(2,1)S(1)}, bf16[528,128]{1,0:T(8,128)(2,1)S(1)}, u32[]{:S(2)}, u32[]{:S(2)}) collective-permute-start(bf16[528,128]{1,0:T(8,128)(2,1)S(1)} %collective-permute-done.3.refs_0_.refs_3_), channel_id=1, source_target_pairs={{0,8},{4,12},{8,0},{12,4},{1,9},{5,13},{9,1},{13,5},{2,10},{6,14},... | collective-permute-start | bytes 405512 | tf_op jit(solution)/shard_map/ppermute | solution.py:251
  20.4 2.1 %collective-permute-start.11 = (bf16[528,128]{1,0:T(8,128)(2,1)S(1)}, bf16[528,128]{1,0:T(8,128)(2,1)S(1)}, u32[]{:S(2)}, u32[]{:S(2)}) collective-permute-start(bf16[528,128]{1,0:T(8,128)(2,1)S(1)} %get-tuple-element.15.refs_4_), channel_id=1, source_target_pairs={{0,4},{4,0},{8,12},{12,8},{1,5},{5,1},{9,13},{13,9},{2,6},{6,2},{1... | collective-permute-start | bytes 405512 | tf_op jit(solution)/shard_map/ppermute | solution.py:308
  20.5 1.9 %collective-permute-start.10 = (bf16[528,128]{1,0:T(8,128)(2,1)S(1)}, bf16[528,128]{1,0:T(8,128)(2,1)S(1)}, u32[]{:S(2)}, u32[]{:S(2)}) collective-permute-start(bf16[528,128]{1,0:T(8,128)(2,1)S(1)} %collective-permute-done.3.refs_0_.refs_3_), channel_id=1, source_target_pairs={{0,4},{4,0},{8,12},{12,8},{1,5},{5,1},{9,13},{13,9},{2,6},{6,2},{1... | collective-permute-start | bytes 405512 | tf_op jit(solution)/shard_map/ppermute | solution.py:308
  21.0 1.4 %collective-permute-start.13 = (bf16[528,128]{1,0:T(8,128)(2,1)S(1)}, bf16[528,128]{1,0:T(8,128)(2,1)S(1)}, u32[]{:S(2)}, u32[]{:S(2)}) collective-permute-start(bf16[528,128]{1,0:T(8,128)(2,1)S(1)} %collective-permute-done.5.refs_6_), channel_id=1, source_target_pairs={{0,4},{4,0},{8,12},{12,8},{1,5},{5,1},{9,13},{13,9},{2,6},{6,2},{1... | collective-permute-start | bytes 405512 | tf_op jit(solution)/shard_map/ppermute | solution.py:308
  21.1 1.5 %collective-permute-start.12 = (bf16[528,128]{1,0:T(8,128)(2,1)S(1)}, bf16[528,128]{1,0:T(8,128)(2,1)S(1)}, u32[]{:S(2)}, u32[]{:S(2)}) collective-permute-start(bf16[528,128]{1,0:T(8,128)(2,1)S(1)} %collective-permute-done.4.refs_5_), channel_id=1, source_target_pairs={{0,4},{4,0},{8,12},{12,8},{1,5},{5,1},{9,13},{13,9},{2,6},{6,2},{1... | collective-permute-start | bytes 405512 | tf_op jit(solution)/shard_map/ppermute | solution.py:308
  22.3 1.4 %collective-permute-start.14 = (bf16[528,128]{1,0:T(8,128)(2,1)S(1)}, bf16[528,128]{1,0:T(8,128)(2,1)S(1)}, u32[]{:S(2)}, u32[]{:S(2)}) collective-permute-start(bf16[528,128]{1,0:T(8,128)(2,1)S(1)} %collective-permute-done.6.refs_7_), channel_id=1, source_target_pairs={{0,4},{4,0},{8,12},{12,8},{1,5},{5,1},{9,13},{13,9},{2,6},{6,2},{1... | collective-permute-start | bytes 405512 | tf_op jit(solution)/shard_map/ppermute | solution.py:308
  24.6 10.2 %collective-permute-start.15 = (s32[264,128]{1,0:T(8,128)S(1)}, s32[264,128]{1,0:T(8,128)S(1)}, u32[]{:S(2)}, u32[]{:S(2)}) collective-permute-start(s32[264,128]{1,0:T(8,128)S(1)} %get-tuple-element.18), channel_id=1, source_target_pairs={{0,2},{1,3},{2,0},{3,1},{4,6},{5,7},{6,4},{7,5},{8,10},{9,11},{10,... | collective-permute-start | bytes 405512 | tf_op jit(solution)/shard_map/ppermute | solution.py:248
  27.0 11.9 %copy-start = (bf16[2,256,256]{2,1,0:T(8,128)(2,1)S(1)}, bf16[2,256,256]{2,1,0:T(8,128)(2,1)}, u32[]{:S(2)}) copy-start(bf16[2,256,256]{2,1,0:T(8,128)(2,1)} %core_ref.1) | copy-start | bytes 786436
  28.8 10.2 %collective-permute-start.16 = (s32[264,128]{1,0:T(8,128)S(1)}, s32[264,128]{1,0:T(8,128)S(1)}, u32[]{:S(2)}, u32[]{:S(2)}) collective-permute-start(s32[264,128]{1,0:T(8,128)S(1)} %get-tuple-element.19), channel_id=1, source_target_pairs={{0,1},{1,0},{2,3},{3,2},{4,5},{5,4},{6,7},{7,6},{8,9},{9,8},{10,11... | collective-permute-start | bytes 405512 | tf_op jit(solution)/shard_map/ppermute | solution.py:248
  31.3 7.6 %collective-permute-start.17 = (s32[264,128]{1,0:T(8,128)S(1)}, s32[264,128]{1,0:T(8,128)S(1)}, u32[]{:S(2)}, u32[]{:S(2)}) collective-permute-start(s32[264,128]{1,0:T(8,128)S(1)} %get-tuple-element.20), channel_id=1, source_target_pairs={{0,3},{1,2},{2,1},{3,0},{4,7},{5,6},{6,5},{7,4},{8,11},{9,10},{10,... | collective-permute-start | bytes 405512 | tf_op jit(solution)/shard_map/ppermute | solution.py:248

commit v18 on v17

--- a/solution.py
+++ b/solution.py
@@ -330,10 +330,11 @@
     beyond = {top: along_z(beyond, top)}
     for _ in range(5):
         beyond[top] = gate(beyond[top])
-    rest = [k for k in range(1, lanes) if k != top]
-    own, *units = couple([(0, False)] + [(k, True) for k in rest], "couple_rest", [filled])
+    rest = [k for k in range(lanes - 1, 0, -1) if k != top]
+    units = couple([(k, True) for k in rest], "couple_rest", [filled])
     for k, unit in zip(rest, units):
         beyond[k] = along_z(unit, k)
+    (own,) = couple([(0, False)], "couple_own", [filled])
     own = pl.pallas_call(
         add_kernel,
         out_shape=plain,

time: 40.1 us -> 40.9 us (1.020)
    ppermute x7, waiting for transfers between devices: 12 us -> 12.5 us  [along_z(): return lax.ppermute(piece, 'intra', xor_pairs(lanes, bit))]
    pallas_call x2 -> x3, Pallas kernels: 2.63 us -> 2.9 us  [couple(): pl.pallas_call(functools.partial(couple_kernel, groups, lanes, mono_dev,...]
where the time goes in v18:
time: 40.9 us; the launch traced here: 40.7 us
  starting transfers between devices  19.3 us (47%)
  waiting for transfers between devices  14.6 us (36%)
  Pallas kernels  6.61 us (16%)
    ppermute x7, starting transfers between devices, along_z(): return lax.ppermute(piece, 'intra', xor_pairs(lanes, bit))  12.9 us
    ppermute x7, waiting for transfers between devices, along_z(): return lax.ppermute(piece, 'intra', xor_pairs(lanes, bit))  12.5 us
    ppermute x3, starting transfers between devices, along_y(): return lax.ppermute(piece, 'gddi', xor_pairs(groups, 2 * y))  4.85 us
    pallas_call x3, Pallas kernels, couple(): pl.pallas_call(functools.partial(couple_kernel, groups, lanes, mono_dev,...  2.9 us
    pallas_call x1, Pallas kernels, local(): pl.pallas_call(stage_kernel, out_shape=[pltpu.SMEM((nbr.shape[1], nbr.sha...  1.62 us
    ppermute x8, starting transfers between devices, local(): lax.ppermute(piece, 'gddi', xor_pairs(groups, 1))  1.59 us
    ppermute x8, waiting for transfers between devices, local(): lax.ppermute(piece, 'gddi', xor_pairs(groups, 1))  1.36 us
    pallas_call x1, Pallas kernels, local(): pl.pallas_call(fold_kernel, out_shape=pltpu.VMEM((rows, half), density.dt...  1 us
  transfers between devices with their start and end apart: 18, of which 8 were waited for; matrix products, arithmetic and copies ran while one was open for 0% of the time, Pallas kernels for 9%

profile of v18, /device:TPU:0, one launch (start us, length us, event | category | flops | bytes accessed | tf_op | source)
XLA Modules:
  0.0 40.7 jit_solution(9163319565888078395)
XLA Ops:
  0.0 1.0 %fold.1.refs_0_ = bf16[528,128]{1,0:T(8,128)(2,1)S(1)} custom-call(bf16[2,256,256]{2,1,0:T(8,128)(2,1)} %dens_ref.1), custom_call_target="tpu_custom_call" | custom-call | tf_op jit(solution)/shard_map/fold/pallas_call | solution.py:239
  1.0 4.1 %collective-permute-start.1 = (bf16[528,128]{1,0:T(8,128)(2,1)S(1)}, bf16[528,128]{1,0:T(8,128)(2,1)S(1)}, u32[]{:S(2)}, u32[]{:S(2)}) collective-permute-start(bf16[528,128]{1,0:T(8,128)(2,1)S(1)} %fold.1.refs_0_), channel_id=1, source_target_pairs={{0,2},{1,3},{2,0},{3,1},{4,6},{5,7},{6,4},{7,5},{8,10},{9,11},{10,... | collective-permute-start | bytes 405512 | tf_op jit(solution)/shard_map/ppermute | solution.py:248
  5.1 1.6 %collective-permute-start.2 = (bf16[528,128]{1,0:T(8,128)(2,1)S(1)}, bf16[528,128]{1,0:T(8,128)(2,1)S(1)}, u32[]{:S(2)}, u32[]{:S(2)}) collective-permute-start(bf16[528,128]{1,0:T(8,128)(2,1)S(1)} %fold.1.refs_0_), channel_id=1, source_target_pairs={{0,1},{1,0},{2,3},{3,2},{4,5},{5,4},{6,7},{7,6},{8,9},{9,8},{10,11... | collective-permute-start | bytes 405512 | tf_op jit(solution)/shard_map/ppermute | solution.py:248
  6.7 1.5 %collective-permute-start = (bf16[528,128]{1,0:T(8,128)(2,1)S(1)}, bf16[528,128]{1,0:T(8,128)(2,1)S(1)}, u32[]{:S(2)}, u32[]{:S(2)}) collective-permute-start(bf16[528,128]{1,0:T(8,128)(2,1)S(1)} %fold.1.refs_0_), channel_id=1, source_target_pairs={{0,8},{4,12},{8,0},{12,4},{1,9},{5,13},{9,1},{13,5},{2,10},{6,14},... | collective-permute-start | bytes 405512 | tf_op jit(solution)/shard_map/ppermute | solution.py:251
  8.2 3.5 %collective-permute-done.1.piece_ref = bf16[528,128]{1,0:T(8,128)(2,1)S(1)} collective-permute-done((bf16[528,128]{1,0:T(8,128)(2,1)S(1)}, bf16[528,128]{1,0:T(8,128)(2,1)S(1)}, u32[]{:S(2)}, u32[]{:S(2)}) %collective-permute-start.1) | collective-permute-done | bytes 135200 | tf_op jit(solution)/shard_map/ppermute | solution.py:248
  11.9 1.5 %collective-permute-start.3 = (bf16[528,128]{1,0:T(8,128)(2,1)S(1)}, bf16[528,128]{1,0:T(8,128)(2,1)S(1)}, u32[]{:S(2)}, u32[]{:S(2)}) collective-permute-start(bf16[528,128]{1,0:T(8,128)(2,1)S(1)} %gate.8.refs_2_), channel_id=1, source_target_pairs={{0,1},{1,0},{2,3},{3,2},{4,5},{5,4},{6,7},{7,6},{8,9},{9,8},{10,11... | collective-permute-start | bytes 405512 | tf_op jit(solution)/shard_map/ppermute | solution.py:248
  13.4 0.5 %collective-permute-start.9 = (bf16[528,128]{1,0:T(8,128)(2,1)S(1)}, bf16[528,128]{1,0:T(8,128)(2,1)S(1)}, u32[]{:S(2)}, u32[]{:S(2)}) collective-permute-start(bf16[528,128]{1,0:T(8,128)(2,1)S(1)} %gate.8.refs_2_), channel_id=1, source_target_pairs={{0,4},{4,0},{8,12},{12,8},{1,5},{5,1},{9,13},{13,9},{2,6},{6,2},{1... | collective-permute-start | bytes 405512 | tf_op jit(solution)/shard_map/ppermute | solution.py:308
  13.9 1.5 %collective-permute-start.5 = (bf16[528,128]{1,0:T(8,128)(2,1)S(1)}, bf16[528,128]{1,0:T(8,128)(2,1)S(1)}, u32[]{:S(2)}, u32[]{:S(2)}) collective-permute-start(bf16[528,128]{1,0:T(8,128)(2,1)S(1)} %gate.8.refs_2_), channel_id=1, source_target_pairs={{0,8},{4,12},{8,0},{12,4},{1,9},{5,13},{9,1},{13,5},{2,10},{6,14},... | collective-permute-start | bytes 405512 | tf_op jit(solution)/shard_map/ppermute | solution.py:251
  15.5 0.6 %collective-permute-start.4 = (bf16[528,128]{1,0:T(8,128)(2,1)S(1)}, bf16[528,128]{1,0:T(8,128)(2,1)S(1)}, u32[]{:S(2)}, u32[]{:S(2)}) collective-permute-start(bf16[528,128]{1,0:T(8,128)(2,1)S(1)} %collective-permute-done.refs_2_.piece_ref), channel_id=1, source_target_pairs={{0,1},{1,0},{2,3},{3,2},{4,5},{5,4},{6,7},{7,6},{8,9},{9,8},{10,11... | collective-permute-start | bytes 405512 | tf_op jit(solution)/shard_map/ppermute | solution.py:248
  16.1 0.9 %collective-permute-done.3.refs_0_.refs_3_ = bf16[528,128]{1,0:T(8,128)(2,1)S(1)} collective-permute-done((bf16[528,128]{1,0:T(8,128)(2,1)S(1)}, bf16[528,128]{1,0:T(8,128)(2,1)S(1)}, u32[]{:S(2)}, u32[]{:S(2)}) %collective-permute-start.3) | collective-permute-done | bytes 135200 | tf_op jit(solution)/shard_map/ppermute | solution.py:248
  17.0 1.8 %collective-permute-start.6 = (bf16[528,128]{1,0:T(8,128)(2,1)S(1)}, bf16[528,128]{1,0:T(8,128)(2,1)S(1)}, u32[]{:S(2)}, u32[]{:S(2)}) collective-permute-start(bf16[528,128]{1,0:T(8,128)(2,1)S(1)} %collective-permute-done.3.refs_0_.refs_3_), channel_id=1, source_target_pairs={{0,8},{4,12},{8,0},{12,4},{1,9},{5,13},{9,1},{13,5},{2,10},{6,14},... | collective-permute-start | bytes 405512 | tf_op jit(solution)/shard_map/ppermute | solution.py:251
  18.8 1.6 %stage.1 = (s32[8,32]{1,0:T(8,128)S(4)}, bf16[8,2,256,256]{3,2,1,0:T(8,128)(2,1)S(1)}, bf16[528,128]{1,0:T(8,128)(2,1)S(1)}) custom-call(s32[8,32]{1,0:T(8,128)} %bitcast.1, bf16[8,2,256,256]{3,2,1,0:T(8,128)(2,1)} %esp_ref.1, bf16[528,128]{1,0:T(8,128)(2,1)S(1)} %collective-permute-done.refs_2_.piece_ref, ...), custom_call_target="tpu_custom_call" | custom-call | tf_op jit(solution)/shard_map/stage/pallas_call | solution.py:288
  20.5 0.5 %collective-permute-start.10 = (bf16[528,128]{1,0:T(8,128)(2,1)S(1)}, bf16[528,128]{1,0:T(8,128)(2,1)S(1)}, u32[]{:S(2)}, u32[]{:S(2)}) collective-permute-start(bf16[528,128]{1,0:T(8,128)(2,1)S(1)} %collective-permute-done.3.refs_0_.refs_3_), channel_id=1, source_target_pairs={{0,4},{4,0},{8,12},{12,8},{1,5},{5,1},{9,13},{13,9},{2,6},{6,2},{1... | collective-permute-start | bytes 405512 | tf_op jit(solution)/shard_map/ppermute | solution.py:308
  21.5 0.8 %collective-permute-done.6.refs_7_ = bf16[528,128]{1,0:T(8,128)(2,1)S(1)} collective-permute-done((bf16[528,128]{1,0:T(8,128)(2,1)S(1)}, bf16[528,128]{1,0:T(8,128)(2,1)S(1)}, u32[]{:S(2)}, u32[]{:S(2)}) %collective-permute-start.6) | collective-permute-done | bytes 135200 | tf_op jit(solution)/shard_map/ppermute | solution.py:251
  22.6 1.1 %collective-permute-done.14.refs_15_ = bf16[528,128]{1,0:T(8,128)(2,1)S(1)} collective-permute-done((bf16[528,128]{1,0:T(8,128)(2,1)S(1)}, bf16[528,128]{1,0:T(8,128)(2,1)S(1)}, u32[]{:S(2)}, u32[]{:S(2)}) %collective-permute-start.14) | collective-permute-done | bytes 135200 | tf_op jit(solution)/shard_map/ppermute | solution.py:308
  23.7 0.9 %couple_first.1 = (bf16[16,528,128]{2,1,0:T(8,128)(2,1)S(1)}, s32[264,128]{1,0:T(8,128)S(1)}) custom-call(s32[8,32]{1,0:T(8,128)S(4)} %get-tuple-element.12.nbr_ref, bf16[8,2,256,256]{3,2,1,0:T(8,128)(2,1)S(1)} %get-tuple-element.13.esp_ref, bf16[528,128]{1,0:T(8,128)(2,1)S(1)} %fold.1.refs_0_, bf16[528,128]{1,0:T(8,128)(2,1)S(1)} %collective-permute-done.2.refs_1_, ...), custom_call_target="tpu_custom_call" | custom-call | tf_op jit(solution)/shard_map/couple_first/pallas_call | solution.py:318
  24.6 2.4 %collective-permute-start.15 = (s32[264,128]{1,0:T(8,128)S(1)}, s32[264,128]{1,0:T(8,128)S(1)}, u32[]{:S(2)}, u32[]{:S(2)}) collective-permute-start(s32[264,128]{1,0:T(8,128)S(1)} %get-tuple-element.16), channel_id=1, source_target_pairs={{0,2},{1,3},{2,0},{3,1},{4,6},{5,7},{6,4},{7,5},{8,10},{9,11},{10,... | collective-permute-start | bytes 405512 | tf_op jit(solution)/shard_map/ppermute | solution.py:248
  27.0 1.3 %couple_rest.1 = (s32[264,128]{1,0:T(8,128)S(1)}, s32[264,128]{1,0:T(8,128)S(1)}) custom-call(s32[8,32]{1,0:T(8,128)S(4)} %get-tuple-element.12.nbr_ref, bf16[8,2,256,256]{3,2,1,0:T(8,128)(2,1)S(1)} %get-tuple-element.13.esp_ref, bf16[16,528,128]{2,1,0:T(8,128)(2,1)S(1)} %get-tuple-element.15.refs_0_), custom_call_target="tpu_custom_call" | custom-call | tf_op jit(solution)/shard_map/couple_rest/pallas_call | solution.py:318
  28.3 2.1 %collective-permute-start.16 = (s32[264,128]{1,0:T(8,128)S(1)}, s32[264,128]{1,0:T(8,128)S(1)}, u32[]{:S(2)}, u32[]{:S(2)}) collective-permute-start(s32[264,128]{1,0:T(8,128)S(1)} %get-tuple-element.17), channel_id=1, source_target_pairs={{0,3},{1,2},{2,1},{3,0},{4,7},{5,6},{6,5},{7,4},{8,11},{9,10},{10,... | collective-permute-start | bytes 405512 | tf_op jit(solution)/shard_map/ppermute | solution.py:248
  30.4 0.6 %collective-permute-start.17 = (s32[264,128]{1,0:T(8,128)S(1)}, s32[264,128]{1,0:T(8,128)S(1)}, u32[]{:S(2)}, u32[]{:S(2)}) collective-permute-start(s32[264,128]{1,0:T(8,128)S(1)} %get-tuple-element.18), channel_id=1, source_target_pairs={{0,1},{1,0},{2,3},{3,2},{4,5},{5,4},{6,7},{7,6},{8,9},{9,8},{10,11... | collective-permute-start | bytes 405512 | tf_op jit(solution)/shard_map/ppermute | solution.py:248
  31.0 0.7 %couple_own.1.plain_ref = f32[2,264,128]{2,1,0:T(8,128)S(1)} custom-call(s32[8,32]{1,0:T(8,128)S(4)} %get-tuple-element.12.nbr_ref, bf16[8,2,256,256]{3,2,1,0:T(8,128)(2,1)S(1)} %get-tuple-element.13.esp_ref, bf16[16,528,128]{2,1,0:T(8,128)(2,1)S(1)} %get-tuple-element.15.refs_0_), custom_call_target="tpu_custom_call" | custom-call | tf_op jit(solution)/shard_map/couple_own/pallas_call | solution.py:318
  31.7 6.1 %collective-permute-done.15.piece_ref = s32[264,128]{1,0:T(8,128)S(1)} collective-permute-done((s32[264,128]{1,0:T(8,128)S(1)}, s32[264,128]{1,0:T(8,128)S(1)}, u32[]{:S(2)}, u32[]{:S(2)}) %collective-permute-start.15) | collective-permute-done | bytes 135200 | tf_op jit(solution)/shard_map/ppermute | solution.py:248
  38.0 1.7 %collective-permute-done.17.refs_1_ = s32[264,128]{1,0:T(8,128)S(1)} collective-permute-done((s32[264,128]{1,0:T(8,128)S(1)}, s32[264,128]{1,0:T(8,128)S(1)}, u32[]{:S(2)}, u32[]{:S(2)}) %collective-permute-start.17) | collective-permute-done | bytes 135200 | tf_op jit(solution)/shard_map/ppermute | solution.py:248
  39.7 1.0 %finish.1 = f32[2,256,256]{2,1,0:T(8,128)} custom-call(bf16[2,256,256]{2,1,0:T(8,128)(2,1)S(1)} %copy-done, f32[2,264,128]{2,1,0:T(8,128)S(1)} %add.1.own_ref, s32[264,128]{1,0:T(8,128)S(1)} %collective-permute-done.16.refs_0_, s32[264,128]{1,0:T(8,128)S(1)} %collective-permute-done.17.refs_1_), custom_call_target="tpu_custom_call" | custom-call | tf_op jit(solution)/shard_map/finish/pallas_call | solution.py:346
  (28 shorter events, 1.2 us)
Async XLA Ops:
  1.0 10.7 %collective-permute-start.1 = (bf16[528,128]{1,0:T(8,128)(2,1)S(1)}, bf16[528,128]{1,0:T(8,128)(2,1)S(1)}, u32[]{:S(2)}, u32[]{:S(2)}) collective-permute-start(bf16[528,128]{1,0:T(8,128)(2,1)S(1)} %fold.1.refs_0_), channel_id=1, source_target_pairs={{0,2},{1,3},{2,0},{3,1},{4,6},{5,7},{6,4},{7,5},{8,10},{9,11},{10,... | collective-permute-start | bytes 405512 | tf_op jit(solution)/shard_map/ppermute | solution.py:248
  5.1 6.8 %collective-permute-start.2 = (bf16[528,128]{1,0:T(8,128)(2,1)S(1)}, bf16[528,128]{1,0:T(8,128)(2,1)S(1)}, u32[]{:S(2)}, u32[]{:S(2)}) collective-permute-start(bf16[528,128]{1,0:T(8,128)(2,1)S(1)} %fold.1.refs_0_), channel_id=1, source_target_pairs={{0,1},{1,0},{2,3},{3,2},{4,5},{5,4},{6,7},{7,6},{8,9},{9,8},{10,11... | collective-permute-start | bytes 405512 | tf_op jit(solution)/shard_map/ppermute | solution.py:248
  6.7 5.2 %collective-permute-start = (bf16[528,128]{1,0:T(8,128)(2,1)S(1)}, bf16[528,128]{1,0:T(8,128)(2,1)S(1)}, u32[]{:S(2)}, u32[]{:S(2)}) collective-permute-start(bf16[528,128]{1,0:T(8,128)(2,1)S(1)} %fold.1.refs_0_), channel_id=1, source_target_pairs={{0,8},{4,12},{8,0},{12,4},{1,9},{5,13},{9,1},{13,5},{2,10},{6,14},... | collective-permute-start | bytes 405512 | tf_op jit(solution)/shard_map/ppermute | solution.py:251
  8.2 7.3 %collective-permute-start.7 = (bf16[528,128]{1,0:T(8,128)(2,1)S(1)}, bf16[528,128]{1,0:T(8,128)(2,1)S(1)}, u32[]{:S(2)}, u32[]{:S(2)}) collective-permute-start(bf16[528,128]{1,0:T(8,128)(2,1)S(1)} %fold.1.refs_0_), channel_id=1, source_target_pairs={{0,4},{4,0},{8,12},{12,8},{1,5},{5,1},{9,13},{13,9},{2,6},{6,2},{1... | collective-permute-start | bytes 405512 | tf_op jit(solution)/shard_map/ppermute | solution.py:308
  11.9 5.1 %collective-permute-start.3 = (bf16[528,128]{1,0:T(8,128)(2,1)S(1)}, bf16[528,128]{1,0:T(8,128)(2,1)S(1)}, u32[]{:S(2)}, u32[]{:S(2)}) collective-permute-start(bf16[528,128]{1,0:T(8,128)(2,1)S(1)} %gate.8.refs_2_), channel_id=1, source_target_pairs={{0,1},{1,0},{2,3},{3,2},{4,5},{5,4},{6,7},{7,6},{8,9},{9,8},{10,11... | collective-permute-start | bytes 405512 | tf_op jit(solution)/shard_map/ppermute | solution.py:248
  13.4 7.0 %collective-permute-start.8 = (bf16[528,128]{1,0:T(8,128)(2,1)S(1)}, bf16[528,128]{1,0:T(8,128)(2,1)S(1)}, u32[]{:S(2)}, u32[]{:S(2)}) collective-permute-start(bf16[528,128]{1,0:T(8,128)(2,1)S(1)} %collective-permute-done.2.refs_1_), channel_id=1, source_target_pairs={{0,4},{4,0},{8,12},{12,8},{1,5},{5,1},{9,13},{13,9},{2,6},{6,2},{1... | collective-permute-start | bytes 405512 | tf_op jit(solution)/shard_map/ppermute | solution.py:308
  13.4 7.1 %collective-permute-start.9 = (bf16[528,128]{1,0:T(8,128)(2,1)S(1)}, bf16[528,128]{1,0:T(8,128)(2,1)S(1)}, u32[]{:S(2)}, u32[]{:S(2)}) collective-permute-start(bf16[528,128]{1,0:T(8,128)(2,1)S(1)} %gate.8.refs_2_), channel_id=1, source_target_pairs={{0,4},{4,0},{8,12},{12,8},{1,5},{5,1},{9,13},{13,9},{2,6},{6,2},{1... | collective-permute-start | bytes 405512 | tf_op jit(solution)/shard_map/ppermute | solution.py:308
  13.9 7.1 %collective-permute-start.5 = (bf16[528,128]{1,0:T(8,128)(2,1)S(1)}, bf16[528,128]{1,0:T(8,128)(2,1)S(1)}, u32[]{:S(2)}, u32[]{:S(2)}) collective-permute-start(bf16[528,128]{1,0:T(8,128)(2,1)S(1)} %gate.8.refs_2_), channel_id=1, source_target_pairs={{0,8},{4,12},{8,0},{12,4},{1,9},{5,13},{9,1},{13,5},{2,10},{6,14},... | collective-permute-start | bytes 405512 | tf_op jit(solution)/shard_map/ppermute | solution.py:251
  15.5 5.6 %collective-permute-start.4 = (bf16[528,128]{1,0:T(8,128)(2,1)S(1)}, bf16[528,128]{1,0:T(8,128)(2,1)S(1)}, u32[]{:S(2)}, u32[]{:S(2)}) collective-permute-start(bf16[528,128]{1,0:T(8,128)(2,1)S(1)} %collective-permute-done.refs_2_.piece_ref), channel_id=1, source_target_pairs={{0,1},{1,0},{2,3},{3,2},{4,5},{5,4},{6,7},{7,6},{8,9},{9,8},{10,11... | collective-permute-start | bytes 405512 | tf_op jit(solution)/shard_map/ppermute | solution.py:248
  17.0 5.3 %collective-permute-start.6 = (bf16[528,128]{1,0:T(8,128)(2,1)S(1)}, bf16[528,128]{1,0:T(8,128)(2,1)S(1)}, u32[]{:S(2)}, u32[]{:S(2)}) collective-permute-start(bf16[528,128]{1,0:T(8,128)(2,1)S(1)} %collective-permute-done.3.refs_0_.refs_3_), channel_id=1, source_target_pairs={{0,8},{4,12},{8,0},{12,4},{1,9},{5,13},{9,1},{13,5},{2,10},{6,14},... | collective-permute-start | bytes 405512 | tf_op jit(solution)/shard_map/ppermute | solution.py:251
  20.4 2.1 %collective-permute-start.11 = (bf16[528,128]{1,0:T(8,128)(2,1)S(1)}, bf16[528,128]{1,0:T(8,128)(2,1)S(1)}, u32[]{:S(2)}, u32[]{:S(2)}) collective-permute-start(bf16[528,128]{1,0:T(8,128)(2,1)S(1)} %get-tuple-element.14.refs_4_), channel_id=1, source_target_pairs={{0,4},{4,0},{8,12},{12,8},{1,5},{5,1},{9,13},{13,9},{2,6},{6,2},{1... | collective-permute-start | bytes 405512 | tf_op jit(solution)/shard_map/ppermute | solution.py:308
  20.5 1.9 %collective-permute-start.10 = (bf16[528,128]{1,0:T(8,128)(2,1)S(1)}, bf16[528,128]{1,0:T(8,128)(2,1)S(1)}, u32[]{:S(2)}, u32[]{:S(2)}) collective-permute-start(bf16[528,128]{1,0:T(8,128)(2,1)S(1)} %collective-permute-done.3.refs_0_.refs_3_), channel_id=1, source_target_pairs={{0,4},{4,0},{8,12},{12,8},{1,5},{5,1},{9,13},{13,9},{2,6},{6,2},{1... | collective-permute-start | bytes 405512 | tf_op jit(solution)/shard_map/ppermute | solution.py:308
  21.0 1.4 %collective-permute-start.13 = (bf16[528,128]{1,0:T(8,128)(2,1)S(1)}, bf16[528,128]{1,0:T(8,128)(2,1)S(1)}, u32[]{:S(2)}, u32[]{:S(2)}) collective-permute-start(bf16[528,128]{1,0:T(8,128)(2,1)S(1)} %collective-permute-done.5.refs_6_), channel_id=1, source_target_pairs={{0,4},{4,0},{8,12},{12,8},{1,5},{5,1},{9,13},{13,9},{2,6},{6,2},{1... | collective-permute-start | bytes 405512 | tf_op jit(solution)/shard_map/ppermute | solution.py:308
  21.1 1.5 %collective-permute-start.12 = (bf16[528,128]{1,0:T(8,128)(2,1)S(1)}, bf16[528,128]{1,0:T(8,128)(2,1)S(1)}, u32[]{:S(2)}, u32[]{:S(2)}) collective-permute-start(bf16[528,128]{1,0:T(8,128)(2,1)S(1)} %collective-permute-done.4.refs_5_), channel_id=1, source_target_pairs={{0,4},{4,0},{8,12},{12,8},{1,5},{5,1},{9,13},{13,9},{2,6},{6,2},{1... | collective-permute-start | bytes 405512 | tf_op jit(solution)/shard_map/ppermute | solution.py:308
  22.3 1.4 %collective-permute-start.14 = (bf16[528,128]{1,0:T(8,128)(2,1)S(1)}, bf16[528,128]{1,0:T(8,128)(2,1)S(1)}, u32[]{:S(2)}, u32[]{:S(2)}) collective-permute-start(bf16[528,128]{1,0:T(8,128)(2,1)S(1)} %collective-permute-done.6.refs_7_), channel_id=1, source_target_pairs={{0,4},{4,0},{8,12},{12,8},{1,5},{5,1},{9,13},{13,9},{2,6},{6,2},{1... | collective-permute-start | bytes 405512 | tf_op jit(solution)/shard_map/ppermute | solution.py:308
  24.6 13.2 %collective-permute-start.15 = (s32[264,128]{1,0:T(8,128)S(1)}, s32[264,128]{1,0:T(8,128)S(1)}, u32[]{:S(2)}, u32[]{:S(2)}) collective-permute-start(s32[264,128]{1,0:T(8,128)S(1)} %get-tuple-element.16), channel_id=1, source_target_pairs={{0,2},{1,3},{2,0},{3,1},{4,6},{5,7},{6,4},{7,5},{8,10},{9,11},{10,... | collective-permute-start | bytes 405512 | tf_op jit(solution)/shard_map/ppermute | solution.py:248
  28.3 9.6 %collective-permute-start.16 = (s32[264,128]{1,0:T(8,128)S(1)}, s32[264,128]{1,0:T(8,128)S(1)}, u32[]{:S(2)}, u32[]{:S(2)}) collective-permute-start(s32[264,128]{1,0:T(8,128)S(1)} %get-tuple-element.17), channel_id=1, source_target_pairs={{0,3},{1,2},{2,1},{3,0},{4,7},{5,6},{6,5},{7,4},{8,11},{9,10},{10,... | collective-permute-start | bytes 405512 | tf_op jit(solution)/shard_map/ppermute | solution.py:248
  30.4 9.3 %collective-permute-start.17 = (s32[264,128]{1,0:T(8,128)S(1)}, s32[264,128]{1,0:T(8,128)S(1)}, u32[]{:S(2)}, u32[]{:S(2)}) collective-permute-start(s32[264,128]{1,0:T(8,128)S(1)} %get-tuple-element.18), channel_id=1, source_target_pairs={{0,1},{1,0},{2,3},{3,2},{4,5},{5,4},{6,7},{7,6},{8,9},{9,8},{10,11... | collective-permute-start | bytes 405512 | tf_op jit(solution)/shard_map/ppermute | solution.py:248
  31.7 8.1 %copy-start = (bf16[2,256,256]{2,1,0:T(8,128)(2,1)S(1)}, bf16[2,256,256]{2,1,0:T(8,128)(2,1)}, u32[]{:S(2)}) copy-start(bf16[2,256,256]{2,1,0:T(8,128)(2,1)} %core_ref.1) | copy-start | bytes 786436

commit v19 on v18

--- a/solution.py
+++ b/solution.py
@@ -330,7 +330,7 @@
     beyond = {top: along_z(beyond, top)}
     for _ in range(5):
         beyond[top] = gate(beyond[top])
-    rest = [k for k in range(lanes - 1, 0, -1) if k != top]
+    rest = [k for k in range(1, lanes) if k != top]
     units = couple([(k, True) for k in rest], "couple_rest", [filled])
     for k, unit in zip(rest, units):
         beyond[k] = along_z(unit, k)

time: 40.9 us -> 39.9 us (0.976)
  waiting for transfers between devices: 14.6 us -> 13.8 us
    ppermute x7, waiting for transfers between devices: 12.5 us -> 11.6 us  [along_z(): return lax.ppermute(piece, 'intra', xor_pairs(lanes, bit))]
  transfers between devices with their start and end apart: 18 -> 18, of which waited for: 8 -> 9; matrix products, arithmetic and copies ran while one was open for 0% -> 0% of each run, Pallas kernels for 9% -> 9%
where the time goes in v19:
time: 39.9 us; the launch traced here: 39.8 us
  starting transfers between devices  19.2 us (48%)
  waiting for transfers between devices  13.8 us (35%)
  Pallas kernels  6.61 us (17%)
    ppermute x7, starting transfers between devices, along_z(): return lax.ppermute(piece, 'intra', xor_pairs(lanes, bit))  12.8 us
    ppermute x7, waiting for transfers between devices, along_z(): return lax.ppermute(piece, 'intra', xor_pairs(lanes, bit))  11.6 us
    ppermute x3, starting transfers between devices, along_y(): return lax.ppermute(piece, 'gddi', xor_pairs(groups, 2 * y))  4.85 us
    pallas_call x3, Pallas kernels, couple(): pl.pallas_call(functools.partial(couple_kernel, groups, lanes, mono_dev,...  2.9 us
    pallas_call x1, Pallas kernels, local(): pl.pallas_call(stage_kernel, out_shape=[pltpu.SMEM((nbr.shape[1], nbr.sha...  1.62 us
    ppermute x8, starting transfers between devices, local(): lax.ppermute(piece, 'gddi', xor_pairs(groups, 1))  1.59 us
    ppermute x8, waiting for transfers between devices, local(): lax.ppermute(piece, 'gddi', xor_pairs(groups, 1))  1.36 us
    pallas_call x1, Pallas kernels, local(): pl.pallas_call(fold_kernel, out_shape=pltpu.VMEM((rows, half), density.dt...  1 us
  transfers between devices with their start and end apart: 18, of which 9 were waited for; matrix products, arithmetic and copies ran while one was open for 0% of the time, Pallas kernels for 9%

profile of v19, /device:TPU:0, one launch (start us, length us, event | category | flops | bytes accessed | tf_op | source)
XLA Modules:
  0.0 39.8 jit_solution(9975533589239595888)
XLA Ops:
  0.0 1.0 %fold.1.refs_0_ = bf16[528,128]{1,0:T(8,128)(2,1)S(1)} custom-call(bf16[2,256,256]{2,1,0:T(8,128)(2,1)} %dens_ref.1), custom_call_target="tpu_custom_call" | custom-call | tf_op jit(solution)/shard_map/fold/pallas_call | solution.py:239
  1.0 4.1 %collective-permute-start.1 = (bf16[528,128]{1,0:T(8,128)(2,1)S(1)}, bf16[528,128]{1,0:T(8,128)(2,1)S(1)}, u32[]{:S(2)}, u32[]{:S(2)}) collective-permute-start(bf16[528,128]{1,0:T(8,128)(2,1)S(1)} %fold.1.refs_0_), channel_id=1, source_target_pairs={{0,2},{1,3},{2,0},{3,1},{4,6},{5,7},{6,4},{7,5},{8,10},{9,11},{10,... | collective-permute-start | bytes 405512 | tf_op jit(solution)/shard_map/ppermute | solution.py:248
  5.1 1.6 %collective-permute-start.2 = (bf16[528,128]{1,0:T(8,128)(2,1)S(1)}, bf16[528,128]{1,0:T(8,128)(2,1)S(1)}, u32[]{:S(2)}, u32[]{:S(2)}) collective-permute-start(bf16[528,128]{1,0:T(8,128)(2,1)S(1)} %fold.1.refs_0_), channel_id=1, source_target_pairs={{0,1},{1,0},{2,3},{3,2},{4,5},{5,4},{6,7},{7,6},{8,9},{9,8},{10,11... | collective-permute-start | bytes 405512 | tf_op jit(solution)/shard_map/ppermute | solution.py:248
  6.7 1.5 %collective-permute-start = (bf16[528,128]{1,0:T(8,128)(2,1)S(1)}, bf16[528,128]{1,0:T(8,128)(2,1)S(1)}, u32[]{:S(2)}, u32[]{:S(2)}) collective-permute-start(bf16[528,128]{1,0:T(8,128)(2,1)S(1)} %fold.1.refs_0_), channel_id=1, source_target_pairs={{0,8},{4,12},{8,0},{12,4},{1,9},{5,13},{9,1},{13,5},{2,10},{6,14},... | collective-permute-start | bytes 405512 | tf_op jit(solution)/shard_map/ppermute | solution.py:251
  8.2 3.5 %collective-permute-done.1.piece_ref = bf16[528,128]{1,0:T(8,128)(2,1)S(1)} collective-permute-done((bf16[528,128]{1,0:T(8,128)(2,1)S(1)}, bf16[528,128]{1,0:T(8,128)(2,1)S(1)}, u32[]{:S(2)}, u32[]{:S(2)}) %collective-permute-start.1) | collective-permute-done | bytes 135200 | tf_op jit(solution)/shard_map/ppermute | solution.py:248
  11.9 1.5 %collective-permute-start.3 = (bf16[528,128]{1,0:T(8,128)(2,1)S(1)}, bf16[528,128]{1,0:T(8,128)(2,1)S(1)}, u32[]{:S(2)}, u32[]{:S(2)}) collective-permute-start(bf16[528,128]{1,0:T(8,128)(2,1)S(1)} %gate.8.refs_2_), channel_id=1, source_target_pairs={{0,1},{1,0},{2,3},{3,2},{4,5},{5,4},{6,7},{7,6},{8,9},{9,8},{10,11... | collective-permute-start | bytes 405512 | tf_op jit(solution)/shard_map/ppermute | solution.py:248
  13.4 0.5 %collective-permute-start.9 = (bf16[528,128]{1,0:T(8,128)(2,1)S(1)}, bf16[528,128]{1,0:T(8,128)(2,1)S(1)}, u32[]{:S(2)}, u32[]{:S(2)}) collective-permute-start(bf16[528,128]{1,0:T(8,128)(2,1)S(1)} %gate.8.refs_2_), channel_id=1, source_target_pairs={{0,4},{4,0},{8,12},{12,8},{1,5},{5,1},{9,13},{13,9},{2,6},{6,2},{1... | collective-permute-start | bytes 405512 | tf_op jit(solution)/shard_map/ppermute | solution.py:308
  13.9 1.5 %collective-permute-start.5 = (bf16[528,128]{1,0:T(8,128)(2,1)S(1)}, bf16[528,128]{1,0:T(8,128)(2,1)S(1)}, u32[]{:S(2)}, u32[]{:S(2)}) collective-permute-start(bf16[528,128]{1,0:T(8,128)(2,1)S(1)} %gate.8.refs_2_), channel_id=1, source_target_pairs={{0,8},{4,12},{8,0},{12,4},{1,9},{5,13},{9,1},{13,5},{2,10},{6,14},... | collective-permute-start | bytes 405512 | tf_op jit(solution)/shard_map/ppermute | solution.py:251
  15.5 0.6 %collective-permute-start.4 = (bf16[528,128]{1,0:T(8,128)(2,1)S(1)}, bf16[528,128]{1,0:T(8,128)(2,1)S(1)}, u32[]{:S(2)}, u32[]{:S(2)}) collective-permute-start(bf16[528,128]{1,0:T(8,128)(2,1)S(1)} %collective-permute-done.refs_2_.piece_ref), channel_id=1, source_target_pairs={{0,1},{1,0},{2,3},{3,2},{4,5},{5,4},{6,7},{7,6},{8,9},{9,8},{10,11... | collective-permute-start | bytes 405512 | tf_op jit(solution)/shard_map/ppermute | solution.py:248
  16.1 0.9 %collective-permute-done.3.refs_0_.refs_3_ = bf16[528,128]{1,0:T(8,128)(2,1)S(1)} collective-permute-done((bf16[528,128]{1,0:T(8,128)(2,1)S(1)}, bf16[528,128]{1,0:T(8,128)(2,1)S(1)}, u32[]{:S(2)}, u32[]{:S(2)}) %collective-permute-start.3) | collective-permute-done | bytes 135200 | tf_op jit(solution)/shard_map/ppermute | solution.py:248
  17.0 1.8 %collective-permute-start.6 = (bf16[528,128]{1,0:T(8,128)(2,1)S(1)}, bf16[528,128]{1,0:T(8,128)(2,1)S(1)}, u32[]{:S(2)}, u32[]{:S(2)}) collective-permute-start(bf16[528,128]{1,0:T(8,128)(2,1)S(1)} %collective-permute-done.3.refs_0_.refs_3_), channel_id=1, source_target_pairs={{0,8},{4,12},{8,0},{12,4},{1,9},{5,13},{9,1},{13,5},{2,10},{6,14},... | collective-permute-start | bytes 405512 | tf_op jit(solution)/shard_map/ppermute | solution.py:251
  18.8 1.6 %stage.1 = (s32[8,32]{1,0:T(8,128)S(4)}, bf16[8,2,256,256]{3,2,1,0:T(8,128)(2,1)S(1)}, bf16[528,128]{1,0:T(8,128)(2,1)S(1)}) custom-call(s32[8,32]{1,0:T(8,128)} %bitcast.1, bf16[8,2,256,256]{3,2,1,0:T(8,128)(2,1)} %esp_ref.1, bf16[528,128]{1,0:T(8,128)(2,1)S(1)} %collective-permute-done.refs_2_.piece_ref, ...), custom_call_target="tpu_custom_call" | custom-call | tf_op jit(solution)/shard_map/stage/pallas_call | solution.py:288
  20.5 0.5 %collective-permute-start.10 = (bf16[528,128]{1,0:T(8,128)(2,1)S(1)}, bf16[528,128]{1,0:T(8,128)(2,1)S(1)}, u32[]{:S(2)}, u32[]{:S(2)}) collective-permute-start(bf16[528,128]{1,0:T(8,128)(2,1)S(1)} %collective-permute-done.3.refs_0_.refs_3_), channel_id=1, source_target_pairs={{0,4},{4,0},{8,12},{12,8},{1,5},{5,1},{9,13},{13,9},{2,6},{6,2},{1... | collective-permute-start | bytes 405512 | tf_op jit(solution)/shard_map/ppermute | solution.py:308
  21.5 0.8 %collective-permute-done.6.refs_7_ = bf16[528,128]{1,0:T(8,128)(2,1)S(1)} collective-permute-done((bf16[528,128]{1,0:T(8,128)(2,1)S(1)}, bf16[528,128]{1,0:T(8,128)(2,1)S(1)}, u32[]{:S(2)}, u32[]{:S(2)}) %collective-permute-start.6) | collective-permute-done | bytes 135200 | tf_op jit(solution)/shard_map/ppermute | solution.py:251
  22.6 1.1 %collective-permute-done.14.refs_15_ = bf16[528,128]{1,0:T(8,128)(2,1)S(1)} collective-permute-done((bf16[528,128]{1,0:T(8,128)(2,1)S(1)}, bf16[528,128]{1,0:T(8,128)(2,1)S(1)}, u32[]{:S(2)}, u32[]{:S(2)}) %collective-permute-start.14) | collective-permute-done | bytes 135200 | tf_op jit(solution)/shard_map/ppermute | solution.py:308
  23.7 0.9 %couple_first.1 = (bf16[16,528,128]{2,1,0:T(8,128)(2,1)S(1)}, s32[264,128]{1,0:T(8,128)S(1)}) custom-call(s32[8,32]{1,0:T(8,128)S(4)} %get-tuple-element.12.nbr_ref, bf16[8,2,256,256]{3,2,1,0:T(8,128)(2,1)S(1)} %get-tuple-element.13.esp_ref, bf16[528,128]{1,0:T(8,128)(2,1)S(1)} %fold.1.refs_0_, bf16[528,128]{1,0:T(8,128)(2,1)S(1)} %collective-permute-done.2.refs_1_, ...), custom_call_target="tpu_custom_call" | custom-call | tf_op jit(solution)/shard_map/couple_first/pallas_call | solution.py:318
  24.6 2.4 %collective-permute-start.15 = (s32[264,128]{1,0:T(8,128)S(1)}, s32[264,128]{1,0:T(8,128)S(1)}, u32[]{:S(2)}, u32[]{:S(2)}) collective-permute-start(s32[264,128]{1,0:T(8,128)S(1)} %get-tuple-element.16), channel_id=1, source_target_pairs={{0,2},{1,3},{2,0},{3,1},{4,6},{5,7},{6,4},{7,5},{8,10},{9,11},{10,... | collective-permute-start | bytes 405512 | tf_op jit(solution)/shard_map/ppermute | solution.py:248
  27.0 1.3 %couple_rest.1 = (s32[264,128]{1,0:T(8,128)S(1)}, s32[264,128]{1,0:T(8,128)S(1)}) custom-call(s32[8,32]{1,0:T(8,128)S(4)} %get-tuple-element.12.nbr_ref, bf16[8,2,256,256]{3,2,1,0:T(8,128)(2,1)S(1)} %get-tuple-element.13.esp_ref, bf16[16,528,128]{2,1,0:T(8,128)(2,1)S(1)} %get-tuple-element.15.refs_0_), custom_call_target="tpu_custom_call" | custom-call | tf_op jit(solution)/shard_map/couple_rest/pallas_call | solution.py:318
  28.3 2.5 %collective-permute-start.16 = (s32[264,128]{1,0:T(8,128)S(1)}, s32[264,128]{1,0:T(8,128)S(1)}, u32[]{:S(2)}, u32[]{:S(2)}) collective-permute-start(s32[264,128]{1,0:T(8,128)S(1)} %get-tuple-element.17), channel_id=1, source_target_pairs={{0,1},{1,0},{2,3},{3,2},{4,5},{5,4},{6,7},{7,6},{8,9},{9,8},{10,11... | collective-permute-start | bytes 405512 | tf_op jit(solution)/shard_map/ppermute | solution.py:248
  30.9 0.7 %couple_own.1.plain_ref = f32[2,264,128]{2,1,0:T(8,128)S(1)} custom-call(s32[8,32]{1,0:T(8,128)S(4)} %get-tuple-element.12.nbr_ref, bf16[8,2,256,256]{3,2,1,0:T(8,128)(2,1)S(1)} %get-tuple-element.13.esp_ref, bf16[16,528,128]{2,1,0:T(8,128)(2,1)S(1)} %get-tuple-element.15.refs_0_), custom_call_target="tpu_custom_call" | custom-call | tf_op jit(solution)/shard_map/couple_own/pallas_call | solution.py:318
  31.6 3.3 %collective-permute-done.15.piece_ref = s32[264,128]{1,0:T(8,128)S(1)} collective-permute-done((s32[264,128]{1,0:T(8,128)S(1)}, s32[264,128]{1,0:T(8,128)S(1)}, u32[]{:S(2)}, u32[]{:S(2)}) %collective-permute-start.15) | collective-permute-done | bytes 135200 | tf_op jit(solution)/shard_map/ppermute | solution.py:248
  35.0 0.9 %collective-permute-done.16.refs_0_ = s32[264,128]{1,0:T(8,128)S(1)} collective-permute-done((s32[264,128]{1,0:T(8,128)S(1)}, s32[264,128]{1,0:T(8,128)S(1)}, u32[]{:S(2)}, u32[]{:S(2)}) %collective-permute-start.16) | collective-permute-done | bytes 135200 | tf_op jit(solution)/shard_map/ppermute | solution.py:248
  36.0 2.9 %collective-permute-done.17.refs_1_ = s32[264,128]{1,0:T(8,128)S(1)} collective-permute-done((s32[264,128]{1,0:T(8,128)S(1)}, s32[264,128]{1,0:T(8,128)S(1)}, u32[]{:S(2)}, u32[]{:S(2)}) %collective-permute-start.17) | collective-permute-done | bytes 135200 | tf_op jit(solution)/shard_map/ppermute | solution.py:248
  38.8 1.0 %finish.1 = f32[2,256,256]{2,1,0:T(8,128)} custom-call(bf16[2,256,256]{2,1,0:T(8,128)(2,1)S(1)} %copy-done, f32[2,264,128]{2,1,0:T(8,128)S(1)} %add.1.own_ref, s32[264,128]{1,0:T(8,128)S(1)} %collective-permute-done.16.refs_0_, s32[264,128]{1,0:T(8,128)S(1)} %collective-permute-done.17.refs_1_), custom_call_target="tpu_custom_call" | custom-call | tf_op jit(solution)/shard_map/finish/pallas_call | solution.py:346
  (28 shorter events, 1.2 us)
Async XLA Ops:
  1.0 10.7 %collective-permute-start.1 = (bf16[528,128]{1,0:T(8,128)(2,1)S(1)}, bf16[528,128]{1,0:T(8,128)(2,1)S(1)}, u32[]{:S(2)}, u32[]{:S(2)}) collective-permute-start(bf16[528,128]{1,0:T(8,128)(2,1)S(1)} %fold.1.refs_0_), channel_id=1, source_target_pairs={{0,2},{1,3},{2,0},{3,1},{4,6},{5,7},{6,4},{7,5},{8,10},{9,11},{10,... | collective-permute-start | bytes 405512 | tf_op jit(solution)/shard_map/ppermute | solution.py:248
  5.1 6.8 %collective-permute-start.2 = (bf16[528,128]{1,0:T(8,128)(2,1)S(1)}, bf16[528,128]{1,0:T(8,128)(2,1)S(1)}, u32[]{:S(2)}, u32[]{:S(2)}) collective-permute-start(bf16[528,128]{1,0:T(8,128)(2,1)S(1)} %fold.1.refs_0_), channel_id=1, source_target_pairs={{0,1},{1,0},{2,3},{3,2},{4,5},{5,4},{6,7},{7,6},{8,9},{9,8},{10,11... | collective-permute-start | bytes 405512 | tf_op jit(solution)/shard_map/ppermute | solution.py:248
  6.7 5.2 %collective-permute-start = (bf16[528,128]{1,0:T(8,128)(2,1)S(1)}, bf16[528,128]{1,0:T(8,128)(2,1)S(1)}, u32[]{:S(2)}, u32[]{:S(2)}) collective-permute-start(bf16[528,128]{1,0:T(8,128)(2,1)S(1)} %fold.1.refs_0_), channel_id=1, source_target_pairs={{0,8},{4,12},{8,0},{12,4},{1,9},{5,13},{9,1},{13,5},{2,10},{6,14},... | collective-permute-start | bytes 405512 | tf_op jit(solution)/shard_map/ppermute | solution.py:251
  8.2 7.3 %collective-permute-start.7 = (bf16[528,128]{1,0:T(8,128)(2,1)S(1)}, bf16[528,128]{1,0:T(8,128)(2,1)S(1)}, u32[]{:S(2)}, u32[]{:S(2)}) collective-permute-start(bf16[528,128]{1,0:T(8,128)(2,1)S(1)} %fold.1.refs_0_), channel_id=1, source_target_pairs={{0,4},{4,0},{8,12},{12,8},{1,5},{5,1},{9,13},{13,9},{2,6},{6,2},{1... | collective-permute-start | bytes 405512 | tf_op jit(solution)/shard_map/ppermute | solution.py:308
  11.9 5.1 %collective-permute-start.3 = (bf16[528,128]{1,0:T(8,128)(2,1)S(1)}, bf16[528,128]{1,0:T(8,128)(2,1)S(1)}, u32[]{:S(2)}, u32[]{:S(2)}) collective-permute-start(bf16[528,128]{1,0:T(8,128)(2,1)S(1)} %gate.8.refs_2_), channel_id=1, source_target_pairs={{0,1},{1,0},{2,3},{3,2},{4,5},{5,4},{6,7},{7,6},{8,9},{9,8},{10,11... | collective-permute-start | bytes 405512 | tf_op jit(solution)/shard_map/ppermute | solution.py:248
  13.4 7.0 %collective-permute-start.8 = (bf16[528,128]{1,0:T(8,128)(2,1)S(1)}, bf16[528,128]{1,0:T(8,128)(2,1)S(1)}, u32[]{:S(2)}, u32[]{:S(2)}) collective-permute-start(bf16[528,128]{1,0:T(8,128)(2,1)S(1)} %collective-permute-done.2.refs_1_), channel_id=1, source_target_pairs={{0,4},{4,0},{8,12},{12,8},{1,5},{5,1},{9,13},{13,9},{2,6},{6,2},{1... | collective-permute-start | bytes 405512 | tf_op jit(solution)/shard_map/ppermute | solution.py:308
  13.4 7.1 %collective-permute-start.9 = (bf16[528,128]{1,0:T(8,128)(2,1)S(1)}, bf16[528,128]{1,0:T(8,128)(2,1)S(1)}, u32[]{:S(2)}, u32[]{:S(2)}) collective-permute-start(bf16[528,128]{1,0:T(8,128)(2,1)S(1)} %gate.8.refs_2_), channel_id=1, source_target_pairs={{0,4},{4,0},{8,12},{12,8},{1,5},{5,1},{9,13},{13,9},{2,6},{6,2},{1... | collective-permute-start | bytes 405512 | tf_op jit(solution)/shard_map/ppermute | solution.py:308
  13.9 7.1 %collective-permute-start.5 = (bf16[528,128]{1,0:T(8,128)(2,1)S(1)}, bf16[528,128]{1,0:T(8,128)(2,1)S(1)}, u32[]{:S(2)}, u32[]{:S(2)}) collective-permute-start(bf16[528,128]{1,0:T(8,128)(2,1)S(1)} %gate.8.refs_2_), channel_id=1, source_target_pairs={{0,8},{4,12},{8,0},{12,4},{1,9},{5,13},{9,1},{13,5},{2,10},{6,14},... | collective-permute-start | bytes 405512 | tf_op jit(solution)/shard_map/ppermute | solution.py:251
  15.5 5.6 %collective-permute-start.4 = (bf16[528,128]{1,0:T(8,128)(2,1)S(1)}, bf16[528,128]{1,0:T(8,128)(2,1)S(1)}, u32[]{:S(2)}, u32[]{:S(2)}) collective-permute-start(bf16[528,128]{1,0:T(8,128)(2,1)S(1)} %collective-permute-done.refs_2_.piece_ref), channel_id=1, source_target_pairs={{0,1},{1,0},{2,3},{3,2},{4,5},{5,4},{6,7},{7,6},{8,9},{9,8},{10,11... | collective-permute-start | bytes 405512 | tf_op jit(solution)/shard_map/ppermute | solution.py:248
  17.0 5.3 %collective-permute-start.6 = (bf16[528,128]{1,0:T(8,128)(2,1)S(1)}, bf16[528,128]{1,0:T(8,128)(2,1)S(1)}, u32[]{:S(2)}, u32[]{:S(2)}) collective-permute-start(bf16[528,128]{1,0:T(8,128)(2,1)S(1)} %collective-permute-done.3.refs_0_.refs_3_), channel_id=1, source_target_pairs={{0,8},{4,12},{8,0},{12,4},{1,9},{5,13},{9,1},{13,5},{2,10},{6,14},... | collective-permute-start | bytes 405512 | tf_op jit(solution)/shard_map/ppermute | solution.py:251
  20.4 2.1 %collective-permute-start.11 = (bf16[528,128]{1,0:T(8,128)(2,1)S(1)}, bf16[528,128]{1,0:T(8,128)(2,1)S(1)}, u32[]{:S(2)}, u32[]{:S(2)}) collective-permute-start(bf16[528,128]{1,0:T(8,128)(2,1)S(1)} %get-tuple-element.14.refs_4_), channel_id=1, source_target_pairs={{0,4},{4,0},{8,12},{12,8},{1,5},{5,1},{9,13},{13,9},{2,6},{6,2},{1... | collective-permute-start | bytes 405512 | tf_op jit(solution)/shard_map/ppermute | solution.py:308
  20.5 1.9 %collective-permute-start.10 = (bf16[528,128]{1,0:T(8,128)(2,1)S(1)}, bf16[528,128]{1,0:T(8,128)(2,1)S(1)}, u32[]{:S(2)}, u32[]{:S(2)}) collective-permute-start(bf16[528,128]{1,0:T(8,128)(2,1)S(1)} %collective-permute-done.3.refs_0_.refs_3_), channel_id=1, source_target_pairs={{0,4},{4,0},{8,12},{12,8},{1,5},{5,1},{9,13},{13,9},{2,6},{6,2},{1... | collective-permute-start | bytes 405512 | tf_op jit(solution)/shard_map/ppermute | solution.py:308
  21.0 1.4 %collective-permute-start.13 = (bf16[528,128]{1,0:T(8,128)(2,1)S(1)}, bf16[528,128]{1,0:T(8,128)(2,1)S(1)}, u32[]{:S(2)}, u32[]{:S(2)}) collective-permute-start(bf16[528,128]{1,0:T(8,128)(2,1)S(1)} %collective-permute-done.5.refs_6_), channel_id=1, source_target_pairs={{0,4},{4,0},{8,12},{12,8},{1,5},{5,1},{9,13},{13,9},{2,6},{6,2},{1... | collective-permute-start | bytes 405512 | tf_op jit(solution)/shard_map/ppermute | solution.py:308
  21.1 1.5 %collective-permute-start.12 = (bf16[528,128]{1,0:T(8,128)(2,1)S(1)}, bf16[528,128]{1,0:T(8,128)(2,1)S(1)}, u32[]{:S(2)}, u32[]{:S(2)}) collective-permute-start(bf16[528,128]{1,0:T(8,128)(2,1)S(1)} %collective-permute-done.4.refs_5_), channel_id=1, source_target_pairs={{0,4},{4,0},{8,12},{12,8},{1,5},{5,1},{9,13},{13,9},{2,6},{6,2},{1... | collective-permute-start | bytes 405512 | tf_op jit(solution)/shard_map/ppermute | solution.py:308
  22.3 1.4 %collective-permute-start.14 = (bf16[528,128]{1,0:T(8,128)(2,1)S(1)}, bf16[528,128]{1,0:T(8,128)(2,1)S(1)}, u32[]{:S(2)}, u32[]{:S(2)}) collective-permute-start(bf16[528,128]{1,0:T(8,128)(2,1)S(1)} %collective-permute-done.6.refs_7_), channel_id=1, source_target_pairs={{0,4},{4,0},{8,12},{12,8},{1,5},{5,1},{9,13},{13,9},{2,6},{6,2},{1... | collective-permute-start | bytes 405512 | tf_op jit(solution)/shard_map/ppermute | solution.py:308
  24.6 10.3 %collective-permute-start.15 = (s32[264,128]{1,0:T(8,128)S(1)}, s32[264,128]{1,0:T(8,128)S(1)}, u32[]{:S(2)}, u32[]{:S(2)}) collective-permute-start(s32[264,128]{1,0:T(8,128)S(1)} %get-tuple-element.16), channel_id=1, source_target_pairs={{0,2},{1,3},{2,0},{3,1},{4,6},{5,7},{6,4},{7,5},{8,10},{9,11},{10,... | collective-permute-start | bytes 405512 | tf_op jit(solution)/shard_map/ppermute | solution.py:248
  28.3 7.6 %collective-permute-start.16 = (s32[264,128]{1,0:T(8,128)S(1)}, s32[264,128]{1,0:T(8,128)S(1)}, u32[]{:S(2)}, u32[]{:S(2)}) collective-permute-start(s32[264,128]{1,0:T(8,128)S(1)} %get-tuple-element.17), channel_id=1, source_target_pairs={{0,1},{1,0},{2,3},{3,2},{4,5},{5,4},{6,7},{7,6},{8,9},{9,8},{10,11... | collective-permute-start | bytes 405512 | tf_op jit(solution)/shard_map/ppermute | solution.py:248
  30.9 7.9 %collective-permute-start.17 = (s32[264,128]{1,0:T(8,128)S(1)}, s32[264,128]{1,0:T(8,128)S(1)}, u32[]{:S(2)}, u32[]{:S(2)}) collective-permute-start(s32[264,128]{1,0:T(8,128)S(1)} %get-tuple-element.18), channel_id=1, source_target_pairs={{0,3},{1,2},{2,1},{3,0},{4,7},{5,6},{6,5},{7,4},{8,11},{9,10},{10,... | collective-permute-start | bytes 405512 | tf_op jit(solution)/shard_map/ppermute | solution.py:248
  31.6 7.2 %copy-start = (bf16[2,256,256]{2,1,0:T(8,128)(2,1)S(1)}, bf16[2,256,256]{2,1,0:T(8,128)(2,1)}, u32[]{:S(2)}) copy-start(bf16[2,256,256]{2,1,0:T(8,128)(2,1)} %core_ref.1) | copy-start | bytes 786436

commit v20 on v19

--- a/solution.py
+++ b/solution.py
@@ -53,13 +53,13 @@
 
 
 def encode(x, code):
-    units = jnp.exp(code.astype(jnp.float32) * (-1.0 / STEPS)) * TOP
-    return jnp.floor(x * SHRINK * units + 0.5).astype(jnp.int32)
+    inverse = jnp.exp(code.astype(jnp.float32) * (-1.0 / STEPS))
+    return jnp.floor(x * SHRINK * inverse * TOP + 0.5).astype(jnp.int32)
 
 
 def decode(q, code):
-    units = jnp.exp(code.astype(jnp.float32) * (1.0 / STEPS)) * (1.0 / TOP)
-    return q.astype(jnp.float32) * units * (1.0 / SHRINK)
+    scale = jnp.exp(code.astype(jnp.float32) * (1.0 / STEPS))
+    return q.astype(jnp.float32) * (1.0 / TOP) * scale * (1.0 / SHRINK)
 
 
 def pack(high, low):

time: 39.9 us -> 40 us (level)
  no operation moved by 1% of the time
where the time goes in v20:
time: 40 us; the launch traced here: 39.8 us
  starting transfers between devices  19.3 us (48%)
  waiting for transfers between devices  13.7 us (34%)
  Pallas kernels  6.66 us (17%)
    ppermute x7, starting transfers between devices, along_z(): return lax.ppermute(piece, 'intra', xor_pairs(lanes, bit))  12.8 us
    ppermute x7, waiting for transfers between devices, along_z(): return lax.ppermute(piece, 'intra', xor_pairs(lanes, bit))  11.6 us
    ppermute x3, starting transfers between devices, along_y(): return lax.ppermute(piece, 'gddi', xor_pairs(groups, 2 * y))  4.85 us
    pallas_call x3, Pallas kernels, couple(): pl.pallas_call(functools.partial(couple_kernel, groups, lanes, mono_dev,...  2.93 us
    pallas_call x1, Pallas kernels, local(): pl.pallas_call(stage_kernel, out_shape=[pltpu.SMEM((nbr.shape[1], nbr.sha...  1.62 us
    ppermute x8, starting transfers between devices, local(): lax.ppermute(piece, 'gddi', xor_pairs(groups, 1))  1.59 us
    ppermute x8, waiting for transfers between devices, local(): lax.ppermute(piece, 'gddi', xor_pairs(groups, 1))  1.36 us
    pallas_call x1, Pallas kernels, local(): pl.pallas_call(fold_kernel, out_shape=pltpu.VMEM((rows, half), density.dt...  1 us
  transfers between devices with their start and end apart: 18, of which 9 were waited for; matrix products, arithmetic and copies ran while one was open for 0% of the time, Pallas kernels for 9%

profile of v20, /device:TPU:0, one launch (start us, length us, event | category | flops | bytes accessed | tf_op | source)
XLA Modules:
  0.0 39.8 jit_solution(15620499355781475610)
XLA Ops:
  0.0 1.0 %fold.1.refs_0_ = bf16[528,128]{1,0:T(8,128)(2,1)S(1)} custom-call(bf16[2,256,256]{2,1,0:T(8,128)(2,1)} %dens_ref.1), custom_call_target="tpu_custom_call" | custom-call | tf_op jit(solution)/shard_map/fold/pallas_call | solution.py:239
  1.0 4.1 %collective-permute-start.1 = (bf16[528,128]{1,0:T(8,128)(2,1)S(1)}, bf16[528,128]{1,0:T(8,128)(2,1)S(1)}, u32[]{:S(2)}, u32[]{:S(2)}) collective-permute-start(bf16[528,128]{1,0:T(8,128)(2,1)S(1)} %fold.1.refs_0_), channel_id=1, source_target_pairs={{0,2},{1,3},{2,0},{3,1},{4,6},{5,7},{6,4},{7,5},{8,10},{9,11},{10,... | collective-permute-start | bytes 405512 | tf_op jit(solution)/shard_map/ppermute | solution.py:248
  5.1 1.6 %collective-permute-start.2 = (bf16[528,128]{1,0:T(8,128)(2,1)S(1)}, bf16[528,128]{1,0:T(8,128)(2,1)S(1)}, u32[]{:S(2)}, u32[]{:S(2)}) collective-permute-start(bf16[528,128]{1,0:T(8,128)(2,1)S(1)} %fold.1.refs_0_), channel_id=1, source_target_pairs={{0,1},{1,0},{2,3},{3,2},{4,5},{5,4},{6,7},{7,6},{8,9},{9,8},{10,11... | collective-permute-start | bytes 405512 | tf_op jit(solution)/shard_map/ppermute | solution.py:248
  6.7 1.5 %collective-permute-start = (bf16[528,128]{1,0:T(8,128)(2,1)S(1)}, bf16[528,128]{1,0:T(8,128)(2,1)S(1)}, u32[]{:S(2)}, u32[]{:S(2)}) collective-permute-start(bf16[528,128]{1,0:T(8,128)(2,1)S(1)} %fold.1.refs_0_), channel_id=1, source_target_pairs={{0,8},{4,12},{8,0},{12,4},{1,9},{5,13},{9,1},{13,5},{2,10},{6,14},... | collective-permute-start | bytes 405512 | tf_op jit(solution)/shard_map/ppermute | solution.py:251
  8.2 3.5 %collective-permute-done.1.piece_ref = bf16[528,128]{1,0:T(8,128)(2,1)S(1)} collective-permute-done((bf16[528,128]{1,0:T(8,128)(2,1)S(1)}, bf16[528,128]{1,0:T(8,128)(2,1)S(1)}, u32[]{:S(2)}, u32[]{:S(2)}) %collective-permute-start.1) | collective-permute-done | bytes 135200 | tf_op jit(solution)/shard_map/ppermute | solution.py:248
  11.9 1.5 %collective-permute-start.3 = (bf16[528,128]{1,0:T(8,128)(2,1)S(1)}, bf16[528,128]{1,0:T(8,128)(2,1)S(1)}, u32[]{:S(2)}, u32[]{:S(2)}) collective-permute-start(bf16[528,128]{1,0:T(8,128)(2,1)S(1)} %gate.8.refs_2_), channel_id=1, source_target_pairs={{0,1},{1,0},{2,3},{3,2},{4,5},{5,4},{6,7},{7,6},{8,9},{9,8},{10,11... | collective-permute-start | bytes 405512 | tf_op jit(solution)/shard_map/ppermute | solution.py:248
  13.4 0.5 %collective-permute-start.9 = (bf16[528,128]{1,0:T(8,128)(2,1)S(1)}, bf16[528,128]{1,0:T(8,128)(2,1)S(1)}, u32[]{:S(2)}, u32[]{:S(2)}) collective-permute-start(bf16[528,128]{1,0:T(8,128)(2,1)S(1)} %gate.8.refs_2_), channel_id=1, source_target_pairs={{0,4},{4,0},{8,12},{12,8},{1,5},{5,1},{9,13},{13,9},{2,6},{6,2},{1... | collective-permute-start | bytes 405512 | tf_op jit(solution)/shard_map/ppermute | solution.py:308
  13.9 1.5 %collective-permute-start.5 = (bf16[528,128]{1,0:T(8,128)(2,1)S(1)}, bf16[528,128]{1,0:T(8,128)(2,1)S(1)}, u32[]{:S(2)}, u32[]{:S(2)}) collective-permute-start(bf16[528,128]{1,0:T(8,128)(2,1)S(1)} %gate.8.refs_2_), channel_id=1, source_target_pairs={{0,8},{4,12},{8,0},{12,4},{1,9},{5,13},{9,1},{13,5},{2,10},{6,14},... | collective-permute-start | bytes 405512 | tf_op jit(solution)/shard_map/ppermute | solution.py:251
  15.5 0.6 %collective-permute-start.4 = (bf16[528,128]{1,0:T(8,128)(2,1)S(1)}, bf16[528,128]{1,0:T(8,128)(2,1)S(1)}, u32[]{:S(2)}, u32[]{:S(2)}) collective-permute-start(bf16[528,128]{1,0:T(8,128)(2,1)S(1)} %collective-permute-done.refs_2_.piece_ref), channel_id=1, source_target_pairs={{0,1},{1,0},{2,3},{3,2},{4,5},{5,4},{6,7},{7,6},{8,9},{9,8},{10,11... | collective-permute-start | bytes 405512 | tf_op jit(solution)/shard_map/ppermute | solution.py:248
  16.1 0.9 %collective-permute-done.3.refs_0_.refs_3_ = bf16[528,128]{1,0:T(8,128)(2,1)S(1)} collective-permute-done((bf16[528,128]{1,0:T(8,128)(2,1)S(1)}, bf16[528,128]{1,0:T(8,128)(2,1)S(1)}, u32[]{:S(2)}, u32[]{:S(2)}) %collective-permute-start.3) | collective-permute-done | bytes 135200 | tf_op jit(solution)/shard_map/ppermute | solution.py:248
  17.0 1.8 %collective-permute-start.6 = (bf16[528,128]{1,0:T(8,128)(2,1)S(1)}, bf16[528,128]{1,0:T(8,128)(2,1)S(1)}, u32[]{:S(2)}, u32[]{:S(2)}) collective-permute-start(bf16[528,128]{1,0:T(8,128)(2,1)S(1)} %collective-permute-done.3.refs_0_.refs_3_), channel_id=1, source_target_pairs={{0,8},{4,12},{8,0},{12,4},{1,9},{5,13},{9,1},{13,5},{2,10},{6,14},... | collective-permute-start | bytes 405512 | tf_op jit(solution)/shard_map/ppermute | solution.py:251
  18.8 1.6 %stage.1 = (s32[8,32]{1,0:T(8,128)S(4)}, bf16[8,2,256,256]{3,2,1,0:T(8,128)(2,1)S(1)}, bf16[528,128]{1,0:T(8,128)(2,1)S(1)}) custom-call(s32[8,32]{1,0:T(8,128)} %bitcast.1, bf16[8,2,256,256]{3,2,1,0:T(8,128)(2,1)} %esp_ref.1, bf16[528,128]{1,0:T(8,128)(2,1)S(1)} %collective-permute-done.refs_2_.piece_ref, ...), custom_call_target="tpu_custom_call" | custom-call | tf_op jit(solution)/shard_map/stage/pallas_call | solution.py:288
  20.5 0.5 %collective-permute-start.10 = (bf16[528,128]{1,0:T(8,128)(2,1)S(1)}, bf16[528,128]{1,0:T(8,128)(2,1)S(1)}, u32[]{:S(2)}, u32[]{:S(2)}) collective-permute-start(bf16[528,128]{1,0:T(8,128)(2,1)S(1)} %collective-permute-done.3.refs_0_.refs_3_), channel_id=1, source_target_pairs={{0,4},{4,0},{8,12},{12,8},{1,5},{5,1},{9,13},{13,9},{2,6},{6,2},{1... | collective-permute-start | bytes 405512 | tf_op jit(solution)/shard_map/ppermute | solution.py:308
  21.5 0.8 %collective-permute-done.6.refs_7_ = bf16[528,128]{1,0:T(8,128)(2,1)S(1)} collective-permute-done((bf16[528,128]{1,0:T(8,128)(2,1)S(1)}, bf16[528,128]{1,0:T(8,128)(2,1)S(1)}, u32[]{:S(2)}, u32[]{:S(2)}) %collective-permute-start.6) | collective-permute-done | bytes 135200 | tf_op jit(solution)/shard_map/ppermute | solution.py:251
  22.6 1.1 %collective-permute-done.14.refs_15_ = bf16[528,128]{1,0:T(8,128)(2,1)S(1)} collective-permute-done((bf16[528,128]{1,0:T(8,128)(2,1)S(1)}, bf16[528,128]{1,0:T(8,128)(2,1)S(1)}, u32[]{:S(2)}, u32[]{:S(2)}) %collective-permute-start.14) | collective-permute-done | bytes 135200 | tf_op jit(solution)/shard_map/ppermute | solution.py:308
  23.7 0.9 %couple_first.1 = (bf16[16,528,128]{2,1,0:T(8,128)(2,1)S(1)}, s32[264,128]{1,0:T(8,128)S(1)}) custom-call(s32[8,32]{1,0:T(8,128)S(4)} %get-tuple-element.12.nbr_ref, bf16[8,2,256,256]{3,2,1,0:T(8,128)(2,1)S(1)} %get-tuple-element.13.esp_ref, bf16[528,128]{1,0:T(8,128)(2,1)S(1)} %fold.1.refs_0_, bf16[528,128]{1,0:T(8,128)(2,1)S(1)} %collective-permute-done.2.refs_1_, ...), custom_call_target="tpu_custom_call" | custom-call | tf_op jit(solution)/shard_map/couple_first/pallas_call | solution.py:318
  24.6 2.4 %collective-permute-start.15 = (s32[264,128]{1,0:T(8,128)S(1)}, s32[264,128]{1,0:T(8,128)S(1)}, u32[]{:S(2)}, u32[]{:S(2)}) collective-permute-start(s32[264,128]{1,0:T(8,128)S(1)} %get-tuple-element.16), channel_id=1, source_target_pairs={{0,2},{1,3},{2,0},{3,1},{4,6},{5,7},{6,4},{7,5},{8,10},{9,11},{10,... | collective-permute-start | bytes 405512 | tf_op jit(solution)/shard_map/ppermute | solution.py:248
  27.0 1.3 %couple_rest.1 = (s32[264,128]{1,0:T(8,128)S(1)}, s32[264,128]{1,0:T(8,128)S(1)}) custom-call(s32[8,32]{1,0:T(8,128)S(4)} %get-tuple-element.12.nbr_ref, bf16[8,2,256,256]{3,2,1,0:T(8,128)(2,1)S(1)} %get-tuple-element.13.esp_ref, bf16[16,528,128]{2,1,0:T(8,128)(2,1)S(1)} %get-tuple-element.15.refs_0_), custom_call_target="tpu_custom_call" | custom-call | tf_op jit(solution)/shard_map/couple_rest/pallas_call | solution.py:318
  28.4 2.6 %collective-permute-start.16 = (s32[264,128]{1,0:T(8,128)S(1)}, s32[264,128]{1,0:T(8,128)S(1)}, u32[]{:S(2)}, u32[]{:S(2)}) collective-permute-start(s32[264,128]{1,0:T(8,128)S(1)} %get-tuple-element.17), channel_id=1, source_target_pairs={{0,1},{1,0},{2,3},{3,2},{4,5},{5,4},{6,7},{7,6},{8,9},{9,8},{10,11... | collective-permute-start | bytes 405512 | tf_op jit(solution)/shard_map/ppermute | solution.py:248
  30.9 0.7 %couple_own.1.plain_ref = f32[2,264,128]{2,1,0:T(8,128)S(1)} custom-call(s32[8,32]{1,0:T(8,128)S(4)} %get-tuple-element.12.nbr_ref, bf16[8,2,256,256]{3,2,1,0:T(8,128)(2,1)S(1)} %get-tuple-element.13.esp_ref, bf16[16,528,128]{2,1,0:T(8,128)(2,1)S(1)} %get-tuple-element.15.refs_0_), custom_call_target="tpu_custom_call" | custom-call | tf_op jit(solution)/shard_map/couple_own/pallas_call | solution.py:318
  31.6 3.2 %collective-permute-done.15.piece_ref = s32[264,128]{1,0:T(8,128)S(1)} collective-permute-done((s32[264,128]{1,0:T(8,128)S(1)}, s32[264,128]{1,0:T(8,128)S(1)}, u32[]{:S(2)}, u32[]{:S(2)}) %collective-permute-start.15) | collective-permute-done | bytes 135200 | tf_op jit(solution)/shard_map/ppermute | solution.py:248
  35.1 0.9 %collective-permute-done.16.refs_0_ = s32[264,128]{1,0:T(8,128)S(1)} collective-permute-done((s32[264,128]{1,0:T(8,128)S(1)}, s32[264,128]{1,0:T(8,128)S(1)}, u32[]{:S(2)}, u32[]{:S(2)}) %collective-permute-start.16) | collective-permute-done | bytes 135200 | tf_op jit(solution)/shard_map/ppermute | solution.py:248
  36.0 2.8 %collective-permute-done.17.refs_1_ = s32[264,128]{1,0:T(8,128)S(1)} collective-permute-done((s32[264,128]{1,0:T(8,128)S(1)}, s32[264,128]{1,0:T(8,128)S(1)}, u32[]{:S(2)}, u32[]{:S(2)}) %collective-permute-start.17) | collective-permute-done | bytes 135200 | tf_op jit(solution)/shard_map/ppermute | solution.py:248
  38.8 1.0 %finish.1 = f32[2,256,256]{2,1,0:T(8,128)} custom-call(bf16[2,256,256]{2,1,0:T(8,128)(2,1)S(1)} %copy-done, f32[2,264,128]{2,1,0:T(8,128)S(1)} %add.1.own_ref, s32[264,128]{1,0:T(8,128)S(1)} %collective-permute-done.16.refs_0_, s32[264,128]{1,0:T(8,128)S(1)} %collective-permute-done.17.refs_1_), custom_call_target="tpu_custom_call" | custom-call | tf_op jit(solution)/shard_map/finish/pallas_call | solution.py:346
  (28 shorter events, 1.2 us)
Async XLA Ops:
  1.0 10.7 %collective-permute-start.1 = (bf16[528,128]{1,0:T(8,128)(2,1)S(1)}, bf16[528,128]{1,0:T(8,128)(2,1)S(1)}, u32[]{:S(2)}, u32[]{:S(2)}) collective-permute-start(bf16[528,128]{1,0:T(8,128)(2,1)S(1)} %fold.1.refs_0_), channel_id=1, source_target_pairs={{0,2},{1,3},{2,0},{3,1},{4,6},{5,7},{6,4},{7,5},{8,10},{9,11},{10,... | collective-permute-start | bytes 405512 | tf_op jit(solution)/shard_map/ppermute | solution.py:248
  5.1 6.8 %collective-permute-start.2 = (bf16[528,128]{1,0:T(8,128)(2,1)S(1)}, bf16[528,128]{1,0:T(8,128)(2,1)S(1)}, u32[]{:S(2)}, u32[]{:S(2)}) collective-permute-start(bf16[528,128]{1,0:T(8,128)(2,1)S(1)} %fold.1.refs_0_), channel_id=1, source_target_pairs={{0,1},{1,0},{2,3},{3,2},{4,5},{5,4},{6,7},{7,6},{8,9},{9,8},{10,11... | collective-permute-start | bytes 405512 | tf_op jit(solution)/shard_map/ppermute | solution.py:248
  6.7 5.2 %collective-permute-start = (bf16[528,128]{1,0:T(8,128)(2,1)S(1)}, bf16[528,128]{1,0:T(8,128)(2,1)S(1)}, u32[]{:S(2)}, u32[]{:S(2)}) collective-permute-start(bf16[528,128]{1,0:T(8,128)(2,1)S(1)} %fold.1.refs_0_), channel_id=1, source_target_pairs={{0,8},{4,12},{8,0},{12,4},{1,9},{5,13},{9,1},{13,5},{2,10},{6,14},... | collective-permute-start | bytes 405512 | tf_op jit(solution)/shard_map/ppermute | solution.py:251
  8.2 7.3 %collective-permute-start.7 = (bf16[528,128]{1,0:T(8,128)(2,1)S(1)}, bf16[528,128]{1,0:T(8,128)(2,1)S(1)}, u32[]{:S(2)}, u32[]{:S(2)}) collective-permute-start(bf16[528,128]{1,0:T(8,128)(2,1)S(1)} %fold.1.refs_0_), channel_id=1, source_target_pairs={{0,4},{4,0},{8,12},{12,8},{1,5},{5,1},{9,13},{13,9},{2,6},{6,2},{1... | collective-permute-start | bytes 405512 | tf_op jit(solution)/shard_map/ppermute | solution.py:308
  11.9 5.1 %collective-permute-start.3 = (bf16[528,128]{1,0:T(8,128)(2,1)S(1)}, bf16[528,128]{1,0:T(8,128)(2,1)S(1)}, u32[]{:S(2)}, u32[]{:S(2)}) collective-permute-start(bf16[528,128]{1,0:T(8,128)(2,1)S(1)} %gate.8.refs_2_), channel_id=1, source_target_pairs={{0,1},{1,0},{2,3},{3,2},{4,5},{5,4},{6,7},{7,6},{8,9},{9,8},{10,11... | collective-permute-start | bytes 405512 | tf_op jit(solution)/shard_map/ppermute | solution.py:248
  13.4 7.0 %collective-permute-start.8 = (bf16[528,128]{1,0:T(8,128)(2,1)S(1)}, bf16[528,128]{1,0:T(8,128)(2,1)S(1)}, u32[]{:S(2)}, u32[]{:S(2)}) collective-permute-start(bf16[528,128]{1,0:T(8,128)(2,1)S(1)} %collective-permute-done.2.refs_1_), channel_id=1, source_target_pairs={{0,4},{4,0},{8,12},{12,8},{1,5},{5,1},{9,13},{13,9},{2,6},{6,2},{1... | collective-permute-start | bytes 405512 | tf_op jit(solution)/shard_map/ppermute | solution.py:308
  13.4 7.1 %collective-permute-start.9 = (bf16[528,128]{1,0:T(8,128)(2,1)S(1)}, bf16[528,128]{1,0:T(8,128)(2,1)S(1)}, u32[]{:S(2)}, u32[]{:S(2)}) collective-permute-start(bf16[528,128]{1,0:T(8,128)(2,1)S(1)} %gate.8.refs_2_), channel_id=1, source_target_pairs={{0,4},{4,0},{8,12},{12,8},{1,5},{5,1},{9,13},{13,9},{2,6},{6,2},{1... | collective-permute-start | bytes 405512 | tf_op jit(solution)/shard_map/ppermute | solution.py:308
  13.9 7.1 %collective-permute-start.5 = (bf16[528,128]{1,0:T(8,128)(2,1)S(1)}, bf16[528,128]{1,0:T(8,128)(2,1)S(1)}, u32[]{:S(2)}, u32[]{:S(2)}) collective-permute-start(bf16[528,128]{1,0:T(8,128)(2,1)S(1)} %gate.8.refs_2_), channel_id=1, source_target_pairs={{0,8},{4,12},{8,0},{12,4},{1,9},{5,13},{9,1},{13,5},{2,10},{6,14},... | collective-permute-start | bytes 405512 | tf_op jit(solution)/shard_map/ppermute | solution.py:251
  15.5 5.6 %collective-permute-start.4 = (bf16[528,128]{1,0:T(8,128)(2,1)S(1)}, bf16[528,128]{1,0:T(8,128)(2,1)S(1)}, u32[]{:S(2)}, u32[]{:S(2)}) collective-permute-start(bf16[528,128]{1,0:T(8,128)(2,1)S(1)} %collective-permute-done.refs_2_.piece_ref), channel_id=1, source_target_pairs={{0,1},{1,0},{2,3},{3,2},{4,5},{5,4},{6,7},{7,6},{8,9},{9,8},{10,11... | collective-permute-start | bytes 405512 | tf_op jit(solution)/shard_map/ppermute | solution.py:248
  17.0 5.3 %collective-permute-start.6 = (bf16[528,128]{1,0:T(8,128)(2,1)S(1)}, bf16[528,128]{1,0:T(8,128)(2,1)S(1)}, u32[]{:S(2)}, u32[]{:S(2)}) collective-permute-start(bf16[528,128]{1,0:T(8,128)(2,1)S(1)} %collective-permute-done.3.refs_0_.refs_3_), channel_id=1, source_target_pairs={{0,8},{4,12},{8,0},{12,4},{1,9},{5,13},{9,1},{13,5},{2,10},{6,14},... | collective-permute-start | bytes 405512 | tf_op jit(solution)/shard_map/ppermute | solution.py:251
  20.4 2.1 %collective-permute-start.11 = (bf16[528,128]{1,0:T(8,128)(2,1)S(1)}, bf16[528,128]{1,0:T(8,128)(2,1)S(1)}, u32[]{:S(2)}, u32[]{:S(2)}) collective-permute-start(bf16[528,128]{1,0:T(8,128)(2,1)S(1)} %get-tuple-element.14.refs_4_), channel_id=1, source_target_pairs={{0,4},{4,0},{8,12},{12,8},{1,5},{5,1},{9,13},{13,9},{2,6},{6,2},{1... | collective-permute-start | bytes 405512 | tf_op jit(solution)/shard_map/ppermute | solution.py:308
  20.5 1.9 %collective-permute-start.10 = (bf16[528,128]{1,0:T(8,128)(2,1)S(1)}, bf16[528,128]{1,0:T(8,128)(2,1)S(1)}, u32[]{:S(2)}, u32[]{:S(2)}) collective-permute-start(bf16[528,128]{1,0:T(8,128)(2,1)S(1)} %collective-permute-done.3.refs_0_.refs_3_), channel_id=1, source_target_pairs={{0,4},{4,0},{8,12},{12,8},{1,5},{5,1},{9,13},{13,9},{2,6},{6,2},{1... | collective-permute-start | bytes 405512 | tf_op jit(solution)/shard_map/ppermute | solution.py:308
  21.0 1.4 %collective-permute-start.13 = (bf16[528,128]{1,0:T(8,128)(2,1)S(1)}, bf16[528,128]{1,0:T(8,128)(2,1)S(1)}, u32[]{:S(2)}, u32[]{:S(2)}) collective-permute-start(bf16[528,128]{1,0:T(8,128)(2,1)S(1)} %collective-permute-done.5.refs_6_), channel_id=1, source_target_pairs={{0,4},{4,0},{8,12},{12,8},{1,5},{5,1},{9,13},{13,9},{2,6},{6,2},{1... | collective-permute-start | bytes 405512 | tf_op jit(solution)/shard_map/ppermute | solution.py:308
  21.1 1.5 %collective-permute-start.12 = (bf16[528,128]{1,0:T(8,128)(2,1)S(1)}, bf16[528,128]{1,0:T(8,128)(2,1)S(1)}, u32[]{:S(2)}, u32[]{:S(2)}) collective-permute-start(bf16[528,128]{1,0:T(8,128)(2,1)S(1)} %collective-permute-done.4.refs_5_), channel_id=1, source_target_pairs={{0,4},{4,0},{8,12},{12,8},{1,5},{5,1},{9,13},{13,9},{2,6},{6,2},{1... | collective-permute-start | bytes 405512 | tf_op jit(solution)/shard_map/ppermute | solution.py:308
  22.3 1.4 %collective-permute-start.14 = (bf16[528,128]{1,0:T(8,128)(2,1)S(1)}, bf16[528,128]{1,0:T(8,128)(2,1)S(1)}, u32[]{:S(2)}, u32[]{:S(2)}) collective-permute-start(bf16[528,128]{1,0:T(8,128)(2,1)S(1)} %collective-permute-done.6.refs_7_), channel_id=1, source_target_pairs={{0,4},{4,0},{8,12},{12,8},{1,5},{5,1},{9,13},{13,9},{2,6},{6,2},{1... | collective-permute-start | bytes 405512 | tf_op jit(solution)/shard_map/ppermute | solution.py:308
  24.6 10.3 %collective-permute-start.15 = (s32[264,128]{1,0:T(8,128)S(1)}, s32[264,128]{1,0:T(8,128)S(1)}, u32[]{:S(2)}, u32[]{:S(2)}) collective-permute-start(s32[264,128]{1,0:T(8,128)S(1)} %get-tuple-element.16), channel_id=1, source_target_pairs={{0,2},{1,3},{2,0},{3,1},{4,6},{5,7},{6,4},{7,5},{8,10},{9,11},{10,... | collective-permute-start | bytes 405512 | tf_op jit(solution)/shard_map/ppermute | solution.py:248
  28.4 7.6 %collective-permute-start.16 = (s32[264,128]{1,0:T(8,128)S(1)}, s32[264,128]{1,0:T(8,128)S(1)}, u32[]{:S(2)}, u32[]{:S(2)}) collective-permute-start(s32[264,128]{1,0:T(8,128)S(1)} %get-tuple-element.17), channel_id=1, source_target_pairs={{0,1},{1,0},{2,3},{3,2},{4,5},{5,4},{6,7},{7,6},{8,9},{9,8},{10,11... | collective-permute-start | bytes 405512 | tf_op jit(solution)/shard_map/ppermute | solution.py:248
  30.9 7.9 %collective-permute-start.17 = (s32[264,128]{1,0:T(8,128)S(1)}, s32[264,128]{1,0:T(8,128)S(1)}, u32[]{:S(2)}, u32[]{:S(2)}) collective-permute-start(s32[264,128]{1,0:T(8,128)S(1)} %get-tuple-element.18), channel_id=1, source_target_pairs={{0,3},{1,2},{2,1},{3,0},{4,7},{5,6},{6,5},{7,4},{8,11},{9,10},{10,... | collective-permute-start | bytes 405512 | tf_op jit(solution)/shard_map/ppermute | solution.py:248
  31.6 7.2 %copy-start = (bf16[2,256,256]{2,1,0:T(8,128)(2,1)S(1)}, bf16[2,256,256]{2,1,0:T(8,128)(2,1)}, u32[]{:S(2)}) copy-start(bf16[2,256,256]{2,1,0:T(8,128)(2,1)} %core_ref.1) | copy-start | bytes 786436

commit v21 on v20

--- a/solution.py
+++ b/solution.py
@@ -97,6 +97,11 @@
     refs[-1][...] = piece_ref[...]
 
 
+def pair_kernel(one_ref, two_ref, out_ref):
+    out_ref[pl.ds(0, one_ref.shape[0])] = one_ref[...]
+    out_ref[pl.ds(one_ref.shape[0], two_ref.shape[0])] = two_ref[...]
+
+
 def stage_kernel(nbr_ref, esp_ref, piece_ref, *refs):
     nbr_out, esp_out, piece_out, sems = refs[-4:]
     copies = [
@@ -110,12 +115,15 @@
         copy.wait()
 
 
-def couple_kernel(groups, lanes, mono_dev, units, nbr_ref, esp_ref, *refs):
+def couple_kernel(groups, lanes, mono_dev, units, places, nbr_ref, esp_ref, *refs):
     outs = refs[len(refs) - len(units) :]
     if len(refs) > len(units) + 1:
         pieces, store = refs[: -1 - len(units)], refs[-1 - len(units)]
-        for i, piece in enumerate(pieces):
-            store[i] = piece[...]
+        at, rows = 0, store.shape[1]
+        for piece in pieces:
+            for part in range(piece.shape[0] // rows):
+                store[places[at]] = piece[pl.ds(part * rows, rows)]
+                at += 1
     else:
         store = refs[0]
     my_group = lax.axis_index("gddi")
@@ -305,7 +313,19 @@
     )
     keys = [(y, k) for y in range(rows_y) for k in range(lanes)]
     mine = [near[key] for key in keys]
-    pieces = mine + [lax.ppermute(piece, "gddi", xor_pairs(groups, 1)) for piece in mine]
+    pair = [1, top] if top > 1 else [0, top]
+    both = pl.pallas_call(
+        pair_kernel,
+        out_shape=pltpu.VMEM((2 * rows, half), density.dtype),
+        in_specs=[IN_VMEM] * 2,
+        out_specs=IN_VMEM,
+        compiler_params=small,
+        name="pair",
+    )(*[mine[i] for i in pair])
+    both = lax.ppermute(both, "gddi", xor_pairs(groups, 1))
+    single = [i for i in range(len(mine)) if i not in pair]
+    pieces = mine + [both] + [lax.ppermute(mine[i], "gddi", xor_pairs(groups, 1)) for i in single]
+    places = list(range(len(mine))) + [len(mine) + i for i in pair + single]
 
     plain = pltpu.VMEM((mono_dev, basis + 8, half), jnp.float32)
     coded = pltpu.VMEM((mono_dev * half + round_up(2 * mono_dev, 8), half), jnp.int32)
@@ -316,7 +336,7 @@
 
     def couple(units, name, pieces, fill=False):
         return pl.pallas_call(
-            functools.partial(couple_kernel, groups, lanes, mono_dev, units),
+            functools.partial(couple_kernel, groups, lanes, mono_dev, units, places),
             out_shape=[store] * fill + [coded if is_coded else plain for _, is_coded in units],
             in_specs=[IN_SMEM] + [IN_VMEM] * (1 + len(pieces)),
             out_specs=[IN_VMEM] * (fill + len(units)),

time: 40 us -> 41.7 us (1.042)
  waiting for transfers between devices: 13.7 us -> 17.4 us
  starting transfers between devices: 19.3 us -> 17.2 us
    ppermute x3, waiting for transfers between devices: 0.81 us -> 3.5 us  [along_y(): return lax.ppermute(piece, 'gddi', xor_pairs(groups, 2 * y))]
    ppermute x3, starting transfers between devices: 4.85 us -> 3.55 us  [along_y(): return lax.ppermute(piece, 'gddi', xor_pairs(groups, 2 * y))]
    ppermute x7, waiting for transfers between devices: 11.6 us -> 12.6 us  [along_z(): return lax.ppermute(piece, 'intra', xor_pairs(lanes, bit))]
    ppermute x8 -> x7, starting transfers between devices: 1.59 us -> 1.1 us  [the longest x6 0.59 us: local(): lax.ppermute(mine[i], 'gddi', xor_pairs(groups, 1))]
    ppermute x8 -> x7, waiting for transfers between devices: 1.36 us -> 1.34 us  [the longest x6 1.33 us: local(): lax.ppermute(mine[i], 'gddi', xor_pairs(groups, 1))]
  transfers between devices with their start and end apart: 18 -> 17, of which waited for: 9 -> 10; matrix products, arithmetic and copies ran while one was open for 0% -> 0% of each run, Pallas kernels for 9% -> 9%
where the time goes in v21:
time: 41.7 us; the launch traced here: 41.5 us
  waiting for transfers between devices  17.4 us (42%)
  starting transfers between devices  17.2 us (41%)
  Pallas kernels  6.68 us (16%)
    ppermute x7, starting transfers between devices, along_z(): return lax.ppermute(piece, 'intra', xor_pairs(lanes, bit))  12.6 us
    ppermute x7, waiting for transfers between devices, along_z(): return lax.ppermute(piece, 'intra', xor_pairs(lanes, bit))  12.6 us
    ppermute x3, starting transfers between devices, along_y(): return lax.ppermute(piece, 'gddi', xor_pairs(groups, 2 * y))  3.55 us
    ppermute x3, waiting for transfers between devices, along_y(): return lax.ppermute(piece, 'gddi', xor_pairs(groups, 2 * y))  3.5 us
    pallas_call x3, Pallas kernels, couple(): pl.pallas_call(functools.partial(couple_kernel, groups, lanes, mono_dev,...  2.92 us
    pallas_call x1, Pallas kernels, local(): pl.pallas_call(stage_kernel, out_shape=[pltpu.SMEM((nbr.shape[1], nbr.sha...  1.62 us
    ppermute x6, waiting for transfers between devices, local(): lax.ppermute(mine[i], 'gddi', xor_pairs(groups, 1))  1.33 us
    pallas_call x1, Pallas kernels, local(): pl.pallas_call(fold_kernel, out_shape=pltpu.VMEM((rows, half), density.dt...  1 us
  transfers between devices with their start and end apart: 17, of which 10 were waited for; matrix products, arithmetic and copies ran while one was open for 0% of the time, Pallas kernels for 9%

profile of v21, /device:TPU:0, one launch (start us, length us, event | category | flops | bytes accessed | tf_op | source)
XLA Modules:
  0.0 41.5 jit_solution(3343707919014347167)
XLA Ops:
  0.0 1.0 %fold.1.refs_0_ = bf16[528,128]{1,0:T(8,128)(2,1)S(1)} custom-call(bf16[2,256,256]{2,1,0:T(8,128)(2,1)} %dens_ref.1), custom_call_target="tpu_custom_call" | custom-call | tf_op jit(solution)/shard_map/fold/pallas_call | solution.py:247
  1.0 4.1 %collective-permute-start.1 = (bf16[528,128]{1,0:T(8,128)(2,1)S(1)}, bf16[528,128]{1,0:T(8,128)(2,1)S(1)}, u32[]{:S(2)}, u32[]{:S(2)}) collective-permute-start(bf16[528,128]{1,0:T(8,128)(2,1)S(1)} %fold.1.refs_0_), channel_id=1, source_target_pairs={{0,2},{1,3},{2,0},{3,1},{4,6},{5,7},{6,4},{7,5},{8,10},{9,11},{10,... | collective-permute-start | bytes 405512 | tf_op jit(solution)/shard_map/ppermute | solution.py:256
  5.1 1.6 %collective-permute-start.2 = (bf16[528,128]{1,0:T(8,128)(2,1)S(1)}, bf16[528,128]{1,0:T(8,128)(2,1)S(1)}, u32[]{:S(2)}, u32[]{:S(2)}) collective-permute-start(bf16[528,128]{1,0:T(8,128)(2,1)S(1)} %fold.1.refs_0_), channel_id=1, source_target_pairs={{0,1},{1,0},{2,3},{3,2},{4,5},{5,4},{6,7},{7,6},{8,9},{9,8},{10,11... | collective-permute-start | bytes 405512 | tf_op jit(solution)/shard_map/ppermute | solution.py:256
  6.7 1.5 %collective-permute-start = (bf16[528,128]{1,0:T(8,128)(2,1)S(1)}, bf16[528,128]{1,0:T(8,128)(2,1)S(1)}, u32[]{:S(2)}, u32[]{:S(2)}) collective-permute-start(bf16[528,128]{1,0:T(8,128)(2,1)S(1)} %fold.1.refs_0_), channel_id=1, source_target_pairs={{0,8},{4,12},{8,0},{12,4},{1,9},{5,13},{9,1},{13,5},{2,10},{6,14},... | collective-permute-start | bytes 405512 | tf_op jit(solution)/shard_map/ppermute | solution.py:259
  8.2 3.5 %collective-permute-done.1.piece_ref = bf16[528,128]{1,0:T(8,128)(2,1)S(1)} collective-permute-done((bf16[528,128]{1,0:T(8,128)(2,1)S(1)}, bf16[528,128]{1,0:T(8,128)(2,1)S(1)}, u32[]{:S(2)}, u32[]{:S(2)}) %collective-permute-start.1) | collective-permute-done | bytes 135200 | tf_op jit(solution)/shard_map/ppermute | solution.py:256
  11.9 1.6 %collective-permute-start.5 = (bf16[528,128]{1,0:T(8,128)(2,1)S(1)}, bf16[528,128]{1,0:T(8,128)(2,1)S(1)}, u32[]{:S(2)}, u32[]{:S(2)}) collective-permute-start(bf16[528,128]{1,0:T(8,128)(2,1)S(1)} %gate.8.two_ref.refs_2_), channel_id=1, source_target_pairs={{0,8},{4,12},{8,0},{12,4},{1,9},{5,13},{9,1},{13,5},{2,10},{6,14},... | collective-permute-start | bytes 405512 | tf_op jit(solution)/shard_map/ppermute | solution.py:259
  13.5 1.4 %collective-permute-start.3 = (bf16[528,128]{1,0:T(8,128)(2,1)S(1)}, bf16[528,128]{1,0:T(8,128)(2,1)S(1)}, u32[]{:S(2)}, u32[]{:S(2)}) collective-permute-start(bf16[528,128]{1,0:T(8,128)(2,1)S(1)} %gate.8.two_ref.refs_2_), channel_id=1, source_target_pairs={{0,1},{1,0},{2,3},{3,2},{4,5},{5,4},{6,7},{7,6},{8,9},{9,8},{10,11... | collective-permute-start | bytes 405512 | tf_op jit(solution)/shard_map/ppermute | solution.py:256
  14.9 0.6 %collective-permute-start.4 = (bf16[528,128]{1,0:T(8,128)(2,1)S(1)}, bf16[528,128]{1,0:T(8,128)(2,1)S(1)}, u32[]{:S(2)}, u32[]{:S(2)}) collective-permute-start(bf16[528,128]{1,0:T(8,128)(2,1)S(1)} %collective-permute-done.refs_2_.piece_ref), channel_id=1, source_target_pairs={{0,1},{1,0},{2,3},{3,2},{4,5},{5,4},{6,7},{7,6},{8,9},{9,8},{10,11... | collective-permute-start | bytes 405512 | tf_op jit(solution)/shard_map/ppermute | solution.py:256
  15.6 1.4 %collective-permute-done.5.refs_6_ = bf16[528,128]{1,0:T(8,128)(2,1)S(1)} collective-permute-done((bf16[528,128]{1,0:T(8,128)(2,1)S(1)}, bf16[528,128]{1,0:T(8,128)(2,1)S(1)}, u32[]{:S(2)}, u32[]{:S(2)}) %collective-permute-start.5) | collective-permute-done | bytes 135200 | tf_op jit(solution)/shard_map/ppermute | solution.py:259
  17.0 0.5 %collective-permute-start.7 = (bf16[1056,128]{1,0:T(8,128)(2,1)S(1)}, bf16[1056,128]{1,0:T(8,128)(2,1)S(1)}, u32[]{:S(2)}, u32[]{:S(2)}) collective-permute-start(bf16[1056,128]{1,0:T(8,128)(2,1)S(1)} %pair.1), channel_id=1, source_target_pairs={{0,4},{4,0},{8,12},{12,8},{1,5},{5,1},{9,13},{13,9},{2,6},{6,2},{1... | collective-permute-start | bytes 811016 | tf_op jit(solution)/shard_map/ppermute | solution.py:325
  17.5 1.6 %collective-permute-done.3.refs_0_.refs_3_ = bf16[528,128]{1,0:T(8,128)(2,1)S(1)} collective-permute-done((bf16[528,128]{1,0:T(8,128)(2,1)S(1)}, bf16[528,128]{1,0:T(8,128)(2,1)S(1)}, u32[]{:S(2)}, u32[]{:S(2)}) %collective-permute-start.3) | collective-permute-done | bytes 135200 | tf_op jit(solution)/shard_map/ppermute | solution.py:256
  19.1 0.4 collective-permute-start.6
  19.4 1.6 %stage.1 = (s32[8,32]{1,0:T(8,128)S(4)}, bf16[8,2,256,256]{3,2,1,0:T(8,128)(2,1)S(1)}, bf16[528,128]{1,0:T(8,128)(2,1)S(1)}) custom-call(s32[8,32]{1,0:T(8,128)} %bitcast.1, bf16[8,2,256,256]{3,2,1,0:T(8,128)(2,1)} %esp_ref.1, bf16[528,128]{1,0:T(8,128)(2,1)S(1)} %collective-permute-done.refs_2_.piece_ref, ...), custom_call_target="tpu_custom_call" | custom-call | tf_op jit(solution)/shard_map/stage/pallas_call | solution.py:296
  22.0 2.1 %collective-permute-done.6.refs_7_ = bf16[528,128]{1,0:T(8,128)(2,1)S(1)} collective-permute-done((bf16[528,128]{1,0:T(8,128)(2,1)S(1)}, bf16[528,128]{1,0:T(8,128)(2,1)S(1)}, u32[]{:S(2)}, u32[]{:S(2)}) %collective-permute-start.6) | collective-permute-done | bytes 135200 | tf_op jit(solution)/shard_map/ppermute | solution.py:259
  24.1 1.3 %collective-permute-done.13.refs_14_ = bf16[528,128]{1,0:T(8,128)(2,1)S(1)} collective-permute-done((bf16[528,128]{1,0:T(8,128)(2,1)S(1)}, bf16[528,128]{1,0:T(8,128)(2,1)S(1)}, u32[]{:S(2)}, u32[]{:S(2)}) %collective-permute-start.13) | collective-permute-done | bytes 135200 | tf_op jit(solution)/shard_map/ppermute | solution.py:327
  25.4 0.9 %couple_first.1 = (bf16[16,528,128]{2,1,0:T(8,128)(2,1)S(1)}, s32[264,128]{1,0:T(8,128)S(1)}) custom-call(s32[8,32]{1,0:T(8,128)S(4)} %get-tuple-element.12.nbr_ref, bf16[8,2,256,256]{3,2,1,0:T(8,128)(2,1)S(1)} %get-tuple-element.13.esp_ref, bf16[528,128]{1,0:T(8,128)(2,1)S(1)} %fold.1.refs_0_, bf16[528,128]{1,0:T(8,128)(2,1)S(1)} %collective-permute-done.2.refs_1_.one_ref, ...), custom_call_target="tpu_custom_call" | custom-call | tf_op jit(solution)/shard_map/couple_first/pallas_call | solution.py:338
  26.3 2.3 %collective-permute-start.14 = (s32[264,128]{1,0:T(8,128)S(1)}, s32[264,128]{1,0:T(8,128)S(1)}, u32[]{:S(2)}, u32[]{:S(2)}) collective-permute-start(s32[264,128]{1,0:T(8,128)S(1)} %get-tuple-element.16), channel_id=1, source_target_pairs={{0,2},{1,3},{2,0},{3,1},{4,6},{5,7},{6,4},{7,5},{8,10},{9,11},{10,... | collective-permute-start | bytes 405512 | tf_op jit(solution)/shard_map/ppermute | solution.py:256
  28.7 1.3 %couple_rest.1 = (s32[264,128]{1,0:T(8,128)S(1)}, s32[264,128]{1,0:T(8,128)S(1)}) custom-call(s32[8,32]{1,0:T(8,128)S(4)} %get-tuple-element.12.nbr_ref, bf16[8,2,256,256]{3,2,1,0:T(8,128)(2,1)S(1)} %get-tuple-element.13.esp_ref, bf16[16,528,128]{2,1,0:T(8,128)(2,1)S(1)} %get-tuple-element.15.refs_0_), custom_call_target="tpu_custom_call" | custom-call | tf_op jit(solution)/shard_map/couple_rest/pallas_call | solution.py:338
  30.0 2.5 %collective-permute-start.15 = (s32[264,128]{1,0:T(8,128)S(1)}, s32[264,128]{1,0:T(8,128)S(1)}, u32[]{:S(2)}, u32[]{:S(2)}) collective-permute-start(s32[264,128]{1,0:T(8,128)S(1)} %get-tuple-element.17), channel_id=1, source_target_pairs={{0,1},{1,0},{2,3},{3,2},{4,5},{5,4},{6,7},{7,6},{8,9},{9,8},{10,11... | collective-permute-start | bytes 405512 | tf_op jit(solution)/shard_map/ppermute | solution.py:256
  32.6 0.7 %couple_own.1.plain_ref = f32[2,264,128]{2,1,0:T(8,128)S(1)} custom-call(s32[8,32]{1,0:T(8,128)S(4)} %get-tuple-element.12.nbr_ref, bf16[8,2,256,256]{3,2,1,0:T(8,128)(2,1)S(1)} %get-tuple-element.13.esp_ref, bf16[16,528,128]{2,1,0:T(8,128)(2,1)S(1)} %get-tuple-element.15.refs_0_), custom_call_target="tpu_custom_call" | custom-call | tf_op jit(solution)/shard_map/couple_own/pallas_call | solution.py:338
  33.3 3.4 %collective-permute-done.14.piece_ref = s32[264,128]{1,0:T(8,128)S(1)} collective-permute-done((s32[264,128]{1,0:T(8,128)S(1)}, s32[264,128]{1,0:T(8,128)S(1)}, u32[]{:S(2)}, u32[]{:S(2)}) %collective-permute-start.14) | collective-permute-done | bytes 135200 | tf_op jit(solution)/shard_map/ppermute | solution.py:256
  36.8 1.2 %collective-permute-done.15.refs_0_ = s32[264,128]{1,0:T(8,128)S(1)} collective-permute-done((s32[264,128]{1,0:T(8,128)S(1)}, s32[264,128]{1,0:T(8,128)S(1)}, u32[]{:S(2)}, u32[]{:S(2)}) %collective-permute-start.15) | collective-permute-done | bytes 135200 | tf_op jit(solution)/shard_map/ppermute | solution.py:256
  38.0 2.5 %collective-permute-done.16.refs_1_ = s32[264,128]{1,0:T(8,128)S(1)} collective-permute-done((s32[264,128]{1,0:T(8,128)S(1)}, s32[264,128]{1,0:T(8,128)S(1)}, u32[]{:S(2)}, u32[]{:S(2)}) %collective-permute-start.16) | collective-permute-done | bytes 135200 | tf_op jit(solution)/shard_map/ppermute | solution.py:256
  40.5 1.0 %finish.1 = f32[2,256,256]{2,1,0:T(8,128)} custom-call(bf16[2,256,256]{2,1,0:T(8,128)(2,1)S(1)} %copy-done, f32[2,264,128]{2,1,0:T(8,128)S(1)} %add.1.own_ref, s32[264,128]{1,0:T(8,128)S(1)} %collective-permute-done.15.refs_0_, s32[264,128]{1,0:T(8,128)S(1)} %collective-permute-done.16.refs_1_), custom_call_target="tpu_custom_call" | custom-call | tf_op jit(solution)/shard_map/finish/pallas_call | solution.py:366
  (27 shorter events, 1.2 us)
Async XLA Ops:
  1.0 10.7 %collective-permute-start.1 = (bf16[528,128]{1,0:T(8,128)(2,1)S(1)}, bf16[528,128]{1,0:T(8,128)(2,1)S(1)}, u32[]{:S(2)}, u32[]{:S(2)}) collective-permute-start(bf16[528,128]{1,0:T(8,128)(2,1)S(1)} %fold.1.refs_0_), channel_id=1, source_target_pairs={{0,2},{1,3},{2,0},{3,1},{4,6},{5,7},{6,4},{7,5},{8,10},{9,11},{10,... | collective-permute-start | bytes 405512 | tf_op jit(solution)/shard_map/ppermute | solution.py:256
  5.1 6.8 %collective-permute-start.2 = (bf16[528,128]{1,0:T(8,128)(2,1)S(1)}, bf16[528,128]{1,0:T(8,128)(2,1)S(1)}, u32[]{:S(2)}, u32[]{:S(2)}) collective-permute-start(bf16[528,128]{1,0:T(8,128)(2,1)S(1)} %fold.1.refs_0_), channel_id=1, source_target_pairs={{0,1},{1,0},{2,3},{3,2},{4,5},{5,4},{6,7},{7,6},{8,9},{9,8},{10,11... | collective-permute-start | bytes 405512 | tf_op jit(solution)/shard_map/ppermute | solution.py:256
  6.7 5.2 %collective-permute-start = (bf16[528,128]{1,0:T(8,128)(2,1)S(1)}, bf16[528,128]{1,0:T(8,128)(2,1)S(1)}, u32[]{:S(2)}, u32[]{:S(2)}) collective-permute-start(bf16[528,128]{1,0:T(8,128)(2,1)S(1)} %fold.1.refs_0_), channel_id=1, source_target_pairs={{0,8},{4,12},{8,0},{12,4},{1,9},{5,13},{9,1},{13,5},{2,10},{6,14},... | collective-permute-start | bytes 405512 | tf_op jit(solution)/shard_map/ppermute | solution.py:259
  11.9 5.1 %collective-permute-start.5 = (bf16[528,128]{1,0:T(8,128)(2,1)S(1)}, bf16[528,128]{1,0:T(8,128)(2,1)S(1)}, u32[]{:S(2)}, u32[]{:S(2)}) collective-permute-start(bf16[528,128]{1,0:T(8,128)(2,1)S(1)} %gate.8.two_ref.refs_2_), channel_id=1, source_target_pairs={{0,8},{4,12},{8,0},{12,4},{1,9},{5,13},{9,1},{13,5},{2,10},{6,14},... | collective-permute-start | bytes 405512 | tf_op jit(solution)/shard_map/ppermute | solution.py:259
  13.5 5.5 %collective-permute-start.3 = (bf16[528,128]{1,0:T(8,128)(2,1)S(1)}, bf16[528,128]{1,0:T(8,128)(2,1)S(1)}, u32[]{:S(2)}, u32[]{:S(2)}) collective-permute-start(bf16[528,128]{1,0:T(8,128)(2,1)S(1)} %gate.8.two_ref.refs_2_), channel_id=1, source_target_pairs={{0,1},{1,0},{2,3},{3,2},{4,5},{5,4},{6,7},{7,6},{8,9},{9,8},{10,11... | collective-permute-start | bytes 405512 | tf_op jit(solution)/shard_map/ppermute | solution.py:256
  14.9 6.1 %collective-permute-start.8 = (bf16[528,128]{1,0:T(8,128)(2,1)S(1)}, bf16[528,128]{1,0:T(8,128)(2,1)S(1)}, u32[]{:S(2)}, u32[]{:S(2)}) collective-permute-start(bf16[528,128]{1,0:T(8,128)(2,1)S(1)} %fold.1.refs_0_), channel_id=1, source_target_pairs={{0,4},{4,0},{8,12},{12,8},{1,5},{5,1},{9,13},{13,9},{2,6},{6,2},{1... | collective-permute-start | bytes 405512 | tf_op jit(solution)/shard_map/ppermute | solution.py:327
  14.9 6.5 %collective-permute-start.4 = (bf16[528,128]{1,0:T(8,128)(2,1)S(1)}, bf16[528,128]{1,0:T(8,128)(2,1)S(1)}, u32[]{:S(2)}, u32[]{:S(2)}) collective-permute-start(bf16[528,128]{1,0:T(8,128)(2,1)S(1)} %collective-permute-done.refs_2_.piece_ref), channel_id=1, source_target_pairs={{0,1},{1,0},{2,3},{3,2},{4,5},{5,4},{6,7},{7,6},{8,9},{9,8},{10,11... | collective-permute-start | bytes 405512 | tf_op jit(solution)/shard_map/ppermute | solution.py:256
  17.0 4.7 %collective-permute-start.12 = (bf16[528,128]{1,0:T(8,128)(2,1)S(1)}, bf16[528,128]{1,0:T(8,128)(2,1)S(1)}, u32[]{:S(2)}, u32[]{:S(2)}) collective-permute-start(bf16[528,128]{1,0:T(8,128)(2,1)S(1)} %collective-permute-done.5.refs_6_), channel_id=1, source_target_pairs={{0,4},{4,0},{8,12},{12,8},{1,5},{5,1},{9,13},{13,9},{2,6},{6,2},{1... | collective-permute-start | bytes 405512 | tf_op jit(solution)/shard_map/ppermute | solution.py:327
  17.0 7.1 %collective-permute-start.7 = (bf16[1056,128]{1,0:T(8,128)(2,1)S(1)}, bf16[1056,128]{1,0:T(8,128)(2,1)S(1)}, u32[]{:S(2)}, u32[]{:S(2)}) collective-permute-start(bf16[1056,128]{1,0:T(8,128)(2,1)S(1)} %pair.1), channel_id=1, source_target_pairs={{0,4},{4,0},{8,12},{12,8},{1,5},{5,1},{9,13},{13,9},{2,6},{6,2},{1... | collective-permute-start | bytes 811016 | tf_op jit(solution)/shard_map/ppermute | solution.py:325
  19.1 5.0 %collective-permute-start.6 = (bf16[528,128]{1,0:T(8,128)(2,1)S(1)}, bf16[528,128]{1,0:T(8,128)(2,1)S(1)}, u32[]{:S(2)}, u32[]{:S(2)}) collective-permute-start(bf16[528,128]{1,0:T(8,128)(2,1)S(1)} %collective-permute-done.3.refs_0_.refs_3_), channel_id=1, source_target_pairs={{0,8},{4,12},{8,0},{12,4},{1,9},{5,13},{9,1},{13,5},{2,10},{6,14},... | collective-permute-start | bytes 405512 | tf_op jit(solution)/shard_map/ppermute | solution.py:259
  21.1 3.0 %collective-permute-start.9 = (bf16[528,128]{1,0:T(8,128)(2,1)S(1)}, bf16[528,128]{1,0:T(8,128)(2,1)S(1)}, u32[]{:S(2)}, u32[]{:S(2)}) collective-permute-start(bf16[528,128]{1,0:T(8,128)(2,1)S(1)} %collective-permute-done.3.refs_0_.refs_3_), channel_id=1, source_target_pairs={{0,4},{4,0},{8,12},{12,8},{1,5},{5,1},{9,13},{13,9},{2,6},{6,2},{1... | collective-permute-start | bytes 405512 | tf_op jit(solution)/shard_map/ppermute | solution.py:327
  21.4 2.6 %collective-permute-start.11 = (bf16[528,128]{1,0:T(8,128)(2,1)S(1)}, bf16[528,128]{1,0:T(8,128)(2,1)S(1)}, u32[]{:S(2)}, u32[]{:S(2)}) collective-permute-start(bf16[528,128]{1,0:T(8,128)(2,1)S(1)} %collective-permute-done.4.refs_5_), channel_id=1, source_target_pairs={{0,4},{4,0},{8,12},{12,8},{1,5},{5,1},{9,13},{13,9},{2,6},{6,2},{1... | collective-permute-start | bytes 405512 | tf_op jit(solution)/shard_map/ppermute | solution.py:327
  21.7 2.4 %collective-permute-start.10 = (bf16[528,128]{1,0:T(8,128)(2,1)S(1)}, bf16[528,128]{1,0:T(8,128)(2,1)S(1)}, u32[]{:S(2)}, u32[]{:S(2)}) collective-permute-start(bf16[528,128]{1,0:T(8,128)(2,1)S(1)} %get-tuple-element.14.refs_4_), channel_id=1, source_target_pairs={{0,4},{4,0},{8,12},{12,8},{1,5},{5,1},{9,13},{13,9},{2,6},{6,2},{1... | collective-permute-start | bytes 405512 | tf_op jit(solution)/shard_map/ppermute | solution.py:327
  24.1 1.4 %collective-permute-start.13 = (bf16[528,128]{1,0:T(8,128)(2,1)S(1)}, bf16[528,128]{1,0:T(8,128)(2,1)S(1)}, u32[]{:S(2)}, u32[]{:S(2)}) collective-permute-start(bf16[528,128]{1,0:T(8,128)(2,1)S(1)} %collective-permute-done.6.refs_7_), channel_id=1, source_target_pairs={{0,4},{4,0},{8,12},{12,8},{1,5},{5,1},{9,13},{13,9},{2,6},{6,2},{1... | collective-permute-start | bytes 405512 | tf_op jit(solution)/shard_map/ppermute | solution.py:327
  26.3 10.3 %collective-permute-start.14 = (s32[264,128]{1,0:T(8,128)S(1)}, s32[264,128]{1,0:T(8,128)S(1)}, u32[]{:S(2)}, u32[]{:S(2)}) collective-permute-start(s32[264,128]{1,0:T(8,128)S(1)} %get-tuple-element.16), channel_id=1, source_target_pairs={{0,2},{1,3},{2,0},{3,1},{4,6},{5,7},{6,4},{7,5},{8,10},{9,11},{10,... | collective-permute-start | bytes 405512 | tf_op jit(solution)/shard_map/ppermute | solution.py:256
  30.0 8.0 %collective-permute-start.15 = (s32[264,128]{1,0:T(8,128)S(1)}, s32[264,128]{1,0:T(8,128)S(1)}, u32[]{:S(2)}, u32[]{:S(2)}) collective-permute-start(s32[264,128]{1,0:T(8,128)S(1)} %get-tuple-element.17), channel_id=1, source_target_pairs={{0,1},{1,0},{2,3},{3,2},{4,5},{5,4},{6,7},{7,6},{8,9},{9,8},{10,11... | collective-permute-start | bytes 405512 | tf_op jit(solution)/shard_map/ppermute | solution.py:256
  32.5 8.0 %collective-permute-start.16 = (s32[264,128]{1,0:T(8,128)S(1)}, s32[264,128]{1,0:T(8,128)S(1)}, u32[]{:S(2)}, u32[]{:S(2)}) collective-permute-start(s32[264,128]{1,0:T(8,128)S(1)} %get-tuple-element.18), channel_id=1, source_target_pairs={{0,3},{1,2},{2,1},{3,0},{4,7},{5,6},{6,5},{7,4},{8,11},{9,10},{10,... | collective-permute-start | bytes 405512 | tf_op jit(solution)/shard_map/ppermute | solution.py:256
  33.3 7.2 %copy-start = (bf16[2,256,256]{2,1,0:T(8,128)(2,1)S(1)}, bf16[2,256,256]{2,1,0:T(8,128)(2,1)}, u32[]{:S(2)}) copy-start(bf16[2,256,256]{2,1,0:T(8,128)(2,1)} %core_ref.1) | copy-start | bytes 786436

commit v22 on v20

--- a/solution.py
+++ b/solution.py
@@ -335,14 +335,16 @@
     for k, unit in zip(rest, units):
         beyond[k] = along_z(unit, k)
     (own,) = couple([(0, False)], "couple_own", [filled])
-    own = pl.pallas_call(
-        add_kernel,
-        out_shape=plain,
-        in_specs=[IN_VMEM] * 2,
-        out_specs=IN_VMEM,
-        compiler_params=small,
-        name="add",
-    )(own, beyond[top])
+    for k in [top] + [k for k in rest if k < top]:
+        own = pl.pallas_call(
+            add_kernel,
+            out_shape=plain,
+            in_specs=[IN_VMEM] * 2,
+            out_specs=IN_VMEM,
+            compiler_params=small,
+            name="add",
+        )(own, beyond[k])
+    rest = [k for k in rest if k > top]
     return pl.pallas_call(
         finish_kernel,
         out_shape=jax.ShapeDtypeStruct((mono_dev, basis, basis), jnp.float32),

time: 40 us -> 39.9 us (level)
  transfers between devices with their start and end apart: 18 -> 18, of which waited for: 9 -> 9; matrix products, arithmetic and copies ran while one was open for 0% -> 0% of each run, Pallas kernels for 9% -> 10%
where the time goes in v22:
time: 39.9 us; the launch traced here: 39.7 us
  starting transfers between devices  19.2 us (48%)
  waiting for transfers between devices  13.7 us (34%)
  Pallas kernels  6.69 us (17%)
    ppermute x7, starting transfers between devices, along_z(): return lax.ppermute(piece, 'intra', xor_pairs(lanes, bit))  12.8 us
    ppermute x7, waiting for transfers between devices, along_z(): return lax.ppermute(piece, 'intra', xor_pairs(lanes, bit))  11.5 us
    ppermute x3, starting transfers between devices, along_y(): return lax.ppermute(piece, 'gddi', xor_pairs(groups, 2 * y))  4.85 us
    pallas_call x3, Pallas kernels, couple(): pl.pallas_call(functools.partial(couple_kernel, groups, lanes, mono_dev,...  2.93 us
    pallas_call x1, Pallas kernels, local(): pl.pallas_call(stage_kernel, out_shape=[pltpu.SMEM((nbr.shape[1], nbr.sha...  1.62 us
    ppermute x8, starting transfers between devices, local(): lax.ppermute(piece, 'gddi', xor_pairs(groups, 1))  1.59 us
    ppermute x8, waiting for transfers between devices, local(): lax.ppermute(piece, 'gddi', xor_pairs(groups, 1))  1.36 us
    pallas_call x1, Pallas kernels, local(): pl.pallas_call(fold_kernel, out_shape=pltpu.VMEM((rows, half), density.dt...  1 us
  transfers between devices with their start and end apart: 18, of which 9 were waited for; matrix products, arithmetic and copies ran while one was open for 0% of the time, Pallas kernels for 10%

profile of v22, /device:TPU:0, one launch (start us, length us, event | category | flops | bytes accessed | tf_op | source)
XLA Modules:
  0.0 39.7 jit_solution(10067558770247350221)
XLA Ops:
  0.0 1.0 %fold.1.refs_0_ = bf16[528,128]{1,0:T(8,128)(2,1)S(1)} custom-call(bf16[2,256,256]{2,1,0:T(8,128)(2,1)} %dens_ref.1), custom_call_target="tpu_custom_call" | custom-call | tf_op jit(solution)/shard_map/fold/pallas_call | solution.py:239
  1.0 4.1 %collective-permute-start.1 = (bf16[528,128]{1,0:T(8,128)(2,1)S(1)}, bf16[528,128]{1,0:T(8,128)(2,1)S(1)}, u32[]{:S(2)}, u32[]{:S(2)}) collective-permute-start(bf16[528,128]{1,0:T(8,128)(2,1)S(1)} %fold.1.refs_0_), channel_id=1, source_target_pairs={{0,2},{1,3},{2,0},{3,1},{4,6},{5,7},{6,4},{7,5},{8,10},{9,11},{10,... | collective-permute-start | bytes 405512 | tf_op jit(solution)/shard_map/ppermute | solution.py:248
  5.1 1.6 %collective-permute-start.2 = (bf16[528,128]{1,0:T(8,128)(2,1)S(1)}, bf16[528,128]{1,0:T(8,128)(2,1)S(1)}, u32[]{:S(2)}, u32[]{:S(2)}) collective-permute-start(bf16[528,128]{1,0:T(8,128)(2,1)S(1)} %fold.1.refs_0_), channel_id=1, source_target_pairs={{0,1},{1,0},{2,3},{3,2},{4,5},{5,4},{6,7},{7,6},{8,9},{9,8},{10,11... | collective-permute-start | bytes 405512 | tf_op jit(solution)/shard_map/ppermute | solution.py:248
  6.7 1.5 %collective-permute-start = (bf16[528,128]{1,0:T(8,128)(2,1)S(1)}, bf16[528,128]{1,0:T(8,128)(2,1)S(1)}, u32[]{:S(2)}, u32[]{:S(2)}) collective-permute-start(bf16[528,128]{1,0:T(8,128)(2,1)S(1)} %fold.1.refs_0_), channel_id=1, source_target_pairs={{0,8},{4,12},{8,0},{12,4},{1,9},{5,13},{9,1},{13,5},{2,10},{6,14},... | collective-permute-start | bytes 405512 | tf_op jit(solution)/shard_map/ppermute | solution.py:251
  8.2 3.5 %collective-permute-done.1.piece_ref = bf16[528,128]{1,0:T(8,128)(2,1)S(1)} collective-permute-done((bf16[528,128]{1,0:T(8,128)(2,1)S(1)}, bf16[528,128]{1,0:T(8,128)(2,1)S(1)}, u32[]{:S(2)}, u32[]{:S(2)}) %collective-permute-start.1) | collective-permute-done | bytes 135200 | tf_op jit(solution)/shard_map/ppermute | solution.py:248
  11.9 1.5 %collective-permute-start.3 = (bf16[528,128]{1,0:T(8,128)(2,1)S(1)}, bf16[528,128]{1,0:T(8,128)(2,1)S(1)}, u32[]{:S(2)}, u32[]{:S(2)}) collective-permute-start(bf16[528,128]{1,0:T(8,128)(2,1)S(1)} %gate.8.refs_2_), channel_id=1, source_target_pairs={{0,1},{1,0},{2,3},{3,2},{4,5},{5,4},{6,7},{7,6},{8,9},{9,8},{10,11... | collective-permute-start | bytes 405512 | tf_op jit(solution)/shard_map/ppermute | solution.py:248
  13.4 0.5 %collective-permute-start.9 = (bf16[528,128]{1,0:T(8,128)(2,1)S(1)}, bf16[528,128]{1,0:T(8,128)(2,1)S(1)}, u32[]{:S(2)}, u32[]{:S(2)}) collective-permute-start(bf16[528,128]{1,0:T(8,128)(2,1)S(1)} %gate.8.refs_2_), channel_id=1, source_target_pairs={{0,4},{4,0},{8,12},{12,8},{1,5},{5,1},{9,13},{13,9},{2,6},{6,2},{1... | collective-permute-start | bytes 405512 | tf_op jit(solution)/shard_map/ppermute | solution.py:308
  13.9 1.5 %collective-permute-start.5 = (bf16[528,128]{1,0:T(8,128)(2,1)S(1)}, bf16[528,128]{1,0:T(8,128)(2,1)S(1)}, u32[]{:S(2)}, u32[]{:S(2)}) collective-permute-start(bf16[528,128]{1,0:T(8,128)(2,1)S(1)} %gate.8.refs_2_), channel_id=1, source_target_pairs={{0,8},{4,12},{8,0},{12,4},{1,9},{5,13},{9,1},{13,5},{2,10},{6,14},... | collective-permute-start | bytes 405512 | tf_op jit(solution)/shard_map/ppermute | solution.py:251
  15.5 0.6 %collective-permute-start.4 = (bf16[528,128]{1,0:T(8,128)(2,1)S(1)}, bf16[528,128]{1,0:T(8,128)(2,1)S(1)}, u32[]{:S(2)}, u32[]{:S(2)}) collective-permute-start(bf16[528,128]{1,0:T(8,128)(2,1)S(1)} %collective-permute-done.refs_2_.piece_ref), channel_id=1, source_target_pairs={{0,1},{1,0},{2,3},{3,2},{4,5},{5,4},{6,7},{7,6},{8,9},{9,8},{10,11... | collective-permute-start | bytes 405512 | tf_op jit(solution)/shard_map/ppermute | solution.py:248
  16.1 0.9 %collective-permute-done.3.refs_0_.refs_3_ = bf16[528,128]{1,0:T(8,128)(2,1)S(1)} collective-permute-done((bf16[528,128]{1,0:T(8,128)(2,1)S(1)}, bf16[528,128]{1,0:T(8,128)(2,1)S(1)}, u32[]{:S(2)}, u32[]{:S(2)}) %collective-permute-start.3) | collective-permute-done | bytes 135200 | tf_op jit(solution)/shard_map/ppermute | solution.py:248
  17.0 1.8 %collective-permute-start.6 = (bf16[528,128]{1,0:T(8,128)(2,1)S(1)}, bf16[528,128]{1,0:T(8,128)(2,1)S(1)}, u32[]{:S(2)}, u32[]{:S(2)}) collective-permute-start(bf16[528,128]{1,0:T(8,128)(2,1)S(1)} %collective-permute-done.3.refs_0_.refs_3_), channel_id=1, source_target_pairs={{0,8},{4,12},{8,0},{12,4},{1,9},{5,13},{9,1},{13,5},{2,10},{6,14},... | collective-permute-start | bytes 405512 | tf_op jit(solution)/shard_map/ppermute | solution.py:251
  18.8 1.6 %stage.1 = (s32[8,32]{1,0:T(8,128)S(4)}, bf16[8,2,256,256]{3,2,1,0:T(8,128)(2,1)S(1)}, bf16[528,128]{1,0:T(8,128)(2,1)S(1)}) custom-call(s32[8,32]{1,0:T(8,128)} %bitcast.1, bf16[8,2,256,256]{3,2,1,0:T(8,128)(2,1)} %esp_ref.1, bf16[528,128]{1,0:T(8,128)(2,1)S(1)} %collective-permute-done.refs_2_.piece_ref, ...), custom_call_target="tpu_custom_call" | custom-call | tf_op jit(solution)/shard_map/stage/pallas_call | solution.py:288
  20.5 0.5 %collective-permute-start.10 = (bf16[528,128]{1,0:T(8,128)(2,1)S(1)}, bf16[528,128]{1,0:T(8,128)(2,1)S(1)}, u32[]{:S(2)}, u32[]{:S(2)}) collective-permute-start(bf16[528,128]{1,0:T(8,128)(2,1)S(1)} %collective-permute-done.3.refs_0_.refs_3_), channel_id=1, source_target_pairs={{0,4},{4,0},{8,12},{12,8},{1,5},{5,1},{9,13},{13,9},{2,6},{6,2},{1... | collective-permute-start | bytes 405512 | tf_op jit(solution)/shard_map/ppermute | solution.py:308
  21.5 0.8 %collective-permute-done.6.refs_7_ = bf16[528,128]{1,0:T(8,128)(2,1)S(1)} collective-permute-done((bf16[528,128]{1,0:T(8,128)(2,1)S(1)}, bf16[528,128]{1,0:T(8,128)(2,1)S(1)}, u32[]{:S(2)}, u32[]{:S(2)}) %collective-permute-start.6) | collective-permute-done | bytes 135200 | tf_op jit(solution)/shard_map/ppermute | solution.py:251
  22.6 1.1 %collective-permute-done.14.refs_15_ = bf16[528,128]{1,0:T(8,128)(2,1)S(1)} collective-permute-done((bf16[528,128]{1,0:T(8,128)(2,1)S(1)}, bf16[528,128]{1,0:T(8,128)(2,1)S(1)}, u32[]{:S(2)}, u32[]{:S(2)}) %collective-permute-start.14) | collective-permute-done | bytes 135200 | tf_op jit(solution)/shard_map/ppermute | solution.py:308
  23.7 0.9 %couple_first.1 = (bf16[16,528,128]{2,1,0:T(8,128)(2,1)S(1)}, s32[264,128]{1,0:T(8,128)S(1)}) custom-call(s32[8,32]{1,0:T(8,128)S(4)} %get-tuple-element.12.nbr_ref, bf16[8,2,256,256]{3,2,1,0:T(8,128)(2,1)S(1)} %get-tuple-element.13.esp_ref, bf16[528,128]{1,0:T(8,128)(2,1)S(1)} %fold.1.refs_0_, bf16[528,128]{1,0:T(8,128)(2,1)S(1)} %collective-permute-done.2.refs_1_, ...), custom_call_target="tpu_custom_call" | custom-call | tf_op jit(solution)/shard_map/couple_first/pallas_call | solution.py:318
  24.6 2.4 %collective-permute-start.15 = (s32[264,128]{1,0:T(8,128)S(1)}, s32[264,128]{1,0:T(8,128)S(1)}, u32[]{:S(2)}, u32[]{:S(2)}) collective-permute-start(s32[264,128]{1,0:T(8,128)S(1)} %get-tuple-element.16), channel_id=1, source_target_pairs={{0,2},{1,3},{2,0},{3,1},{4,6},{5,7},{6,4},{7,5},{8,10},{9,11},{10,... | collective-permute-start | bytes 405512 | tf_op jit(solution)/shard_map/ppermute | solution.py:248
  27.0 1.3 %couple_rest.1 = (s32[264,128]{1,0:T(8,128)S(1)}, s32[264,128]{1,0:T(8,128)S(1)}) custom-call(s32[8,32]{1,0:T(8,128)S(4)} %get-tuple-element.12.nbr_ref, bf16[8,2,256,256]{3,2,1,0:T(8,128)(2,1)S(1)} %get-tuple-element.13.esp_ref, bf16[16,528,128]{2,1,0:T(8,128)(2,1)S(1)} %get-tuple-element.15.refs_0_), custom_call_target="tpu_custom_call" | custom-call | tf_op jit(solution)/shard_map/couple_rest/pallas_call | solution.py:318
  28.4 2.5 %collective-permute-start.16 = (s32[264,128]{1,0:T(8,128)S(1)}, s32[264,128]{1,0:T(8,128)S(1)}, u32[]{:S(2)}, u32[]{:S(2)}) collective-permute-start(s32[264,128]{1,0:T(8,128)S(1)} %get-tuple-element.17), channel_id=1, source_target_pairs={{0,1},{1,0},{2,3},{3,2},{4,5},{5,4},{6,7},{7,6},{8,9},{9,8},{10,11... | collective-permute-start | bytes 405512 | tf_op jit(solution)/shard_map/ppermute | solution.py:248
  30.9 0.7 %couple_own.1.plain_ref = f32[2,264,128]{2,1,0:T(8,128)S(1)} custom-call(s32[8,32]{1,0:T(8,128)S(4)} %get-tuple-element.12.nbr_ref, bf16[8,2,256,256]{3,2,1,0:T(8,128)(2,1)S(1)} %get-tuple-element.13.esp_ref, bf16[16,528,128]{2,1,0:T(8,128)(2,1)S(1)} %get-tuple-element.15.refs_0_), custom_call_target="tpu_custom_call" | custom-call | tf_op jit(solution)/shard_map/couple_own/pallas_call | solution.py:318
  31.6 3.3 %collective-permute-done.15.piece_ref = s32[264,128]{1,0:T(8,128)S(1)} collective-permute-done((s32[264,128]{1,0:T(8,128)S(1)}, s32[264,128]{1,0:T(8,128)S(1)}, u32[]{:S(2)}, u32[]{:S(2)}) %collective-permute-start.15) | collective-permute-done | bytes 135200 | tf_op jit(solution)/shard_map/ppermute | solution.py:248
  35.1 0.9 %collective-permute-done.16.refs_0_ = s32[264,128]{1,0:T(8,128)S(1)} collective-permute-done((s32[264,128]{1,0:T(8,128)S(1)}, s32[264,128]{1,0:T(8,128)S(1)}, u32[]{:S(2)}, u32[]{:S(2)}) %collective-permute-start.16) | collective-permute-done | bytes 135200 | tf_op jit(solution)/shard_map/ppermute | solution.py:248
  36.1 2.7 %collective-permute-done.17.refs_0_ = s32[264,128]{1,0:T(8,128)S(1)} collective-permute-done((s32[264,128]{1,0:T(8,128)S(1)}, s32[264,128]{1,0:T(8,128)S(1)}, u32[]{:S(2)}, u32[]{:S(2)}) %collective-permute-start.17) | collective-permute-done | bytes 135200 | tf_op jit(solution)/shard_map/ppermute | solution.py:248
  38.8 0.9 %finish.1 = f32[2,256,256]{2,1,0:T(8,128)} custom-call(bf16[2,256,256]{2,1,0:T(8,128)(2,1)S(1)} %copy-done, f32[2,264,128]{2,1,0:T(8,128)S(1)} %add.3.own_ref, s32[264,128]{1,0:T(8,128)S(1)} %collective-permute-done.17.refs_0_), custom_call_target="tpu_custom_call" | custom-call | tf_op jit(solution)/shard_map/finish/pallas_call | solution.py:348
  (29 shorter events, 1.2 us)
Async XLA Ops:
  1.0 10.7 %collective-permute-start.1 = (bf16[528,128]{1,0:T(8,128)(2,1)S(1)}, bf16[528,128]{1,0:T(8,128)(2,1)S(1)}, u32[]{:S(2)}, u32[]{:S(2)}) collective-permute-start(bf16[528,128]{1,0:T(8,128)(2,1)S(1)} %fold.1.refs_0_), channel_id=1, source_target_pairs={{0,2},{1,3},{2,0},{3,1},{4,6},{5,7},{6,4},{7,5},{8,10},{9,11},{10,... | collective-permute-start | bytes 405512 | tf_op jit(solution)/shard_map/ppermute | solution.py:248
  5.1 6.8 %collective-permute-start.2 = (bf16[528,128]{1,0:T(8,128)(2,1)S(1)}, bf16[528,128]{1,0:T(8,128)(2,1)S(1)}, u32[]{:S(2)}, u32[]{:S(2)}) collective-permute-start(bf16[528,128]{1,0:T(8,128)(2,1)S(1)} %fold.1.refs_0_), channel_id=1, source_target_pairs={{0,1},{1,0},{2,3},{3,2},{4,5},{5,4},{6,7},{7,6},{8,9},{9,8},{10,11... | collective-permute-start | bytes 405512 | tf_op jit(solution)/shard_map/ppermute | solution.py:248
  6.7 5.2 %collective-permute-start = (bf16[528,128]{1,0:T(8,128)(2,1)S(1)}, bf16[528,128]{1,0:T(8,128)(2,1)S(1)}, u32[]{:S(2)}, u32[]{:S(2)}) collective-permute-start(bf16[528,128]{1,0:T(8,128)(2,1)S(1)} %fold.1.refs_0_), channel_id=1, source_target_pairs={{0,8},{4,12},{8,0},{12,4},{1,9},{5,13},{9,1},{13,5},{2,10},{6,14},... | collective-permute-start | bytes 405512 | tf_op jit(solution)/shard_map/ppermute | solution.py:251
  8.2 7.3 %collective-permute-start.7 = (bf16[528,128]{1,0:T(8,128)(2,1)S(1)}, bf16[528,128]{1,0:T(8,128)(2,1)S(1)}, u32[]{:S(2)}, u32[]{:S(2)}) collective-permute-start(bf16[528,128]{1,0:T(8,128)(2,1)S(1)} %fold.1.refs_0_), channel_id=1, source_target_pairs={{0,4},{4,0},{8,12},{12,8},{1,5},{5,1},{9,13},{13,9},{2,6},{6,2},{1... | collective-permute-start | bytes 405512 | tf_op jit(solution)/shard_map/ppermute | solution.py:308
  11.9 5.1 %collective-permute-start.3 = (bf16[528,128]{1,0:T(8,128)(2,1)S(1)}, bf16[528,128]{1,0:T(8,128)(2,1)S(1)}, u32[]{:S(2)}, u32[]{:S(2)}) collective-permute-start(bf16[528,128]{1,0:T(8,128)(2,1)S(1)} %gate.8.refs_2_), channel_id=1, source_target_pairs={{0,1},{1,0},{2,3},{3,2},{4,5},{5,4},{6,7},{7,6},{8,9},{9,8},{10,11... | collective-permute-start | bytes 405512 | tf_op jit(solution)/shard_map/ppermute | solution.py:248
  13.4 7.0 %collective-permute-start.8 = (bf16[528,128]{1,0:T(8,128)(2,1)S(1)}, bf16[528,128]{1,0:T(8,128)(2,1)S(1)}, u32[]{:S(2)}, u32[]{:S(2)}) collective-permute-start(bf16[528,128]{1,0:T(8,128)(2,1)S(1)} %collective-permute-done.2.refs_1_), channel_id=1, source_target_pairs={{0,4},{4,0},{8,12},{12,8},{1,5},{5,1},{9,13},{13,9},{2,6},{6,2},{1... | collective-permute-start | bytes 405512 | tf_op jit(solution)/shard_map/ppermute | solution.py:308
  13.4 7.1 %collective-permute-start.9 = (bf16[528,128]{1,0:T(8,128)(2,1)S(1)}, bf16[528,128]{1,0:T(8,128)(2,1)S(1)}, u32[]{:S(2)}, u32[]{:S(2)}) collective-permute-start(bf16[528,128]{1,0:T(8,128)(2,1)S(1)} %gate.8.refs_2_), channel_id=1, source_target_pairs={{0,4},{4,0},{8,12},{12,8},{1,5},{5,1},{9,13},{13,9},{2,6},{6,2},{1... | collective-permute-start | bytes 405512 | tf_op jit(solution)/shard_map/ppermute | solution.py:308
  13.9 7.1 %collective-permute-start.5 = (bf16[528,128]{1,0:T(8,128)(2,1)S(1)}, bf16[528,128]{1,0:T(8,128)(2,1)S(1)}, u32[]{:S(2)}, u32[]{:S(2)}) collective-permute-start(bf16[528,128]{1,0:T(8,128)(2,1)S(1)} %gate.8.refs_2_), channel_id=1, source_target_pairs={{0,8},{4,12},{8,0},{12,4},{1,9},{5,13},{9,1},{13,5},{2,10},{6,14},... | collective-permute-start | bytes 405512 | tf_op jit(solution)/shard_map/ppermute | solution.py:251
  15.5 5.6 %collective-permute-start.4 = (bf16[528,128]{1,0:T(8,128)(2,1)S(1)}, bf16[528,128]{1,0:T(8,128)(2,1)S(1)}, u32[]{:S(2)}, u32[]{:S(2)}) collective-permute-start(bf16[528,128]{1,0:T(8,128)(2,1)S(1)} %collective-permute-done.refs_2_.piece_ref), channel_id=1, source_target_pairs={{0,1},{1,0},{2,3},{3,2},{4,5},{5,4},{6,7},{7,6},{8,9},{9,8},{10,11... | collective-permute-start | bytes 405512 | tf_op jit(solution)/shard_map/ppermute | solution.py:248
  17.0 5.3 %collective-permute-start.6 = (bf16[528,128]{1,0:T(8,128)(2,1)S(1)}, bf16[528,128]{1,0:T(8,128)(2,1)S(1)}, u32[]{:S(2)}, u32[]{:S(2)}) collective-permute-start(bf16[528,128]{1,0:T(8,128)(2,1)S(1)} %collective-permute-done.3.refs_0_.refs_3_), channel_id=1, source_target_pairs={{0,8},{4,12},{8,0},{12,4},{1,9},{5,13},{9,1},{13,5},{2,10},{6,14},... | collective-permute-start | bytes 405512 | tf_op jit(solution)/shard_map/ppermute | solution.py:251
  20.4 2.1 %collective-permute-start.11 = (bf16[528,128]{1,0:T(8,128)(2,1)S(1)}, bf16[528,128]{1,0:T(8,128)(2,1)S(1)}, u32[]{:S(2)}, u32[]{:S(2)}) collective-permute-start(bf16[528,128]{1,0:T(8,128)(2,1)S(1)} %get-tuple-element.14.refs_4_), channel_id=1, source_target_pairs={{0,4},{4,0},{8,12},{12,8},{1,5},{5,1},{9,13},{13,9},{2,6},{6,2},{1... | collective-permute-start | bytes 405512 | tf_op jit(solution)/shard_map/ppermute | solution.py:308
  20.5 1.9 %collective-permute-start.10 = (bf16[528,128]{1,0:T(8,128)(2,1)S(1)}, bf16[528,128]{1,0:T(8,128)(2,1)S(1)}, u32[]{:S(2)}, u32[]{:S(2)}) collective-permute-start(bf16[528,128]{1,0:T(8,128)(2,1)S(1)} %collective-permute-done.3.refs_0_.refs_3_), channel_id=1, source_target_pairs={{0,4},{4,0},{8,12},{12,8},{1,5},{5,1},{9,13},{13,9},{2,6},{6,2},{1... | collective-permute-start | bytes 405512 | tf_op jit(solution)/shard_map/ppermute | solution.py:308
  21.0 1.4 %collective-permute-start.13 = (bf16[528,128]{1,0:T(8,128)(2,1)S(1)}, bf16[528,128]{1,0:T(8,128)(2,1)S(1)}, u32[]{:S(2)}, u32[]{:S(2)}) collective-permute-start(bf16[528,128]{1,0:T(8,128)(2,1)S(1)} %collective-permute-done.5.refs_6_), channel_id=1, source_target_pairs={{0,4},{4,0},{8,12},{12,8},{1,5},{5,1},{9,13},{13,9},{2,6},{6,2},{1... | collective-permute-start | bytes 405512 | tf_op jit(solution)/shard_map/ppermute | solution.py:308
  21.1 1.5 %collective-permute-start.12 = (bf16[528,128]{1,0:T(8,128)(2,1)S(1)}, bf16[528,128]{1,0:T(8,128)(2,1)S(1)}, u32[]{:S(2)}, u32[]{:S(2)}) collective-permute-start(bf16[528,128]{1,0:T(8,128)(2,1)S(1)} %collective-permute-done.4.refs_5_), channel_id=1, source_target_pairs={{0,4},{4,0},{8,12},{12,8},{1,5},{5,1},{9,13},{13,9},{2,6},{6,2},{1... | collective-permute-start | bytes 405512 | tf_op jit(solution)/shard_map/ppermute | solution.py:308
  22.3 1.4 %collective-permute-start.14 = (bf16[528,128]{1,0:T(8,128)(2,1)S(1)}, bf16[528,128]{1,0:T(8,128)(2,1)S(1)}, u32[]{:S(2)}, u32[]{:S(2)}) collective-permute-start(bf16[528,128]{1,0:T(8,128)(2,1)S(1)} %collective-permute-done.6.refs_7_), channel_id=1, source_target_pairs={{0,4},{4,0},{8,12},{12,8},{1,5},{5,1},{9,13},{13,9},{2,6},{6,2},{1... | collective-permute-start | bytes 405512 | tf_op jit(solution)/shard_map/ppermute | solution.py:308
  24.6 10.3 %collective-permute-start.15 = (s32[264,128]{1,0:T(8,128)S(1)}, s32[264,128]{1,0:T(8,128)S(1)}, u32[]{:S(2)}, u32[]{:S(2)}) collective-permute-start(s32[264,128]{1,0:T(8,128)S(1)} %get-tuple-element.16), channel_id=1, source_target_pairs={{0,2},{1,3},{2,0},{3,1},{4,6},{5,7},{6,4},{7,5},{8,10},{9,11},{10,... | collective-permute-start | bytes 405512 | tf_op jit(solution)/shard_map/ppermute | solution.py:248
  28.4 7.6 %collective-permute-start.16 = (s32[264,128]{1,0:T(8,128)S(1)}, s32[264,128]{1,0:T(8,128)S(1)}, u32[]{:S(2)}, u32[]{:S(2)}) collective-permute-start(s32[264,128]{1,0:T(8,128)S(1)} %get-tuple-element.17), channel_id=1, source_target_pairs={{0,1},{1,0},{2,3},{3,2},{4,5},{5,4},{6,7},{7,6},{8,9},{9,8},{10,11... | collective-permute-start | bytes 405512 | tf_op jit(solution)/shard_map/ppermute | solution.py:248
  30.9 7.9 %collective-permute-start.17 = (s32[264,128]{1,0:T(8,128)S(1)}, s32[264,128]{1,0:T(8,128)S(1)}, u32[]{:S(2)}, u32[]{:S(2)}) collective-permute-start(s32[264,128]{1,0:T(8,128)S(1)} %get-tuple-element.18), channel_id=1, source_target_pairs={{0,3},{1,2},{2,1},{3,0},{4,7},{5,6},{6,5},{7,4},{8,11},{9,10},{10,... | collective-permute-start | bytes 405512 | tf_op jit(solution)/shard_map/ppermute | solution.py:248
  31.6 7.2 %copy-start = (bf16[2,256,256]{2,1,0:T(8,128)(2,1)S(1)}, bf16[2,256,256]{2,1,0:T(8,128)(2,1)}, u32[]{:S(2)}) copy-start(bf16[2,256,256]{2,1,0:T(8,128)(2,1)} %core_ref.1) | copy-start | bytes 786436
